TPU v7x, 32 devices: a whole 2x2x4 slice. The times are simulated.
32 devices in a mesh: ctx: 8 (over z, core), fsdp: 4 (over y, x).
Axes of the slice: x: 2, y: 2, z: 4, core: 2. Of those that a mesh axis runs over, the one named last changes fastest.
Arguments:
- inputs: bfloat16 [4, 4096, 1280], P('fsdp', 'ctx'), may hold values from -6 to 6
- cotangent: bfloat16 [4, 4096, 1280], P('fsdp', 'ctx'), may hold values from -6 to 6
- block_order: int32 [4, 16], P('fsdp'), may hold values from 0 to 15, each once within a row
- w_qkv: float32 [1280, 3840], P('fsdp'), may hold values from -0.15625 to 0.15625
- m_qkv: float32 [1280, 3840], P('fsdp'), may hold values from -768 to 768
- v_qkv: float32 [1280, 3840], P('fsdp'), may hold values from 16384 to 65536
- w_out: float32 [1280, 1280], P('fsdp'), may hold values from -2.5 to 2.5
- m_out: float32 [1280, 1280], P('fsdp'), may hold values from -64 to 64
- v_out: float32 [1280, 1280], P('fsdp'), may hold values from 124 to 496
- w_up: float32 [1280, 1280], P('fsdp'), may hold values from -0.15625 to 0.15625
- m_up: float32 [1280, 1280], P('fsdp'), may hold values from -384 to 384
- v_up: float32 [1280, 1280], P('fsdp'), may hold values from 4096 to 16384
- w_down: float32 [1280, 1280], P('fsdp'), may hold values from -0.15625 to 0.15625
- m_down: float32 [1280, 1280], P('fsdp'), may hold values from -448 to 448
- v_down: float32 [1280, 1280], P('fsdp'), may hold values from 5898.24 to 23592.96
- small_params: float32 [2640], replicated, may hold values from -1 to 2, as said below
- small_m: float32 [2640], replicated, may hold values from -576 to 576
- small_v: float32 [2640], replicated, may hold values from 4096 to 147456
Outputs:
- output: bfloat16 [4, 4096, 1280], P('fsdp', 'ctx')
- input_grad: bfloat16 [4, 4096, 1280], P('fsdp', 'ctx')
- qkv_new: float32 [1280, 3840], P('fsdp')
- qkv_first: float32 [1280, 3840], P('fsdp')
- qkv_second: float32 [1280, 3840], P('fsdp')
- qkv_low: bfloat16 [1280, 3840], P('fsdp')
- out_new: float32 [1280, 1280], P('fsdp')
- out_first: float32 [1280, 1280], P('fsdp')
- out_second: float32 [1280, 1280], P('fsdp')
- out_low: bfloat16 [1280, 1280], P('fsdp')
- up_new: float32 [1280, 1280], P('fsdp')
- up_first: float32 [1280, 1280], P('fsdp')
- up_second: float32 [1280, 1280], P('fsdp')
- up_low: bfloat16 [1280, 1280], P('fsdp')
- down_new: float32 [1280, 1280], P('fsdp')
- down_first: float32 [1280, 1280], P('fsdp')
- down_second: float32 [1280, 1280], P('fsdp')
- down_low: bfloat16 [1280, 1280], P('fsdp')
- small_new: float32 [2640], replicated
- small_first: float32 [2640], replicated
- small_second: float32 [2640], replicated
Inputs may be any that keep to these rules, and one draw needn't show every extreme that they name: `block_order`: each row lists the 16 causal blocks of its group once each. ctx index c holds the blocks at entries 2 c to 2 c + 1, in that order. Blocks below 8 form the prompt in order; block 8 + j is part (j % 2) of continuation j // 2. `small_params`: entries 0 to 2559 are gains; the last 80 are query scale parameters.
All inputs are finite; a program needn't handle non-finite values.
Results may differ from a plain program's by a relative error of at most 0.025.
Values may be sent and summed in bfloat16 or wider, within the bound.
A program may use at most 384 MiB of HBM per device.

v0:
```python
import functools
import math

import jax
import jax.numpy as jnp
from jax import lax
from jax.sharding import PartitionSpec as P

D = 1280
H = 16
HD = 80
FF = 1280
BLOCK = 256
CONT = 512
STEP = 3


norm_eps = 1e-06
beta_one = 0.5
beta_two = 0.5
adam_eps = 1e-08
decay_rate = 0.1
small_rate = 0.75
qkv_rate_base = 1.0
scale_base = 1.442695


def token_layout(block_ids):
    num_blocks = block_ids.shape[0]
    prompt_blocks = num_blocks // 2
    cont_blocks = CONT // BLOCK
    later = block_ids - prompt_blocks
    block_seg = jnp.where(block_ids < prompt_blocks, 0, 1 + later // cont_blocks)
    block_base = jnp.where(
        block_ids < prompt_blocks, block_ids * BLOCK, (prompt_blocks + later % cont_blocks) * BLOCK
    )
    offset = jnp.arange(BLOCK, dtype=jnp.int32)
    seg_ids = jnp.broadcast_to(block_seg[:, None], (num_blocks, BLOCK)).reshape(-1)
    positions = (block_base[:, None] + offset[None, :]).reshape(-1)
    return (seg_ids, positions)


def pair_mask(seg_query, pos_query, seg_key, pos_key):
    same_doc = (seg_key[None, :] == 0) | (seg_key[None, :] == seg_query[:, None])
    return (same_doc & (pos_key[None, :] <= pos_query[:, None]))[None]


def rms_scale(values):
    return lax.rsqrt(jnp.mean(values * values, axis=-1, keepdims=True) + norm_eps)


def head_scores(query_heads, key_heads):
    return jnp.einsum("qhd,khd->hqk", query_heads, key_heads, preferred_element_type=jnp.float32)


def adamw(weight, first, second, gradient, step_rate, decay_on):
    first_new = beta_one * first + (1.0 - beta_one) * gradient
    second_new = beta_two * second + (1.0 - beta_two) * gradient * gradient
    corr_one = 1.0 - beta_one**STEP
    corr_two = 1.0 - beta_two**STEP
    update = first_new / corr_one / (jnp.sqrt(second_new / corr_two) + adam_eps)
    weight_new = weight - step_rate * (update + decay_on * weight)
    return (weight_new, first_new, second_new)


def body(
    inputs,
    cotangent,
    block_order,
    w_qkv,
    m_qkv,
    v_qkv,
    w_out,
    m_out,
    v_out,
    w_up,
    m_up,
    v_up,
    w_down,
    m_down,
    v_down,
    small_params,
    small_m,
    small_v,
):
    rows_dev = inputs.shape[1]
    bf16 = jnp.bfloat16
    f32 = jnp.float32
    qkv_full, out_full, up_full, down_full = (
        lax.all_gather(w_qkv.astype(bf16), "fsdp", axis=0, tiled=True),
        lax.all_gather(w_out.astype(bf16), "fsdp", axis=0, tiled=True),
        lax.all_gather(w_up.astype(bf16), "fsdp", axis=0, tiled=True),
        lax.all_gather(w_down.astype(bf16), "fsdp", axis=0, tiled=True),
    )
    seg_all, pos_all = token_layout(block_order[0])
    here_row = lax.axis_index("ctx") * rows_dev
    seg_here = lax.dynamic_slice_in_dim(seg_all, here_row, rows_dev, 0)
    pos_here = lax.dynamic_slice_in_dim(pos_all, here_row, rows_dev, 0)
    gain_one = small_params[:D]
    gain_two = small_params[D : 2 * D]
    query_scale = small_params[2 * D :]
    layer_in = inputs[0].astype(f32)
    scale_one = rms_scale(layer_in)
    unit_one = layer_in * scale_one
    normed = (unit_one * gain_one).astype(bf16)
    qkv = jnp.dot(normed, qkv_full, preferred_element_type=f32)
    factor = scale_base / math.sqrt(HD) * jax.nn.softplus(query_scale)
    query_raw = qkv[:, :D].reshape(rows_dev, H, HD)
    queries = (query_raw * factor).astype(bf16)
    keys_here = qkv[:, D : 2 * D].astype(bf16)
    values_here = qkv[:, 2 * D :].astype(bf16)
    keys_all, values_all = (
        lax.all_gather(keys_here, "ctx", axis=0, tiled=True),
        lax.all_gather(values_here, "ctx", axis=0, tiled=True),
    )
    key_total = keys_all.shape[0]
    key_block = math.gcd(key_total, 512)
    num_blocks = key_total // key_block
    key_stack = (
        keys_all.reshape(num_blocks, key_block, H, HD),
        values_all.reshape(num_blocks, key_block, H, HD),
        seg_all.reshape(num_blocks, key_block),
        pos_all.reshape(num_blocks, key_block),
    )

    def stat_step(running, key_set):
        row_top, row_mass = running
        scores = head_scores(queries, key_set[0])
        allowed = pair_mask(seg_here, pos_here, key_set[2], key_set[3])
        block_top = jnp.max(jnp.where(allowed, scores, -1e30), axis=-1)
        new_top = jnp.maximum(row_top, block_top)
        row_mass = row_mass * jnp.exp(row_top - new_top) + jnp.sum(
            jnp.where(allowed, jnp.exp(scores - new_top[..., None]), 0.0), axis=-1
        )
        return ((new_top, row_mass), None)

    start_stats = (jnp.full((H, rows_dev), -1e30, f32), jnp.zeros((H, rows_dev), f32))
    (row_top, row_mass), unused = lax.scan(stat_step, start_stats, key_stack)
    row_lse = row_top + jnp.log(row_mass)

    def value_step(mixed_acc, key_set):
        scores = head_scores(queries, key_set[0])
        allowed = pair_mask(seg_here, pos_here, key_set[2], key_set[3])
        prob_rows = jnp.where(allowed, jnp.exp(scores - row_lse[..., None]), 0.0).astype(bf16)
        return (
            mixed_acc
            + jnp.einsum("hqk,khd->qhd", prob_rows, key_set[1], preferred_element_type=f32),
            None,
        )

    mixed, unused = lax.scan(value_step, jnp.zeros((rows_dev, H, HD), f32), key_stack)
    attn_low = mixed.reshape(rows_dev, D).astype(bf16)
    mid = layer_in + jnp.dot(attn_low, out_full, preferred_element_type=f32)
    scale_two = rms_scale(mid)
    unit_two = mid * scale_two
    normed_two = (unit_two * gain_two).astype(bf16)
    hidden = jnp.dot(normed_two, up_full, preferred_element_type=f32)
    gate_sig = jax.nn.sigmoid(hidden)
    act = (hidden * gate_sig).astype(bf16)
    output = (mid + jnp.dot(act, down_full, preferred_element_type=f32)).astype(bf16)
    grad_in = cotangent[0]
    grad_down = jnp.dot(act.T, grad_in, preferred_element_type=f32)
    dact = jnp.dot(grad_in, down_full.T, preferred_element_type=f32)
    dhidden = (dact * gate_sig * (1.0 + hidden * (1.0 - gate_sig))).astype(bf16)
    grad_up = jnp.dot(normed_two.T, dhidden, preferred_element_type=f32)
    dnormed_two = jnp.dot(dhidden, up_full.T, preferred_element_type=f32)
    dunit_two = dnormed_two * gain_two
    dmid = grad_in.astype(f32) + scale_two * (
        dunit_two - unit_two * jnp.mean(dunit_two * unit_two, axis=-1, keepdims=True)
    )
    gain_two_grad = jnp.sum(dnormed_two * unit_two, axis=0)
    dbranch = dmid.astype(bf16)
    grad_out = jnp.dot(attn_low.T, dbranch, preferred_element_type=f32)
    dattn = jnp.dot(dbranch, out_full.T, preferred_element_type=f32).astype(bf16)
    dattn_heads = dattn.reshape(rows_dev, H, HD)
    row_delta = jnp.sum(dattn_heads.astype(f32) * mixed, axis=-1).T

    def back_step(dq_acc, key_set, want_keys):
        scores = head_scores(queries, key_set[0])
        allowed = pair_mask(seg_here, pos_here, key_set[2], key_set[3])
        prob_rows = jnp.where(allowed, jnp.exp(scores - row_lse[..., None]), 0.0)
        grad_probs = jnp.einsum("qhd,khd->hqk", dattn_heads, key_set[1], preferred_element_type=f32)
        grad_scores = (prob_rows * (grad_probs - row_delta[..., None])).astype(bf16)
        dq_acc = dq_acc + jnp.einsum(
            "hqk,khd->qhd", grad_scores, key_set[0], preferred_element_type=f32
        )
        grad_keys = jnp.einsum("hqk,qhd->khd", grad_scores, queries, preferred_element_type=f32)
        grad_values = jnp.einsum(
            "hqk,qhd->khd", prob_rows.astype(bf16), dattn_heads, preferred_element_type=f32
        )
        return (dq_acc, (grad_keys.reshape(-1, D), grad_values.reshape(-1, D)))

    dq_start = jnp.zeros((rows_dev, H, HD), f32)
    dq_acc, key_parts = lax.scan(functools.partial(back_step, want_keys=True), dq_start, key_stack)
    dkeys_all = key_parts[0].reshape(key_total, D)
    dvalues_all = key_parts[1].reshape(key_total, D)
    dkeys_here, dvalues_here = (
        lax.psum_scatter(
            dkeys_all.astype(jnp.bfloat16), "ctx", scatter_dimension=0, tiled=True
        ).astype(jnp.float32),
        lax.psum_scatter(
            dvalues_all.astype(jnp.bfloat16), "ctx", scatter_dimension=0, tiled=True
        ).astype(jnp.float32),
    )
    dqkv = jnp.concatenate(
        [(dq_acc * factor).reshape(rows_dev, D), dkeys_here, dvalues_here], axis=1
    ).astype(bf16)
    scale_grad = (
        jnp.sum(dq_acc * query_raw, axis=(0, 1))
        * (scale_base / math.sqrt(HD))
        * jax.nn.sigmoid(query_scale)
    )
    grad_qkv = jnp.dot(normed.T, dqkv, preferred_element_type=f32)
    dnormed = jnp.dot(dqkv, qkv_full.T, preferred_element_type=f32)
    dunit_one = dnormed * gain_one
    input_grad = dmid + scale_one * (
        dunit_one - unit_one * jnp.mean(dunit_one * unit_one, axis=-1, keepdims=True)
    )
    gain_one_grad = jnp.sum(dnormed * unit_one, axis=0)
    small_grad = jnp.concatenate([gain_one_grad, gain_two_grad, scale_grad])
    small_total = lax.psum(small_grad, ("ctx", "fsdp"))
    rate_qkv = qkv_rate_base / math.sqrt(D)
    rate_out = 0.5 / math.sqrt(max(D // 256, 1))
    rate_up = 0.5 / math.sqrt(D)
    rate_down = 0.5 / math.sqrt(FF)
    shard_qkv, shard_out, shard_up, shard_down = (
        lax.psum_scatter(
            grad_qkv.astype(jnp.bfloat16), "fsdp", scatter_dimension=0, tiled=True
        ).astype(jnp.float32),
        lax.psum_scatter(
            grad_out.astype(jnp.bfloat16), "fsdp", scatter_dimension=0, tiled=True
        ).astype(jnp.float32),
        lax.psum_scatter(
            grad_up.astype(jnp.bfloat16), "fsdp", scatter_dimension=0, tiled=True
        ).astype(jnp.float32),
        lax.psum_scatter(
            grad_down.astype(jnp.bfloat16), "fsdp", scatter_dimension=0, tiled=True
        ).astype(jnp.float32),
    )
    total_qkv, total_out, total_up, total_down = (
        lax.psum(shard_qkv.astype(jnp.bfloat16), "ctx").astype(jnp.float32),
        lax.psum(shard_out.astype(jnp.bfloat16), "ctx").astype(jnp.float32),
        lax.psum(shard_up.astype(jnp.bfloat16), "ctx").astype(jnp.float32),
        lax.psum(shard_down.astype(jnp.bfloat16), "ctx").astype(jnp.float32),
    )
    qkv_set = adamw(w_qkv, m_qkv, v_qkv, total_qkv, rate_qkv, decay_rate)
    out_set = adamw(w_out, m_out, v_out, total_out, rate_out, decay_rate)
    up_set = adamw(w_up, m_up, v_up, total_up, rate_up, decay_rate)
    down_set = adamw(w_down, m_down, v_down, total_down, rate_down, decay_rate)
    small_set = adamw(small_params, small_m, small_v, small_total, small_rate, 0.0)
    return (
        output[None],
        input_grad.astype(bf16)[None],
        qkv_set[0],
        qkv_set[1],
        qkv_set[2],
        qkv_set[0].astype(bf16),
        out_set[0],
        out_set[1],
        out_set[2],
        out_set[0].astype(bf16),
        up_set[0],
        up_set[1],
        up_set[2],
        up_set[0].astype(bf16),
        down_set[0],
        down_set[1],
        down_set[2],
        down_set[0].astype(bf16),
        small_set[0],
        small_set[1],
        small_set[2],
    )


def solution(mesh):
    in_specs = (
        P("fsdp", "ctx", None),
        P("fsdp", "ctx", None),
        P("fsdp", None),
        P("fsdp", None),
        P("fsdp", None),
        P("fsdp", None),
        P("fsdp", None),
        P("fsdp", None),
        P("fsdp", None),
        P("fsdp", None),
        P("fsdp", None),
        P("fsdp", None),
        P("fsdp", None),
        P("fsdp", None),
        P("fsdp", None),
        P(),
        P(),
        P(),
    )
    out_specs = (
        P("fsdp", "ctx", None),
        P("fsdp", "ctx", None),
        P("fsdp", None),
        P("fsdp", None),
        P("fsdp", None),
        P("fsdp", None),
        P("fsdp", None),
        P("fsdp", None),
        P("fsdp", None),
        P("fsdp", None),
        P("fsdp", None),
        P("fsdp", None),
        P("fsdp", None),
        P("fsdp", None),
        P("fsdp", None),
        P("fsdp", None),
        P("fsdp", None),
        P("fsdp", None),
        P(),
        P(),
        P(),
    )
    return jax.shard_map(body, mesh=mesh, in_specs=in_specs, out_specs=out_specs, check_vma=False)
```

profile of v0, /device:TPU:0, one launch (start us, length us, event | category | flops | bytes accessed | tf_op | source)
XLA Modules:
  0.0 1684.9 jit_solution(14041899212990422532)
XLA Ops:
  13.6 100.2 %all-gather.7.cloned.1.call-done = bf16[1280,3840]{1,0:T(8,128)(2,1)} async-done(((bf16[320,3840]{1,0:T(8,128)(2,1)}), bf16[1280,3840]{1,0:T(8,128)(2,1)}) %all-gather.7.cloned.1.call-update) | async-done | bytes 9830416 | tf_op jit(solution)/shard_map/all_gather | solution.py:90
  113.8 11.3 fusion.97
  142.8 83.6 %all-gather.11.cloned.1.call-done = bf16[4096,1280]{1,0:T(8,128)(2,1)} async-done(((bf16[512,1280]{1,0:T(8,128)(2,1)}), bf16[4096,1280]{1,0:T(8,128)(2,1)}) %all-gather.11.cloned.1.call-update) | async-done | bytes 10485776 | tf_op jit(solution)/shard_map/all_gather | solution.py:113
  226.4 14.5 copy.59
  240.9 15.1 copy.93
  256.0 16.3 copy.63
  272.4 11.7 copy.61
  284.1 42.4 %all-gather.9.cloned.1.call-done = bf16[4096,1280]{1,0:T(8,128)(2,1)} async-done(((bf16[512,1280]{1,0:T(8,128)(2,1)}), bf16[4096,1280]{1,0:T(8,128)(2,1)}) %all-gather.9.cloned.1.call-update) | async-done | bytes 10485776 | tf_op jit(solution)/shard_map/all_gather | solution.py:114
  326.4 29.8 %reshape.410 = bf16[8,512,16,80]{3,2,1,0:T(8,128)(2,1)} reshape(bf16[4096,1280]{1,0:T(8,128)(2,1)} %all-gather.9.cloned.1.call-done) | data formatting | bytes 20971520 | tf_op jit(solution)/shard_map/reshape | solution.py:121
  356.2 21.7 %copy.62 = bf16[8,512,16,80]{1,3,2,0:T(8,128)(2,1)} copy(bf16[8,512,16,80]{3,2,1,0:T(8,128)(2,1)} %reshape.410) | data formatting | bytes 20971520
  378.0 150.4 %while.39 = (s32[]{:T(128)}, f32[16,512]{1,0:T(8,128)S(1)}, f32[16,512]{1,0:T(8,128)S(1)}, s32[8,512]{1,0:T(8,128)S(1)}, s32[512]{0:T(512)S(1)}, /*index=5*/s32[...) while((s32[]{:T(128)}, f32[16,512]{1,0:T(8,128)S(1)}, ...), condition=%wide.region_4.5_spmd.clone, body=%wide.region_1.4_spmd.clone.sunk | while | flops 693150208 | bytes 37405832 | solution.py:138
  528.4 95.2 %while.40 = (s32[]{:T(128)}, f32[512,16,80]{0,2,1:T(8,128)}, bf16[8,512,16,80]{1,3,2,0:T(8,128)(2,1)}, s32[8,512]{1,0:T(8,128)S(1)}, s32[512]{0:T(512)S(1)}, /*i...) while((s32[]{:T(128)}, f32[512,16,80]{0,2,1:T(8,128)}, ...), condition=%wide.region_6.7_spmd.clone, body=%wide.region_5.6_spmd.clone.sunk | while | flops 1357120000 | bytes 13157527 | solution.py:151
  655.5 418.3 %while.41 = (s32[]{:T(128)}, f32[512,16,80]{0,2,1:T(8,128)}, bf16[8,512,1280]{2,1,0:T(8,128)(2,1)}, bf16[8,512,1280]{2,1,0:T(8,128)(2,1)}, bf16[8,512,16,80]{1,3...) while((s32[]{:T(128)}, f32[512,16,80]{0,2,1:T(8,128)}, ...), condition=%wide.region_11.12_spmd.clone, body=%wide.region_10.11_spmd.clone.sunk | while | flops 3391357440 | bytes 103924920 | solution.py:194
  665.3 11.1 fusion.157
  717.0 11.1 fusion.157
  735.5 9.9 fusion.158
  769.4 11.1 fusion.157
  821.7 11.1 fusion.157
  874.1 11.1 fusion.157
  926.4 11.1 fusion.157
  978.7 11.1 fusion.157
  1031.1 11.1 fusion.157
  1100.8 81.0 %reduce-scatter.9.cloned.1.call-done = bf16[512,1280]{1,0:T(8,128)(2,1)} async-done(((bf16[4096,1280]{1,0:T(8,128)(2,1)}), bf16[512,1280]{1,0:T(8,128)(2,1)}) %reduce-scatter.9.cloned.1.call-update) | async-done | bytes 1310736 | tf_op jit(solution)/shard_map/reduce_scatter | solution.py:201
  1181.9 110.1 %reduce-scatter.7.cloned.1.call-done = bf16[512,1280]{1,0:T(8,128)(2,1)} async-done(((bf16[4096,1280]{1,0:T(8,128)(2,1)}), bf16[512,1280]{1,0:T(8,128)(2,1)}) %reduce-scatter.7.cloned.1.call-update) | async-done | bytes 1310736 | tf_op jit(solution)/shard_map/reduce_scatter | solution.py:198
  1309.2 29.9 %reduce-scatter.13.cloned.1.call-done = bf16[320,1280]{1,0:T(8,128)(2,1)} async-done(((bf16[1280,1280]{1,0:T(8,128)(2,1)}), bf16[320,1280]{1,0:T(8,128)(2,1)}) %reduce-scatter.13.cloned.1.call-update) | async-done | bytes 819216 | tf_op jit(solution)/shard_map/reduce_scatter | solution.py:230
  1339.0 48.5 %reduce-scatter.15.cloned.1.call-done = bf16[320,1280]{1,0:T(8,128)(2,1)} async-done(((bf16[1280,1280]{1,0:T(8,128)(2,1)}), bf16[320,1280]{1,0:T(8,128)(2,1)}) %reduce-scatter.15.cloned.1.call-update) | async-done | bytes 819216 | tf_op jit(solution)/shard_map/reduce_scatter | solution.py:233
  1387.6 48.7 %reduce-scatter.17.cloned.1.call-done = bf16[320,1280]{1,0:T(8,128)(2,1)} async-done(((bf16[1280,1280]{1,0:T(8,128)(2,1)}), bf16[320,1280]{1,0:T(8,128)(2,1)}) %reduce-scatter.17.cloned.1.call-update) | async-done | bytes 819216 | tf_op jit(solution)/shard_map/reduce_scatter | solution.py:236
  1436.3 101.2 %reduce-scatter.11.cloned.1.call-done = bf16[320,3840]{1,0:T(8,128)(2,1)} async-done(((bf16[1280,3840]{1,0:T(8,128)(2,1)}), bf16[320,3840]{1,0:T(8,128)(2,1)}) %reduce-scatter.11.cloned.1.call-update) | async-done | bytes 2457616 | tf_op jit(solution)/shard_map/reduce_scatter | solution.py:227
  1537.5 10.9 fusion.56
  1548.4 41.1 %psum.39 = f32[2640]{0:T(1024)S(1)} all-reduce(f32[2640]{0:T(1024)S(1)} %pad_maximum_fusion.3), channel_id=1, replica_groups=mesh['ctx'=8,'fsdp'=4] {'ctx','fsdp'}, use_global_device_ids=true, to_apply=%region_26.27 | all-reduce | flops 2640 | bytes 21120 | tf_op jit(solution)/shard_map/psum | solution.py:221
  1594.5 57.8 %all-reduce.3.cloned.1.call-done = (bf16[320,3840]{1,0:T(8,128)(2,1)}, bf16[320,1280]{1,0:T(8,128)(2,1)}, bf16[320,1280]{1,0:T(8,128)(2,1)}, bf16[320,1280]{1,0:T(8,128)(2,1)}) async-done(((bf16[320,3840]{1,0:T(8,128)(2,1)}, bf16[320,1280]{1,0:T(8,128)(2,1)}, bf16[320,1280]{1,0:T(8,128)(2,1)}, bf16[320,1280]{1,0:T(8,128)(2,1)}), (bf16[320,3840]{1,0:T(8,128)(2,1)}, bf16[320,1280]{1,0:T(8,128)(2,1)}, ...) | async-done | bytes 4915216 | tf_op jit(solution)/shard_map/psum | solution.py:241
  1652.3 12.6 fusion.93
  (365 shorter events, 682.3 us)
Async XLA Ops:
  7.2 106.6 %all-gather.7.cloned.1.call-start = ((), (), s32[]{:S(2)}) async-start(), calls=%async_computation.6 | async-start | bytes 12288000 | tf_op jit(solution)/shard_map/all_gather | solution.py:90
  11.3 215.0 %all-gather.11.cloned.1.call-start = ((), (), s32[]{:S(2)}) async-start(), calls=%async_computation.8 | async-start | bytes 11796480 | tf_op jit(solution)/shard_map/all_gather | solution.py:113
  13.0 112.2 %copy-start.37 = (f32[512]{0:T(512)}, f32[512]{0:T(512)S(1)}, u32[]{:S(2)}) copy-start(f32[512]{0:T(512)S(1)} %add_rsqrt_fusion.1) | copy-start | bytes 6148
  13.6 111.5 %copy-start.30 = (f32[1280]{0:T(1024)}, f32[1280]{0:T(1024)S(1)}, u32[]{:S(2)}) copy-start(f32[1280]{0:T(1024)S(1)} %get-tuple-element.485) | copy-start | bytes 15364
  126.8 199.6 %all-gather.9.cloned.1.call-start = ((), (), s32[]{:S(2)}) async-start(), calls=%async_computation.7 | async-start | bytes 11796480 | tf_op jit(solution)/shard_map/all_gather | solution.py:114
  127.6 499.1 %all-gather.13.cloned.1.call-start = ((), (), s32[]{:S(2)}) async-start(), calls=%async_computation.9 | async-start | bytes 4096000 | tf_op jit(solution)/shard_map/all_gather | solution.py:91
  129.2 503.3 %all-gather.15.cloned.1.call-start = ((), (), s32[]{:S(2)}) async-start(), calls=%async_computation.10 | async-start | bytes 4096000 | tf_op jit(solution)/shard_map/all_gather | solution.py:92
  130.3 508.6 %all-gather.17.cloned.1.call-start = ((), (), s32[]{:S(2)}) async-start(), calls=%async_computation.11 | async-start | bytes 4096000 | tf_op jit(solution)/shard_map/all_gather | solution.py:93
  131.9 1049.9 %reduce-scatter.9.cloned.1.call-start = ((), (), s32[]{:S(2)}) async-start(), calls=%async_computation.13 | async-start | bytes 11796480 | tf_op jit(solution)/shard_map/reduce_scatter | solution.py:201
  132.3 5.3 copy-start.39
  626.7 5.9 copy-start.28
  632.5 14.2 copy-start.34
  632.6 6.3 copy-start.21
  638.9 5.1 copy-start.5
  638.9 5.1 copy-start.41
  1073.7 218.2 %reduce-scatter.7.cloned.1.call-start = ((), (), s32[]{:S(2)}) async-start(), calls=%async_computation.12 | async-start | bytes 11796480 | tf_op jit(solution)/shard_map/reduce_scatter | solution.py:198
  1074.5 264.5 %reduce-scatter.13.cloned.1.call-start = ((), (), s32[]{:S(2)}) async-start(), calls=%async_computation.15 | async-start | bytes 4096000 | tf_op jit(solution)/shard_map/reduce_scatter | solution.py:230
  1080.5 307.1 %reduce-scatter.15.cloned.1.call-start = ((), (), s32[]{:S(2)}) async-start(), calls=%async_computation.16 | async-start | bytes 4096000 | tf_op jit(solution)/shard_map/reduce_scatter | solution.py:233
  1087.2 349.0 %reduce-scatter.17.cloned.1.call-start = ((), (), s32[]{:S(2)}) async-start(), calls=%async_computation.17 | async-start | bytes 4096000 | tf_op jit(solution)/shard_map/reduce_scatter | solution.py:236
  1093.9 443.5 %reduce-scatter.11.cloned.1.call-start = ((), (), s32[]{:S(2)}) async-start(), calls=%async_computation.14 | async-start | bytes 12288000 | tf_op jit(solution)/shard_map/reduce_scatter | solution.py:227
  1099.1 192.9 %copy-start.3 = (bf16[1,512,1280]{2,1,0:T(8,128)(2,1)S(1)}, bf16[1,512,1280]{2,1,0:T(8,128)(2,1)}, u32[]{:S(2)}) copy-start(bf16[1,512,1280]{2,1,0:T(8,128)(2,1)} %param.24) | copy-start | bytes 3932164
  1099.1 192.9 %copy-start.31 = (f32[1280]{0:T(1024)S(1)}, f32[1280]{0:T(1024)}, u32[]{:S(2)}) copy-start(f32[1280]{0:T(1024)} %copy-done.30) | copy-start | bytes 15364
  1099.1 192.9 %copy-start.38 = (f32[512]{0:T(512)S(1)}, f32[512]{0:T(512)}, u32[]{:S(2)}) copy-start(f32[512]{0:T(512)} %copy-done.37) | copy-start | bytes 6148
  1301.7 350.6 %all-reduce.3.cloned.1.call-start = ((), (), s32[]{:S(2)}) async-start(), calls=%async_computation.18 | async-start | bytes 9830400 | tf_op jit(solution)/shard_map/psum | solution.py:241
  1537.5 10.9 copy-start.36
  1537.5 52.0 %copy-start.32 = (f32[2640]{0:T(1024)S(1)}, f32[2640]{0:T(1024)}, u32[]{:S(2)}) copy-start(f32[2640]{0:T(1024)} %param.40) | copy-start | bytes 31684
  1537.5 52.0 %copy-start.33 = (f32[2640]{0:T(1024)S(1)}, f32[2640]{0:T(1024)}, u32[]{:S(2)}) copy-start(f32[2640]{0:T(1024)} %param.41) | copy-start | bytes 31684
  1652.3 12.6 copy-start.10
  1652.3 12.6 copy-start.15
  1652.3 12.6 copy-start.16
  1652.3 13.0 copy-start.25
  1665.3 4.7 copy-start.24
  (25 other events, 60.2 us)
Sparse Core Ops, SparseCore 0:
  11.5 102.2 all-gather.6
  126.9 99.3 all-gather.10
  228.6 97.7 all-gather.8
  328.7 43.4 all-gather.12
  374.4 45.0 all-gather.14
  421.8 45.0 all-gather.16
  1073.9 107.9 reduce-scatter.8
  1184.2 107.7 reduce-scatter.6
  1295.6 43.4 reduce-scatter.12
  1342.5 45.0 reduce-scatter.14
  1391.2 45.0 reduce-scatter.16
  1439.2 98.1 reduce-scatter.10
  1540.0 112.2 all-reduce.2
where the time goes:
time: 1690 us; the launch traced here: 1680 us
  waiting for transfers between devices  705 us (42%)
  matrix products  582 us (34%)
  local copies, waits for them, and re-layouts  208 us (12%)
  other arithmetic  132 us (8%)
  blocking collectives  41.1 us (2%)
    dot_general x16, matrix products, head_scores(): jnp.einsum('qhd,khd->hqk', query_heads, key_heads, preferred_element_type...  152 us
    reduce_scatter x1, waiting for transfers between devices, body(): lax.psum_scatter(dkeys_all.astype(jnp.bfloat16), 'ctx', scatter_dimension...  110 us
    reduce_scatter x1, waiting for transfers between devices, body(): lax.psum_scatter(grad_qkv.astype(jnp.bfloat16), 'fsdp', scatter_dimension...  101 us
    all_gather x1, waiting for transfers between devices, body(): lax.all_gather(w_qkv.astype(bf16), 'fsdp', axis=0, tiled=True)  100 us
    dot_general x8, matrix products, back_step(): jnp.einsum('qhd,khd->hqk', dattn_heads, key_set[1], preferred_element_typ...  88.4 us
    all_gather x1, waiting for transfers between devices, body(): lax.all_gather(keys_here, 'ctx', axis=0, tiled=True)  83.6 us
    reduce_scatter x1, waiting for transfers between devices, body(): lax.psum_scatter(dvalues_all.astype(jnp.bfloat16), 'ctx', scatter_dimensi...  81 us
    unnamed x97, local copies, waits for them, and re-layouts  81 us
  transfers between devices with their start and end apart: 13, of which 10 were waited for; matrix products, arithmetic and copies ran while one was open for 26% of the time, Pallas kernels for 0%

commit v1 on v0

v1 whole, which is shorter than its diff:
```python
import functools
import math

import jax
import jax.numpy as jnp
from jax import lax
from jax.experimental import pallas as pl
from jax.experimental.pallas import tpu as pltpu
from jax.sharding import PartitionSpec as P

D = 1280
H = 16
HD = 80
FF = 1280
BLOCK = 256
CONT = 512
STEP = 3
PAD = 128
EXTRA = 16
TILE = CONT

bf16 = jnp.bfloat16
f32 = jnp.float32

norm_eps = 1e-06
beta_one = 0.5
beta_two = 0.5
adam_eps = 1e-08
decay_rate = 0.1
small_rate = 0.75
qkv_rate_base = 1.0
scale_base = 1.442695
LOG2E = math.log2(math.e)
LN2 = math.log(2.0)


def rms_scale(values):
    return lax.rsqrt(jnp.mean(values * values, axis=-1, keepdims=True) + norm_eps)


def adamw(weight, first, second, gradient, step_rate, decay_on):
    first_new = beta_one * first + (1.0 - beta_one) * gradient
    second_new = beta_two * second + (1.0 - beta_two) * gradient * gradient
    corr_one = 1.0 - beta_one**STEP
    corr_two = 1.0 - beta_two**STEP
    update = first_new / corr_one / (jnp.sqrt(second_new / corr_two) + adam_eps)
    weight_new = weight - step_rate * (update + decay_on * weight)
    return (weight_new, first_new, second_new)


def dot(left, right, contract=(1, 0)):
    return lax.dot_general(
        left, right, (((contract[0],), (contract[1],)), ((), ())), preferred_element_type=f32
    )


def fill_slots(order_ref, slot_ref, num_blocks):
    def place(slot, carry):
        slot_ref[order_ref[slot]] = slot
        return carry

    lax.fori_loop(0, num_blocks, place, 0)


def three_rows(row):
    high = row.astype(bf16)
    rest = row - high.astype(f32)
    middle = rest.astype(bf16)
    low = (rest - middle.astype(f32)).astype(bf16)
    index = lax.broadcasted_iota(jnp.int32, (EXTRA, row.shape[1]), 0)
    zero = jnp.zeros((EXTRA, row.shape[1]), f32)
    rows = jnp.where(index == 0, high.astype(f32), zero)
    rows = jnp.where(index == 1, middle.astype(f32), rows)
    rows = jnp.where(index == 2, low.astype(f32), rows)
    return rows.astype(bf16)


def tile_at(tile):
    return pl.ds(pl.multiple_of(tile * TILE, TILE), TILE)


def half_at(slot):
    return pl.ds(pl.multiple_of(lax.rem(slot, 2) * BLOCK, BLOCK), BLOCK)


def causal():
    key = lax.broadcasted_iota(jnp.int32, (TILE, TILE), 0)
    query = lax.broadcasted_iota(jnp.int32, (TILE, TILE), 1)
    return key <= query


def forward_kernel(
    heads,
    order_ref,
    x_ref,
    wn_ref,
    wt_ref,
    factor_ref,
    qt_ref,
    kt_ref,
    kn_ref,
    vn_ref,
    lse_ref,
    ot_ref,
    slot_ref,
    vt_ref,
    acc_ref,
    top_ref,
):
    tokens = x_ref.shape[0]
    num_blocks = tokens // BLOCK
    num_tiles = tokens // TILE
    prompt_tiles = num_tiles // 2
    fill_slots(order_ref, slot_ref, num_blocks)
    width = heads * HD
    lane = lax.broadcasted_iota(jnp.int32, (BLOCK, PAD), 1)
    is_extra = (lane >= HD) & (lane < HD + 3)

    def project(slot, carry):
        rows = x_ref[pl.ds(pl.multiple_of(slot * BLOCK, BLOCK), BLOCK), :]
        to = pl.ds(pl.multiple_of(order_ref[slot] * BLOCK, BLOCK), BLOCK)
        natural = dot(rows, wn_ref[...])
        flipped = dot(wt_ref[...], rows, (1, 1))
        for head in range(heads):
            key = natural[:, 2 * head * PAD : (2 * head + 1) * PAD]
            value = natural[:, (2 * head + 1) * PAD : (2 * head + 2) * PAD]
            kn_ref[head, to, :] = jnp.where(is_extra, 1.0, key).astype(bf16)
            vn_ref[head, to, :] = jnp.where(is_extra, 1.0, value).astype(bf16)
            at = head * HD
            qt_ref[head, :HD, to] = (flipped[at : at + HD] * factor_ref[...]).astype(bf16)
            qt_ref[head, HD:, to] = jnp.zeros((PAD - HD, BLOCK), bf16)
            kt_ref[head, :, to] = flipped[width + at : width + at + HD].astype(bf16)
            at = 2 * width + head * HD
            vt_ref[head, :HD, to] = flipped[at : at + HD].astype(bf16)
            vt_ref[head, HD:, to] = jnp.ones((EXTRA, BLOCK), bf16)
        return carry

    lax.fori_loop(0, num_blocks, project, 0)
    allowed = causal()

    def query_tile(tile, carry):
        here = tile_at(tile)
        top_ref[...] = jnp.full(top_ref.shape, -1e30, f32)
        acc_ref[...] = jnp.zeros(acc_ref.shape, f32)

        def step(keys, masked):
            for head in range(heads):
                scores = dot(kn_ref[head, keys, :], qt_ref[head, :, here])
                if masked:
                    scores = jnp.where(allowed, scores, -1e30)
                old = top_ref[head]
                top = jnp.maximum(old, jnp.max(scores, axis=0, keepdims=True))
                probs = jnp.exp2(scores - top).astype(bf16)
                acc_ref[head] = acc_ref[head] * jnp.exp2(old - top) + dot(
                    vt_ref[head, :, keys], probs
                )
                top_ref[head] = top

        def full(key_tile, inner):
            step(tile_at(key_tile), False)
            return inner

        lax.fori_loop(0, jnp.minimum(tile, prompt_tiles), full, 0)
        step(here, True)
        for head in range(heads):
            acc = acc_ref[head]
            mass = acc[HD : HD + 1]
            mixed = (acc[:HD] / mass).astype(bf16)
            lse_ref[head, :, here] = top_ref[head] + jnp.log2(mass)
            for part in range(TILE // BLOCK):
                slot = slot_ref[tile * (TILE // BLOCK) + part]
                ot_ref[slot // 2, head * HD : (head + 1) * HD, half_at(slot)] = mixed[
                    :, part * BLOCK : (part + 1) * BLOCK
                ]
        return carry

    lax.fori_loop(0, num_tiles, query_tile, 0)


def backward_kernel(
    heads,
    order_ref,
    qt_ref,
    kt_ref,
    kn_ref,
    vn_ref,
    lse_ref,
    ot_ref,
    dt_ref,
    factor_ref,
    dqkv_ref,
    dscale_ref,
    slot_ref,
    qa_ref,
    da_ref,
    dq_ref,
    dk_ref,
    dv_ref,
):
    tokens = kn_ref.shape[1]
    num_blocks = tokens // BLOCK
    num_tiles = tokens // TILE
    prompt_tiles = num_tiles // 2
    width = heads * HD
    fill_slots(order_ref, slot_ref, num_blocks)

    def prepare(block, carry):
        slot = slot_ref[block]
        to = pl.ds(pl.multiple_of(block * BLOCK, BLOCK), BLOCK)
        for head in range(heads):
            rows = slice(head * HD, (head + 1) * HD)
            grad = dt_ref[slot // 2, rows, half_at(slot)]
            mixed = ot_ref[slot // 2, rows, half_at(slot)]
            delta = jnp.sum(grad.astype(f32) * mixed.astype(f32), axis=0, keepdims=True)
            da_ref[head, :HD, to] = grad
            da_ref[head, HD : HD + EXTRA, to] = three_rows(-delta)
            da_ref[head, HD + EXTRA :, to] = jnp.zeros((PAD - HD - EXTRA, BLOCK), bf16)
            qa_ref[head, :HD, to] = qt_ref[head, :HD, to]
            qa_ref[head, HD : HD + EXTRA, to] = three_rows(-lse_ref[head, :, to])
            qa_ref[head, HD + EXTRA :, to] = jnp.zeros((PAD - HD - EXTRA, BLOCK), bf16)
        return carry

    lax.fori_loop(0, num_blocks, prepare, 0)
    dk_ref[...] = jnp.zeros(dk_ref.shape, f32)
    dv_ref[...] = jnp.zeros(dv_ref.shape, f32)
    dscale_ref[...] = jnp.zeros(dscale_ref.shape, f32)
    allowed = causal()

    def query_tile(tile, carry):
        here = tile_at(tile)
        dq_ref[...] = jnp.zeros(dq_ref.shape, f32)

        def step(keys, masked):
            for head in range(heads):
                probs = jnp.exp2(dot(kn_ref[head, keys, :], qa_ref[head, :, here]))
                if masked:
                    probs = jnp.where(allowed, probs, 0.0)
                spread = dot(vn_ref[head, keys, :], da_ref[head, :, here])
                dscores = (probs * spread).astype(bf16)
                dv_ref[head, :, keys] += dot(da_ref[head, :HD, here], probs.astype(bf16), (1, 1))
                dk_ref[head, :, keys] += dot(qa_ref[head, :HD, here], dscores, (1, 1))
                dq_ref[head] += dot(kt_ref[head, :, keys], dscores)

        def full(key_tile, inner):
            step(tile_at(key_tile), False)
            return inner

        lax.fori_loop(0, jnp.minimum(tile, prompt_tiles), full, 0)
        step(here, True)
        for head in range(heads):
            dq = dq_ref[head]
            product = dq * qt_ref[head, :HD, here].astype(f32)
            for lane in range(TILE // PAD):
                dscale_ref[head] += product[:, lane * PAD : (lane + 1) * PAD]
            scaled = (dq * (factor_ref[...] * LN2)).astype(bf16)
            for part in range(TILE // BLOCK):
                slot = slot_ref[tile * (TILE // BLOCK) + part]
                to = pl.ds(pl.multiple_of(slot * BLOCK, BLOCK), BLOCK)
                dqkv_ref[head * HD : (head + 1) * HD, to] = scaled[
                    :, part * BLOCK : (part + 1) * BLOCK
                ]
        return carry

    lax.fori_loop(0, num_tiles, query_tile, 0)

    def finish(block, carry):
        slot = slot_ref[block]
        to = pl.ds(pl.multiple_of(slot * BLOCK, BLOCK), BLOCK)
        at = pl.ds(pl.multiple_of(block * BLOCK, BLOCK), BLOCK)
        for head in range(heads):
            row = width + head * HD
            dqkv_ref[row : row + HD, to] = (dk_ref[head, :, at] * LN2).astype(bf16)
            row = 2 * width + head * HD
            dqkv_ref[row : row + HD, to] = dv_ref[head, :, at].astype(bf16)
        return carry

    lax.fori_loop(0, num_blocks, finish, 0)


def in_vmem(count):
    return [pl.BlockSpec(memory_space=pltpu.VMEM)] * count


def params():
    return pltpu.CompilerParams(vmem_limit_bytes=60 * 1024 * 1024)


def attention_forward(order, rows, w_natural, w_flipped, factor, parts, heads):
    tokens = rows.shape[0]
    return pl.pallas_call(
        functools.partial(forward_kernel, heads),
        name="attention_forward",
        out_shape=[
            jax.ShapeDtypeStruct((heads, PAD, tokens), bf16),
            jax.ShapeDtypeStruct((heads, HD, tokens), bf16),
            jax.ShapeDtypeStruct((heads, tokens, PAD), bf16),
            jax.ShapeDtypeStruct((heads, tokens, PAD), bf16),
            jax.ShapeDtypeStruct((heads, 1, tokens), f32),
            jax.ShapeDtypeStruct((parts, heads * HD, tokens // parts), bf16),
        ],
        in_specs=[pl.BlockSpec(memory_space=pltpu.SMEM)] + in_vmem(4),
        out_specs=in_vmem(6),
        scratch_shapes=[
            pltpu.SMEM((tokens // BLOCK,), jnp.int32),
            pltpu.VMEM((heads, HD + EXTRA, tokens), bf16),
            pltpu.VMEM((heads, HD + EXTRA, TILE), f32),
            pltpu.VMEM((heads, 1, TILE), f32),
        ],
        compiler_params=params(),
    )(order, rows, w_natural, w_flipped, factor)


def attention_backward(order, kept, mixed, dmixed, factor, heads):
    qt, kt, kn, vn, lse = kept
    tokens = kn.shape[1]
    return pl.pallas_call(
        functools.partial(backward_kernel, heads),
        name="attention_backward",
        out_shape=[
            jax.ShapeDtypeStruct((3 * heads * HD, tokens), bf16),
            jax.ShapeDtypeStruct((heads, HD, PAD), f32),
        ],
        in_specs=[pl.BlockSpec(memory_space=pltpu.SMEM)] + in_vmem(8),
        out_specs=in_vmem(2),
        scratch_shapes=[
            pltpu.SMEM((tokens // BLOCK,), jnp.int32),
            pltpu.VMEM((heads, PAD, tokens), bf16),
            pltpu.VMEM((heads, PAD, tokens), bf16),
            pltpu.VMEM((heads, HD, TILE), f32),
            pltpu.VMEM((heads, HD, tokens), f32),
            pltpu.VMEM((heads, HD, tokens), f32),
        ],
        compiler_params=params(),
    )(order, qt, kt, kn, vn, lse, mixed, dmixed, factor)


def body(
    parts,
    inputs,
    cotangent,
    block_order,
    w_qkv,
    m_qkv,
    v_qkv,
    w_out,
    m_out,
    v_out,
    w_up,
    m_up,
    v_up,
    w_down,
    m_down,
    v_down,
    small_params,
    small_m,
    small_v,
):
    heads = H // parts
    width = heads * HD
    rows_dev = inputs.shape[1]
    tokens = rows_dev * parts
    here = lax.axis_index("ctx")
    order = block_order[0]
    gain_one = small_params[:D]
    gain_two = small_params[D : 2 * D]
    query_scale = small_params[2 * D :]
    own_columns = jnp.concatenate(
        [
            lax.dynamic_slice_in_dim(w_qkv, part * D + here * width, width, 1).astype(bf16)
            for part in range(3)
        ],
        axis=1,
    )
    own_qkv = lax.all_gather(own_columns, "fsdp", axis=0, tiled=True)
    layer_in = inputs[0].astype(f32)
    scale_one = rms_scale(layer_in)
    unit_one = layer_in * scale_one
    normed = (unit_one * gain_one).astype(bf16)
    normed_all = lax.all_gather(normed, "ctx", axis=0, tiled=True)
    out_full, up_full, down_full = (
        lax.all_gather(w_out.astype(bf16), "fsdp", axis=0, tiled=True),
        lax.all_gather(w_up.astype(bf16), "fsdp", axis=0, tiled=True),
        lax.all_gather(w_down.astype(bf16), "fsdp", axis=0, tiled=True),
    )
    factor = scale_base / math.sqrt(HD) * jax.nn.softplus(query_scale)
    factor_two = (factor * LOG2E)[:, None]
    w_flipped = own_qkv.T
    pieces = []
    for head in range(heads):
        for part in (1, 2):
            at = part * width + head * HD
            pieces.append(jnp.pad(own_qkv[:, at : at + HD], ((0, 0), (0, PAD - HD))))
    w_natural = jnp.concatenate(pieces, axis=1)
    *kept, mixed = attention_forward(
        order, normed_all, w_natural, w_flipped, factor_two, parts, heads
    )
    attn_flipped = lax.all_to_all(mixed, "ctx", 0, 0, tiled=True).reshape(D, rows_dev)
    mid = layer_in + dot(attn_flipped, out_full, (0, 0))
    scale_two = rms_scale(mid)
    unit_two = mid * scale_two
    normed_two = (unit_two * gain_two).astype(bf16)
    hidden = dot(normed_two, up_full)
    gate_sig = jax.nn.sigmoid(hidden)
    act = (hidden * gate_sig).astype(bf16)
    output = (mid + dot(act, down_full)).astype(bf16)
    grad_in = cotangent[0]
    grad_down = dot(act, grad_in, (0, 0))
    dact = dot(grad_in, down_full, (1, 1))
    dhidden = (dact * gate_sig * (1.0 + hidden * (1.0 - gate_sig))).astype(bf16)
    grad_up = dot(normed_two, dhidden, (0, 0))
    dnormed_two = dot(dhidden, up_full, (1, 1))
    dunit_two = dnormed_two * gain_two
    dmid = grad_in.astype(f32) + scale_two * (
        dunit_two - unit_two * jnp.mean(dunit_two * unit_two, axis=-1, keepdims=True)
    )
    gain_two_grad = jnp.sum(dnormed_two * unit_two, axis=0)
    dbranch = dmid.astype(bf16)
    grad_out = dot(attn_flipped, dbranch)
    dattn = dot(out_full, dbranch, (1, 1)).astype(bf16)
    dmixed = lax.all_to_all(dattn.reshape(parts, width, rows_dev), "ctx", 0, 0, tiled=True)
    dqkv, dscale = attention_backward(order, kept, mixed, dmixed, factor_two, heads)
    grad_qkv = dot(normed_all, dqkv, (0, 1))
    dnormed_part = dot(dqkv, w_flipped, (0, 0)).astype(bf16)
    dnormed = lax.psum_scatter(dnormed_part, "ctx", scatter_dimension=0, tiled=True).astype(f32)
    scale_grad = (
        jnp.sum(dscale, axis=(0, 2))
        / factor_two[:, 0]
        * (scale_base / math.sqrt(HD))
        * jax.nn.sigmoid(query_scale)
    )
    dunit_one = dnormed * gain_one
    input_grad = dmid + scale_one * (
        dunit_one - unit_one * jnp.mean(dunit_one * unit_one, axis=-1, keepdims=True)
    )
    gain_one_grad = jnp.sum(dnormed * unit_one, axis=0)
    small_grad = jnp.concatenate([gain_one_grad, gain_two_grad, scale_grad])
    small_total = lax.psum(small_grad, ("ctx", "fsdp"))
    rate_qkv = qkv_rate_base / math.sqrt(D)
    rate_out = 0.5 / math.sqrt(max(D // 256, 1))
    rate_up = 0.5 / math.sqrt(D)
    rate_down = 0.5 / math.sqrt(FF)
    shard_out, shard_up, shard_down = (
        lax.psum_scatter(grad.astype(bf16), "fsdp", scatter_dimension=0, tiled=True)
        for grad in (grad_out, grad_up, grad_down)
    )
    total_out, total_up, total_down = (
        lax.psum(shard, "ctx").astype(f32) for shard in (shard_out, shard_up, shard_down)
    )
    shard_qkv = lax.psum_scatter(grad_qkv.astype(bf16), "fsdp", scatter_dimension=0, tiled=True)
    rows = shard_qkv.shape[0]
    total_qkv = (
        lax.all_gather(shard_qkv, "ctx", axis=0)
        .reshape(parts, rows, 3, width)
        .transpose(1, 2, 0, 3)
        .reshape(rows, 3 * D)
        .astype(f32)
    )
    qkv_set = adamw(w_qkv, m_qkv, v_qkv, total_qkv, rate_qkv, decay_rate)
    out_set = adamw(w_out, m_out, v_out, total_out, rate_out, decay_rate)
    up_set = adamw(w_up, m_up, v_up, total_up, rate_up, decay_rate)
    down_set = adamw(w_down, m_down, v_down, total_down, rate_down, decay_rate)
    small_set = adamw(small_params, small_m, small_v, small_total, small_rate, 0.0)
    return (
        output[None],
        input_grad.astype(bf16)[None],
        qkv_set[0],
        qkv_set[1],
        qkv_set[2],
        qkv_set[0].astype(bf16),
        out_set[0],
        out_set[1],
        out_set[2],
        out_set[0].astype(bf16),
        up_set[0],
        up_set[1],
        up_set[2],
        up_set[0].astype(bf16),
        down_set[0],
        down_set[1],
        down_set[2],
        down_set[0].astype(bf16),
        small_set[0],
        small_set[1],
        small_set[2],
    )


def solution(mesh):
    rows = P("fsdp", "ctx", None)
    weight = P("fsdp", None)
    return jax.shard_map(
        functools.partial(body, mesh.shape["ctx"]),
        mesh=mesh,
        in_specs=(rows, rows, weight) + (weight,) * 12 + (P(),) * 3,
        out_specs=(rows, rows) + (weight,) * 16 + (P(),) * 3,
        check_vma=False,
    )
```

time: 1690 us -> 747 us (0.44)
  matrix products: 582 us -> 68.7 us
  waiting for transfers between devices: 705 us -> 361 us
  local copies, waits for them, and re-layouts: 208 us -> 70.8 us
  Pallas kernels: 0 us -> 104 us
  other arithmetic: 132 us -> 41.1 us
  blocking collectives: 41.1 us -> 74.8 us
    dot_general x68 -> x11, matrix products: 582 us -> 68.7 us  [dot(): lax.dot_general(left, right, (((contract[0],), (contract[1],)), ((), ()))...]
    reduce_scatter x6 -> x5, waiting for transfers between devices: 419 us -> 114 us  [the longest x1 57.9 us: body(): lax.psum_scatter(dnormed_part, 'ctx', scatter_dimension=0, tiled=True)]
    pallas_call x0 -> x2, Pallas kernels: none -> 104 us  [the longest x1 53.7 us: attention_forward(): pl.pallas_call(functools.partial(forward_kernel, heads), name='attention_...]
    all_gather x3, waiting for transfers between devices: 226 us -> 144 us  [the longest x1 97.2 us: body(): normed_all = lax.all_gather(normed, 'ctx', axis=0, tiled=True)]
    reduce_sum x10 -> x2, other arithmetic: 76.3 us -> 2.4 us  [the longest x1 2.3 us: body(): gain_one_grad = jnp.sum(dnormed * unit_one, axis=0)]
    dynamic_update_slice x24 -> x0, local copies, waits for them, and re-layouts: 56.1 us -> none  [body(): lax.scan(functools.partial(back_step, want_keys=True), dq_start, key_stack)]
    all_gather x1, waiting for transfers between devices: 0.01 us -> 39.8 us  [body(): lax.all_gather(w_down.astype(bf16), 'fsdp', axis=0, tiled=True)]
    all_to_all x0 -> x1, blocking collectives: none -> 36.8 us  [body(): lax.all_to_all(dattn.reshape(parts, width, rows_dev), 'ctx', 0, 0, tiled=...]
  transfers between devices with their start and end apart: 13 -> 13, of which waited for: 10 -> 9; matrix products, arithmetic and copies ran while one was open for 26% -> 21% of each run, Pallas kernels for 0% -> 14%
where the time goes in v1:
time: 747 us; the launch traced here: 740 us
  waiting for transfers between devices  361 us (48%)
  Pallas kernels  104 us (14%)
  blocking collectives  74.8 us (10%)
  local copies, waits for them, and re-layouts  70.8 us (9%)
  matrix products  68.7 us (9%)
  other arithmetic  41.1 us (6%)
  between operations  14.7 us (2%)
    all_gather x1, waiting for transfers between devices, body(): normed_all = lax.all_gather(normed, 'ctx', axis=0, tiled=True)  97.2 us
    dot_general x11, matrix products, dot(): lax.dot_general(left, right, (((contract[0],), (contract[1],)), ((), ()))...  68.7 us
    reduce_scatter x1, waiting for transfers between devices, body(): lax.psum_scatter(dnormed_part, 'ctx', scatter_dimension=0, tiled=True)  57.9 us
    pallas_call x1, Pallas kernels, attention_forward(): pl.pallas_call(functools.partial(forward_kernel, heads), name='attention_...  53.7 us
    pallas_call x1, Pallas kernels, attention_backward(): pl.pallas_call(functools.partial(backward_kernel, heads), name='attention...  50.4 us
    unnamed x61, local copies, waits for them, and re-layouts  46.9 us
    all_gather x1, waiting for transfers between devices, body(): lax.all_gather(w_down.astype(bf16), 'fsdp', axis=0, tiled=True)  39.8 us
    psum x1, blocking collectives, body(): small_total = lax.psum(small_grad, ('ctx', 'fsdp'))  38 us
  transfers between devices with their start and end apart: 13, of which 9 were waited for; matrix products, arithmetic and copies ran while one was open for 21% of the time, Pallas kernels for 14%

profile of v1, /device:TPU:0, one launch (start us, length us, event | category | flops | bytes accessed | tf_op | source)
XLA Modules:
  0.0 740.4 jit_solution(2940010667367486517)
XLA Ops:
  18.6 23.4 %all-gather.10.cloned.1.call-done = bf16[1280,480]{1,0:T(8,128)(2,1)} async-done(((bf16[320,480]{1,0:T(8,128)(2,1)}), bf16[1280,480]{1,0:T(8,128)(2,1)}) %all-gather.10.cloned.1.call-update) | async-done | bytes 1228816 | tf_op jit(solution)/shard_map/all_gather | solution.py:374
  46.4 97.2 %all-gather.8.cloned.1.call-done.x_ref = bf16[4096,1280]{1,0:T(8,128)(2,1)} async-done(((bf16[512,1280]{1,0:T(8,128)(2,1)}), bf16[4096,1280]{1,0:T(8,128)(2,1)}) %all-gather.8.cloned.1.call-update) | async-done | bytes 10485776 | tf_op jit(solution)/shard_map/all_gather | solution.py:379
  143.6 53.7 %attention_forward.1 = (bf16[2,128,4096]{2,1,0:T(8,128)(2,1)}, bf16[2,80,4096]{2,1,0:T(8,128)(2,1)}, bf16[2,4096,128]{2,1,0:T(8,128)(2,1)}, bf16[2,4096,128]{2,1...) custom-call(s32[16]{0:T(128)} %bitcast.56, bf16[4096,1280]{1,0:T(8,128)(2,1)} %all-gather.8.cloned.1.call-done.x_ref, ...), custom_call_target="tpu_custom_call" | custom-call | tf_op jit(solution)/shard_map/attention_forward/pallas_call | solution.py:290
  201.2 31.9 %all-to-all-done = bf16[8,160,512]{2,1,0:T(8,128)(2,1)S(1)} async-done(((bf16[8,160,512]{2,1,0:T(8,128)(2,1)}), bf16[8,160,512]{2,1,0:T(8,128)(2,1)S(1)}, u32[]{:S(2)}, u32[]{:S(2)}) %all-to-all-start) | async-done | bytes 1310752 | tf_op jit(solution)/shard_map/all_to_all | solution.py:397
  233.1 5.3 multiply_reduce_fusion.2
  238.5 6.1 fusion.37
  244.6 39.8 %all-gather.16.cloned.1.call-done = bf16[1280,1280]{1,0:T(8,128)(2,1)} async-done(((bf16[320,1280]{1,0:T(8,128)(2,1)}), bf16[1280,1280]{1,0:T(8,128)(2,1)}) %all-gather.16.cloned.1.call-update) | async-done | bytes 3276816 | tf_op jit(solution)/shard_map/all_gather | solution.py:383
  284.4 5.5 fusion.7
  299.1 5.4 convolution_convert_fusion.2
  305.9 5.4 convolution_convert_fusion.1
  311.3 5.9 fusion.10
  318.8 36.8 %all_to_all.10.dt_ref = bf16[8,160,512]{2,1,0:T(8,128)(2,1)} all-to-all(bf16[8,160,512]{2,1,0:T(8,128)(2,1)S(1)} %bitcast.54), channel_id=1, replica_groups=mesh['ctx'=8,'fsdp'=4] {'ctx'}, dimensions={0} | all-to-all | bytes 2621440 | tf_op jit(solution)/shard_map/all_to_all | solution.py:420
  355.7 50.4 %attention_backward.1 = (bf16[480,4096]{1,0:T(8,128)(2,1)}, f32[2,80,128]{2,1,0:T(8,128)}) custom-call(s32[16]{0:T(128)} %bitcast.57, bf16[2,128,4096]{2,1,0:T(8,128)(2,1)} %get-tuple-element.30.qt_ref, bf16[2,80,4096]{2,1,0:T(8,128)(2,1)} %get-tuple-element.31.kt_ref, bf16[2,4096,128]{2,1,0:T(8,128)(2,1)} %get-tuple-element.32.kn_ref, ...), custom_call_target="tpu_custom_call" | custom-call | tf_op jit(solution)/shard_map/attention_backward/pallas_call | solution.py:316
  406.1 10.8 %convolution_convert_fusion.5 = bf16[1280,480]{1,0:T(8,128)(2,1)} fusion(bf16[4096,1280]{1,0:T(8,128)(2,1)} %all-gather.8.cloned.1.call-done.x_ref, bf16[480,4096]{1,0:T(8,128)(2,1)} %get-tuple-element.35), kind=kOutput, calls=%fused_computation.27 | convolution fusion | flops 5033779200 | bytes 15646720 | tf_op jit(solution)/shard_map/dot_general | solution.py:52
  417.0 22.8 %reduce-scatter.14.cloned.1.call-done = bf16[320,1280]{1,0:T(8,128)(2,1)} async-done(((bf16[1280,1280]{1,0:T(8,128)(2,1)}), bf16[320,1280]{1,0:T(8,128)(2,1)}) %reduce-scatter.14.cloned.1.call-update) | async-done | bytes 819216 | tf_op jit(solution)/shard_map/reduce_scatter | solution.py:443
  439.9 32.8 %reduce-scatter.16.cloned.1.call-done = bf16[320,480]{1,0:T(8,128)(2,1)} async-done(((bf16[1280,480]{1,0:T(8,128)(2,1)}), bf16[320,480]{1,0:T(8,128)(2,1)}) %reduce-scatter.16.cloned.1.call-update) | async-done | bytes 307216 | tf_op jit(solution)/shard_map/reduce_scatter | solution.py:449
  473.2 11.7 %convolution_convert_fusion = bf16[4096,1280]{1,0:T(8,128)(2,1)} fusion(bf16[480,4096]{1,0:T(8,128)(2,1)} %get-tuple-element.35, bf16[1280,480]{1,0:T(8,128)(2,1)S(1)} %copy-done.8), kind=kOutput, calls=%fused_computation | convolution fusion | flops 5038407680 | bytes 15646720 | tf_op jit(solution)/shard_map/dot_general | solution.py:52
  484.9 6.2 copy.103
  491.1 6.1 copy.96
  497.2 6.1 copy.101
  503.4 6.9 fusion.9
  510.5 32.4 %all-reduce.7.cloned.1.call-done = (bf16[320,1280]{1,0:T(8,128)(2,1)}, bf16[320,1280]{1,0:T(8,128)(2,1)}, bf16[320,1280]{1,0:T(8,128)(2,1)}) async-done(((bf16[320,1280]{1,0:T(8,128)(2,1)}, bf16[320,1280]{1,0:T(8,128)(2,1)}, bf16[320,1280]{1,0:T(8,128)(2,1)}), (bf16[320,1280]{1,0:T(8,128)(2,1)}, bf16[320,1280]{1,0:T(8,128)(2,1)}, bf16[320,1280]{1,0:T(8,128)(2,1)})) %all-reduce.7.cloned.1.call-update) | async-done | bytes 2457616 | tf_op jit(solution)/shard_map/psum | solution.py:447
  542.9 5.7 fusion.43
  555.3 22.8 %all-gather.18.cloned.1.call-done = bf16[2560,480]{1,0:T(8,128)(2,1)} async-done(((bf16[320,480]{1,0:T(8,128)(2,1)}), bf16[2560,480]{1,0:T(8,128)(2,1)}) %all-gather.18.cloned.1.call-update) | async-done | bytes 2457616 | tf_op jit(solution)/shard_map/all_gather | solution.py:452
  582.6 6.2 reshape.86
  588.8 6.3 copy.100
  595.1 13.1 %fusion.45 = (bf16[320,3840]{0,1:T(8,128)(2,1)}, f32[320,3840]{0,1:T(8,128)}, f32[320,3840]{0,1:T(8,128)}, f32[320,3840]{0,1:T(8,128)}) fusion(f32[320,3840]{0,1:T(8,128)S(1)} %bitcast.50, f32[320,3,8,160]{0,3,2,1:T(8,128)} %copy.100, f32[320,3840]{0,1:T(8,128)} %copy.96, f32[320,3840]{0,1:T(8,128)} %copy.101), kind=kLoop, calls=%fused_computation.92 | loop fusion | flops 18432000 | bytes 36864000 | tf_op jit(solution)/shard_map/convert_element_type | solution.py:469
  608.2 6.1 copy.104
  614.3 6.2 copy.105
  620.5 6.1 copy.106
  631.0 57.9 %reduce-scatter.8.cloned.1.call-done = bf16[512,1280]{1,0:T(8,128)(2,1)} async-done(((bf16[4096,1280]{1,0:T(8,128)(2,1)}), bf16[512,1280]{1,0:T(8,128)(2,1)}) %reduce-scatter.8.cloned.1.call-update) | async-done | bytes 1310736 | tf_op jit(solution)/shard_map/reduce_scatter | solution.py:424
  691.2 38.0 %psum.31 = f32[2640]{0:T(1024)S(1)} all-reduce(f32[2640]{0:T(1024)S(1)} %pad_maximum_fusion.1), channel_id=1, replica_groups=mesh['ctx'=8,'fsdp'=4] {'ctx','fsdp'}, use_global_device_ids=true, to_apply=%region_15.16 | all-reduce | flops 2640 | bytes 21120 | tf_op jit(solution)/shard_map/psum | solution.py:437
  (114 shorter events, 54.5 us)
Async XLA Ops:
  7.2 3.0 copy-start.19
  7.2 34.8 %all-gather.10.cloned.1.call-start = ((), (), s32[]{:S(2)}) async-start(), calls=%async_computation.8 | async-start | bytes 1638400 | tf_op jit(solution)/shard_map/all_gather | solution.py:374
  9.8 133.8 %all-gather.8.cloned.1.call-start = ((), (), s32[]{:S(2)}) async-start(), calls=%async_computation.7 | async-start | bytes 11796480 | tf_op jit(solution)/shard_map/all_gather | solution.py:379
  11.7 189.5 %all-gather.12.cloned.1.call-start = ((), (), s32[]{:S(2)}) async-start(), calls=%async_computation.9 | async-start | bytes 4096000 | tf_op jit(solution)/shard_map/all_gather | solution.py:381
  14.3 224.1 %all-gather.14.cloned.1.call-start = ((), (), s32[]{:S(2)}) async-start(), calls=%async_computation.10 | async-start | bytes 4096000 | tf_op jit(solution)/shard_map/all_gather | solution.py:382
  15.4 269.0 %all-gather.16.cloned.1.call-start = ((), (), s32[]{:S(2)}) async-start(), calls=%async_computation.11 | async-start | bytes 4096000 | tf_op jit(solution)/shard_map/all_gather | solution.py:383
  197.4 35.7 %all-to-all-start = ((bf16[8,160,512]{2,1,0:T(8,128)(2,1)}), bf16[8,160,512]{2,1,0:T(8,128)(2,1)S(1)}, u32[]{:S(2)}, u32[]{:S(2)}) async-start(bf16[8,160,512]{2,1,0:T(8,128)(2,1)} %get-tuple-element.29.ot_ref), calls=%async_computation | async-start | bytes 2621440 | tf_op jit(solution)/shard_map/all_to_all | solution.py:397
  201.0 216.0 %reduce-scatter.10.cloned.1.call-start = ((), (), s32[]{:S(2)}) async-start(), calls=%async_computation.13 | async-start | bytes 4096000 | tf_op jit(solution)/shard_map/reduce_scatter | solution.py:443
  284.4 5.5 copy-start.1
  284.4 5.5 copy-start.22
  297.8 119.2 %reduce-scatter.12.cloned.1.call-start = ((), (), s32[]{:S(2)}) async-start(), calls=%async_computation.14 | async-start | bytes 4096000 | tf_op jit(solution)/shard_map/reduce_scatter | solution.py:443
  304.6 135.3 %reduce-scatter.14.cloned.1.call-start = ((), (), s32[]{:S(2)}) async-start(), calls=%async_computation.15 | async-start | bytes 4096000 | tf_op jit(solution)/shard_map/reduce_scatter | solution.py:443
  311.3 161.4 %reduce-scatter.16.cloned.1.call-start = ((), (), s32[]{:S(2)}) async-start(), calls=%async_computation.17 | async-start | bytes 1638400 | tf_op jit(solution)/shard_map/reduce_scatter | solution.py:449
  416.9 56.3 %copy-start.8 = (bf16[1280,480]{1,0:T(8,128)(2,1)S(1)}, bf16[1280,480]{1,0:T(8,128)(2,1)}, u32[]{:S(2)}) copy-start(bf16[1280,480]{1,0:T(8,128)(2,1)} %all-gather.10.cloned.1.call-done) | copy-start | bytes 3686404
  416.9 125.9 %all-reduce.7.cloned.1.call-start = ((), (), s32[]{:S(2)}) async-start(), calls=%async_computation.18 | async-start | bytes 4915200 | tf_op jit(solution)/shard_map/psum | solution.py:447
  439.9 138.3 %all-gather.18.cloned.1.call-start = ((), (), s32[]{:S(2)}) async-start(), calls=%async_computation.16 | async-start | bytes 2949120 | tf_op jit(solution)/shard_map/all_gather | solution.py:452
  472.7 216.1 %reduce-scatter.8.cloned.1.call-start = ((), (), s32[]{:S(2)}) async-start(), calls=%async_computation.12 | async-start | bytes 11796480 | tf_op jit(solution)/shard_map/reduce_scatter | solution.py:424
  503.4 6.9 copy-start.18
  503.4 39.5 %copy-start.6 = (f32[320,1280]{1,0:T(8,128)S(1)}, f32[320,1280]{1,0:T(8,128)}, u32[]{:S(2)}) copy-start(f32[320,1280]{1,0:T(8,128)} %param.24) | copy-start | bytes 4915204
  542.8 5.7 copy-start.4
  542.8 5.7 copy-start.5
  542.8 5.7 copy-start.10
  542.8 5.7 copy-start.11
  542.9 6.5 copy-start.12
  542.9 7.1 copy-start.13
  542.9 7.3 copy-start.16
  542.9 7.5 %copy-start.17 = (bf16[320,1280]{1,0:T(8,128)(2,1)S(1)}, bf16[320,1280]{1,0:T(8,128)(2,1)}, u32[]{:S(2)}) copy-start(bf16[320,1280]{1,0:T(8,128)(2,1)} %get-tuple-element.127) | copy-start | bytes 2457604
  582.6 12.5 %slice-start = ((s8[5898240]{0:T(1024)(128)(4,1)}), s8[1703936]{0:T(1024)(128)(4,1)S(1)}, s32[]{:S(2)}) async-start(s8[5898240]{0:T(1024)(128)(4,1)} %bitcast.49), calls=%async_computation.19 | async-start | bytes 3407872
  588.8 6.3 slice-start.1
  631.0 98.2 %copy-start.20 = (f32[2640]{0:T(1024)S(1)}, f32[2640]{0:T(1024)}, u32[]{:S(2)}) copy-start(f32[2640]{0:T(1024)} %param.34) | copy-start | bytes 31684
  631.0 98.2 %copy-start.21 = (f32[2640]{0:T(1024)S(1)}, f32[2640]{0:T(1024)}, u32[]{:S(2)}) copy-start(f32[2640]{0:T(1024)} %param.35) | copy-start | bytes 31684
  688.9 40.9 %copy-start.9 = (bf16[512,1280]{1,0:T(8,128)(2,1)S(1)}, bf16[512,1280]{1,0:T(8,128)(2,1)}, u32[]{:S(2)}) copy-start(bf16[512,1280]{1,0:T(8,128)(2,1)} %reduce-scatter.8.cloned.1.call-done) | copy-start | bytes 3932164
  (8 other events, 16.4 us)
Sparse Core Ops, SparseCore 0:
  10.5 31.5 all-gather.9
  44.2 99.3 all-gather.7
  146.1 43.5 all-gather.11
  191.9 45.0 all-gather.13
  239.3 45.0 all-gather.15
  297.9 45.0 reduce-scatter.9
  346.6 45.0 reduce-scatter.11
  394.8 45.0 reduce-scatter.13
  443.4 29.3 reduce-scatter.15
  475.2 67.6 all-reduce.6
  544.6 33.5 all-gather.17
  580.4 108.3 reduce-scatter.7

commit v2 on v1

--- a/solution.py
+++ b/solution.py
@@ -255,8 +255,7 @@
             scaled = (dq * (factor_ref[...] * LN2)).astype(bf16)
             for part in range(TILE // BLOCK):
                 slot = slot_ref[tile * (TILE // BLOCK) + part]
-                to = pl.ds(pl.multiple_of(slot * BLOCK, BLOCK), BLOCK)
-                dqkv_ref[head * HD : (head + 1) * HD, to] = scaled[
+                dqkv_ref[slot // 2, head * HD : (head + 1) * HD, half_at(slot)] = scaled[
                     :, part * BLOCK : (part + 1) * BLOCK
                 ]
         return carry
@@ -265,13 +264,13 @@
 
     def finish(block, carry):
         slot = slot_ref[block]
-        to = pl.ds(pl.multiple_of(slot * BLOCK, BLOCK), BLOCK)
+        owner, to = slot // 2, half_at(slot)
         at = pl.ds(pl.multiple_of(block * BLOCK, BLOCK), BLOCK)
         for head in range(heads):
             row = width + head * HD
-            dqkv_ref[row : row + HD, to] = (dk_ref[head, :, at] * LN2).astype(bf16)
+            dqkv_ref[owner, row : row + HD, to] = (dk_ref[head, :, at] * LN2).astype(bf16)
             row = 2 * width + head * HD
-            dqkv_ref[row : row + HD, to] = dv_ref[head, :, at].astype(bf16)
+            dqkv_ref[owner, row : row + HD, to] = dv_ref[head, :, at].astype(bf16)
         return carry
 
     lax.fori_loop(0, num_blocks, finish, 0)
@@ -317,7 +316,7 @@
         functools.partial(backward_kernel, heads),
         name="attention_backward",
         out_shape=[
-            jax.ShapeDtypeStruct((3 * heads * HD, tokens), bf16),
+            jax.ShapeDtypeStruct((mixed.shape[0], 3 * heads * HD, mixed.shape[2]), bf16),
             jax.ShapeDtypeStruct((heads, HD, PAD), f32),
         ],
         in_specs=[pl.BlockSpec(memory_space=pltpu.SMEM)] + in_vmem(8),
@@ -334,8 +333,352 @@
     )(order, qt, kt, kn, vn, lse, mixed, dmixed, factor)
 
 
+def reduce_kernel(
+    parts,
+    groups,
+    dq_ref,
+    wt_ref,
+    u_ref,
+    wc_ref,
+    mlp_ref,
+    small_ref,
+    down_ref,
+    up_ref,
+    own_ref,
+    ugather_ref,
+    mgather_ref,
+    sgather_ref,
+    pair_ref,
+    sum_ref,
+    urecv_ref,
+    mrecv_ref,
+    part_ref,
+    column_ref,
+    smine_ref,
+    srecv_ref,
+    pair_sem,
+    sum_sem,
+    u_sem,
+    m_sem,
+    line_sem,
+    side_sem,
+    small_sem,
+    cross_sem,
+):
+    chips = parts // 2
+    here = lax.axis_index("ctx")
+    group = lax.axis_index("fsdp")
+    core = lax.rem(here, 2)
+    chip = here // 2
+    other = here + 1 - 2 * core
+    ctx_peers = [lax.rem(here + step, parts) for step in range(1, parts)]
+    chip_peers = [lax.rem(chip + step, chips) for step in range(1, chips)]
+    group_peers = [lax.rem(group + step, groups) for step in range(1, groups)]
+
+    barrier = pltpu.get_barrier_semaphore()
+    for peer in ctx_peers:
+        pl.semaphore_signal(barrier, inc=1, device_id={"ctx": peer})
+    for peer in group_peers:
+        pl.semaphore_signal(barrier, inc=1, device_id={"fsdp": peer})
+    pl.semaphore_wait(barrier, parts + groups - 2)
+
+    def send(source, target, sems, device):
+        return pltpu.make_async_remote_copy(
+            src_ref=source,
+            dst_ref=target,
+            send_sem=sems[0],
+            recv_sem=sems[1],
+            device_id=device,
+        )
+
+    def pair_copy(index):
+        return send(
+            dq_ref.at[index, 1 - core],
+            pair_ref.at[index],
+            (pair_sem.at[0, index], pair_sem.at[1, index]),
+            {"ctx": other},
+        )
+
+    def u_copy(peer, source):
+        return send(
+            u_ref.at[peer],
+            urecv_ref.at[source],
+            (u_sem.at[0, peer], u_sem.at[1, source]),
+            {"fsdp": peer},
+        )
+
+    def m_copy(peer, source):
+        return send(
+            mlp_ref.at[peer],
+            mrecv_ref.at[source],
+            (m_sem.at[0, peer], m_sem.at[1, source]),
+            {"ctx": 2 * peer + core},
+        )
+
+    for index in range(chips):
+        pair_copy(index).start()
+    for peer in group_peers:
+        u_copy(peer, group).start()
+    for peer in chip_peers:
+        m_copy(peer, chip).start()
+    for index in range(chips):
+        pair_copy(index).wait_recv()
+
+    rows_half = own_ref.shape[0] // 2
+
+    def partial(target):
+        def half(index, carry):
+            rows = pl.ds(pl.multiple_of(index * rows_half, rows_half), rows_half)
+            part_ref[rows, :] = dot(dq_ref[target, core, :, rows], wt_ref[core], (0, 0)) + dot(
+                pair_ref[target, :, rows], wt_ref[1 - core], (0, 0)
+            )
+            return carry
+
+        lax.fori_loop(0, 2, half, 0)
+
+    def sum_copy(way, target):
+        return send(
+            sum_ref.at[way, target],
+            sum_ref.at[way, target],
+            (sum_sem.at[0, way, target], sum_sem.at[1, way, target]),
+            {"ctx": here + (2 if way else -2)},
+        )
+
+    def reduce_step(step):
+        last = step == chips - 2
+        for way, target, active, first, out_ref in (
+            (0, step - (chips - 1) + chip, step >= chips - 1 - chip, chip == chips - 1, down_ref),
+            (1, chips - 1 - step + chip, step >= chip, chip == 0, up_ref),
+        ):
+
+            @pl.when(active)
+            def _():
+                partial(target)
+
+                @pl.when(first)
+                def _():
+                    sum_ref[way, target] = part_ref[...].astype(bf16)
+
+                @pl.when(jnp.logical_not(first))
+                def _():
+                    sum_copy(way, target).wait_recv()
+                    sum_ref[way, target] = (
+                        part_ref[...] + sum_ref[way, target].astype(f32)
+                    ).astype(bf16)
+
+                if last:
+                    out_ref[...] = sum_ref[way, target]
+                else:
+                    sum_copy(way, target).start()
+
+            if last:
+
+                @pl.when(jnp.logical_not(active))
+                def _():
+                    out_ref[...] = jnp.zeros(out_ref.shape, bf16)
+
+    gathers = (ugather_ref, mgather_ref)
+
+    def line_copy(which, way, step, piece):
+        ref = gathers[which].at[2 * piece + core]
+        sems = (line_sem.at[0, which, way, step], line_sem.at[1, which, way, step])
+        return send(ref, ref, sems, {"ctx": here + (2 if way else -2)})
+
+    def side_copy(which, piece, lane):
+        ref = gathers[which].at[2 * piece + lane]
+        sems = (side_sem.at[0, which, piece], side_sem.at[1, which, piece])
+        return send(ref, ref, sems, {"ctx": other})
+
+    def line_sends(which, step, go):
+        @pl.when((chip < chips - 1) & (chip - step >= 0))
+        def _():
+            go(line_copy(which, 1, step, chip - step))
+
+        @pl.when((chip > 0) & (chip + step <= chips - 1))
+        def _():
+            go(line_copy(which, 0, step, chip + step))
+
+    def line_receive(which, step):
+        @pl.when(chip - 1 - step >= 0)
+        def _():
+            line_copy(which, 1, step, chip - 1 - step).wait_recv()
+            side_copy(which, chip - 1 - step, core).start()
+
+        @pl.when(chip + 1 + step <= chips - 1)
+        def _():
+            line_copy(which, 0, step, chip + 1 + step).wait_recv()
+            side_copy(which, chip + 1 + step, core).start()
+
+    def small_copy(peer, source):
+        return send(
+            smine_ref,
+            srecv_ref.at[source],
+            (small_sem.at[0, peer], small_sem.at[1, source]),
+            {"ctx": peer},
+        )
+
+    def cross_copy(peer, source):
+        return send(
+            sgather_ref.at[group],
+            sgather_ref.at[source],
+            (cross_sem.at[0, peer], cross_sem.at[1, source]),
+            {"fsdp": peer},
+        )
+
+    reduce_step(0)
+
+    total = u_ref[group].astype(f32)
+    for peer in group_peers:
+        u_copy(group, peer).wait_recv()
+        total = total + urecv_ref[peer].astype(f32)
+    ugather_ref[here] = total.astype(bf16)
+    side_copy(0, chip, core).start()
+    line_sends(0, 0, lambda copy: copy.start())
+    held = total.shape[0]
+    gain = jnp.sum(total * wc_ref[...].astype(f32), axis=1, keepdims=True)
+    column_ref[...] = jnp.zeros(column_ref.shape, f32)
+    column_ref[:held, :] = jnp.broadcast_to(gain, (held, PAD))
+    flat = column_ref[...].T[:1]
+    smine_ref[...] = small_ref[...]
+    for row in range(column_ref.shape[0] // PAD):
+        smine_ref[row : row + 1, :] = flat[:, row * PAD : (row + 1) * PAD]
+    for peer in ctx_peers:
+        small_copy(peer, here).start()
+
+    total = mlp_ref[chip].astype(f32)
+    for peer in chip_peers:
+        m_copy(chip, peer).wait_recv()
+        total = total + mrecv_ref[peer].astype(f32)
+    mgather_ref[here] = total.astype(bf16)
+    side_copy(1, chip, core).start()
+    line_sends(1, 0, lambda copy: copy.start())
+
+    for step in range(1, chips):
+        if step <= chips - 2:
+            reduce_step(step)
+        for which in range(2):
+            line_receive(which, step - 1)
+            if step <= chips - 2:
+                line_sends(which, step, lambda copy: copy.start())
+        if step == 1:
+            small = smine_ref[...]
+            for peer in ctx_peers:
+                small_copy(here, peer).wait_recv()
+                small = small + srecv_ref[peer]
+            sgather_ref[group] = small
+            for peer in group_peers:
+                cross_copy(peer, group).start()
+
+    partial(chip)
+    own_ref[...] = part_ref[...]
+
+    for which in range(2):
+        for piece in range(chips):
+            side_copy(which, piece, 1 - core).wait_recv()
+            side_copy(which, piece, core).wait_send()
+        for step in range(chips - 1):
+            line_sends(which, step, lambda copy: copy.wait_send())
+    for index in range(chips):
+        pair_copy(index).wait_send()
+    for peer in group_peers:
+        cross_copy(group, peer).wait_recv()
+        cross_copy(peer, group).wait_send()
+        u_copy(peer, group).wait_send()
+    for peer in chip_peers:
+        m_copy(peer, chip).wait_send()
+    for peer in ctx_peers:
+        small_copy(peer, here).wait_send()
+    for step in range(chips - 2):
+
+        @pl.when(step >= chips - 1 - chip)
+        def _():
+            sum_copy(0, step - (chips - 1) + chip).wait_send()
+
+        @pl.when(step >= chip)
+        def _():
+            sum_copy(1, chips - 1 - step + chip).wait_send()
+
+
+def reduce_gradients(parts, groups, dqkv, w_pair, u_parts, w_columns, mlp, small):
+    chips = parts // 2
+    rows_dev = dqkv.shape[3]
+    rows, width = w_columns.shape
+    lanes = -(-rows // PAD) * PAD
+    dma = pltpu.SemaphoreType.DMA
+    return pl.pallas_call(
+        functools.partial(reduce_kernel, parts, groups),
+        name="reduce_gradients",
+        out_shape=[
+            jax.ShapeDtypeStruct((rows_dev, D), bf16),
+            jax.ShapeDtypeStruct((rows_dev, D), bf16),
+            jax.ShapeDtypeStruct((rows_dev, D), f32),
+            jax.ShapeDtypeStruct((parts, rows, width), bf16),
+            jax.ShapeDtypeStruct((parts,) + mlp.shape[1:], bf16),
+            jax.ShapeDtypeStruct((groups,) + small.shape, f32),
+        ],
+        in_specs=in_vmem(6),
+        out_specs=in_vmem(6),
+        scratch_shapes=[
+            pltpu.VMEM((chips,) + dqkv.shape[2:], bf16),
+            pltpu.VMEM((2, chips, rows_dev, D), bf16),
+            pltpu.VMEM(u_parts.shape, bf16),
+            pltpu.VMEM(mlp.shape, bf16),
+            pltpu.VMEM((rows_dev, D), f32),
+            pltpu.VMEM((lanes, PAD), f32),
+            pltpu.VMEM(small.shape, f32),
+            pltpu.VMEM((parts,) + small.shape, f32),
+            dma((2, chips)),
+            dma((2, 2, chips)),
+            dma((2, groups)),
+            dma((2, chips)),
+            dma((2, 2, 2, chips)),
+            dma((2, 2, chips)),
+            dma((2, parts)),
+            dma((2, groups)),
+        ],
+        compiler_params=pltpu.CompilerParams(
+            vmem_limit_bytes=60 * 1024 * 1024, collective_id=1, has_side_effects=True
+        ),
+    )(dqkv, w_pair, u_parts, w_columns, mlp, small)
+
+
+def update_kernel(rates, *refs):
+    sets = len(rates)
+    for index, rate in enumerate(rates):
+        weight, first, second, gradient = (ref[...] for ref in refs[4 * index : 4 * index + 4])
+        outs = refs[4 * (sets + index) : 4 * (sets + index) + 4]
+        new, first, second = adamw(weight, first, second, gradient.astype(f32), rate, decay_rate)
+        outs[0][...] = new
+        outs[1][...] = first
+        outs[2][...] = second
+        outs[3][...] = new.astype(bf16)
+
+
+def update(rates, *arrays):
+    step_rows = 32
+    rows = arrays[0].shape[0]
+    specs, shapes, moved = [], [], 0
+    for array in arrays:
+        specs.append(pl.BlockSpec((step_rows, array.shape[1]), lambda i: (i, 0)))
+    for index in range(len(rates)):
+        shape = arrays[4 * index].shape
+        shapes += [jax.ShapeDtypeStruct(shape, f32)] * 3 + [jax.ShapeDtypeStruct(shape, bf16)]
+        moved += shape[0] * shape[1] * 28
+    return pl.pallas_call(
+        functools.partial(update_kernel, rates),
+        name="update_weights",
+        grid=(rows // step_rows,),
+        in_specs=specs,
+        out_specs=specs,
+        out_shape=shapes,
+        compiler_params=params(),
+        cost_estimate=pl.CostEstimate(flops=moved, bytes_accessed=moved, transcendentals=0),
+    )(*arrays)
+
+
 def body(
     parts,
+    groups,
     inputs,
     cotangent,
     block_order,
@@ -364,19 +707,30 @@
     gain_one = small_params[:D]
     gain_two = small_params[D : 2 * D]
     query_scale = small_params[2 * D :]
-    own_columns = jnp.concatenate(
-        [
-            lax.dynamic_slice_in_dim(w_qkv, part * D + here * width, width, 1).astype(bf16)
-            for part in range(3)
-        ],
-        axis=1,
-    )
-    own_qkv = lax.all_gather(own_columns, "fsdp", axis=0, tiled=True)
+    core = lax.rem(here, 2)
+    group = lax.axis_index("fsdp")
+    rows = w_qkv.shape[0]
+
+    def head_columns(owner):
+        return jnp.concatenate(
+            [
+                lax.dynamic_slice_in_dim(w_qkv, part * D + owner * width, width, 1)
+                for part in range(3)
+            ],
+            axis=1,
+        )
+
+    gain_rows = lax.dynamic_slice_in_dim(gain_one, group * rows, rows, 0)[:, None]
+    columns = [head_columns(here - core + lane) for lane in range(2)]
+    gained = jnp.concatenate([(gain_rows * part).astype(bf16) for part in columns], axis=1)
+    w_pair = lax.all_gather(gained, "fsdp", axis=0, tiled=True).T.reshape(2, 3 * width, D)
+    w_flipped = lax.dynamic_index_in_dim(w_pair, core, 0, False)
+    own_qkv = w_flipped.T
+    w_columns = head_columns(here).astype(bf16)
     layer_in = inputs[0].astype(f32)
     scale_one = rms_scale(layer_in)
     unit_one = layer_in * scale_one
-    normed = (unit_one * gain_one).astype(bf16)
-    normed_all = lax.all_gather(normed, "ctx", axis=0, tiled=True)
+    unit_all = lax.all_gather(unit_one.astype(bf16), "ctx", axis=0, tiled=True)
     out_full, up_full, down_full = (
         lax.all_gather(w_out.astype(bf16), "fsdp", axis=0, tiled=True),
         lax.all_gather(w_up.astype(bf16), "fsdp", axis=0, tiled=True),
@@ -384,7 +738,6 @@
     )
     factor = scale_base / math.sqrt(HD) * jax.nn.softplus(query_scale)
     factor_two = (factor * LOG2E)[:, None]
-    w_flipped = own_qkv.T
     pieces = []
     for head in range(heads):
         for part in (1, 2):
@@ -392,7 +745,7 @@
             pieces.append(jnp.pad(own_qkv[:, at : at + HD], ((0, 0), (0, PAD - HD))))
     w_natural = jnp.concatenate(pieces, axis=1)
     *kept, mixed = attention_forward(
-        order, normed_all, w_natural, w_flipped, factor_two, parts, heads
+        order, unit_all, w_natural, w_flipped, factor_two, parts, heads
     )
     attn_flipped = lax.all_to_all(mixed, "ctx", 0, 0, tiled=True).reshape(D, rows_dev)
     mid = layer_in + dot(attn_flipped, out_full, (0, 0))
@@ -417,71 +770,100 @@
     dbranch = dmid.astype(bf16)
     grad_out = dot(attn_flipped, dbranch)
     dattn = dot(out_full, dbranch, (1, 1)).astype(bf16)
+    half = rows // 2
+    grads = jnp.stack([grad_out.astype(bf16), grad_up.astype(bf16), grad_down.astype(bf16)])
+    grads = grads.reshape(3, groups, 2, half, D)
+    pair = [(i, i ^ 1) for i in range(parts)]
+    theirs = lax.dynamic_index_in_dim(grads, 1 - core, 2, False)
+    mine = lax.dynamic_index_in_dim(grads, core, 2, False)
+    mine = (mine.astype(f32) + lax.ppermute(theirs, "ctx", pair).astype(f32)).astype(bf16)
+    mlp_sum = lax.dynamic_index_in_dim(mine, group, 1, False).astype(f32)
+    for step in range(1, groups):
+        chunk = lax.dynamic_index_in_dim(mine, group ^ step, 1, False)
+        swap = [(i, i ^ step) for i in range(groups)]
+        mlp_sum = mlp_sum + lax.ppermute(chunk, "fsdp", swap).astype(f32)
+    mlp_part = (
+        mlp_sum.astype(bf16).reshape(3, parts // 2, rows // parts, D).transpose(1, 0, 2, 3)
+    )
     dmixed = lax.all_to_all(dattn.reshape(parts, width, rows_dev), "ctx", 0, 0, tiled=True)
     dqkv, dscale = attention_backward(order, kept, mixed, dmixed, factor_two, heads)
-    grad_qkv = dot(normed_all, dqkv, (0, 1))
-    dnormed_part = dot(dqkv, w_flipped, (0, 0)).astype(bf16)
-    dnormed = lax.psum_scatter(dnormed_part, "ctx", scatter_dimension=0, tiled=True).astype(f32)
+    u_parts = (
+        lax.dot_general(
+            unit_all.reshape(parts, rows_dev, D),
+            dqkv,
+            (((0, 1), (0, 2)), ((), ())),
+            preferred_element_type=f32,
+        )
+        .astype(bf16)
+        .reshape(groups, rows, 3 * width)
+    )
     scale_grad = (
         jnp.sum(dscale, axis=(0, 2))
         / factor_two[:, 0]
         * (scale_base / math.sqrt(HD))
         * jax.nn.sigmoid(query_scale)
     )
-    dunit_one = dnormed * gain_one
-    input_grad = dmid + scale_one * (
-        dunit_one - unit_one * jnp.mean(dunit_one * unit_one, axis=-1, keepdims=True)
-    )
-    gain_one_grad = jnp.sum(dnormed * unit_one, axis=0)
-    small_grad = jnp.concatenate([gain_one_grad, gain_two_grad, scale_grad])
-    small_total = lax.psum(small_grad, ("ctx", "fsdp"))
+    lanes = -(-rows // PAD) * PAD
+    small_rows = -(-(lanes + D + PAD) // (8 * PAD)) * 8
+    small = jnp.concatenate([jnp.zeros((lanes,), f32), gain_two_grad, scale_grad])
+    small = jnp.pad(small, (0, small_rows * PAD - small.shape[0])).reshape(small_rows, PAD)
+    send_down, send_up, own_part, u_all, mlp_all, small_all = reduce_gradients(
+        parts,
+        groups,
+        dqkv.reshape(parts // 2, 2, 3 * width, rows_dev),
+        w_pair,
+        u_parts,
+        w_columns,
+        mlp_part,
+        small,
+    )
+    got_down = lax.ppermute(send_down, "ctx", [(i, i - 2) for i in range(2, parts)])
+    got_up = lax.ppermute(send_up, "ctx", [(i, i + 2) for i in range(parts - 2)])
+    total_qkv = (
+        u_all.reshape(parts, rows, 3, width).transpose(1, 2, 0, 3).reshape(rows, 3 * D)
+        * gain_rows
+    ).astype(bf16)
+    total_mlp = (
+        mlp_all.reshape(parts // 2, 2, 3, rows // parts, D)
+        .transpose(2, 1, 0, 3, 4)
+        .reshape(3, rows, D)
+    )
     rate_qkv = qkv_rate_base / math.sqrt(D)
     rate_out = 0.5 / math.sqrt(max(D // 256, 1))
     rate_up = 0.5 / math.sqrt(D)
     rate_down = 0.5 / math.sqrt(FF)
-    shard_out, shard_up, shard_down = (
-        lax.psum_scatter(grad.astype(bf16), "fsdp", scatter_dimension=0, tiled=True)
-        for grad in (grad_out, grad_up, grad_down)
-    )
-    total_out, total_up, total_down = (
-        lax.psum(shard, "ctx").astype(f32) for shard in (shard_out, shard_up, shard_down)
-    )
-    shard_qkv = lax.psum_scatter(grad_qkv.astype(bf16), "fsdp", scatter_dimension=0, tiled=True)
-    rows = shard_qkv.shape[0]
-    total_qkv = (
-        lax.all_gather(shard_qkv, "ctx", axis=0)
-        .reshape(parts, rows, 3, width)
-        .transpose(1, 2, 0, 3)
-        .reshape(rows, 3 * D)
-        .astype(f32)
-    )
-    qkv_set = adamw(w_qkv, m_qkv, v_qkv, total_qkv, rate_qkv, decay_rate)
-    out_set = adamw(w_out, m_out, v_out, total_out, rate_out, decay_rate)
-    up_set = adamw(w_up, m_up, v_up, total_up, rate_up, decay_rate)
-    down_set = adamw(w_down, m_down, v_down, total_down, rate_down, decay_rate)
+    updated = update(
+        (rate_qkv, rate_out, rate_up, rate_down),
+        w_qkv,
+        m_qkv,
+        v_qkv,
+        total_qkv,
+        w_out,
+        m_out,
+        v_out,
+        total_mlp[0],
+        w_up,
+        m_up,
+        v_up,
+        total_mlp[1],
+        w_down,
+        m_down,
+        v_down,
+        total_mlp[2],
+    )
+    flat = small_all.reshape(groups, small_rows * PAD)
+    rest = jnp.sum(flat[:, lanes : lanes + D + HD], axis=0)
+    small_total = jnp.concatenate([flat[:, :rows].reshape(D), rest])
     small_set = adamw(small_params, small_m, small_v, small_total, small_rate, 0.0)
+    dunit_one = own_part + got_down.astype(f32) + got_up.astype(f32)
+    input_grad = dmid + scale_one * (
+        dunit_one - unit_one * jnp.mean(dunit_one * unit_one, axis=-1, keepdims=True)
+    )
     return (
         output[None],
         input_grad.astype(bf16)[None],
-        qkv_set[0],
-        qkv_set[1],
-        qkv_set[2],
-        qkv_set[0].astype(bf16),
-        out_set[0],
-        out_set[1],
-        out_set[2],
-        out_set[0].astype(bf16),
-        up_set[0],
-        up_set[1],
-        up_set[2],
-        up_set[0].astype(bf16),
-        down_set[0],
-        down_set[1],
-        down_set[2],
-        down_set[0].astype(bf16),
-        small_set[0],
-        small_set[1],
-        small_set[2],
+        *updated,
+        *small_set,
     )
 
 
@@ -489,7 +871,7 @@
     rows = P("fsdp", "ctx", None)
     weight = P("fsdp", None)
     return jax.shard_map(
-        functools.partial(body, mesh.shape["ctx"]),
+        functools.partial(body, mesh.shape["ctx"], mesh.shape["fsdp"]),
         mesh=mesh,
         in_specs=(rows, rows, weight) + (weight,) * 12 + (P(),) * 3,
         out_specs=(rows, rows) + (weight,) * 16 + (P(),) * 3,

time: 747 us -> 683 us (0.914)
  Pallas kernels: 104 us -> 249 us
  waiting for transfers between devices: 361 us -> 263 us
  blocking collectives: 74.8 us -> 0 us
  matrix products: 68.7 us -> 40.2 us
  local copies, waits for them, and re-layouts: 70.8 us -> 58.1 us
  starting transfers between devices: 4.87 us -> 16.2 us
    pallas_call x0 -> x2, Pallas kernels: none -> 145 us  [the longest x1 120 us: reduce_gradients(): pl.pallas_call(functools.partial(reduce_kernel, parts, groups), name='red...]
    reduce_scatter x5 -> x0, waiting for transfers between devices: 114 us -> none  [the longest x1 57.9 us: body(): lax.psum_scatter(dnormed_part, 'ctx', scatter_dimension=0, tiled=True)]
    ppermute x0 -> x6, waiting for transfers between devices: none -> 43.2 us  [the longest x3 43.2 us: body(): mlp_sum = mlp_sum + lax.ppermute(chunk, 'fsdp', swap).astype(f32)]
    psum x1 -> x0, blocking collectives: 38 us -> none  [body(): small_total = lax.psum(small_grad, ('ctx', 'fsdp'))]
    all_to_all x1 -> x0, blocking collectives: 36.8 us -> none  [body(): lax.all_to_all(dattn.reshape(parts, width, rows_dev), 'ctx', 0, 0, tiled=...]
    unnamed x61 -> x52, local copies, waits for them, and re-layouts: 46.9 us -> 10.3 us
    dot_general x11 -> x9, matrix products: 68.7 us -> 33.9 us  [dot(): lax.dot_general(left, right, (((contract[0],), (contract[1],)), ((), ()))...]
    psum x1 -> x0, waiting for transfers between devices: 32.4 us -> none  [body(): lax.psum(shard, 'ctx').astype(f32)]
  transfers between devices with their start and end apart: 13 -> 13, of which waited for: 9 -> 7; matrix products, arithmetic and copies ran while one was open for 21% -> 11% of each run, Pallas kernels for 14% -> 19%
where the time goes in v2:
time: 683 us; the launch traced here: 675 us
  waiting for transfers between devices  263 us (39%)
  Pallas kernels  249 us (36%)
  local copies, waits for them, and re-layouts  58.1 us (9%)
  matrix products  40.2 us (6%)
  other arithmetic  34.3 us (5%)
  starting transfers between devices  16.2 us (2%)
  between operations  14.4 us (2%)
    pallas_call x1, Pallas kernels, reduce_gradients(): pl.pallas_call(functools.partial(reduce_kernel, parts, groups), name='red...  120 us
    all_gather x1, waiting for transfers between devices, body(): unit_all = lax.all_gather(unit_one.astype(bf16), 'ctx', axis=0, tiled=True)  93.2 us
    pallas_call x1, Pallas kernels, attention_forward(): pl.pallas_call(functools.partial(forward_kernel, heads), name='attention_...  53.7 us
    pallas_call x1, Pallas kernels, attention_backward(): pl.pallas_call(functools.partial(backward_kernel, heads), name='attention...  50.4 us
    ppermute x3, waiting for transfers between devices, body(): mlp_sum = mlp_sum + lax.ppermute(chunk, 'fsdp', swap).astype(f32)  43.2 us
    all_gather x1, waiting for transfers between devices, body(): lax.all_gather(w_down.astype(bf16), 'fsdp', axis=0, tiled=True)  36 us
    all_gather x1, waiting for transfers between devices, body(): lax.all_gather(gained, 'fsdp', axis=0, tiled=True)  35.3 us
    dot_general x9, matrix products, dot(): lax.dot_general(left, right, (((contract[0],), (contract[1],)), ((), ()))...  33.9 us
  transfers between devices with their start and end apart: 13, of which 7 were waited for; matrix products, arithmetic and copies ran while one was open for 11% of the time, Pallas kernels for 19%

profile of v2, /device:TPU:0, one launch (start us, length us, event | category | flops | bytes accessed | tf_op | source)
XLA Modules:
  0.0 674.9 jit_solution(9835664694053876544)
XLA Ops:
  15.0 2.5 convert_element_type.129
  19.4 35.3 %all-gather.8.cloned.1.call-done = bf16[1280,960]{1,0:T(8,128)(2,1)} async-done(((bf16[320,960]{1,0:T(8,128)(2,1)}), bf16[1280,960]{1,0:T(8,128)(2,1)}) %all-gather.8.cloned.1.call-update) | async-done | bytes 2457616 | tf_op jit(solution)/shard_map/all_gather | solution.py:726
  54.7 4.3 copy.47
  63.1 93.2 %all-gather.6.cloned.1.call-done.x_ref = bf16[4096,1280]{1,0:T(8,128)(2,1)} async-done(((bf16[512,1280]{1,0:T(8,128)(2,1)}), bf16[4096,1280]{1,0:T(8,128)(2,1)}) %all-gather.6.cloned.1.call-update) | async-done | bytes 10485776 | tf_op jit(solution)/shard_map/all_gather | solution.py:733
  156.3 53.7 %attention_forward.1 = (bf16[2,128,4096]{2,1,0:T(8,128)(2,1)}, bf16[2,80,4096]{2,1,0:T(8,128)(2,1)}, bf16[2,4096,128]{2,1,0:T(8,128)(2,1)}, bf16[2,4096,128]{2,1...) custom-call(s32[16]{0:T(128)} %bitcast.117, ...), custom_call_target="tpu_custom_call" | custom-call | tf_op jit(solution)/shard_map/attention_forward/pallas_call | solution.py:289
  210.1 3.8 all-to-all-start
  213.9 31.9 %all-to-all-done = bf16[8,160,512]{2,1,0:T(8,128)(2,1)S(1)} async-done(((bf16[8,160,512]{2,1,0:T(8,128)(2,1)}), bf16[8,160,512]{2,1,0:T(8,128)(2,1)S(1)}, u32[]{:S(2)}, u32[]{:S(2)}) %all-to-all-start) | async-done | bytes 1310752 | tf_op jit(solution)/shard_map/all_to_all | solution.py:750
  245.8 5.4 multiply_reduce_fusion.2
  251.2 4.7 fusion.38
  257.4 3.7 convolution_convert_fusion
  261.1 36.0 %all-gather.14.cloned.1.call-done = bf16[1280,1280]{1,0:T(8,128)(2,1)} async-done(((bf16[320,1280]{1,0:T(8,128)(2,1)}), bf16[1280,1280]{1,0:T(8,128)(2,1)}) %all-gather.14.cloned.1.call-update) | async-done | bytes 3276816 | tf_op jit(solution)/shard_map/all_gather | solution.py:737
  297.1 5.5 fusion.5
  310.3 4.5 pad_maximum_fusion
  314.8 6.8 %constant_dynamic-slice_fusion.1 = (bf16[3,4,1,160,1280]{4,3,2,1,0:T(8,128)(2,1)}, bf16[3,4,1,160,1280]{4,3,2,1,0:T(8,128)(2,1)S(1)}) fusion(bf16[3,4,2,160,1280]{4,3,2,1,0:T(8,128)(2,1)} %pad_maximum_fusion, s32[]{:T(128)S(6)} %select_n.63, s32[]{:T(128)S(6)} %select_n.68), kind=kLoop, calls=%fused_computation.91 | loop fusion | bytes 19660808 | tf_op jit(solution)/shard_map/jit(dynamic_index_in_dim)/dynamic_slice | solution.py:778
  321.6 2.8 copy.72
  329.5 4.8 all-to-all-start.1
  336.8 6.8 %fusion.8 = bf16[1,512,1280]{2,1,0:T(8,128)(2,1)} fusion(f32[512,1280]{1,0:T(8,128)} %get-tuple-element.114, bf16[1280,1280]{1,0:T(8,128)(2,1)} %all-gather.14.cloned.1.call-done, f32[512,1280]{1,0:T(8,128)} %copy-done.21), kind=kOutput, calls=%fused_computation.27 | convolution fusion | flops 1682309120 | bytes 9830400 | tf_op jit(solution)/shard_map/dot_general | solution.py:52
  343.6 22.9 %all-to-all-done.1.dt_ref = bf16[8,160,512]{2,1,0:T(8,128)(2,1)S(1)} async-done(((bf16[8,160,512]{2,1,0:T(8,128)(2,1)}), bf16[8,160,512]{2,1,0:T(8,128)(2,1)S(1)}, u32[]{:S(2)}, u32[]{:S(2)}) %all-to-all-start.1) | async-done | bytes 1310752 | tf_op jit(solution)/shard_map/all_to_all | solution.py:788
  367.6 50.4 %attention_backward.1 = (bf16[8,480,512]{2,1,0:T(8,128)(2,1)}, f32[2,80,128]{2,1,0:T(8,128)}) custom-call(s32[16]{0:T(128)} %bitcast.118, bf16[2,128,4096]{2,1,0:T(8,128)(2,1)} %get-tuple-element.52.qt_ref, bf16[2,80,4096]{2,1,0:T(8,128)(2,1)} %get-tuple-element.53.kt_ref, bf16[2,4096,128]{2,1,0:T(8,128)(2,1)} %get-tuple-element.54.kn_ref, ...), custom_call_target="tpu_custom_call" | custom-call | tf_op jit(solution)/shard_map/attention_backward/pallas_call | solution.py:315
  418.0 5.3 fusion
  430.9 6.3 fusion.7
  440.4 18.2 %collective-permute-done.3 = bf16[3,160,1280]{2,1,0:T(8,128)(2,1)} collective-permute-done((bf16[3,160,1280]{2,1,0:T(8,128)(2,1)}, bf16[3,160,1280]{2,1,0:T(8,128)(2,1)}, u32[]{:S(2)}, u32[]{:S(2)}) %collective-permute-start.3) | collective-permute-done | bytes 1228832 | tf_op jit(solution)/shard_map/ppermute | solution.py:784
  458.6 24.9 %collective-permute-done.2 = bf16[3,160,1280]{2,1,0:T(8,128)(2,1)} collective-permute-done((bf16[3,160,1280]{2,1,0:T(8,128)(2,1)}, bf16[3,160,1280]{2,1,0:T(8,128)(2,1)}, u32[]{:S(2)}, u32[]{:S(2)}) %collective-permute-start.2) | collective-permute-done | bytes 1228832 | tf_op jit(solution)/shard_map/ppermute | solution.py:784
  483.6 3.0 fusion.24
  487.7 120.3 %reduce_gradients.1 = (bf16[512,1280]{1,0:T(8,128)(2,1)}, bf16[512,1280]{1,0:T(8,128)(2,1)}, f32[512,1280]{1,0:T(8,128)}, bf16[8,320,480]{2,1,0:T(8,128)(2,1)}, ...) custom-call(bf16[4,2,480,512]{3,2,1,0:T(8,128)(2,1)} %bitcast.105, bf16[2,480,1280]{2,1,0:T(8,128)(2,1)} %bitcast.94, ...), custom_call_target="tpu_custom_call" | custom-call | tf_op jit(solution)/shard_map/reduce_gradients/pallas_call | solution.py:608
  611.9 5.1 copy.57
  617.0 5.6 copy.58
  622.6 6.1 copy.59
  632.2 4.3 multiply_convert_fusion.refs_3_
  636.5 24.7 %update_weights.1 = (f32[320,3840]{1,0:T(8,128)}, f32[320,3840]{1,0:T(8,128)}, f32[320,3840]{1,0:T(8,128)}, bf16[320,3840]{1,0:T(8,128)(2,1)}, f32[320,1280]{1,0...) custom-call(f32[320,3840]{1,0:T(8,128)} %refs_0_.1, ...), custom_call_target="tpu_custom_call" | custom-call | flops 68812800 | bytes 68812800 | tf_op jit(solution)/shard_map/update_weights/pallas_call | solution.py:667
  661.8 2.6 fusion.10
  664.5 3.7 fusion.28
  (114 shorter events, 51.2 us)
Async XLA Ops:
  7.2 47.5 %all-gather.8.cloned.1.call-start = ((), (), s32[]{:S(2)}) async-start(), calls=%async_computation.3 | async-start | bytes 3276800 | tf_op jit(solution)/shard_map/all_gather | solution.py:726
  12.2 144.2 %all-gather.6.cloned.1.call-start = ((), (), s32[]{:S(2)}) async-start(), calls=%async_computation.2 | async-start | bytes 11796480 | tf_op jit(solution)/shard_map/all_gather | solution.py:733
  13.9 199.9 %all-gather.10.cloned.1.call-start = ((), (), s32[]{:S(2)}) async-start(), calls=%async_computation.4 | async-start | bytes 4096000 | tf_op jit(solution)/shard_map/all_gather | solution.py:735
  15.0 2.7 copy-start.9
  15.0 236.2 %all-gather.12.cloned.1.call-start = ((), (), s32[]{:S(2)}) async-start(), calls=%async_computation.5 | async-start | bytes 4096000 | tf_op jit(solution)/shard_map/all_gather | solution.py:736
  17.6 279.5 %all-gather.14.cloned.1.call-start = ((), (), s32[]{:S(2)}) async-start(), calls=%async_computation.6 | async-start | bytes 4096000 | tf_op jit(solution)/shard_map/all_gather | solution.py:737
  210.1 35.7 %all-to-all-start = ((bf16[8,160,512]{2,1,0:T(8,128)(2,1)}), bf16[8,160,512]{2,1,0:T(8,128)(2,1)S(1)}, u32[]{:S(2)}, u32[]{:S(2)}) async-start(bf16[8,160,512]{2,1,0:T(8,128)(2,1)} %get-tuple-element.51.ot_ref), calls=%async_computation | async-start | bytes 2621440 | tf_op jit(solution)/shard_map/all_to_all | solution.py:750
  251.2 6.2 copy-start.13
  297.1 5.5 copy-start.3
  302.6 2.0 copy-start.20
  304.6 2.1 copy-start.14
  307.4 1.9 copy-start.4
  307.4 2.9 copy-start.12
  321.6 3.5 copy-start.2
  321.6 4.5 copy-start.5
  324.5 93.5 %collective-permute-start = (bf16[3,4,160,1280]{3,2,0,1:T(8,128)(2,1)}, bf16[3,4,160,1280]{3,2,0,1:T(8,128)(2,1)}, u32[]{:S(2)}, u32[]{:S(2)}) collective-permute-start(bf16[3,4,160,1280]{3,2,0,1:T(8,128)(2,1)} %bitcast.87), channel_id=1, source_target_pairs={{0,4},{4,0},{8,12},{12,8},{16,20},{20,16},{24,28},{28,24},{1,5},{5... | collective-permute-start | bytes 14745608 | tf_op jit(solution)/shard_map/ppermute | solution.py:779
  329.5 37.0 %all-to-all-start.1 = ((bf16[8,160,512]{2,1,0:T(8,128)(2,1)}), bf16[8,160,512]{2,1,0:T(8,128)(2,1)S(1)}, u32[]{:S(2)}, u32[]{:S(2)}) async-start(bf16[8,160,512]{2,1,0:T(8,128)(2,1)} %bitcast.101), calls=%async_computation.1 | async-start | bytes 2621440 | tf_op jit(solution)/shard_map/all_to_all | solution.py:788
  367.6 63.3 %slice-start = ((s8[10485760]{0:T(1024)(128)(4,1)}), s8[2097152]{0:T(1024)(128)(4,1)S(1)}, s32[]{:S(2)}) async-start(s8[10485760]{0:T(1024)(128)(4,1)} %bitcast.95), calls=%async_computation.7 | async-start | bytes 4194304
  418.0 13.0 %slice-start.1 = ((s8[10485760]{0:T(1024)(128)(4,1)}), s8[4194304]{0:T(1024)(128)(4,1)S(1)}, s32[]{:S(2)}) async-start(s8[10485760]{0:T(1024)(128)(4,1)} %bitcast.95), calls=%async_computation.8 | async-start | bytes 8388608
  418.0 13.0 %slice-start.2 = ((s8[10485760]{0:T(1024)(128)(4,1)}), s8[4194304]{0:T(1024)(128)(4,1)S(1)}, s32[]{:S(2)}) async-start(s8[10485760]{0:T(1024)(128)(4,1)} %bitcast.95), calls=%async_computation.9 | async-start | bytes 8388608
  423.3 4.1 copy-start.1
  423.3 7.6 %copy-start.11 = (bf16[8,480,512]{2,1,0:T(8,128)(2,1)S(1)}, bf16[8,480,512]{2,1,0:T(8,128)(2,1)}, u32[]{:S(2)}) copy-start(bf16[8,480,512]{2,1,0:T(8,128)(2,1)} %get-tuple-element.57) | copy-start | bytes 11796484
  427.4 31.2 %collective-permute-start.3 = (bf16[3,160,1280]{2,1,0:T(8,128)(2,1)}, bf16[3,160,1280]{2,1,0:T(8,128)(2,1)}, u32[]{:S(2)}, u32[]{:S(2)}) collective-permute-start(bf16[3,160,1280]{2,1,0:T(8,128)(2,1)} %get-tuple-element.89), channel_id=1, source_target_pairs={{0,3},{1,2},{2,1},{3,0},{4,7},{5,6},{6,5},{7,4},{8,11},{9,10},{10,... | collective-permute-start | bytes 3686408 | tf_op jit(solution)/shard_map/ppermute | solution.py:784
  428.9 54.6 %collective-permute-start.2 = (bf16[3,160,1280]{2,1,0:T(8,128)(2,1)}, bf16[3,160,1280]{2,1,0:T(8,128)(2,1)}, u32[]{:S(2)}, u32[]{:S(2)}) collective-permute-start(bf16[3,160,1280]{2,1,0:T(8,128)(2,1)} %get-tuple-element.90), channel_id=1, source_target_pairs={{0,2},{1,3},{2,0},{3,1},{4,6},{5,7},{6,4},{7,5},{8,10},{9,11},{10,... | collective-permute-start | bytes 3686408 | tf_op jit(solution)/shard_map/ppermute | solution.py:784
  430.4 53.2 %collective-permute-start.1 = (bf16[3,160,1280]{2,1,0:T(8,128)(2,1)}, bf16[3,160,1280]{2,1,0:T(8,128)(2,1)}, u32[]{:S(2)}, u32[]{:S(2)}) collective-permute-start(bf16[3,160,1280]{2,1,0:T(8,128)(2,1)} %get-tuple-element.88), channel_id=1, source_target_pairs={{0,1},{1,0},{2,3},{3,2},{4,5},{5,4},{6,7},{7,6},{8,9},{9,8},{10,11... | collective-permute-start | bytes 3686408 | tf_op jit(solution)/shard_map/ppermute | solution.py:784
  430.9 8.7 %copy-start.15 = (f32[2,80,128]{2,1,0:T(8,128)S(1)}, f32[2,80,128]{2,1,0:T(8,128)}, u32[]{:S(2)}) copy-start(f32[2,80,128]{2,1,0:T(8,128)} %get-tuple-element.58) | copy-start | bytes 245764
  608.0 53.8 %collective-permute-start.5 = (bf16[512,1280]{1,0:T(8,128)(2,1)}, bf16[512,1280]{1,0:T(8,128)(2,1)}, u32[]{:S(2)}, u32[]{:S(2)}) collective-permute-start(bf16[512,1280]{1,0:T(8,128)(2,1)} %get-tuple-element.61), channel_id=1, source_target_pairs={{0,8},{4,12},{8,16},{12,20},{16,24},{20,28},{1,9},{5,13},{9,17},{1... | collective-permute-start | bytes 3932168 | tf_op jit(solution)/shard_map/ppermute | solution.py:821
  610.4 51.4 %collective-permute-start.4 = (bf16[512,1280]{1,0:T(8,128)(2,1)}, bf16[512,1280]{1,0:T(8,128)(2,1)}, u32[]{:S(2)}, u32[]{:S(2)}) collective-permute-start(bf16[512,1280]{1,0:T(8,128)(2,1)} %get-tuple-element.60), channel_id=1, source_target_pairs={{8,0},{12,4},{16,8},{20,12},{24,16},{28,20},{9,1},{13,5},{17,9},{2... | collective-permute-start | bytes 3932168 | tf_op jit(solution)/shard_map/ppermute | solution.py:820
  636.4 24.7 %copy-start.18 = (f32[2640]{0:T(1024)S(1)}, f32[2640]{0:T(1024)}, u32[]{:S(2)}) copy-start(f32[2640]{0:T(1024)} %param.34) | copy-start | bytes 31684
  636.4 24.7 %copy-start.19 = (f32[2640]{0:T(1024)S(1)}, f32[2640]{0:T(1024)}, u32[]{:S(2)}) copy-start(f32[2640]{0:T(1024)} %param.35) | copy-start | bytes 31684
  636.5 25.4 %copy-start.7 = (f32[512,1280]{1,0:T(8,128)S(1)}, f32[512,1280]{1,0:T(8,128)}, u32[]{:S(2)}) copy-start(f32[512,1280]{1,0:T(8,128)} %get-tuple-element.59) | copy-start | bytes 7864324
  661.8 2.6 copy-start.6
  (6 other events, 8.7 us)
Sparse Core Ops, SparseCore 0:
  12.3 42.3 all-gather.7
  56.9 99.3 all-gather.5
  158.8 43.5 all-gather.9
  204.7 45.0 all-gather.11
  252.0 45.0 all-gather.13

commit v3 on v2

--- a/solution.py
+++ b/solution.py
@@ -52,14 +52,6 @@
     return lax.dot_general(
         left, right, (((contract[0],), (contract[1],)), ((), ())), preferred_element_type=f32
     )
-
-
-def fill_slots(order_ref, slot_ref, num_blocks):
-    def place(slot, carry):
-        slot_ref[order_ref[slot]] = slot
-        return carry
-
-    lax.fori_loop(0, num_blocks, place, 0)
 
 
 def three_rows(row):
@@ -79,6 +71,22 @@
     return pl.ds(pl.multiple_of(tile * TILE, TILE), TILE)
 
 
+def block_at(slot):
+    return pl.ds(pl.multiple_of(slot * BLOCK, BLOCK), BLOCK)
+
+
+def tile_lanes(ref, head, slot_ref, tile, rows=slice(None)):
+    first, second = slot_ref[2 * tile], slot_ref[2 * tile + 1]
+    return jnp.concatenate(
+        [ref[head, rows, block_at(first)], ref[head, rows, block_at(second)]], axis=1
+    )
+
+
+def tile_rows(ref, head, slot_ref, tile):
+    first, second = slot_ref[2 * tile], slot_ref[2 * tile + 1]
+    return jnp.concatenate([ref[head, block_at(first), :], ref[head, block_at(second), :]], axis=0)
+
+
 def half_at(slot):
     return pl.ds(pl.multiple_of(lax.rem(slot, 2) * BLOCK, BLOCK), BLOCK)
 
@@ -89,53 +97,245 @@
     return key <= query
 
 
+def gather_kernel(
+    parts,
+    groups,
+    heads,
+    x_ref,
+    gained_ref,
+    mlp_ref,
+    factor_ref,
+    unit_ref,
+    full_ref,
+    wpair_ref,
+    qt_ref,
+    kt_ref,
+    vt_ref,
+    kn_ref,
+    vn_ref,
+    rows_ref,
+    wrecv_ref,
+    wflip_ref,
+    line_sem,
+    side_sem,
+    keep_sem,
+    w_sem,
+    mlp_sem,
+    cross_sem,
+    own_sem,
+):
+    chips = parts // 2
+    here = lax.axis_index("ctx")
+    group = lax.axis_index("fsdp")
+    core = lax.rem(here, 2)
+    chip = here // 2
+    other = here + 1 - 2 * core
+    width = heads * HD
+    group_peers = [lax.rem(group + step, groups) for step in range(1, groups)]
+
+    barrier = pltpu.get_barrier_semaphore()
+    pl.semaphore_signal(barrier, inc=1, device_id={"ctx": other})
+    for peer in group_peers:
+        pl.semaphore_signal(barrier, inc=1, device_id={"fsdp": peer})
+    for step in (1, chips - 1):
+        peer = lax.rem(chip + step, chips) * 2 + core
+        pl.semaphore_signal(barrier, inc=1, device_id={"ctx": peer})
+    pl.semaphore_wait(barrier, groups + 2)
+
+    def send(source, target, sems, device):
+        return pltpu.make_async_remote_copy(
+            src_ref=source,
+            dst_ref=target,
+            send_sem=sems[0],
+            recv_sem=sems[1],
+            device_id=device,
+        )
+
+    def line_copy(way, step, piece):
+        ref = rows_ref.at[2 * piece + core]
+        sems = (line_sem.at[0, way, step], line_sem.at[1, way, step])
+        return send(ref, ref, sems, {"ctx": here + (2 if way else -2)})
+
+    def side_copy(piece, lane):
+        ref = rows_ref.at[2 * piece + lane]
+        return send(ref, ref, (side_sem.at[0, piece], side_sem.at[1, piece]), {"ctx": other})
+
+    def w_copy(peer, source):
+        sems = (w_sem.at[0, peer], w_sem.at[1, source])
+        return send(gained_ref, wrecv_ref.at[source], sems, {"fsdp": peer})
+
+    def mlp_copy(peer, source):
+        sems = (mlp_sem.at[0, peer], mlp_sem.at[1, source])
+        return send(mlp_ref.at[:, core], full_ref.at[:, source, core], sems, {"fsdp": peer})
+
+    def cross_copy(source, lane):
+        ref = full_ref.at[:, source, lane]
+        sems = (cross_sem.at[0, source], cross_sem.at[1, source])
+        return send(ref, ref, sems, {"ctx": other})
+
+    def keep_copy(piece):
+        return pltpu.make_async_copy(rows_ref.at[piece], unit_ref.at[piece], keep_sem.at[piece])
+
+    own_copy = pltpu.make_async_copy(mlp_ref, full_ref.at[:, group], own_sem)
+
+    rows = x_ref[...].astype(f32)
+    rows_ref[here] = (rows * rms_scale(rows)).astype(bf16)
+
+    def forward(way, step, piece):
+        @pl.when((chip < chips - 1) if way else (chip > 0))
+        def _():
+            line_copy(way, step, piece).start()
+
+    for way in range(2):
+        forward(way, 0, chip)
+    side_copy(chip, core).start()
+    for peer in group_peers:
+        w_copy(peer, group).start()
+    own_copy.start()
+    keep_copy(here).start()
+    wrecv_ref[group] = gained_ref[...]
+    for peer in group_peers:
+        w_copy(group, peer).wait_recv()
+    for peer in group_peers:
+        mlp_copy(peer, group).start()
+    flipped = wrecv_ref[...].reshape(D, 6 * width).T
+    wpair_ref[0] = flipped[: 3 * width]
+    wpair_ref[1] = flipped[3 * width :]
+    wflip_ref[...] = wpair_ref[core]
+
+    extra_row = lax.broadcasted_iota(jnp.int32, (PAD - HD, BLOCK), 0)
+    extra = jnp.where(extra_row < 3, 1.0, 0.0)
+    spare = jnp.zeros((PAD - HD, BLOCK), bf16)
+
+    def project(piece):
+        def half(index, carry):
+            at = pl.ds(pl.multiple_of(index * BLOCK, BLOCK), BLOCK)
+            to = pl.ds(pl.multiple_of((piece * 2 + index) * BLOCK, BLOCK), BLOCK)
+            result = dot(wflip_ref[...], rows_ref[piece, at, :], (1, 1))
+            for head in range(heads):
+                query, key, value = (
+                    result[part * width + head * HD : part * width + (head + 1) * HD]
+                    for part in range(3)
+                )
+                qt_ref[head, :HD, to] = (query * factor_ref[...]).astype(bf16)
+                qt_ref[head, HD:, to] = spare
+                kt_ref[head, :, to] = key.astype(bf16)
+                vt_ref[head, :HD, to] = value.astype(bf16)
+                vt_ref[head, HD:, to] = jnp.ones((EXTRA, BLOCK), bf16)
+                kn_ref[head, to, :] = jnp.concatenate([key, extra], axis=0).T.astype(bf16)
+                vn_ref[head, to, :] = jnp.concatenate([value, extra], axis=0).T.astype(bf16)
+            return carry
+
+        lax.fori_loop(0, TILE // BLOCK, half, 0)
+
+    def visit(distance, carry):
+        for way in range(2):
+            piece = chip - distance if way else chip + distance
+            valid = (piece >= 0) if way else (piece <= chips - 1)
+
+            @pl.when(valid & (distance > 0))
+            def _():
+                line_copy(way, distance - 1, piece).wait_recv()
+                side_copy(piece, core).start()
+                forward(way, distance, piece)
+                keep_copy(2 * piece + core).start()
+
+        for way in range(2):
+            piece = chip - distance if way else chip + distance
+            valid = (piece >= 0) if way else ((piece <= chips - 1) & (distance > 0))
+
+            @pl.when(valid)
+            def _():
+                project(2 * piece + core)
+                side_copy(piece, 1 - core).wait_recv()
+                keep_copy(2 * piece + 1 - core).start()
+                project(2 * piece + 1 - core)
+
+        return carry
+
+    lax.fori_loop(0, chips, visit, 0)
+
+    for peer in group_peers:
+        mlp_copy(group, peer).wait_recv()
+        cross_copy(peer, core).start()
+    for peer in group_peers:
+        cross_copy(peer, 1 - core).wait_recv()
+        cross_copy(peer, core).wait_send()
+        w_copy(peer, group).wait_send()
+        mlp_copy(peer, group).wait_send()
+    own_copy.wait()
+
+    def drain(piece, carry):
+        keep_copy(2 * piece).wait()
+        keep_copy(2 * piece + 1).wait()
+        side_copy(piece, core).wait_send()
+
+        @pl.when((piece <= chip) & (chip < chips - 1))
+        def _():
+            line_copy(1, chip - piece, piece).wait_send()
+
+        @pl.when((piece >= chip) & (chip > 0))
+        def _():
+            line_copy(0, piece - chip, piece).wait_send()
+
+        return carry
+
+    lax.fori_loop(0, chips, drain, 0)
+
+
+def gather_rows(parts, groups, heads, rows, gained, mlp, factor):
+    rows_dev = rows.shape[0]
+    tokens = parts * rows_dev
+    dma = pltpu.SemaphoreType.DMA
+    chips = parts // 2
+    anywhere = pl.BlockSpec(memory_space=pl.ANY)
+    return pl.pallas_call(
+        functools.partial(gather_kernel, parts, groups, heads),
+        name="gather_rows",
+        out_shape=[
+            jax.ShapeDtypeStruct((parts, rows_dev, D), bf16),
+            jax.ShapeDtypeStruct((3, groups) + mlp.shape[1:], bf16),
+            jax.ShapeDtypeStruct((2, 3 * heads * HD, D), bf16),
+            jax.ShapeDtypeStruct((heads, PAD, tokens), bf16),
+            jax.ShapeDtypeStruct((heads, HD, tokens), bf16),
+            jax.ShapeDtypeStruct((heads, HD + EXTRA, tokens), bf16),
+            jax.ShapeDtypeStruct((heads, tokens, PAD), bf16),
+            jax.ShapeDtypeStruct((heads, tokens, PAD), bf16),
+        ],
+        in_specs=in_vmem(2) + [anywhere] + in_vmem(1),
+        out_specs=[anywhere] * 2 + in_vmem(6),
+        scratch_shapes=[
+            pltpu.VMEM((parts, rows_dev, D), bf16),
+            pltpu.VMEM((groups,) + gained.shape, bf16),
+            pltpu.VMEM((3 * heads * HD, D), bf16),
+            dma((2, 2, chips)),
+            dma((2, chips)),
+            dma((parts,)),
+            dma((2, groups)),
+            dma((2, groups)),
+            dma((2, groups)),
+            dma,
+        ],
+        compiler_params=pltpu.CompilerParams(
+            vmem_limit_bytes=60 * 1024 * 1024, collective_id=2, has_side_effects=True
+        ),
+    )(rows, gained, mlp, factor)
+
+
 def forward_kernel(
     heads,
-    order_ref,
-    x_ref,
-    wn_ref,
-    wt_ref,
-    factor_ref,
+    slot_ref,
     qt_ref,
-    kt_ref,
     kn_ref,
-    vn_ref,
+    vt_ref,
     lse_ref,
     ot_ref,
-    slot_ref,
-    vt_ref,
     acc_ref,
     top_ref,
 ):
-    tokens = x_ref.shape[0]
-    num_blocks = tokens // BLOCK
+    tokens = kn_ref.shape[1]
     num_tiles = tokens // TILE
     prompt_tiles = num_tiles // 2
-    fill_slots(order_ref, slot_ref, num_blocks)
-    width = heads * HD
-    lane = lax.broadcasted_iota(jnp.int32, (BLOCK, PAD), 1)
-    is_extra = (lane >= HD) & (lane < HD + 3)
-
-    def project(slot, carry):
-        rows = x_ref[pl.ds(pl.multiple_of(slot * BLOCK, BLOCK), BLOCK), :]
-        to = pl.ds(pl.multiple_of(order_ref[slot] * BLOCK, BLOCK), BLOCK)
-        natural = dot(rows, wn_ref[...])
-        flipped = dot(wt_ref[...], rows, (1, 1))
-        for head in range(heads):
-            key = natural[:, 2 * head * PAD : (2 * head + 1) * PAD]
-            value = natural[:, (2 * head + 1) * PAD : (2 * head + 2) * PAD]
-            kn_ref[head, to, :] = jnp.where(is_extra, 1.0, key).astype(bf16)
-            vn_ref[head, to, :] = jnp.where(is_extra, 1.0, value).astype(bf16)
-            at = head * HD
-            qt_ref[head, :HD, to] = (flipped[at : at + HD] * factor_ref[...]).astype(bf16)
-            qt_ref[head, HD:, to] = jnp.zeros((PAD - HD, BLOCK), bf16)
-            kt_ref[head, :, to] = flipped[width + at : width + at + HD].astype(bf16)
-            at = 2 * width + head * HD
-            vt_ref[head, :HD, to] = flipped[at : at + HD].astype(bf16)
-            vt_ref[head, HD:, to] = jnp.ones((EXTRA, BLOCK), bf16)
-        return carry
-
-    lax.fori_loop(0, num_blocks, project, 0)
     allowed = causal()
 
     def query_tile(tile, carry):
@@ -143,25 +343,27 @@
         top_ref[...] = jnp.full(top_ref.shape, -1e30, f32)
         acc_ref[...] = jnp.zeros(acc_ref.shape, f32)
 
-        def step(keys, masked):
+        queries = [tile_lanes(qt_ref, head, slot_ref, tile) for head in range(heads)]
+
+        def step(key_tile, masked):
             for head in range(heads):
-                scores = dot(kn_ref[head, keys, :], qt_ref[head, :, here])
+                scores = dot(tile_rows(kn_ref, head, slot_ref, key_tile), queries[head])
                 if masked:
                     scores = jnp.where(allowed, scores, -1e30)
                 old = top_ref[head]
                 top = jnp.maximum(old, jnp.max(scores, axis=0, keepdims=True))
                 probs = jnp.exp2(scores - top).astype(bf16)
                 acc_ref[head] = acc_ref[head] * jnp.exp2(old - top) + dot(
-                    vt_ref[head, :, keys], probs
+                    tile_lanes(vt_ref, head, slot_ref, key_tile), probs
                 )
                 top_ref[head] = top
 
         def full(key_tile, inner):
-            step(tile_at(key_tile), False)
+            step(key_tile, False)
             return inner
 
         lax.fori_loop(0, jnp.minimum(tile, prompt_tiles), full, 0)
-        step(here, True)
+        step(tile, True)
         for head in range(heads):
             acc = acc_ref[head]
             mass = acc[HD : HD + 1]
@@ -179,7 +381,7 @@
 
 def backward_kernel(
     heads,
-    order_ref,
+    slot_ref,
     qt_ref,
     kt_ref,
     kn_ref,
@@ -190,7 +392,6 @@
     factor_ref,
     dqkv_ref,
     dscale_ref,
-    slot_ref,
     qa_ref,
     da_ref,
     dq_ref,
@@ -202,7 +403,6 @@
     num_tiles = tokens // TILE
     prompt_tiles = num_tiles // 2
     width = heads * HD
-    fill_slots(order_ref, slot_ref, num_blocks)
 
     def prepare(block, carry):
         slot = slot_ref[block]
@@ -215,7 +415,7 @@
             da_ref[head, :HD, to] = grad
             da_ref[head, HD : HD + EXTRA, to] = three_rows(-delta)
             da_ref[head, HD + EXTRA :, to] = jnp.zeros((PAD - HD - EXTRA, BLOCK), bf16)
-            qa_ref[head, :HD, to] = qt_ref[head, :HD, to]
+            qa_ref[head, :HD, to] = qt_ref[head, :HD, block_at(slot)]
             qa_ref[head, HD : HD + EXTRA, to] = three_rows(-lse_ref[head, :, to])
             qa_ref[head, HD + EXTRA :, to] = jnp.zeros((PAD - HD - EXTRA, BLOCK), bf16)
         return carry
@@ -230,26 +430,29 @@
         here = tile_at(tile)
         dq_ref[...] = jnp.zeros(dq_ref.shape, f32)
 
-        def step(keys, masked):
+        def step(key_tile, masked):
+            keys = tile_at(key_tile)
             for head in range(heads):
-                probs = jnp.exp2(dot(kn_ref[head, keys, :], qa_ref[head, :, here]))
+                key_rows = tile_rows(kn_ref, head, slot_ref, key_tile)
+                value_rows = tile_rows(vn_ref, head, slot_ref, key_tile)
+                probs = jnp.exp2(dot(key_rows, qa_ref[head, :, here]))
                 if masked:
                     probs = jnp.where(allowed, probs, 0.0)
-                spread = dot(vn_ref[head, keys, :], da_ref[head, :, here])
+                spread = dot(value_rows, da_ref[head, :, here])
                 dscores = (probs * spread).astype(bf16)
                 dv_ref[head, :, keys] += dot(da_ref[head, :HD, here], probs.astype(bf16), (1, 1))
                 dk_ref[head, :, keys] += dot(qa_ref[head, :HD, here], dscores, (1, 1))
-                dq_ref[head] += dot(kt_ref[head, :, keys], dscores)
+                dq_ref[head] += dot(tile_lanes(kt_ref, head, slot_ref, key_tile), dscores)
 
         def full(key_tile, inner):
-            step(tile_at(key_tile), False)
+            step(key_tile, False)
             return inner
 
         lax.fori_loop(0, jnp.minimum(tile, prompt_tiles), full, 0)
-        step(here, True)
+        step(tile, True)
         for head in range(heads):
             dq = dq_ref[head]
-            product = dq * qt_ref[head, :HD, here].astype(f32)
+            product = dq * qa_ref[head, :HD, here].astype(f32)
             for lane in range(TILE // PAD):
                 dscale_ref[head] += product[:, lane * PAD : (lane + 1) * PAD]
             scaled = (dq * (factor_ref[...] * LN2)).astype(bf16)
@@ -284,34 +487,36 @@
     return pltpu.CompilerParams(vmem_limit_bytes=60 * 1024 * 1024)
 
 
-def attention_forward(order, rows, w_natural, w_flipped, factor, parts, heads):
-    tokens = rows.shape[0]
+def attention_forward(slots, qt, kn, vt, parts):
+    heads, tokens = kn.shape[:2]
     return pl.pallas_call(
         functools.partial(forward_kernel, heads),
         name="attention_forward",
         out_shape=[
-            jax.ShapeDtypeStruct((heads, PAD, tokens), bf16),
-            jax.ShapeDtypeStruct((heads, HD, tokens), bf16),
-            jax.ShapeDtypeStruct((heads, tokens, PAD), bf16),
-            jax.ShapeDtypeStruct((heads, tokens, PAD), bf16),
             jax.ShapeDtypeStruct((heads, 1, tokens), f32),
             jax.ShapeDtypeStruct((parts, heads * HD, tokens // parts), bf16),
         ],
-        in_specs=[pl.BlockSpec(memory_space=pltpu.SMEM)] + in_vmem(4),
-        out_specs=in_vmem(6),
+        in_specs=[pl.BlockSpec(memory_space=pltpu.SMEM)] + in_vmem(3),
+        out_specs=in_vmem(2),
         scratch_shapes=[
-            pltpu.SMEM((tokens // BLOCK,), jnp.int32),
-            pltpu.VMEM((heads, HD + EXTRA, tokens), bf16),
             pltpu.VMEM((heads, HD + EXTRA, TILE), f32),
             pltpu.VMEM((heads, 1, TILE), f32),
         ],
         compiler_params=params(),
-    )(order, rows, w_natural, w_flipped, factor)
-
-
-def attention_backward(order, kept, mixed, dmixed, factor, heads):
+        cost_estimate=attention_cost(heads, tokens, 2),
+    )(slots, qt, kn, vt)
+
+
+def attention_cost(heads, tokens, passes):
+    pairs = heads * tokens * tokens // 2
+    return pl.CostEstimate(
+        flops=2 * passes * pairs * BLOCK, bytes_accessed=tokens * D, transcendentals=pairs
+    )
+
+
+def attention_backward(slots, kept, mixed, dmixed, factor):
     qt, kt, kn, vn, lse = kept
-    tokens = kn.shape[1]
+    heads, tokens = kn.shape[:2]
     return pl.pallas_call(
         functools.partial(backward_kernel, heads),
         name="attention_backward",
@@ -322,7 +527,6 @@
         in_specs=[pl.BlockSpec(memory_space=pltpu.SMEM)] + in_vmem(8),
         out_specs=in_vmem(2),
         scratch_shapes=[
-            pltpu.SMEM((tokens // BLOCK,), jnp.int32),
             pltpu.VMEM((heads, PAD, tokens), bf16),
             pltpu.VMEM((heads, PAD, tokens), bf16),
             pltpu.VMEM((heads, HD, TILE), f32),
@@ -330,7 +534,8 @@
             pltpu.VMEM((heads, HD, tokens), f32),
         ],
         compiler_params=params(),
-    )(order, qt, kt, kn, vn, lse, mixed, dmixed, factor)
+        cost_estimate=attention_cost(heads, tokens, 5),
+    )(slots, qt, kt, kn, vn, lse, mixed, dmixed, factor)
 
 
 def reduce_kernel(
@@ -703,7 +908,8 @@
     rows_dev = inputs.shape[1]
     tokens = rows_dev * parts
     here = lax.axis_index("ctx")
-    order = block_order[0]
+    index = jnp.arange(block_order.shape[1], dtype=jnp.int32)
+    slots = jnp.sum(jnp.where(block_order[0][None] == index[:, None], index[None], 0), axis=1)
     gain_one = small_params[:D]
     gain_two = small_params[D : 2 * D]
     query_scale = small_params[2 * D :]
@@ -723,30 +929,21 @@
     gain_rows = lax.dynamic_slice_in_dim(gain_one, group * rows, rows, 0)[:, None]
     columns = [head_columns(here - core + lane) for lane in range(2)]
     gained = jnp.concatenate([(gain_rows * part).astype(bf16) for part in columns], axis=1)
-    w_pair = lax.all_gather(gained, "fsdp", axis=0, tiled=True).T.reshape(2, 3 * width, D)
-    w_flipped = lax.dynamic_index_in_dim(w_pair, core, 0, False)
-    own_qkv = w_flipped.T
     w_columns = head_columns(here).astype(bf16)
     layer_in = inputs[0].astype(f32)
     scale_one = rms_scale(layer_in)
     unit_one = layer_in * scale_one
-    unit_all = lax.all_gather(unit_one.astype(bf16), "ctx", axis=0, tiled=True)
-    out_full, up_full, down_full = (
-        lax.all_gather(w_out.astype(bf16), "fsdp", axis=0, tiled=True),
-        lax.all_gather(w_up.astype(bf16), "fsdp", axis=0, tiled=True),
-        lax.all_gather(w_down.astype(bf16), "fsdp", axis=0, tiled=True),
-    )
     factor = scale_base / math.sqrt(HD) * jax.nn.softplus(query_scale)
     factor_two = (factor * LOG2E)[:, None]
-    pieces = []
-    for head in range(heads):
-        for part in (1, 2):
-            at = part * width + head * HD
-            pieces.append(jnp.pad(own_qkv[:, at : at + HD], ((0, 0), (0, PAD - HD))))
-    w_natural = jnp.concatenate(pieces, axis=1)
-    *kept, mixed = attention_forward(
-        order, unit_all, w_natural, w_flipped, factor_two, parts, heads
-    )
+    half = rows // 2
+    mlp = jnp.stack([w_out.astype(bf16), w_up.astype(bf16), w_down.astype(bf16)])
+    mlp = mlp.reshape(3, 2, half, D)
+    unit_all, mlp_full, w_pair, qt, kt, vt, kn, vn = gather_rows(
+        parts, groups, heads, inputs[0], gained, mlp, factor_two
+    )
+    out_full, up_full, down_full = mlp_full.reshape(3, D, D)
+    lse, mixed = attention_forward(slots, qt, kn, vt, parts)
+    kept = (qt, kt, kn, vn, lse)
     attn_flipped = lax.all_to_all(mixed, "ctx", 0, 0, tiled=True).reshape(D, rows_dev)
     mid = layer_in + dot(attn_flipped, out_full, (0, 0))
     scale_two = rms_scale(mid)
@@ -770,13 +967,14 @@
     dbranch = dmid.astype(bf16)
     grad_out = dot(attn_flipped, dbranch)
     dattn = dot(out_full, dbranch, (1, 1)).astype(bf16)
-    half = rows // 2
     grads = jnp.stack([grad_out.astype(bf16), grad_up.astype(bf16), grad_down.astype(bf16)])
     grads = grads.reshape(3, groups, 2, half, D)
     pair = [(i, i ^ 1) for i in range(parts)]
     theirs = lax.dynamic_index_in_dim(grads, 1 - core, 2, False)
     mine = lax.dynamic_index_in_dim(grads, core, 2, False)
     mine = (mine.astype(f32) + lax.ppermute(theirs, "ctx", pair).astype(f32)).astype(bf16)
+    dmixed = lax.all_to_all(dattn.reshape(parts, width, rows_dev), "ctx", 0, 0, tiled=True)
+    dmixed, mine = lax.optimization_barrier((dmixed, mine))
     mlp_sum = lax.dynamic_index_in_dim(mine, group, 1, False).astype(f32)
     for step in range(1, groups):
         chunk = lax.dynamic_index_in_dim(mine, group ^ step, 1, False)
@@ -785,11 +983,10 @@
     mlp_part = (
         mlp_sum.astype(bf16).reshape(3, parts // 2, rows // parts, D).transpose(1, 0, 2, 3)
     )
-    dmixed = lax.all_to_all(dattn.reshape(parts, width, rows_dev), "ctx", 0, 0, tiled=True)
-    dqkv, dscale = attention_backward(order, kept, mixed, dmixed, factor_two, heads)
+    dqkv, dscale = attention_backward(slots, kept, mixed, dmixed, factor_two)
     u_parts = (
         lax.dot_general(
-            unit_all.reshape(parts, rows_dev, D),
+            unit_all,
             dqkv,
             (((0, 1), (0, 2)), ((), ())),
             preferred_element_type=f32,

time: 683 us -> 540 us (0.79)
  waiting for transfers between devices: 263 us -> 42.7 us
  Pallas kernels: 249 us -> 343 us
  between operations: 14.4 us -> 1.25 us
    all_gather x5 -> x0, waiting for transfers between devices: 165 us -> none  [the longest x1 93.2 us: body(): unit_all = lax.all_gather(unit_one.astype(bf16), 'ctx', axis=0, tiled=True)]
    pallas_call x0 -> x1, Pallas kernels: none -> 113 us  [gather_rows(): pl.pallas_call(functools.partial(gather_kernel, parts, groups, heads), na...]
    ppermute x3, waiting for transfers between devices: 43.2 us -> 0.01 us  [body(): mlp_sum = mlp_sum + lax.ppermute(chunk, 'fsdp', swap).astype(f32)]
    pallas_call x1, Pallas kernels: 53.7 us -> 36.2 us  [attention_forward(): pl.pallas_call(functools.partial(forward_kernel, heads), name='attention_...]
    another operation x1 -> x2, local copies, waits for them, and re-layouts: 1.55 us -> 8.76 us  [the longest x1 7.23 us: body(): out_full, up_full, down_full = mlp_full.reshape(3, D, D)]
    all_to_all x1, waiting for transfers between devices: 31.9 us -> 24.9 us  [body(): lax.all_to_all(mixed, 'ctx', 0, 0, tiled=True).reshape(D, rows_dev)]
  transfers between devices with their start and end apart: 13 -> 8, of which waited for: 7 -> 2; matrix products, arithmetic and copies ran while one was open for 11% -> 13% of each run, Pallas kernels for 19% -> 14%
where the time goes in v3:
time: 540 us; the launch traced here: 530 us
  Pallas kernels  343 us (64%)
  local copies, waits for them, and re-layouts  51.7 us (10%)
  waiting for transfers between devices  42.7 us (8%)
  matrix products  39.8 us (7%)
  other arithmetic  35.2 us (7%)
  starting transfers between devices  16.1 us (3%)
    pallas_call x1, Pallas kernels, reduce_gradients(): pl.pallas_call(functools.partial(reduce_kernel, parts, groups), name='red...  119 us
    pallas_call x1, Pallas kernels, gather_rows(): pl.pallas_call(functools.partial(gather_kernel, parts, groups, heads), na...  113 us
    pallas_call x1, Pallas kernels, attention_backward(): pl.pallas_call(functools.partial(backward_kernel, heads), name='attention...  50.2 us
    pallas_call x1, Pallas kernels, attention_forward(): pl.pallas_call(functools.partial(forward_kernel, heads), name='attention_...  36.2 us
    dot_general x9, matrix products, dot(): lax.dot_general(left, right, (((contract[0],), (contract[1],)), ((), ()))...  28.8 us
    all_to_all x1, waiting for transfers between devices, body(): lax.all_to_all(mixed, 'ctx', 0, 0, tiled=True).reshape(D, rows_dev)  24.9 us
    pallas_call x1, Pallas kernels, update(): pl.pallas_call(functools.partial(update_kernel, rates), name='update_weig...  24.7 us
    all_to_all x1, waiting for transfers between devices, body(): lax.all_to_all(dattn.reshape(parts, width, rows_dev), 'ctx', 0, 0, tiled=...  17.8 us
  transfers between devices with their start and end apart: 8, of which 2 were waited for; matrix products, arithmetic and copies ran while one was open for 13% of the time, Pallas kernels for 14%

profile of v3, /device:TPU:0, one launch (start us, length us, event | category | flops | bytes accessed | tf_op | source)
XLA Modules:
  0.0 529.8 jit_solution(15233556391359697233)
XLA Ops:
  7.0 2.4 constant_dynamic-slice_fusion.7
  12.8 112.8 %gather_rows.1 = (bf16[8,512,1280]{2,1,0:T(8,128)(2,1)}, bf16[3,4,2,160,1280]{4,3,2,1,0:T(8,128)(2,1)}, bf16[2,480,1280]{2,1,0:T(8,128)(2,1)}, bf16[2,128,4096]{...) custom-call(bf16[512,1280]{1,0:T(8,128)(2,1)} %bitcast.93, ...), custom_call_target="tpu_custom_call" | custom-call | tf_op jit(solution)/shard_map/gather_rows/pallas_call | solution.py:292
  125.5 36.2 %attention_forward.1 = (f32[2,1,4096]{2,1,0:T(1,128)}, bf16[8,160,512]{2,1,0:T(8,128)(2,1)}) custom-call(s32[16]{0:T(128)} %select_reduce_fusion.slot_ref, bf16[2,128,4096]{2,1,0:T(8,128)(2,1)} %get-tuple-element.57.qt_ref, bf16[2,4096,128]{2,1,0:T(8,128)(2,1)} %get-tuple-element.58.kn_ref, bf16[2,96,4096]{2,1,0:T(8,128)(2,1)} %get-tuple-element.59.vt_ref), custom_call_target="tpu_custom_call" | custom-call | flops 17179869184 | bytes 5242880 | tf_op jit(solution)/shard_map/attention_forward/pallas_call | solution.py:492
  161.7 3.6 all-to-all-start
  165.3 7.2 %fusion.30 = (bf16[1,4,2,160,1280]{4,3,2,1,0:T(8,128)(2,1)}, bf16[1,4,2,160,1280]{4,3,2,1,0:T(8,128)(2,1)}, bf16[1,4,2,160,1280]{4,3,2,1,0:T(8,128)(2,1)}) fusion(bf16[3,4,2,160,1280]{4,3,2,1,0:T(8,128)(2,1)} %get-tuple-element.61), kind=kLoop, calls=%fused_computation.91 | loop fusion | bytes 19660800 | tf_op jit(solution)/shard_map/unstack | solution.py:944
  172.6 24.9 %all-to-all-done = bf16[8,160,512]{2,1,0:T(8,128)(2,1)S(1)} async-done(((bf16[8,160,512]{2,1,0:T(8,128)(2,1)}), bf16[8,160,512]{2,1,0:T(8,128)(2,1)S(1)}, u32[]{:S(2)}, u32[]{:S(2)}) %all-to-all-start) | async-done | bytes 1310752 | tf_op jit(solution)/shard_map/all_to_all | solution.py:947
  197.4 4.1 multiply_reduce_fusion.2
  206.8 2.2 fusion.5
  209.0 2.1 multiply_reduce_fusion
  215.7 4.5 pad_maximum_fusion
  220.2 6.8 %constant_dynamic-slice_fusion.1 = (bf16[3,4,1,160,1280]{4,3,2,1,0:T(8,128)(2,1)}, bf16[3,4,1,160,1280]{4,3,2,1,0:T(8,128)(2,1)S(1)}) fusion(bf16[3,4,2,160,1280]{4,3,2,1,0:T(8,128)(2,1)} %pad_maximum_fusion, s32[]{:T(128)S(6)} %select_n.67, s32[]{:T(128)S(6)} %select_n.68), kind=kLoop, calls=%fused_computation.76 | loop fusion | bytes 19660808 | tf_op jit(solution)/shard_map/jit(dynamic_index_in_dim)/dynamic_slice | solution.py:974
  227.0 2.6 copy.81
  231.1 5.7 %convolution_convert_fusion.3 = bf16[1280,512]{1,0:T(8,128)(2,1)} fusion(bf16[1280,1280]{1,0:T(8,128)(2,1)} %bitcast.95, f32[512,1280]{1,0:T(8,128)} %copy-done.2), kind=kOutput, calls=%fused_computation.20 | convolution fusion | flops 1679032320 | bytes 7208960 | tf_op jit(solution)/shard_map/dot_general | solution.py:52
  236.8 4.0 all-to-all-start.1
  242.1 6.9 %fusion.8 = bf16[1,512,1280]{2,1,0:T(8,128)(2,1)} fusion(f32[512,1280]{1,0:T(8,128)} %copy-done.1, bf16[1280,1280]{1,0:T(8,128)(2,1)} %bitcast.107, f32[512,1280]{1,0:T(8,128)} %copy-done.19), kind=kOutput, calls=%fused_computation.23 | convolution fusion | flops 1682309120 | bytes 9830400 | tf_op jit(solution)/shard_map/dot_general | solution.py:52
  249.0 6.1 %fusion = bf16[3,4,160,1280]{3,2,0,1:T(8,128)(2,1)} fusion(bf16[3,4,160,1280]{3,2,0,1:T(8,128)(2,1)} %collective-permute-done, bf16[3,4,1,160,1280]{4,3,2,1,0:T(8,128)(2,1)S(1)} %bitcast.99), kind=kLoop, calls=%fused_computation.2 | loop fusion | flops 9830400 | bytes 14745600 | tf_op jit(solution)/shard_map/convert_element_type | solution.py:975
  255.1 17.8 %all-to-all-done.1.dt_ref = bf16[8,160,512]{2,1,0:T(8,128)(2,1)S(1)} async-done(((bf16[8,160,512]{2,1,0:T(8,128)(2,1)}), bf16[8,160,512]{2,1,0:T(8,128)(2,1)S(1)}, u32[]{:S(2)}, u32[]{:S(2)}) %all-to-all-start.1) | async-done | bytes 1310752 | tf_op jit(solution)/shard_map/all_to_all | solution.py:976
  272.9 4.4 dynamic-slice_bitcast_fusion.2
  277.4 2.1 collective-permute-start.3
  282.3 50.2 %attention_backward.1 = (bf16[8,480,512]{2,1,0:T(8,128)(2,1)}, f32[2,80,128]{2,1,0:T(8,128)}) custom-call(s32[16]{0:T(128)} %select_reduce_fusion.slot_ref, bf16[2,128,4096]{2,1,0:T(8,128)(2,1)} %get-tuple-element.57.qt_ref, bf16[2,80,4096]{2,1,0:T(8,128)(2,1)} %get-tuple-element.62.kt_ref, bf16[2,4096,128]{2,1,0:T(8,128)(2,1)} %get-tuple-element.58.kn_ref, ...), custom_call_target="tpu_custom_call" | custom-call | flops 42949672960 | bytes 5242880 | tf_op jit(solution)/shard_map/attention_backward/pallas_call | solution.py:520
  332.5 11.0 %fusion.7 = bf16[1280,480]{0,1:T(8,128)(2,1)} fusion(bf16[8,480,512]{2,1,0:T(8,128)(2,1)} %get-tuple-element.66, bf16[8,512,1280]{2,1,0:T(8,128)(2,1)} %get-tuple-element.68), kind=kOutput, calls=%fused_computation.22 | convolution fusion | flops 5033779200 | bytes 15646720 | tf_op jit(solution)/shard_map/dot_general | solution.py:988
  343.4 2.4 copy.63
  346.6 2.6 fusion.17
  350.4 119.2 %reduce_gradients.1 = (bf16[512,1280]{1,0:T(8,128)(2,1)}, bf16[512,1280]{1,0:T(8,128)(2,1)}, f32[512,1280]{1,0:T(8,128)}, bf16[8,320,480]{2,1,0:T(8,128)(2,1)}, ...) custom-call(bf16[4,2,480,512]{3,2,1,0:T(8,128)(2,1)} %bitcast.106, ...), custom_call_target="tpu_custom_call" | custom-call | tf_op jit(solution)/shard_map/reduce_gradients/pallas_call | solution.py:813
  469.6 2.4 collective-permute-start.5
  473.3 5.1 copy.65
  478.4 5.6 %copy.66 = f32[320,3,8,160]{0,3,2,1:T(8,128)} copy(f32[320,3,8,160]{0,3,1,2:T(8,128)} %bitcast.96) | data formatting | bytes 9830400 | tf_op jit(solution)/shard_map/convert_element_type | solution.py:1020
  484.0 6.1 %copy.67 = f32[320,3840]{1,0:T(8,128)} copy(f32[320,3840]{0,1:T(8,128)} %bitcast.97) | data formatting | bytes 9830400 | tf_op jit(solution)/shard_map/convert_element_type | solution.py:1020
  493.6 4.2 multiply_convert_fusion.refs_3_
  497.9 24.7 %update_weights.1 = (f32[320,3840]{1,0:T(8,128)}, f32[320,3840]{1,0:T(8,128)}, f32[320,3840]{1,0:T(8,128)}, bf16[320,3840]{1,0:T(8,128)(2,1)}, f32[320,1280]{1,0...) custom-call(f32[320,3840]{1,0:T(8,128)} %refs_0_.1, ...), custom_call_target="tpu_custom_call" | custom-call | flops 68812800 | bytes 68812800 | tf_op jit(solution)/shard_map/update_weights/pallas_call | solution.py:872
  523.3 2.6 fusion.9
  525.9 3.7 fusion.18
  (90 shorter events, 32.3 us)
Async XLA Ops:
  0.7 4.5 copy-start.5
  3.5 2.6 copy-start.6
  7.0 3.0 copy-start.15
  9.4 1.7 copy-start.9
  161.7 35.7 %all-to-all-start = ((bf16[8,160,512]{2,1,0:T(8,128)(2,1)}), bf16[8,160,512]{2,1,0:T(8,128)(2,1)S(1)}, u32[]{:S(2)}, u32[]{:S(2)}) async-start(bf16[8,160,512]{2,1,0:T(8,128)(2,1)} %get-tuple-element.60.ot_ref), calls=%async_computation | async-start | bytes 2621440 | tf_op jit(solution)/shard_map/all_to_all | solution.py:947
  165.3 32.1 %copy-start = (bf16[1,512,1280]{2,1,0:T(8,128)(2,1)S(1)}, bf16[1,512,1280]{2,1,0:T(8,128)(2,1)}, u32[]{:S(2)}) copy-start(bf16[1,512,1280]{2,1,0:T(8,128)(2,1)} %param.18) | copy-start | bytes 3932164
  197.4 4.2 copy-start.8
  201.6 11.5 %copy-start.1 = (f32[512,1280]{1,0:T(8,128)}, f32[512,1280]{1,0:T(8,128)S(1)}, u32[]{:S(2)}) copy-start(f32[512,1280]{1,0:T(8,128)S(1)} %get-tuple-element.123) | copy-start | bytes 7864324
  201.6 2.3 copy-start.10
  203.9 2.0 copy-start.19
  203.9 2.9 copy-start.7
  213.8 1.9 copy-start.2
  229.6 19.4 %collective-permute-start = (bf16[3,4,160,1280]{3,2,0,1:T(8,128)(2,1)}, bf16[3,4,160,1280]{3,2,0,1:T(8,128)(2,1)}, u32[]{:S(2)}, u32[]{:S(2)}) collective-permute-start(bf16[3,4,160,1280]{3,2,0,1:T(8,128)(2,1)} %bitcast.89), channel_id=1, source_target_pairs={{0,4},{4,0},{8,12},{12,8},{16,20},{20,16},{24,28},{28,24},{1,5},{5... | collective-permute-start | bytes 14745608 | tf_op jit(solution)/shard_map/ppermute | solution.py:975
  236.8 36.1 %all-to-all-start.1 = ((bf16[8,160,512]{2,1,0:T(8,128)(2,1)}), bf16[8,160,512]{2,1,0:T(8,128)(2,1)S(1)}, u32[]{:S(2)}, u32[]{:S(2)}) async-start(bf16[8,160,512]{2,1,0:T(8,128)(2,1)} %bitcast.121), calls=%async_computation.1 | async-start | bytes 2621440 | tf_op jit(solution)/shard_map/all_to_all | solution.py:976
  242.1 6.9 %slice-start = ((s8[4915200]{0:T(1024)(128)(4,1)}), s8[4194304]{0:T(1024)(128)(4,1)S(1)}, s32[]{:S(2)}) async-start(s8[4915200]{0:T(1024)(128)(4,1)} %bitcast.98), calls=%async_computation.2 | async-start | bytes 8388608
  242.1 6.9 %slice-start.1 = ((s8[4915200]{0:T(1024)(128)(4,1)}), s8[720896]{0:T(1024)(128)(4,1)S(1)}, s32[]{:S(2)}) async-start(s8[4915200]{0:T(1024)(128)(4,1)} %bitcast.98), calls=%async_computation.3 | async-start | bytes 1441792
  272.9 4.4 copy-start.11
  277.4 69.3 %collective-permute-start.3 = (bf16[3,160,1280]{2,1,0:T(8,128)(2,1)}, bf16[3,160,1280]{2,1,0:T(8,128)(2,1)S(1)}, u32[]{:S(2)}, u32[]{:S(2)}) collective-permute-start(bf16[3,160,1280]{2,1,0:T(8,128)(2,1)} %get-tuple-element.104), channel_id=1, source_target_pairs={{0,3},{1,2},{2,1},{3,0},{4,7},{5,6},{6,5},{7,4},{8,11},{9,10},{10,... | collective-permute-start | bytes 3686408 | tf_op jit(solution)/shard_map/ppermute | solution.py:982
  279.5 67.2 %collective-permute-start.2 = (bf16[3,160,1280]{2,1,0:T(8,128)(2,1)}, bf16[3,160,1280]{2,1,0:T(8,128)(2,1)}, u32[]{:S(2)}, u32[]{:S(2)}) collective-permute-start(bf16[3,160,1280]{2,1,0:T(8,128)(2,1)} %get-tuple-element.105), channel_id=1, source_target_pairs={{0,2},{1,3},{2,0},{3,1},{4,6},{5,7},{6,4},{7,5},{8,10},{9,11},{10,... | collective-permute-start | bytes 3686408 | tf_op jit(solution)/shard_map/ppermute | solution.py:982
  280.8 65.8 %collective-permute-start.1 = (bf16[3,160,1280]{2,1,0:T(8,128)(2,1)}, bf16[3,160,1280]{2,1,0:T(8,128)(2,1)}, u32[]{:S(2)}, u32[]{:S(2)}) collective-permute-start(bf16[3,160,1280]{2,1,0:T(8,128)(2,1)} %get-tuple-element.103), channel_id=1, source_target_pairs={{0,1},{1,0},{2,3},{3,2},{4,5},{5,4},{6,7},{7,6},{8,9},{9,8},{10,11... | collective-permute-start | bytes 3686408 | tf_op jit(solution)/shard_map/ppermute | solution.py:982
  332.5 13.4 %copy-start.12 = (f32[2,80,128]{2,1,0:T(8,128)S(1)}, f32[2,80,128]{2,1,0:T(8,128)}, u32[]{:S(2)}) copy-start(f32[2,80,128]{2,1,0:T(8,128)} %get-tuple-element.70) | copy-start | bytes 245764
  343.4 2.5 copy-start.13
  469.6 53.6 %collective-permute-start.5 = (bf16[512,1280]{1,0:T(8,128)(2,1)}, bf16[512,1280]{1,0:T(8,128)(2,1)}, u32[]{:S(2)}, u32[]{:S(2)}) collective-permute-start(bf16[512,1280]{1,0:T(8,128)(2,1)} %get-tuple-element.73), channel_id=1, source_target_pairs={{0,8},{4,12},{8,16},{12,20},{16,24},{20,28},{1,9},{5,13},{9,17},{1... | collective-permute-start | bytes 3932168 | tf_op jit(solution)/shard_map/ppermute | solution.py:1018
  472.0 51.2 %collective-permute-start.4 = (bf16[512,1280]{1,0:T(8,128)(2,1)}, bf16[512,1280]{1,0:T(8,128)(2,1)}, u32[]{:S(2)}, u32[]{:S(2)}) collective-permute-start(bf16[512,1280]{1,0:T(8,128)(2,1)} %get-tuple-element.72), channel_id=1, source_target_pairs={{8,0},{12,4},{16,8},{20,12},{24,16},{28,20},{9,1},{13,5},{17,9},{2... | collective-permute-start | bytes 3932168 | tf_op jit(solution)/shard_map/ppermute | solution.py:1017
  492.0 1.5 copy-start.14
  492.0 1.6 copy-start.16
  497.9 24.7 %copy-start.17 = (f32[2640]{0:T(1024)S(1)}, f32[2640]{0:T(1024)}, u32[]{:S(2)}) copy-start(f32[2640]{0:T(1024)} %param.34) | copy-start | bytes 31684
  497.9 24.7 %copy-start.18 = (f32[2640]{0:T(1024)S(1)}, f32[2640]{0:T(1024)}, u32[]{:S(2)}) copy-start(f32[2640]{0:T(1024)} %param.35) | copy-start | bytes 31684
  497.9 25.4 %copy-start.4 = (f32[512,1280]{1,0:T(8,128)S(1)}, f32[512,1280]{1,0:T(8,128)}, u32[]{:S(2)}) copy-start(f32[512,1280]{1,0:T(8,128)} %get-tuple-element.71) | copy-start | bytes 7864324
  523.3 2.6 copy-start.3

commit v4 on v3

--- a/solution.py
+++ b/solution.py
@@ -390,14 +390,27 @@
     ot_ref,
     dt_ref,
     factor_ref,
+    units_ref,
     dqkv_ref,
     dscale_ref,
+    u_ref,
     qa_ref,
     da_ref,
     dq_ref,
     dk_ref,
     dv_ref,
+    held_ref,
+    total_ref,
+    load_sem,
 ):
+    parts = units_ref.shape[0]
+
+    def load(piece):
+        slot = lax.rem(piece, 2)
+        return pltpu.make_async_copy(units_ref.at[piece], held_ref.at[slot], load_sem.at[slot])
+
+    for piece in range(2):
+        load(piece).start()
     tokens = kn_ref.shape[1]
     num_blocks = tokens // BLOCK
     num_tiles = tokens // TILE
@@ -477,6 +490,20 @@
         return carry
 
     lax.fori_loop(0, num_blocks, finish, 0)
+    total_ref[...] = jnp.zeros(total_ref.shape, f32)
+
+    def project(piece, carry):
+        load(piece).wait()
+        total_ref[...] += dot(dqkv_ref[piece], held_ref[lax.rem(piece, 2)])
+
+        @pl.when(piece + 2 < parts)
+        def _():
+            load(piece + 2).start()
+
+        return carry
+
+    lax.fori_loop(0, parts, project, 0)
+    u_ref[...] = total_ref[...].T.astype(bf16)
 
 
 def in_vmem(count):
@@ -514,7 +541,7 @@
     )
 
 
-def attention_backward(slots, kept, mixed, dmixed, factor):
+def attention_backward(slots, kept, mixed, dmixed, factor, units):
     qt, kt, kn, vn, lse = kept
     heads, tokens = kn.shape[:2]
     return pl.pallas_call(
@@ -523,19 +550,231 @@
         out_shape=[
             jax.ShapeDtypeStruct((mixed.shape[0], 3 * heads * HD, mixed.shape[2]), bf16),
             jax.ShapeDtypeStruct((heads, HD, PAD), f32),
+            jax.ShapeDtypeStruct((D, 3 * heads * HD), bf16),
         ],
-        in_specs=[pl.BlockSpec(memory_space=pltpu.SMEM)] + in_vmem(8),
-        out_specs=in_vmem(2),
+        in_specs=[pl.BlockSpec(memory_space=pltpu.SMEM)]
+        + in_vmem(8)
+        + [pl.BlockSpec(memory_space=pl.ANY)],
+        out_specs=in_vmem(3),
         scratch_shapes=[
             pltpu.VMEM((heads, PAD, tokens), bf16),
             pltpu.VMEM((heads, PAD, tokens), bf16),
             pltpu.VMEM((heads, HD, TILE), f32),
             pltpu.VMEM((heads, HD, tokens), f32),
             pltpu.VMEM((heads, HD, tokens), f32),
+            pltpu.VMEM((2,) + units.shape[1:], bf16),
+            pltpu.VMEM((3 * heads * HD, D), f32),
+            pltpu.SemaphoreType.DMA((2,)),
         ],
         compiler_params=params(),
         cost_estimate=attention_cost(heads, tokens, 5),
-    )(slots, qt, kt, kn, vn, lse, mixed, dmixed, factor)
+    )(slots, qt, kt, kn, vn, lse, mixed, dmixed, factor, units)
+
+
+def middle_kernel(
+    parts,
+    groups,
+    mixed_ref,
+    x_ref,
+    dy_ref,
+    weights_ref,
+    gain_ref,
+    *refs,
+):
+    out_ref, dmid_ref, dmixed_ref, gain_grad_ref = refs[:4]
+    chunk_refs = refs[4 : 4 + groups]
+    (
+        w_ref,
+        attn_ref,
+        dattn_ref,
+        act_ref,
+        normed_ref,
+        dhidden_ref,
+        dbranch_ref,
+        grad_ref,
+        theirs_ref,
+        w_sem,
+        attn_sem,
+        dattn_sem,
+        pair_sem,
+    ) = refs[4 + groups :]
+    here = lax.axis_index("ctx")
+    group = lax.axis_index("fsdp")
+    core = lax.rem(here, 2)
+    other = here + 1 - 2 * core
+    peers = [lax.rem(here + step, parts) for step in range(1, parts)]
+    tokens = x_ref.shape[0]
+    width = mixed_ref.shape[1]
+    held = theirs_ref.shape[2]
+    loads = [
+        pltpu.make_async_copy(weights_ref.at[index], w_ref.at[index], w_sem.at[index])
+        for index in range(3)
+    ]
+    for load in loads:
+        load.start()
+
+    barrier = pltpu.get_barrier_semaphore()
+    for peer in peers:
+        pl.semaphore_signal(barrier, inc=1, device_id={"ctx": peer})
+    pl.semaphore_wait(barrier, parts - 1)
+
+    def lanes(part):
+        return pl.ds(pl.multiple_of(part * BLOCK, BLOCK), BLOCK)
+
+    def attn_copy(part, peer, source):
+        return pltpu.make_async_remote_copy(
+            src_ref=mixed_ref.at[peer, :, lanes(part)],
+            dst_ref=attn_ref.at[source, :, lanes(part)],
+            send_sem=attn_sem.at[0, part, peer],
+            recv_sem=attn_sem.at[1, part, source],
+            device_id={"ctx": peer},
+        )
+
+    def dattn_copy(part, peer, source):
+        return pltpu.make_async_remote_copy(
+            src_ref=dattn_ref.at[peer, :, lanes(part)],
+            dst_ref=dmixed_ref.at[source, :, lanes(part)],
+            send_sem=dattn_sem.at[0, part, peer],
+            recv_sem=dattn_sem.at[1, part, source],
+            device_id={"ctx": peer},
+        )
+
+    def rows_of(owner, lane):
+        start = pl.multiple_of((owner * 2 + lane) * held, 16)
+        return pl.ds(start, held)
+
+    def pair_copy(index, owner, lane):
+        return pltpu.make_async_remote_copy(
+            src_ref=grad_ref.at[index, rows_of(owner, lane), :],
+            dst_ref=theirs_ref.at[index, owner],
+            send_sem=pair_sem.at[0, index, owner],
+            recv_sem=pair_sem.at[1, index, owner],
+            device_id={"ctx": other},
+        )
+
+    for part in range(tokens // BLOCK):
+        for peer in peers:
+            attn_copy(part, peer, here).start()
+    attn_ref[here] = mixed_ref[here]
+    gain_grad_ref[...] = jnp.zeros(gain_grad_ref.shape, f32)
+    for load in loads:
+        load.wait()
+    gain = gain_ref[...]
+
+    def layer(part, carry):
+        rows = lanes(part)
+        for peer in peers:
+            attn_copy(part, here, peer).wait_recv()
+        attn = attn_ref[:, :, rows].reshape(D, BLOCK)
+        mid = x_ref[rows, :].astype(f32) + dot(attn, w_ref[0], (0, 0))
+        scale = rms_scale(mid)
+        unit = mid * scale
+        normed = (unit * gain).astype(bf16)
+        normed_ref[rows, :] = normed
+        hidden = dot(normed, w_ref[1])
+        gate = jax.nn.sigmoid(hidden)
+        act = (hidden * gate).astype(bf16)
+        act_ref[rows, :] = act
+        dy = dy_ref[rows, :]
+        dact = dot(dy, w_ref[2], (1, 1))
+        dhidden = (dact * gate * (1.0 + hidden * (1.0 - gate))).astype(bf16)
+        dhidden_ref[rows, :] = dhidden
+        dnormed = dot(dhidden, w_ref[1], (1, 1))
+        dunit = dnormed * gain
+        dmid = dy.astype(f32) + scale * (
+            dunit - unit * jnp.mean(dunit * unit, axis=-1, keepdims=True)
+        )
+        dmid_ref[rows, :] = dmid
+        dbranch = dmid.astype(bf16)
+        dbranch_ref[rows, :] = dbranch
+        dattn = dot(w_ref[0], dbranch, (1, 1)).astype(bf16).reshape(parts, width, BLOCK)
+        dattn_ref[:, :, rows] = dattn
+        for peer in peers:
+            dattn_copy(part, peer, here).start()
+        dmixed_ref[here, :, rows] = dattn_ref[here, :, rows]
+        out_ref[rows, :] = (mid + dot(act, w_ref[2])).astype(bf16)
+        gain_grad_ref[...] += jnp.sum(dnormed * unit, axis=0, keepdims=True)
+        return carry
+
+    lax.fori_loop(0, tokens // BLOCK, layer, 0)
+
+    def down_rows(index, carry):
+        rows = lanes(index)
+        grad_ref[2, rows, :] = dot(act_ref[:, rows], dy_ref[...], (0, 0)).astype(bf16)
+        return carry
+
+    def up_rows(index, carry):
+        rows = lanes(index)
+        grad_ref[1, rows, :] = dot(normed_ref[:, rows], dhidden_ref[...], (0, 0)).astype(bf16)
+        return carry
+
+    def out_rows(index, carry):
+        rows = pl.ds(pl.multiple_of(index * width, 16), width)
+        grad_ref[0, rows, :] = dot(attn_ref[index], dbranch_ref[...]).astype(bf16)
+        return carry
+
+    for index, count, run in (
+        (2, D // BLOCK, down_rows),
+        (1, D // BLOCK, up_rows),
+        (0, parts, out_rows),
+    ):
+        lax.fori_loop(0, count, run, 0)
+        for owner in range(groups):
+            pair_copy(index, owner, 1 - core).start()
+    for step in range(groups):
+        owner = group ^ step
+        for index in (2, 1, 0):
+            pair_copy(index, owner, core).wait_recv()
+            chunk_refs[step][index] = (
+                grad_ref[index, rows_of(owner, core), :].astype(f32)
+                + theirs_ref[index, owner].astype(f32)
+            ).astype(bf16)
+    for part in range(tokens // BLOCK):
+        for peer in peers:
+            dattn_copy(part, here, peer).wait_recv()
+            dattn_copy(part, peer, here).wait_send()
+            attn_copy(part, peer, here).wait_send()
+    for index in range(3):
+        for owner in range(groups):
+            pair_copy(index, owner, 1 - core).wait_send()
+
+
+def middle(parts, groups, mixed, rows, cotangent, weights, gain):
+    rows_dev = rows.shape[0]
+    half = D // groups // 2
+    dma = pltpu.SemaphoreType.DMA
+    halves = rows_dev // BLOCK
+    return pl.pallas_call(
+        functools.partial(middle_kernel, parts, groups),
+        name="middle",
+        out_shape=[
+            jax.ShapeDtypeStruct((rows_dev, D), bf16),
+            jax.ShapeDtypeStruct((rows_dev, D), f32),
+            jax.ShapeDtypeStruct(mixed.shape, bf16),
+            jax.ShapeDtypeStruct((1, D), f32),
+        ]
+        + [jax.ShapeDtypeStruct((3, half, D), bf16)] * groups,
+        in_specs=in_vmem(3) + [pl.BlockSpec(memory_space=pl.ANY)] + in_vmem(1),
+        out_specs=in_vmem(4 + groups),
+        scratch_shapes=[
+            pltpu.VMEM((3, D, D), bf16),
+            pltpu.VMEM(mixed.shape, bf16),
+            pltpu.VMEM(mixed.shape, bf16),
+            pltpu.VMEM((rows_dev, D), bf16),
+            pltpu.VMEM((rows_dev, D), bf16),
+            pltpu.VMEM((rows_dev, D), bf16),
+            pltpu.VMEM((rows_dev, D), bf16),
+            pltpu.VMEM((3, D, D), bf16),
+            pltpu.VMEM((3, groups, half, D), bf16),
+            dma((3,)),
+            dma((2, halves, parts)),
+            dma((2, halves, parts)),
+            dma((2, 3, groups)),
+        ],
+        compiler_params=pltpu.CompilerParams(
+            vmem_limit_bytes=60 * 1024 * 1024, collective_id=3, has_side_effects=True
+        ),
+    )(mixed, rows, cotangent, weights, gain)
 
 
 def reduce_kernel(
@@ -941,59 +1180,26 @@
     unit_all, mlp_full, w_pair, qt, kt, vt, kn, vn = gather_rows(
         parts, groups, heads, inputs[0], gained, mlp, factor_two
     )
-    out_full, up_full, down_full = mlp_full.reshape(3, D, D)
     lse, mixed = attention_forward(slots, qt, kn, vt, parts)
     kept = (qt, kt, kn, vn, lse)
-    attn_flipped = lax.all_to_all(mixed, "ctx", 0, 0, tiled=True).reshape(D, rows_dev)
-    mid = layer_in + dot(attn_flipped, out_full, (0, 0))
-    scale_two = rms_scale(mid)
-    unit_two = mid * scale_two
-    normed_two = (unit_two * gain_two).astype(bf16)
-    hidden = dot(normed_two, up_full)
-    gate_sig = jax.nn.sigmoid(hidden)
-    act = (hidden * gate_sig).astype(bf16)
-    output = (mid + dot(act, down_full)).astype(bf16)
-    grad_in = cotangent[0]
-    grad_down = dot(act, grad_in, (0, 0))
-    dact = dot(grad_in, down_full, (1, 1))
-    dhidden = (dact * gate_sig * (1.0 + hidden * (1.0 - gate_sig))).astype(bf16)
-    grad_up = dot(normed_two, dhidden, (0, 0))
-    dnormed_two = dot(dhidden, up_full, (1, 1))
-    dunit_two = dnormed_two * gain_two
-    dmid = grad_in.astype(f32) + scale_two * (
-        dunit_two - unit_two * jnp.mean(dunit_two * unit_two, axis=-1, keepdims=True)
+    output, dmid, dmixed, gain_two_grad, *chunks = middle(
+        parts,
+        groups,
+        mixed,
+        inputs[0],
+        cotangent[0],
+        mlp_full.reshape(3, D, D),
+        gain_two[None],
     )
-    gain_two_grad = jnp.sum(dnormed_two * unit_two, axis=0)
-    dbranch = dmid.astype(bf16)
-    grad_out = dot(attn_flipped, dbranch)
-    dattn = dot(out_full, dbranch, (1, 1)).astype(bf16)
-    grads = jnp.stack([grad_out.astype(bf16), grad_up.astype(bf16), grad_down.astype(bf16)])
-    grads = grads.reshape(3, groups, 2, half, D)
-    pair = [(i, i ^ 1) for i in range(parts)]
-    theirs = lax.dynamic_index_in_dim(grads, 1 - core, 2, False)
-    mine = lax.dynamic_index_in_dim(grads, core, 2, False)
-    mine = (mine.astype(f32) + lax.ppermute(theirs, "ctx", pair).astype(f32)).astype(bf16)
-    dmixed = lax.all_to_all(dattn.reshape(parts, width, rows_dev), "ctx", 0, 0, tiled=True)
-    dmixed, mine = lax.optimization_barrier((dmixed, mine))
-    mlp_sum = lax.dynamic_index_in_dim(mine, group, 1, False).astype(f32)
+    mlp_sum = chunks[0].astype(f32)
     for step in range(1, groups):
-        chunk = lax.dynamic_index_in_dim(mine, group ^ step, 1, False)
         swap = [(i, i ^ step) for i in range(groups)]
-        mlp_sum = mlp_sum + lax.ppermute(chunk, "fsdp", swap).astype(f32)
+        mlp_sum = mlp_sum + lax.ppermute(chunks[step], "fsdp", swap).astype(f32)
     mlp_part = (
         mlp_sum.astype(bf16).reshape(3, parts // 2, rows // parts, D).transpose(1, 0, 2, 3)
     )
-    dqkv, dscale = attention_backward(slots, kept, mixed, dmixed, factor_two)
-    u_parts = (
-        lax.dot_general(
-            unit_all,
-            dqkv,
-            (((0, 1), (0, 2)), ((), ())),
-            preferred_element_type=f32,
-        )
-        .astype(bf16)
-        .reshape(groups, rows, 3 * width)
-    )
+    dqkv, dscale, u_parts = attention_backward(slots, kept, mixed, dmixed, factor_two, unit_all)
+    u_parts = u_parts.reshape(groups, rows, 3 * width)
     scale_grad = (
         jnp.sum(dscale, axis=(0, 2))
         / factor_two[:, 0]
@@ -1002,7 +1208,7 @@
     )
     lanes = -(-rows // PAD) * PAD
     small_rows = -(-(lanes + D + PAD) // (8 * PAD)) * 8
-    small = jnp.concatenate([jnp.zeros((lanes,), f32), gain_two_grad, scale_grad])
+    small = jnp.concatenate([jnp.zeros((lanes,), f32), gain_two_grad[0], scale_grad])
     small = jnp.pad(small, (0, small_rows * PAD - small.shape[0])).reshape(small_rows, PAD)
     send_down, send_up, own_part, u_all, mlp_all, small_all = reduce_gradients(
         parts,

time: 540 us -> 484 us (0.90); the launches traced: 530 us -> 480 us
  Pallas kernels: 343 us -> 417 us
  waiting for transfers between devices: 42.7 us -> 0.01 us
  matrix products: 39.8 us -> 0 us
  local copies, waits for them, and re-layouts: 51.7 us -> 29.4 us
  other arithmetic: 35.2 us -> 25.1 us
  starting transfers between devices: 16.1 us -> 7.79 us
    pallas_call x0 -> x1, Pallas kernels: none -> 62.8 us  [middle(): pl.pallas_call(functools.partial(middle_kernel, parts, groups), name='mid...]
    all_to_all x2 -> x0, waiting for transfers between devices: 42.7 us -> none  [the longest x1 24.9 us: body(): lax.all_to_all(mixed, 'ctx', 0, 0, tiled=True).reshape(D, rows_dev)]
    dot_general x10 -> x0, matrix products: 39.8 us -> none  [the longest x9 28.8 us: dot(): lax.dot_general(left, right, (((contract[0],), (contract[1],)), ((), ()))...]
    all_to_all x2 -> x0, starting transfers between devices: 7.55 us -> none  [the longest x1 3.98 us: body(): lax.all_to_all(dattn.reshape(parts, width, rows_dev), 'ctx', 0, 0, tiled=...]
    another operation x2 -> x1, local copies, waits for them, and re-layouts: 8.76 us -> 1.53 us  [the longest x1 7.23 us: body(): out_full, up_full, down_full = mlp_full.reshape(3, D, D)]
    pallas_call x1, Pallas kernels: 50.2 us -> 57.3 us  [attention_backward(): pl.pallas_call(functools.partial(backward_kernel, heads), name='attention...]
    dynamic_slice x1 -> x0, local copies, waits for them, and re-layouts: 6.78 us -> none  [body(): mine = lax.dynamic_index_in_dim(grads, core, 2, False)]
    convert_element_type x1 -> x0, other arithmetic: 6.09 us -> none  [body(): (mine.astype(f32) + lax.ppermute(theirs, 'ctx', pair).astype(f32)).astype...]
  transfers between devices with their start and end apart: 8 -> 5, of which waited for: 2 -> 0; matrix products, arithmetic and copies ran while one was open for 13% -> 6% of each run, Pallas kernels for 14% -> 17%
where the time goes in v4:
time: 484 us; the launch traced here: 480 us
  Pallas kernels  417 us (86%)
  local copies, waits for them, and re-layouts  29.4 us (6%)
  other arithmetic  25.1 us (5%)
  starting transfers between devices  7.79 us (2%)
    pallas_call x1, Pallas kernels, reduce_gradients(): pl.pallas_call(functools.partial(reduce_kernel, parts, groups), name='red...  124 us
    pallas_call x1, Pallas kernels, gather_rows(): pl.pallas_call(functools.partial(gather_kernel, parts, groups, heads), na...  113 us
    pallas_call x1, Pallas kernels, middle(): pl.pallas_call(functools.partial(middle_kernel, parts, groups), name='mid...  62.8 us
    pallas_call x1, Pallas kernels, attention_backward(): pl.pallas_call(functools.partial(backward_kernel, heads), name='attention...  57.3 us
    pallas_call x1, Pallas kernels, attention_forward(): pl.pallas_call(functools.partial(forward_kernel, heads), name='attention_...  36.2 us
    pallas_call x1, Pallas kernels, update(): pl.pallas_call(functools.partial(update_kernel, rates), name='update_weig...  24.2 us
    convert_element_type x3, local copies, waits for them, and re-layouts, body(): u_all.reshape(parts, rows, 3, width).transpose(1, 2, 0, 3)  16.9 us
  transfers between devices with their start and end apart: 5, of which 0 were waited for; matrix products, arithmetic and copies ran while one was open for 6% of the time, Pallas kernels for 17%

profile of v4, /device:TPU:0, one launch (start us, length us, event | category | flops | bytes accessed | tf_op | source)
XLA Modules:
  0.0 480.3 jit_solution(11284808967046634944)
XLA Ops:
  0.7 0.8 fusion.16
  2.2 1.3 select_reduce_fusion.slot_ref
  3.5 1.6 convert_element_type.64
  5.2 1.0 convert_element_type.63
  7.6 2.4 constant_dynamic-slice_fusion.5
  10.6 1.1 pad_maximum_fusion.1.gained_ref
  11.6 1.7 pad_maximum_fusion.mlp_ref
  13.3 112.9 %gather_rows.1 = (bf16[8,512,1280]{2,1,0:T(8,128)(2,1)}, bf16[3,4,2,160,1280]{4,3,2,1,0:T(8,128)(2,1)}, bf16[2,480,1280]{2,1,0:T(8,128)(2,1)}, bf16[2,128,4096]{...) custom-call(bf16[512,1280]{1,0:T(8,128)(2,1)} %bitcast.38, ...), custom_call_target="tpu_custom_call" | custom-call | tf_op jit(solution)/shard_map/gather_rows/pallas_call | solution.py:292
  126.2 36.2 %attention_forward.1 = (f32[2,1,4096]{2,1,0:T(1,128)}, bf16[8,160,512]{2,1,0:T(8,128)(2,1)}) custom-call(s32[16]{0:T(128)} %select_reduce_fusion.slot_ref, bf16[2,128,4096]{2,1,0:T(8,128)(2,1)} %get-tuple-element.64.qt_ref, bf16[2,4096,128]{2,1,0:T(8,128)(2,1)} %get-tuple-element.65.kn_ref, bf16[2,96,4096]{2,1,0:T(8,128)(2,1)} %get-tuple-element.66.vt_ref), custom_call_target="tpu_custom_call" | custom-call | flops 17179869184 | bytes 5242880 | tf_op jit(solution)/shard_map/attention_forward/pallas_call | solution.py:519
  162.5 62.8 %middle.1 = (bf16[512,1280]{1,0:T(8,128)(2,1)}, f32[512,1280]{1,0:T(8,128)}, bf16[8,160,512]{2,1,0:T(8,128)(2,1)}, f32[1,1280]{1,0:T(1,128)}, bf16[3,160,1280]{2...) custom-call(bf16[8,160,512]{2,1,0:T(8,128)(2,1)} %get-tuple-element., ...), custom_call_target="tpu_custom_call" | custom-call | tf_op jit(solution)/shard_map/middle/pallas_call | solution.py:747
  225.3 3.0 collective-permute-start.2
  228.3 0.7 collective-permute-start.1
  229.0 1.4 collective-permute-start
  230.4 57.3 %attention_backward.1 = (bf16[8,480,512]{2,1,0:T(8,128)(2,1)}, f32[2,80,128]{2,1,0:T(8,128)}, bf16[1280,480]{1,0:T(8,128)(2,1)}) custom-call(s32[16]{0:T(128)} %select_reduce_fusion.slot_ref, bf16[2,128,4096]{2,1,0:T(8,128)(2,1)} %get-tuple-element.64.qt_ref, bf16[2,80,4096]{2,1,0:T(8,128)(2,1)} %get-tuple-element.71.kt_ref, ...), custom_call_target="tpu_custom_call" | custom-call | flops 42949672960 | bytes 5242880 | tf_op jit(solution)/shard_map/attention_backward/pallas_call | solution.py:547
  287.8 1.1 reduce_sum.47
  289.6 1.5 dynamic-slice_convert_fusion.2
  291.2 0.9 pad_maximum_fusion.2.wc_ref
  292.5 2.6 add_convert_fusion
  295.1 1.1 copy.62
  296.2 123.6 %reduce_gradients.1 = (bf16[512,1280]{1,0:T(8,128)(2,1)}, bf16[512,1280]{1,0:T(8,128)(2,1)}, f32[512,1280]{1,0:T(8,128)}, bf16[8,320,480]{2,1,0:T(8,128)(2,1)}, ...) custom-call(bf16[4,2,480,512]{3,2,1,0:T(8,128)(2,1)} %bitcast.46, ...), custom_call_target="tpu_custom_call" | custom-call | tf_op jit(solution)/shard_map/reduce_gradients/pallas_call | solution.py:1052
  419.8 1.4 collective-permute-start.4
  421.2 1.3 collective-permute-start.3
  422.5 5.2 %copy.53 = f32[8,320,480]{1,2,0:T(8,128)} copy(bf16[8,320,480]{2,1,0:T(8,128)(2,1)} %get-tuple-element.88) | data formatting | bytes 7372800 | tf_op jit(solution)/shard_map/convert_element_type | solution.py:1226
  427.7 5.7 %copy.54 = f32[320,3,8,160]{0,3,2,1:T(8,128)} copy(f32[320,3,8,160]{0,3,1,2:T(8,128)} %bitcast.40) | data formatting | bytes 9830400 | tf_op jit(solution)/shard_map/convert_element_type | solution.py:1226
  433.3 6.1 %copy.55 = f32[320,3840]{1,0:T(8,128)} copy(f32[320,3840]{0,1:T(8,128)} %bitcast.41) | data formatting | bytes 9830400 | tf_op jit(solution)/shard_map/convert_element_type | solution.py:1226
  439.4 1.9 copy.61
  441.3 1.5 fusion.15
  442.9 4.2 multiply_convert_fusion.refs_3_
  447.1 24.2 %update_weights.1 = (f32[320,3840]{1,0:T(8,128)}, f32[320,3840]{1,0:T(8,128)}, f32[320,3840]{1,0:T(8,128)}, bf16[320,3840]{1,0:T(8,128)(2,1)}, f32[320,1280]{1,0...) custom-call(f32[320,3840]{1,0:T(8,128)} %refs_0_.1, ...), custom_call_target="tpu_custom_call" | custom-call | flops 68812800 | bytes 68812800 | tf_op jit(solution)/shard_map/update_weights/pallas_call | solution.py:1111
  472.0 3.0 fusion.2
  475.7 3.5 fusion.8
  479.2 1.1 copy.65
  (49 shorter events, 5.2 us)
Async XLA Ops:
  0.7 4.5 copy-start.2
  3.5 2.6 copy-start.3
  10.0 1.7 copy-start.4
  225.3 67.1 %collective-permute-start.2 = (bf16[3,160,1280]{2,1,0:T(8,128)(2,1)}, bf16[3,160,1280]{2,1,0:T(8,128)(2,1)}, u32[]{:S(2)}, u32[]{:S(2)}) collective-permute-start(bf16[3,160,1280]{2,1,0:T(8,128)(2,1)} %get-tuple-element.82), channel_id=1, source_target_pairs={{0,3},{1,2},{2,1},{3,0},{4,7},{5,6},{6,5},{7,4},{8,11},{9,10},{10,... | collective-permute-start | bytes 3686408 | tf_op jit(solution)/shard_map/ppermute | solution.py:1197
  228.3 64.1 %collective-permute-start.1 = (bf16[3,160,1280]{2,1,0:T(8,128)(2,1)}, bf16[3,160,1280]{2,1,0:T(8,128)(2,1)}, u32[]{:S(2)}, u32[]{:S(2)}) collective-permute-start(bf16[3,160,1280]{2,1,0:T(8,128)(2,1)} %get-tuple-element.81), channel_id=1, source_target_pairs={{0,2},{1,3},{2,0},{3,1},{4,6},{5,7},{6,4},{7,5},{8,10},{9,11},{10,... | collective-permute-start | bytes 3686408 | tf_op jit(solution)/shard_map/ppermute | solution.py:1197
  229.0 63.4 %collective-permute-start = (bf16[3,160,1280]{2,1,0:T(8,128)(2,1)}, bf16[3,160,1280]{2,1,0:T(8,128)(2,1)}, u32[]{:S(2)}, u32[]{:S(2)}) collective-permute-start(bf16[3,160,1280]{2,1,0:T(8,128)(2,1)} %get-tuple-element.80), channel_id=1, source_target_pairs={{0,1},{1,0},{2,3},{3,2},{4,5},{5,4},{6,7},{7,6},{8,9},{9,8},{10,11... | collective-permute-start | bytes 3686408 | tf_op jit(solution)/shard_map/ppermute | solution.py:1197
  230.4 58.5 %copy-start.12 = (f32[1,1280]{1,0:T(1,128)S(1)}, f32[1,1280]{1,0:T(1,128)}, u32[]{:S(2)}) copy-start(f32[1,1280]{1,0:T(1,128)} %get-tuple-element.83) | copy-start | bytes 15364
  230.4 58.6 %copy-start.8 = (f32[2640]{0:T(1024)S(1)}, f32[2640]{0:T(1024)}, u32[]{:S(2)}) copy-start(f32[2640]{0:T(1024)} %param.33) | copy-start | bytes 31684
  287.8 4.3 copy-start
  287.8 4.7 copy-start.7
  419.8 52.2 %collective-permute-start.4 = (bf16[512,1280]{1,0:T(8,128)(2,1)}, bf16[512,1280]{1,0:T(8,128)(2,1)S(1)}, u32[]{:S(2)}, u32[]{:S(2)}) collective-permute-start(bf16[512,1280]{1,0:T(8,128)(2,1)} %get-tuple-element.87), channel_id=1, source_target_pairs={{0,8},{4,12},{8,16},{12,20},{16,24},{20,28},{1,9},{5,13},{9,17},{1... | collective-permute-start | bytes 3932168 | tf_op jit(solution)/shard_map/ppermute | solution.py:1224
  421.2 50.8 %collective-permute-start.3 = (bf16[512,1280]{1,0:T(8,128)(2,1)}, bf16[512,1280]{1,0:T(8,128)(2,1)}, u32[]{:S(2)}, u32[]{:S(2)}) collective-permute-start(bf16[512,1280]{1,0:T(8,128)(2,1)} %get-tuple-element.86), channel_id=1, source_target_pairs={{8,0},{12,4},{16,8},{20,12},{24,16},{28,20},{9,1},{13,5},{17,9},{2... | collective-permute-start | bytes 3932168 | tf_op jit(solution)/shard_map/ppermute | solution.py:1223
  441.3 1.5 copy-start.9
  447.1 24.2 %copy-start.10 = (f32[2640]{0:T(1024)S(1)}, f32[2640]{0:T(1024)}, u32[]{:S(2)}) copy-start(f32[2640]{0:T(1024)} %param.34) | copy-start | bytes 31684
  447.1 24.2 %copy-start.11 = (f32[2640]{0:T(1024)S(1)}, f32[2640]{0:T(1024)}, u32[]{:S(2)}) copy-start(f32[2640]{0:T(1024)} %param.35) | copy-start | bytes 31684
  472.0 3.0 copy-start.1
  472.0 3.7 copy-start.5
  475.7 3.5 copy-start.6

commit v5 on v4

--- a/solution.py
+++ b/solution.py
@@ -102,8 +102,11 @@
     groups,
     heads,
     x_ref,
-    gained_ref,
-    mlp_ref,
+    wqkv_ref,
+    gain_ref,
+    wout_ref,
+    wup_ref,
+    wdown_ref,
     factor_ref,
     unit_ref,
     full_ref,
@@ -114,6 +117,8 @@
     kn_ref,
     vn_ref,
     rows_ref,
+    gained_ref,
+    mlp_ref,
     wrecv_ref,
     wflip_ref,
     line_sem,
@@ -189,8 +194,15 @@
     for way in range(2):
         forward(way, 0, chip)
     side_copy(chip, core).start()
+    span = 2 * width
+    shift = lax.rem(D - chip * span, D)
+    for part in range(3):
+        turned = pltpu.roll(wqkv_ref[:, part * D : (part + 1) * D], shift, 1)
+        gained_ref[part] = (turned[:, :span] * gain_ref[...]).astype(bf16)
     for peer in group_peers:
         w_copy(peer, group).start()
+    for index, ref in enumerate((wout_ref, wup_ref, wdown_ref)):
+        mlp_ref[index] = ref[...].astype(bf16).reshape(mlp_ref.shape[1:])
     own_copy.start()
     keep_copy(here).start()
     wrecv_ref[group] = gained_ref[...]
@@ -198,9 +210,12 @@
         w_copy(group, peer).wait_recv()
     for peer in group_peers:
         mlp_copy(peer, group).start()
-    flipped = wrecv_ref[...].reshape(D, 6 * width).T
-    wpair_ref[0] = flipped[: 3 * width]
-    wpair_ref[1] = flipped[3 * width :]
+    for part in range(3):
+        flipped = wrecv_ref[:, part].reshape(D, span).T
+        for lane in range(2):
+            wpair_ref[lane, part * width : (part + 1) * width] = flipped[
+                lane * width : (lane + 1) * width
+            ]
     wflip_ref[...] = wpair_ref[core]
 
     extra_row = lax.broadcasted_iota(jnp.int32, (PAD - HD, BLOCK), 0)
@@ -283,8 +298,9 @@
     lax.fori_loop(0, chips, drain, 0)
 
 
-def gather_rows(parts, groups, heads, rows, gained, mlp, factor):
+def gather_rows(parts, groups, heads, rows, w_qkv, gain, w_out, w_up, w_down, factor):
     rows_dev = rows.shape[0]
+    held = w_qkv.shape[0]
     tokens = parts * rows_dev
     dma = pltpu.SemaphoreType.DMA
     chips = parts // 2
@@ -294,7 +310,7 @@
         name="gather_rows",
         out_shape=[
             jax.ShapeDtypeStruct((parts, rows_dev, D), bf16),
-            jax.ShapeDtypeStruct((3, groups) + mlp.shape[1:], bf16),
+            jax.ShapeDtypeStruct((3, groups, 2, held // 2, D), bf16),
             jax.ShapeDtypeStruct((2, 3 * heads * HD, D), bf16),
             jax.ShapeDtypeStruct((heads, PAD, tokens), bf16),
             jax.ShapeDtypeStruct((heads, HD, tokens), bf16),
@@ -302,11 +318,13 @@
             jax.ShapeDtypeStruct((heads, tokens, PAD), bf16),
             jax.ShapeDtypeStruct((heads, tokens, PAD), bf16),
         ],
-        in_specs=in_vmem(2) + [anywhere] + in_vmem(1),
+        in_specs=in_vmem(7),
         out_specs=[anywhere] * 2 + in_vmem(6),
         scratch_shapes=[
             pltpu.VMEM((parts, rows_dev, D), bf16),
-            pltpu.VMEM((groups,) + gained.shape, bf16),
+            pltpu.VMEM((3, held, 2 * heads * HD), bf16),
+            pltpu.VMEM((3, 2, held // 2, D), bf16),
+            pltpu.VMEM((groups, 3, held, 2 * heads * HD), bf16),
             pltpu.VMEM((3 * heads * HD, D), bf16),
             dma((2, 2, chips)),
             dma((2, chips)),
@@ -319,7 +337,7 @@
         compiler_params=pltpu.CompilerParams(
             vmem_limit_bytes=60 * 1024 * 1024, collective_id=2, has_side_effects=True
         ),
-    )(rows, gained, mlp, factor)
+    )(rows, w_qkv, gain, w_out, w_up, w_down, factor)
 
 
 def forward_kernel(
@@ -1086,38 +1104,69 @@
     )(dqkv, w_pair, u_parts, w_columns, mlp, small)
 
 
-def update_kernel(rates, *refs):
+def update_kernel(rates, qkv_ref, gain_ref, mlp_ref, *refs):
     sets = len(rates)
+    parts, rows, width = qkv_ref.shape
+    width = width // 3
     for index, rate in enumerate(rates):
-        weight, first, second, gradient = (ref[...] for ref in refs[4 * index : 4 * index + 4])
-        outs = refs[4 * (sets + index) : 4 * (sets + index) + 4]
-        new, first, second = adamw(weight, first, second, gradient.astype(f32), rate, decay_rate)
+        weight, first, second = (ref[...] for ref in refs[3 * index : 3 * index + 3])
+        if index == 0:
+            pieces = [qkv_ref[part].astype(f32) for part in range(parts)]
+            gradient = jnp.concatenate(
+                [piece[:, at * width : (at + 1) * width] for at in range(3) for piece in pieces],
+                axis=1,
+            )
+            gradient = gradient * gain_ref[...]
+        else:
+            gradient = mlp_ref[0, index - 1].astype(f32)
+        outs = refs[3 * sets + 4 * index : 3 * sets + 4 * index + 4]
+        new, first, second = adamw(weight, first, second, gradient, rate, decay_rate)
         outs[0][...] = new
         outs[1][...] = first
         outs[2][...] = second
         outs[3][...] = new.astype(bf16)
 
 
-def update(rates, *arrays):
-    step_rows = 32
+def update(rates, parts, qkv, gain, mlp, *arrays):
     rows = arrays[0].shape[0]
+    chips = parts // 2
+    step_rows = rows // parts
+    if step_rows % 8 == 0:
+
+        def owner(i):
+            return (2 * lax.rem(i, chips) + i // chips, 0, 0, 0)
+
+    else:
+        step_rows = 32
+        mlp = mlp.reshape(chips, 2, 3, rows // parts, D).transpose(2, 1, 0, 3, 4)
+        mlp = mlp.reshape(3, rows // step_rows, step_rows, D).transpose(1, 0, 2, 3)
+
+        def owner(i):
+            return (i, 0, 0, 0)
+
+    in_specs = [
+        pl.BlockSpec((parts, step_rows, qkv.shape[2]), lambda i: (0, i, 0)),
+        pl.BlockSpec((step_rows, 1), lambda i: (i, 0)),
+        pl.BlockSpec((1, 3, step_rows, D), owner),
+    ]
     specs, shapes, moved = [], [], 0
     for array in arrays:
-        specs.append(pl.BlockSpec((step_rows, array.shape[1]), lambda i: (i, 0)))
+        in_specs.append(pl.BlockSpec((step_rows, array.shape[1]), lambda i: (i, 0)))
     for index in range(len(rates)):
-        shape = arrays[4 * index].shape
+        shape = arrays[3 * index].shape
         shapes += [jax.ShapeDtypeStruct(shape, f32)] * 3 + [jax.ShapeDtypeStruct(shape, bf16)]
+        specs += [pl.BlockSpec((step_rows, shape[1]), lambda i: (i, 0))] * 4
         moved += shape[0] * shape[1] * 28
     return pl.pallas_call(
         functools.partial(update_kernel, rates),
         name="update_weights",
         grid=(rows // step_rows,),
-        in_specs=specs,
+        in_specs=in_specs,
         out_specs=specs,
         out_shape=shapes,
         compiler_params=params(),
         cost_estimate=pl.CostEstimate(flops=moved, bytes_accessed=moved, transcendentals=0),
-    )(*arrays)
+    )(qkv, gain, mlp, *arrays)
 
 
 def body(
@@ -1152,7 +1201,6 @@
     gain_one = small_params[:D]
     gain_two = small_params[D : 2 * D]
     query_scale = small_params[2 * D :]
-    core = lax.rem(here, 2)
     group = lax.axis_index("fsdp")
     rows = w_qkv.shape[0]
 
@@ -1166,19 +1214,14 @@
         )
 
     gain_rows = lax.dynamic_slice_in_dim(gain_one, group * rows, rows, 0)[:, None]
-    columns = [head_columns(here - core + lane) for lane in range(2)]
-    gained = jnp.concatenate([(gain_rows * part).astype(bf16) for part in columns], axis=1)
     w_columns = head_columns(here).astype(bf16)
     layer_in = inputs[0].astype(f32)
     scale_one = rms_scale(layer_in)
     unit_one = layer_in * scale_one
     factor = scale_base / math.sqrt(HD) * jax.nn.softplus(query_scale)
     factor_two = (factor * LOG2E)[:, None]
-    half = rows // 2
-    mlp = jnp.stack([w_out.astype(bf16), w_up.astype(bf16), w_down.astype(bf16)])
-    mlp = mlp.reshape(3, 2, half, D)
     unit_all, mlp_full, w_pair, qt, kt, vt, kn, vn = gather_rows(
-        parts, groups, heads, inputs[0], gained, mlp, factor_two
+        parts, groups, heads, inputs[0], w_qkv, gain_rows, w_out, w_up, w_down, factor_two
     )
     lse, mixed = attention_forward(slots, qt, kn, vt, parts)
     kept = (qt, kt, kn, vn, lse)
@@ -1222,37 +1265,28 @@
     )
     got_down = lax.ppermute(send_down, "ctx", [(i, i - 2) for i in range(2, parts)])
     got_up = lax.ppermute(send_up, "ctx", [(i, i + 2) for i in range(parts - 2)])
-    total_qkv = (
-        u_all.reshape(parts, rows, 3, width).transpose(1, 2, 0, 3).reshape(rows, 3 * D)
-        * gain_rows
-    ).astype(bf16)
-    total_mlp = (
-        mlp_all.reshape(parts // 2, 2, 3, rows // parts, D)
-        .transpose(2, 1, 0, 3, 4)
-        .reshape(3, rows, D)
-    )
     rate_qkv = qkv_rate_base / math.sqrt(D)
     rate_out = 0.5 / math.sqrt(max(D // 256, 1))
     rate_up = 0.5 / math.sqrt(D)
     rate_down = 0.5 / math.sqrt(FF)
     updated = update(
         (rate_qkv, rate_out, rate_up, rate_down),
+        parts,
+        u_all,
+        gain_rows,
+        mlp_all,
         w_qkv,
         m_qkv,
         v_qkv,
-        total_qkv,
         w_out,
         m_out,
         v_out,
-        total_mlp[0],
         w_up,
         m_up,
         v_up,
-        total_mlp[1],
         w_down,
         m_down,
         v_down,
-        total_mlp[2],
     )
     flat = small_all.reshape(groups, small_rows * PAD)
     rest = jnp.sum(flat[:, lanes : lanes + D + HD], axis=0)

time: 484 us -> 463 us (0.957)
  local copies, waits for them, and re-layouts: 29.4 us -> 8.16 us
  other arithmetic: 25.1 us -> 14.5 us
  Pallas kernels: 417 us -> 426 us
    convert_element_type x3 -> x0, local copies, waits for them, and re-layouts: 16.9 us -> none  [body(): u_all.reshape(parts, rows, 3, width).transpose(1, 2, 0, 3)]
    pallas_call x1, Pallas kernels: 113 us -> 121 us  [gather_rows(): pl.pallas_call(functools.partial(gather_kernel, parts, groups, heads), na...]
    convert_element_type x5 -> x0, other arithmetic: 7.49 us -> none  [the longest x1 4.22 us: body(): total_qkv = (u_all.reshape(parts, rows, 3, width).transpose(1, 2, 0, 3).r...]
  transfers between devices with their start and end apart: 5 -> 5, of which waited for: 0 -> 1; matrix products, arithmetic and copies ran while one was open for 6% -> 1% of each run, Pallas kernels for 17% -> 18%
where the time goes in v5:
time: 463 us; the launch traced here: 462 us
  Pallas kernels  426 us (92%)
  other arithmetic  14.5 us (3%)
  local copies, waits for them, and re-layouts  8.16 us (2%)
  starting transfers between devices  7.89 us (2%)
    pallas_call x1, Pallas kernels, reduce_gradients(): pl.pallas_call(functools.partial(reduce_kernel, parts, groups), name='red...  124 us
    pallas_call x1, Pallas kernels, gather_rows(): pl.pallas_call(functools.partial(gather_kernel, parts, groups, heads), na...  121 us
    pallas_call x1, Pallas kernels, middle(): pl.pallas_call(functools.partial(middle_kernel, parts, groups), name='mid...  62.8 us
    pallas_call x1, Pallas kernels, attention_backward(): pl.pallas_call(functools.partial(backward_kernel, heads), name='attention...  57.3 us
    pallas_call x1, Pallas kernels, attention_forward(): pl.pallas_call(functools.partial(forward_kernel, heads), name='attention_...  36.2 us
    pallas_call x1, Pallas kernels, update(): pl.pallas_call(functools.partial(update_kernel, rates), name='update_weig...  25.5 us
  transfers between devices with their start and end apart: 5, of which 1 were waited for; matrix products, arithmetic and copies ran while one was open for 1% of the time, Pallas kernels for 18%

profile of v5, /device:TPU:0, one launch (start us, length us, event | category | flops | bytes accessed | tf_op | source)
XLA Modules:
  0.0 461.7 jit_solution(5171078390809706317)
XLA Ops:
  0.7 0.8 fusion.13
  1.4 0.7 fusion.14
  2.1 1.3 select_reduce_fusion.slot_ref
  3.5 0.8 broadcast_in_dim.42.gain_ref
  4.3 0.7 copy.47.factor_ref
  5.0 0.6 broadcast_in_dim.38.gain_ref
  5.6 120.9 %gather_rows.1 = (bf16[8,512,1280]{2,1,0:T(8,128)(2,1)}, bf16[3,4,2,160,1280]{4,3,2,1,0:T(8,128)(2,1)}, bf16[2,480,1280]{2,1,0:T(8,128)(2,1)}, bf16[2,128,4096]{...) custom-call(bf16[512,1280]{1,0:T(8,128)(2,1)} %bitcast.24, ...), custom_call_target="tpu_custom_call" | custom-call | tf_op jit(solution)/shard_map/gather_rows/pallas_call | solution.py:308
  126.5 36.2 %attention_forward.1 = (f32[2,1,4096]{2,1,0:T(1,128)}, bf16[8,160,512]{2,1,0:T(8,128)(2,1)}) custom-call(s32[16]{0:T(128)} %select_reduce_fusion.slot_ref, bf16[2,128,4096]{2,1,0:T(8,128)(2,1)} %get-tuple-element.64.qt_ref, bf16[2,4096,128]{2,1,0:T(8,128)(2,1)} %get-tuple-element.65.kn_ref, bf16[2,96,4096]{2,1,0:T(8,128)(2,1)} %get-tuple-element.66.vt_ref), custom_call_target="tpu_custom_call" | custom-call | flops 17179869184 | bytes 5242880 | tf_op jit(solution)/shard_map/attention_forward/pallas_call | solution.py:537
  162.8 62.8 %middle.1 = (bf16[512,1280]{1,0:T(8,128)(2,1)}, f32[512,1280]{1,0:T(8,128)}, bf16[8,160,512]{2,1,0:T(8,128)(2,1)}, f32[1,1280]{1,0:T(1,128)}, bf16[3,160,1280]{2...) custom-call(bf16[8,160,512]{2,1,0:T(8,128)(2,1)} %get-tuple-element., ...), custom_call_target="tpu_custom_call" | custom-call | tf_op jit(solution)/shard_map/middle/pallas_call | solution.py:765
  225.6 3.0 collective-permute-start.2
  228.6 0.8 collective-permute-start.1
  229.4 1.4 collective-permute-start
  230.8 57.3 %attention_backward.1 = (bf16[8,480,512]{2,1,0:T(8,128)(2,1)}, f32[2,80,128]{2,1,0:T(8,128)}, bf16[1280,480]{1,0:T(8,128)(2,1)}) custom-call(s32[16]{0:T(128)} %select_reduce_fusion.slot_ref, bf16[2,128,4096]{2,1,0:T(8,128)(2,1)} %get-tuple-element.64.qt_ref, bf16[2,80,4096]{2,1,0:T(8,128)(2,1)} %get-tuple-element.71.kt_ref, ...), custom_call_target="tpu_custom_call" | custom-call | flops 42949672960 | bytes 5242880 | tf_op jit(solution)/shard_map/attention_backward/pallas_call | solution.py:565
  288.2 1.1 reduce_sum.47
  289.4 0.6 fusion.10.small_ref
  290.0 1.5 dynamic-slice_convert_fusion.2
  291.5 0.9 pad_maximum_fusion.wc_ref
  292.4 2.3 add_convert_fusion
  294.7 1.1 copy.54
  295.9 123.6 %reduce_gradients.1 = (bf16[512,1280]{1,0:T(8,128)(2,1)}, bf16[512,1280]{1,0:T(8,128)(2,1)}, f32[512,1280]{1,0:T(8,128)}, bf16[8,320,480]{2,1,0:T(8,128)(2,1)}, ...) custom-call(bf16[4,2,480,512]{3,2,1,0:T(8,128)(2,1)} %bitcast.29, ...), custom_call_target="tpu_custom_call" | custom-call | tf_op jit(solution)/shard_map/reduce_gradients/pallas_call | solution.py:1070
  419.5 1.4 collective-permute-start.4
  420.9 1.3 collective-permute-start.3
  422.2 0.3 fusion.7
  422.5 0.8 copy.55
  423.3 0.1 reshape.81
  423.4 25.5 %update_weights.1 = (f32[320,3840]{1,0:T(8,128)}, f32[320,3840]{1,0:T(8,128)}, f32[320,3840]{1,0:T(8,128)}, bf16[320,3840]{1,0:T(8,128)(2,1)}, f32[320,1280]{1,0...) custom-call(bf16[8,320,480]{2,1,0:T(8,128)(2,1)} %get-tuple-element., ...), custom_call_target="tpu_custom_call" | custom-call | flops 68812800 | bytes 68812800 | tf_op jit(solution)/shard_map/update_weights/pallas_call | solution.py:1160
  449.0 0.6 multiply_subtract_fusion
  449.6 3.8 collective-permute-done.3
  453.4 3.1 fusion.2
  456.5 0.6 copy-done.2
  457.1 3.5 fusion.8
  460.6 1.1 copy.57
  (29 shorter events, 0.2 us)
Async XLA Ops:
  225.6 66.8 %collective-permute-start.2 = (bf16[3,160,1280]{2,1,0:T(8,128)(2,1)}, bf16[3,160,1280]{2,1,0:T(8,128)(2,1)S(1)}, u32[]{:S(2)}, u32[]{:S(2)}) collective-permute-start(bf16[3,160,1280]{2,1,0:T(8,128)(2,1)} %get-tuple-element.82), channel_id=1, source_target_pairs={{0,3},{1,2},{2,1},{3,0},{4,7},{5,6},{6,5},{7,4},{8,11},{9,10},{10,... | collective-permute-start | bytes 3686408 | tf_op jit(solution)/shard_map/ppermute | solution.py:1240
  228.6 63.8 %collective-permute-start.1 = (bf16[3,160,1280]{2,1,0:T(8,128)(2,1)}, bf16[3,160,1280]{2,1,0:T(8,128)(2,1)}, u32[]{:S(2)}, u32[]{:S(2)}) collective-permute-start(bf16[3,160,1280]{2,1,0:T(8,128)(2,1)} %get-tuple-element.81), channel_id=1, source_target_pairs={{0,2},{1,3},{2,0},{3,1},{4,6},{5,7},{6,4},{7,5},{8,10},{9,11},{10,... | collective-permute-start | bytes 3686408 | tf_op jit(solution)/shard_map/ppermute | solution.py:1240
  229.4 63.0 %collective-permute-start = (bf16[3,160,1280]{2,1,0:T(8,128)(2,1)}, bf16[3,160,1280]{2,1,0:T(8,128)(2,1)}, u32[]{:S(2)}, u32[]{:S(2)}) collective-permute-start(bf16[3,160,1280]{2,1,0:T(8,128)(2,1)} %get-tuple-element.80), channel_id=1, source_target_pairs={{0,1},{1,0},{2,3},{3,2},{4,5},{5,4},{6,7},{7,6},{8,9},{9,8},{10,11... | collective-permute-start | bytes 3686408 | tf_op jit(solution)/shard_map/ppermute | solution.py:1240
  230.8 58.4 %copy-start.8 = (f32[1,1280]{1,0:T(1,128)S(1)}, f32[1,1280]{1,0:T(1,128)}, u32[]{:S(2)}) copy-start(f32[1,1280]{1,0:T(1,128)} %get-tuple-element.83) | copy-start | bytes 15364
  230.8 58.5 %copy-start.5 = (f32[2640]{0:T(1024)S(1)}, f32[2640]{0:T(1024)}, u32[]{:S(2)}) copy-start(f32[2640]{0:T(1024)} %param.33) | copy-start | bytes 31684
  288.2 4.3 copy-start.4
  295.9 126.3 %copy-start = (bf16[1,512,1280]{2,1,0:T(8,128)(2,1)S(1)}, bf16[1,512,1280]{2,1,0:T(8,128)(2,1)}, u32[]{:S(2)}) copy-start(bf16[1,512,1280]{2,1,0:T(8,128)(2,1)} %param.18) | copy-start | bytes 3932164
  419.5 30.1 %collective-permute-start.4 = (bf16[512,1280]{1,0:T(8,128)(2,1)}, bf16[512,1280]{1,0:T(8,128)(2,1)S(1)}, u32[]{:S(2)}, u32[]{:S(2)}) collective-permute-start(bf16[512,1280]{1,0:T(8,128)(2,1)} %get-tuple-element.87), channel_id=1, source_target_pairs={{0,8},{4,12},{8,16},{12,20},{16,24},{20,28},{1,9},{5,13},{9,17},{1... | collective-permute-start | bytes 3932168 | tf_op jit(solution)/shard_map/ppermute | solution.py:1267
  420.9 32.5 %collective-permute-start.3 = (bf16[512,1280]{1,0:T(8,128)(2,1)}, bf16[512,1280]{1,0:T(8,128)(2,1)}, u32[]{:S(2)}, u32[]{:S(2)}) collective-permute-start(bf16[512,1280]{1,0:T(8,128)(2,1)} %get-tuple-element.86), channel_id=1, source_target_pairs={{8,0},{12,4},{16,8},{20,12},{24,16},{28,20},{9,1},{13,5},{17,9},{2... | collective-permute-start | bytes 3932168 | tf_op jit(solution)/shard_map/ppermute | solution.py:1266
  423.4 25.6 %copy-start.6 = (f32[2640]{0:T(1024)S(1)}, f32[2640]{0:T(1024)}, u32[]{:S(2)}) copy-start(f32[2640]{0:T(1024)} %param.34) | copy-start | bytes 31684
  423.4 25.6 %copy-start.7 = (f32[2640]{0:T(1024)S(1)}, f32[2640]{0:T(1024)}, u32[]{:S(2)}) copy-start(f32[2640]{0:T(1024)} %param.35) | copy-start | bytes 31684
  453.4 3.1 copy-start.1
  453.4 3.7 copy-start.2
  457.1 3.5 copy-start.3

commit v6 on v5

--- a/solution.py
+++ b/solution.py
@@ -18,6 +18,7 @@
 PAD = 128
 EXTRA = 16
 TILE = CONT
+SCORE_BOUND = 96.0
 
 bf16 = jnp.bfloat16
 f32 = jnp.float32
@@ -91,9 +92,9 @@
     return pl.ds(pl.multiple_of(lax.rem(slot, 2) * BLOCK, BLOCK), BLOCK)
 
 
-def causal():
-    key = lax.broadcasted_iota(jnp.int32, (TILE, TILE), 0)
-    query = lax.broadcasted_iota(jnp.int32, (TILE, TILE), 1)
+def causal(shape):
+    key = lax.broadcasted_iota(jnp.int32, shape, 0)
+    query = lax.broadcasted_iota(jnp.int32, shape, 1)
     return key <= query
 
 
@@ -117,6 +118,8 @@
     kn_ref,
     vn_ref,
     rows_ref,
+    wstage_ref,
+    mstage_ref,
     gained_ref,
     mlp_ref,
     wrecv_ref,
@@ -125,9 +128,11 @@
     side_sem,
     keep_sem,
     w_sem,
+    lane_sem,
     mlp_sem,
     cross_sem,
     own_sem,
+    stage_sem,
 ):
     chips = parts // 2
     here = lax.axis_index("ctx")
@@ -169,6 +174,10 @@
         sems = (w_sem.at[0, peer], w_sem.at[1, source])
         return send(gained_ref, wrecv_ref.at[source], sems, {"fsdp": peer})
 
+    def lane_copy(lane):
+        ref = wpair_ref.at[lane]
+        return send(ref, ref, (lane_sem.at[0], lane_sem.at[1]), {"ctx": other})
+
     def mlp_copy(peer, source):
         sems = (mlp_sem.at[0, peer], mlp_sem.at[1, source])
         return send(mlp_ref.at[:, core], full_ref.at[:, source, core], sems, {"fsdp": peer})
@@ -183,6 +192,12 @@
 
     own_copy = pltpu.make_async_copy(mlp_ref, full_ref.at[:, group], own_sem)
 
+    stages = [pltpu.make_async_copy(wqkv_ref, wstage_ref, stage_sem.at[0])] + [
+        pltpu.make_async_copy(ref, mstage_ref.at[index], stage_sem.at[index + 1])
+        for index, ref in enumerate((wout_ref, wup_ref, wdown_ref))
+    ]
+    for stage in stages:
+        stage.start()
     rows = x_ref[...].astype(f32)
     rows_ref[here] = (rows * rms_scale(rows)).astype(bf16)
 
@@ -194,15 +209,16 @@
     for way in range(2):
         forward(way, 0, chip)
     side_copy(chip, core).start()
-    span = 2 * width
-    shift = lax.rem(D - chip * span, D)
+    shift = lax.rem(D - here * width, D)
+    stages[0].wait()
     for part in range(3):
-        turned = pltpu.roll(wqkv_ref[:, part * D : (part + 1) * D], shift, 1)
-        gained_ref[part] = (turned[:, :span] * gain_ref[...]).astype(bf16)
+        turned = pltpu.roll(wstage_ref[:, part * D : (part + 1) * D], shift, 1)
+        gained_ref[part] = (turned[:, :width] * gain_ref[...]).astype(bf16)
     for peer in group_peers:
         w_copy(peer, group).start()
-    for index, ref in enumerate((wout_ref, wup_ref, wdown_ref)):
-        mlp_ref[index] = ref[...].astype(bf16).reshape(mlp_ref.shape[1:])
+    for index in range(3):
+        stages[index + 1].wait()
+        mlp_ref[index] = mstage_ref[index].astype(bf16).reshape(mlp_ref.shape[1:])
     own_copy.start()
     keep_copy(here).start()
     wrecv_ref[group] = gained_ref[...]
@@ -211,12 +227,10 @@
     for peer in group_peers:
         mlp_copy(peer, group).start()
     for part in range(3):
-        flipped = wrecv_ref[:, part].reshape(D, span).T
-        for lane in range(2):
-            wpair_ref[lane, part * width : (part + 1) * width] = flipped[
-                lane * width : (lane + 1) * width
-            ]
-    wflip_ref[...] = wpair_ref[core]
+        flipped = wrecv_ref[:, part].reshape(D, width).T
+        wflip_ref[part * width : (part + 1) * width] = flipped
+    wpair_ref[core] = wflip_ref[...]
+    lane_copy(core).start()
 
     extra_row = lax.broadcasted_iota(jnp.int32, (PAD - HD, BLOCK), 0)
     extra = jnp.where(extra_row < 3, 1.0, 0.0)
@@ -279,6 +293,8 @@
         w_copy(peer, group).wait_send()
         mlp_copy(peer, group).wait_send()
     own_copy.wait()
+    lane_copy(1 - core).wait_recv()
+    lane_copy(core).wait_send()
 
     def drain(piece, carry):
         keep_copy(2 * piece).wait()
@@ -318,21 +334,25 @@
             jax.ShapeDtypeStruct((heads, tokens, PAD), bf16),
             jax.ShapeDtypeStruct((heads, tokens, PAD), bf16),
         ],
-        in_specs=in_vmem(7),
+        in_specs=in_vmem(1) + [anywhere] + in_vmem(1) + [anywhere] * 3 + in_vmem(1),
         out_specs=[anywhere] * 2 + in_vmem(6),
         scratch_shapes=[
             pltpu.VMEM((parts, rows_dev, D), bf16),
-            pltpu.VMEM((3, held, 2 * heads * HD), bf16),
+            pltpu.VMEM((held, 3 * D), f32),
+            pltpu.VMEM((3, held, D), f32),
+            pltpu.VMEM((3, held, heads * HD), bf16),
             pltpu.VMEM((3, 2, held // 2, D), bf16),
-            pltpu.VMEM((groups, 3, held, 2 * heads * HD), bf16),
+            pltpu.VMEM((groups, 3, held, heads * HD), bf16),
             pltpu.VMEM((3 * heads * HD, D), bf16),
             dma((2, 2, chips)),
             dma((2, chips)),
             dma((parts,)),
             dma((2, groups)),
+            dma((2,)),
             dma((2, groups)),
             dma((2, groups)),
             dma,
+            dma((4,)),
         ],
         compiler_params=pltpu.CompilerParams(
             vmem_limit_bytes=60 * 1024 * 1024, collective_id=2, has_side_effects=True
@@ -344,6 +364,7 @@
     heads,
     slot_ref,
     qt_ref,
+    kt_ref,
     kn_ref,
     vt_ref,
     lse_ref,
@@ -354,47 +375,84 @@
     tokens = kn_ref.shape[1]
     num_tiles = tokens // TILE
     prompt_tiles = num_tiles // 2
-    allowed = causal()
-
-    def query_tile(tile, carry):
-        here = tile_at(tile)
-        top_ref[...] = jnp.full(top_ref.shape, -1e30, f32)
-        acc_ref[...] = jnp.zeros(acc_ref.shape, f32)
-
-        queries = [tile_lanes(qt_ref, head, slot_ref, tile) for head in range(heads)]
-
-        def step(key_tile, masked):
+
+    def longest(ref):
+        def visit(slot, most):
+            rows = [ref[head, :HD, block_at(slot)].astype(f32) for head in range(heads)]
+            sums = [jnp.sum(row * row, axis=0, keepdims=True) for row in rows]
+            return functools.reduce(jnp.maximum, sums, most)
+
+        return jnp.max(lax.fori_loop(0, tokens // BLOCK, visit, jnp.zeros((1, BLOCK), f32)))
+
+    bounded = longest(qt_ref) * longest(kt_ref) <= SCORE_BOUND * SCORE_BOUND
+
+    def run(shifted):
+        def query_tile(tile, carry):
+            queries = [tile_lanes(qt_ref, head, slot_ref, tile) for head in range(heads)]
+            if shifted:
+                top_ref[...] = jnp.full(top_ref.shape, -1e30, f32)
+            else:
+                top_ref[...] = jnp.zeros(top_ref.shape, f32)
+            acc_ref[...] = jnp.zeros(acc_ref.shape, f32)
+
+            def step(key_rows, value_lanes, start, masked):
+                scores = [dot(key_rows[head], queries[head][:, start:]) for head in range(heads)]
+                if masked:
+                    allowed = causal(scores[0].shape)
+                    scores = [jnp.where(allowed, score, -1e30) for score in scores]
+                if shifted:
+                    olds = [top_ref[head, :, start:] for head in range(heads)]
+                    tops = [
+                        jnp.maximum(old, jnp.max(score, axis=0, keepdims=True))
+                        for old, score in zip(olds, scores)
+                    ]
+                    scores = [score - top for score, top in zip(scores, tops)]
+                    for head in range(heads):
+                        acc_ref[head, :, start:] *= jnp.exp2(olds[head] - tops[head])
+                        top_ref[head, :, start:] = tops[head]
+                probs = [jnp.exp2(score).astype(bf16) for score in scores]
+                for head in range(heads):
+                    acc_ref[head, :, start:] += dot(value_lanes[head], probs[head])
+
+            def full(key_tile, inner):
+                step(
+                    [tile_rows(kn_ref, head, slot_ref, key_tile) for head in range(heads)],
+                    [tile_lanes(vt_ref, head, slot_ref, key_tile) for head in range(heads)],
+                    0,
+                    False,
+                )
+                return inner
+
+            lax.fori_loop(0, jnp.minimum(tile, prompt_tiles), full, 0)
+            for part in range(TILE // BLOCK):
+                block = block_at(slot_ref[tile * (TILE // BLOCK) + part])
+                step(
+                    [kn_ref[head, block, :] for head in range(heads)],
+                    [vt_ref[head, :, block] for head in range(heads)],
+                    part * BLOCK,
+                    True,
+                )
             for head in range(heads):
-                scores = dot(tile_rows(kn_ref, head, slot_ref, key_tile), queries[head])
-                if masked:
-                    scores = jnp.where(allowed, scores, -1e30)
-                old = top_ref[head]
-                top = jnp.maximum(old, jnp.max(scores, axis=0, keepdims=True))
-                probs = jnp.exp2(scores - top).astype(bf16)
-                acc_ref[head] = acc_ref[head] * jnp.exp2(old - top) + dot(
-                    tile_lanes(vt_ref, head, slot_ref, key_tile), probs
-                )
-                top_ref[head] = top
-
-        def full(key_tile, inner):
-            step(key_tile, False)
-            return inner
-
-        lax.fori_loop(0, jnp.minimum(tile, prompt_tiles), full, 0)
-        step(tile, True)
-        for head in range(heads):
-            acc = acc_ref[head]
-            mass = acc[HD : HD + 1]
-            mixed = (acc[:HD] / mass).astype(bf16)
-            lse_ref[head, :, here] = top_ref[head] + jnp.log2(mass)
-            for part in range(TILE // BLOCK):
-                slot = slot_ref[tile * (TILE // BLOCK) + part]
-                ot_ref[slot // 2, head * HD : (head + 1) * HD, half_at(slot)] = mixed[
-                    :, part * BLOCK : (part + 1) * BLOCK
-                ]
-        return carry
-
-    lax.fori_loop(0, num_tiles, query_tile, 0)
+                acc = acc_ref[head]
+                mass = acc[HD : HD + 1]
+                mixed = (acc[:HD] / mass).astype(bf16)
+                lse_ref[head, :, tile_at(tile)] = top_ref[head] + jnp.log2(mass)
+                for part in range(TILE // BLOCK):
+                    slot = slot_ref[tile * (TILE // BLOCK) + part]
+                    ot_ref[slot // 2, head * HD : (head + 1) * HD, half_at(slot)] = mixed[
+                        :, part * BLOCK : (part + 1) * BLOCK
+                    ]
+            return carry
+
+        lax.fori_loop(0, num_tiles, query_tile, 0)
+
+    @pl.when(bounded)
+    def _():
+        run(False)
+
+    @pl.when(jnp.logical_not(bounded))
+    def _():
+        run(True)
 
 
 def backward_kernel(
@@ -455,32 +513,50 @@
     dk_ref[...] = jnp.zeros(dk_ref.shape, f32)
     dv_ref[...] = jnp.zeros(dv_ref.shape, f32)
     dscale_ref[...] = jnp.zeros(dscale_ref.shape, f32)
-    allowed = causal()
 
     def query_tile(tile, carry):
         here = tile_at(tile)
         dq_ref[...] = jnp.zeros(dq_ref.shape, f32)
 
-        def step(key_tile, masked):
-            keys = tile_at(key_tile)
+        def step(keys, key_rows, key_lanes, value_rows, start, masked):
+            to = pl.ds(pl.multiple_of(tile * TILE + start, BLOCK), TILE - start)
+            queries = [qa_ref[head, :, to] for head in range(heads)]
+            grads = [da_ref[head, :, to] for head in range(heads)]
+            scores = [dot(key_rows[head], queries[head]) for head in range(heads)]
+            spreads = [dot(value_rows[head], grads[head]) for head in range(heads)]
+            probs = [jnp.exp2(score) for score in scores]
+            if masked:
+                allowed = causal(scores[0].shape)
+                probs = [jnp.where(allowed, prob, 0.0) for prob in probs]
+            dscores = [(prob * spread).astype(bf16) for prob, spread in zip(probs, spreads)]
             for head in range(heads):
-                key_rows = tile_rows(kn_ref, head, slot_ref, key_tile)
-                value_rows = tile_rows(vn_ref, head, slot_ref, key_tile)
-                probs = jnp.exp2(dot(key_rows, qa_ref[head, :, here]))
-                if masked:
-                    probs = jnp.where(allowed, probs, 0.0)
-                spread = dot(value_rows, da_ref[head, :, here])
-                dscores = (probs * spread).astype(bf16)
-                dv_ref[head, :, keys] += dot(da_ref[head, :HD, here], probs.astype(bf16), (1, 1))
-                dk_ref[head, :, keys] += dot(qa_ref[head, :HD, here], dscores, (1, 1))
-                dq_ref[head] += dot(tile_lanes(kt_ref, head, slot_ref, key_tile), dscores)
+                dv_ref[head, :, keys] += dot(grads[head][:HD], probs[head].astype(bf16), (1, 1))
+                dk_ref[head, :, keys] += dot(queries[head][:HD], dscores[head], (1, 1))
+                dq_ref[head, :, start:] += dot(key_lanes[head], dscores[head])
 
         def full(key_tile, inner):
-            step(key_tile, False)
+            step(
+                tile_at(key_tile),
+                [tile_rows(kn_ref, head, slot_ref, key_tile) for head in range(heads)],
+                [tile_lanes(kt_ref, head, slot_ref, key_tile) for head in range(heads)],
+                [tile_rows(vn_ref, head, slot_ref, key_tile) for head in range(heads)],
+                0,
+                False,
+            )
             return inner
 
         lax.fori_loop(0, jnp.minimum(tile, prompt_tiles), full, 0)
-        step(tile, True)
+        for part in range(TILE // BLOCK):
+            position = tile * (TILE // BLOCK) + part
+            block = block_at(slot_ref[position])
+            step(
+                block_at(position),
+                [kn_ref[head, block, :] for head in range(heads)],
+                [kt_ref[head, :, block] for head in range(heads)],
+                [vn_ref[head, block, :] for head in range(heads)],
+                part * BLOCK,
+                True,
+            )
         for head in range(heads):
             dq = dq_ref[head]
             product = dq * qa_ref[head, :HD, here].astype(f32)
@@ -532,7 +608,7 @@
     return pltpu.CompilerParams(vmem_limit_bytes=60 * 1024 * 1024)
 
 
-def attention_forward(slots, qt, kn, vt, parts):
+def attention_forward(slots, qt, kt, kn, vt, parts):
     heads, tokens = kn.shape[:2]
     return pl.pallas_call(
         functools.partial(forward_kernel, heads),
@@ -541,7 +617,7 @@
             jax.ShapeDtypeStruct((heads, 1, tokens), f32),
             jax.ShapeDtypeStruct((parts, heads * HD, tokens // parts), bf16),
         ],
-        in_specs=[pl.BlockSpec(memory_space=pltpu.SMEM)] + in_vmem(3),
+        in_specs=[pl.BlockSpec(memory_space=pltpu.SMEM)] + in_vmem(4),
         out_specs=in_vmem(2),
         scratch_shapes=[
             pltpu.VMEM((heads, HD + EXTRA, TILE), f32),
@@ -549,7 +625,7 @@
         ],
         compiler_params=params(),
         cost_estimate=attention_cost(heads, tokens, 2),
-    )(slots, qt, kn, vt)
+    )(slots, qt, kt, kn, vt)
 
 
 def attention_cost(heads, tokens, passes):
@@ -1223,7 +1299,7 @@
     unit_all, mlp_full, w_pair, qt, kt, vt, kn, vn = gather_rows(
         parts, groups, heads, inputs[0], w_qkv, gain_rows, w_out, w_up, w_down, factor_two
     )
-    lse, mixed = attention_forward(slots, qt, kn, vt, parts)
+    lse, mixed = attention_forward(slots, qt, kt, kn, vt, parts)
     kept = (qt, kt, kn, vn, lse)
     output, dmid, dmixed, gain_two_grad, *chunks = middle(
         parts,

time: 463 us -> 438 us (0.946)
  Pallas kernels: 426 us -> 403 us
    pallas_call x1, Pallas kernels: 36.2 us -> 24.4 us  [attention_forward(): pl.pallas_call(functools.partial(forward_kernel, heads), name='attention_...]
    pallas_call x1, Pallas kernels: 121 us -> 110 us  [gather_rows(): pl.pallas_call(functools.partial(gather_kernel, parts, groups, heads), na...]
  transfers between devices with their start and end apart: 5 -> 5, of which waited for: 1 -> 1; matrix products, arithmetic and copies ran while one was open for 1% -> 1% of each run, Pallas kernels for 18% -> 19%
where the time goes in v6:
time: 438 us; the launch traced here: 437 us
  Pallas kernels  403 us (92%)
  other arithmetic  14.5 us (3%)
  local copies, waits for them, and re-layouts  8.16 us (2%)
  starting transfers between devices  6.22 us (1%)
    pallas_call x1, Pallas kernels, reduce_gradients(): pl.pallas_call(functools.partial(reduce_kernel, parts, groups), name='red...  125 us
    pallas_call x1, Pallas kernels, gather_rows(): pl.pallas_call(functools.partial(gather_kernel, parts, groups, heads), na...  110 us
    pallas_call x1, Pallas kernels, middle(): pl.pallas_call(functools.partial(middle_kernel, parts, groups), name='mid...  62.6 us
    pallas_call x1, Pallas kernels, attention_backward(): pl.pallas_call(functools.partial(backward_kernel, heads), name='attention...  56.3 us
    pallas_call x1, Pallas kernels, update(): pl.pallas_call(functools.partial(update_kernel, rates), name='update_weig...  25.8 us
    pallas_call x1, Pallas kernels, attention_forward(): pl.pallas_call(functools.partial(forward_kernel, heads), name='attention_...  24.4 us
  transfers between devices with their start and end apart: 5, of which 1 were waited for; matrix products, arithmetic and copies ran while one was open for 1% of the time, Pallas kernels for 19%

profile of v6, /device:TPU:0, one launch (start us, length us, event | category | flops | bytes accessed | tf_op | source)
XLA Modules:
  0.0 436.7 jit_solution(11970097401905932182)
XLA Ops:
  0.7 0.8 fusion.13
  1.4 0.7 fusion.14
  2.1 1.3 select_reduce_fusion.slot_ref
  3.4 0.1 dynamic_slice.12
  3.5 0.8 broadcast_in_dim.42.gain_ref
  4.3 0.7 copy.47.factor_ref
  5.0 0.6 broadcast_in_dim.38.gain_ref
  5.6 109.8 %gather_rows.1 = (bf16[8,512,1280]{2,1,0:T(8,128)(2,1)}, bf16[3,4,2,160,1280]{4,3,2,1,0:T(8,128)(2,1)}, bf16[2,480,1280]{2,1,0:T(8,128)(2,1)}, bf16[2,128,4096]{...) custom-call(bf16[512,1280]{1,0:T(8,128)(2,1)} %bitcast.24, ...), custom_call_target="tpu_custom_call" | custom-call | tf_op jit(solution)/shard_map/gather_rows/pallas_call | solution.py:324
  115.4 24.4 %attention_forward.1 = (f32[2,1,4096]{2,1,0:T(1,128)}, bf16[8,160,512]{2,1,0:T(8,128)(2,1)}) custom-call(s32[16]{0:T(128)} %select_reduce_fusion.slot_ref, bf16[2,128,4096]{2,1,0:T(8,128)(2,1)} %get-tuple-element.64.qt_ref, bf16[2,80,4096]{2,1,0:T(8,128)(2,1)} %get-tuple-element.65.kt_ref, bf16[2,4096,128]{2,1,0:T(8,128)(2,1)} %get-tuple-element.66.kn_ref, ...), custom_call_target="tpu_custom_call" | custom-call | flops 17179869184 | bytes 5242880 | tf_op jit(solution)/shard_map/attention_forward/pallas_call | solution.py:613
  139.8 62.6 %middle.1 = (bf16[512,1280]{1,0:T(8,128)(2,1)}, f32[512,1280]{1,0:T(8,128)}, bf16[8,160,512]{2,1,0:T(8,128)(2,1)}, f32[1,1280]{1,0:T(1,128)}, bf16[3,160,1280]{2...) custom-call(bf16[8,160,512]{2,1,0:T(8,128)(2,1)} %get-tuple-element., ...), custom_call_target="tpu_custom_call" | custom-call | tf_op jit(solution)/shard_map/middle/pallas_call | solution.py:841
  202.4 2.5 collective-permute-start.2
  204.9 1.0 collective-permute-start
  205.9 56.3 %attention_backward.1 = (bf16[8,480,512]{2,1,0:T(8,128)(2,1)}, f32[2,80,128]{2,1,0:T(8,128)}, bf16[1280,480]{1,0:T(8,128)(2,1)}) custom-call(s32[16]{0:T(128)} %select_reduce_fusion.slot_ref, bf16[2,128,4096]{2,1,0:T(8,128)(2,1)} %get-tuple-element.64.qt_ref, bf16[2,80,4096]{2,1,0:T(8,128)(2,1)} %get-tuple-element.65.kt_ref, ...), custom_call_target="tpu_custom_call" | custom-call | flops 42949672960 | bytes 5242880 | tf_op jit(solution)/shard_map/attention_backward/pallas_call | solution.py:641
  262.3 1.1 reduce_sum.47
  263.5 0.6 fusion.10.small_ref
  264.1 1.5 dynamic-slice_convert_fusion.2
  265.6 0.9 pad_maximum_fusion.wc_ref
  266.5 2.3 add_convert_fusion
  268.8 1.1 copy.54
  270.0 124.6 %reduce_gradients.1 = (bf16[512,1280]{1,0:T(8,128)(2,1)}, bf16[512,1280]{1,0:T(8,128)(2,1)}, f32[512,1280]{1,0:T(8,128)}, bf16[8,320,480]{2,1,0:T(8,128)(2,1)}, ...) custom-call(bf16[4,2,480,512]{3,2,1,0:T(8,128)(2,1)} %bitcast.29, ...), custom_call_target="tpu_custom_call" | custom-call | tf_op jit(solution)/shard_map/reduce_gradients/pallas_call | solution.py:1146
  394.5 1.4 collective-permute-start.4
  395.9 1.3 collective-permute-start.3
  397.2 0.3 fusion.7
  397.6 0.8 copy.55
  398.4 0.1 reshape.81
  398.4 25.8 %update_weights.1 = (f32[320,3840]{1,0:T(8,128)}, f32[320,3840]{1,0:T(8,128)}, f32[320,3840]{1,0:T(8,128)}, bf16[320,3840]{1,0:T(8,128)(2,1)}, f32[320,1280]{1,0...) custom-call(bf16[8,320,480]{2,1,0:T(8,128)(2,1)} %get-tuple-element., ...), custom_call_target="tpu_custom_call" | custom-call | flops 68812800 | bytes 68812800 | tf_op jit(solution)/shard_map/update_weights/pallas_call | solution.py:1236
  424.3 0.6 multiply_subtract_fusion
  424.9 3.5 collective-permute-done.3
  428.4 3.1 fusion.2
  431.5 0.6 copy-done.2
  432.2 3.5 fusion.8
  435.7 1.1 copy.57
  (29 shorter events, 0.1 us)
Async XLA Ops:
  202.4 64.1 %collective-permute-start.2 = (bf16[3,160,1280]{2,1,0:T(8,128)(2,1)}, bf16[3,160,1280]{2,1,0:T(8,128)(2,1)S(1)}, u32[]{:S(2)}, u32[]{:S(2)}) collective-permute-start(bf16[3,160,1280]{2,1,0:T(8,128)(2,1)} %get-tuple-element.82), channel_id=1, source_target_pairs={{0,3},{1,2},{2,1},{3,0},{4,7},{5,6},{6,5},{7,4},{8,11},{9,10},{10,... | collective-permute-start | bytes 3686408 | tf_op jit(solution)/shard_map/ppermute | solution.py:1316
  204.9 61.6 %collective-permute-start.1 = (bf16[3,160,1280]{2,1,0:T(8,128)(2,1)}, bf16[3,160,1280]{2,1,0:T(8,128)(2,1)}, u32[]{:S(2)}, u32[]{:S(2)}) collective-permute-start(bf16[3,160,1280]{2,1,0:T(8,128)(2,1)} %get-tuple-element.81), channel_id=1, source_target_pairs={{0,2},{1,3},{2,0},{3,1},{4,6},{5,7},{6,4},{7,5},{8,10},{9,11},{10,... | collective-permute-start | bytes 3686408 | tf_op jit(solution)/shard_map/ppermute | solution.py:1316
  204.9 61.6 %collective-permute-start = (bf16[3,160,1280]{2,1,0:T(8,128)(2,1)}, bf16[3,160,1280]{2,1,0:T(8,128)(2,1)}, u32[]{:S(2)}, u32[]{:S(2)}) collective-permute-start(bf16[3,160,1280]{2,1,0:T(8,128)(2,1)} %get-tuple-element.80), channel_id=1, source_target_pairs={{0,1},{1,0},{2,3},{3,2},{4,5},{5,4},{6,7},{7,6},{8,9},{9,8},{10,11... | collective-permute-start | bytes 3686408 | tf_op jit(solution)/shard_map/ppermute | solution.py:1316
  205.9 57.4 %copy-start.8 = (f32[1,1280]{1,0:T(1,128)S(1)}, f32[1,1280]{1,0:T(1,128)}, u32[]{:S(2)}) copy-start(f32[1,1280]{1,0:T(1,128)} %get-tuple-element.83) | copy-start | bytes 15364
  205.9 57.5 %copy-start.5 = (f32[2640]{0:T(1024)S(1)}, f32[2640]{0:T(1024)}, u32[]{:S(2)}) copy-start(f32[2640]{0:T(1024)} %param.33) | copy-start | bytes 31684
  262.3 4.3 copy-start.4
  270.0 127.3 %copy-start = (bf16[1,512,1280]{2,1,0:T(8,128)(2,1)S(1)}, bf16[1,512,1280]{2,1,0:T(8,128)(2,1)}, u32[]{:S(2)}) copy-start(bf16[1,512,1280]{2,1,0:T(8,128)(2,1)} %param.18) | copy-start | bytes 3932164
  394.5 30.4 %collective-permute-start.4 = (bf16[512,1280]{1,0:T(8,128)(2,1)}, bf16[512,1280]{1,0:T(8,128)(2,1)S(1)}, u32[]{:S(2)}, u32[]{:S(2)}) collective-permute-start(bf16[512,1280]{1,0:T(8,128)(2,1)} %get-tuple-element.87), channel_id=1, source_target_pairs={{0,8},{4,12},{8,16},{12,20},{16,24},{20,28},{1,9},{5,13},{9,17},{1... | collective-permute-start | bytes 3932168 | tf_op jit(solution)/shard_map/ppermute | solution.py:1343
  395.9 32.5 %collective-permute-start.3 = (bf16[512,1280]{1,0:T(8,128)(2,1)}, bf16[512,1280]{1,0:T(8,128)(2,1)}, u32[]{:S(2)}, u32[]{:S(2)}) collective-permute-start(bf16[512,1280]{1,0:T(8,128)(2,1)} %get-tuple-element.86), channel_id=1, source_target_pairs={{8,0},{12,4},{16,8},{20,12},{24,16},{28,20},{9,1},{13,5},{17,9},{2... | collective-permute-start | bytes 3932168 | tf_op jit(solution)/shard_map/ppermute | solution.py:1342
  398.4 25.8 %copy-start.6 = (f32[2640]{0:T(1024)S(1)}, f32[2640]{0:T(1024)}, u32[]{:S(2)}) copy-start(f32[2640]{0:T(1024)} %param.34) | copy-start | bytes 31684
  398.4 25.8 %copy-start.7 = (f32[2640]{0:T(1024)S(1)}, f32[2640]{0:T(1024)}, u32[]{:S(2)}) copy-start(f32[2640]{0:T(1024)} %param.35) | copy-start | bytes 31684
  428.4 3.1 copy-start.1
  428.4 3.7 copy-start.2
  432.2 3.5 copy-start.3

commit v7 on v6

--- a/solution.py
+++ b/solution.py
@@ -117,6 +117,7 @@
     vt_ref,
     kn_ref,
     vn_ref,
+    wcol_ref,
     rows_ref,
     wstage_ref,
     mstage_ref,
@@ -214,6 +215,7 @@
     for part in range(3):
         turned = pltpu.roll(wstage_ref[:, part * D : (part + 1) * D], shift, 1)
         gained_ref[part] = (turned[:, :width] * gain_ref[...]).astype(bf16)
+        wcol_ref[:, part * width : (part + 1) * width] = turned[:, :width].astype(bf16)
     for peer in group_peers:
         w_copy(peer, group).start()
     for index in range(3):
@@ -333,9 +335,10 @@
             jax.ShapeDtypeStruct((heads, HD + EXTRA, tokens), bf16),
             jax.ShapeDtypeStruct((heads, tokens, PAD), bf16),
             jax.ShapeDtypeStruct((heads, tokens, PAD), bf16),
+            jax.ShapeDtypeStruct((held, 3 * heads * HD), bf16),
         ],
         in_specs=in_vmem(1) + [anywhere] + in_vmem(1) + [anywhere] * 3 + in_vmem(1),
-        out_specs=[anywhere] * 2 + in_vmem(6),
+        out_specs=[anywhere] * 2 + in_vmem(7),
         scratch_shapes=[
             pltpu.VMEM((parts, rows_dev, D), bf16),
             pltpu.VMEM((held, 3 * D), f32),
@@ -477,6 +480,7 @@
     dv_ref,
     held_ref,
     total_ref,
+    scale_ref,
     load_sem,
 ):
     parts = units_ref.shape[0]
@@ -512,7 +516,7 @@
     lax.fori_loop(0, num_blocks, prepare, 0)
     dk_ref[...] = jnp.zeros(dk_ref.shape, f32)
     dv_ref[...] = jnp.zeros(dv_ref.shape, f32)
-    dscale_ref[...] = jnp.zeros(dscale_ref.shape, f32)
+    scale_ref[...] = jnp.zeros(scale_ref.shape, f32)
 
     def query_tile(tile, carry):
         here = tile_at(tile)
@@ -561,7 +565,7 @@
             dq = dq_ref[head]
             product = dq * qa_ref[head, :HD, here].astype(f32)
             for lane in range(TILE // PAD):
-                dscale_ref[head] += product[:, lane * PAD : (lane + 1) * PAD]
+                scale_ref[head] += product[:, lane * PAD : (lane + 1) * PAD]
             scaled = (dq * (factor_ref[...] * LN2)).astype(bf16)
             for part in range(TILE // BLOCK):
                 slot = slot_ref[tile * (TILE // BLOCK) + part]
@@ -598,6 +602,9 @@
 
     lax.fori_loop(0, parts, project, 0)
     u_ref[...] = total_ref[...].T.astype(bf16)
+    sums = functools.reduce(jnp.add, [scale_ref[head] for head in range(heads)])
+    sums = jnp.concatenate([sums, jnp.zeros((PAD - HD, PAD), f32)], axis=0).T
+    dscale_ref[...] = jnp.sum(sums, axis=0, keepdims=True)
 
 
 def in_vmem(count):
@@ -643,7 +650,7 @@
         name="attention_backward",
         out_shape=[
             jax.ShapeDtypeStruct((mixed.shape[0], 3 * heads * HD, mixed.shape[2]), bf16),
-            jax.ShapeDtypeStruct((heads, HD, PAD), f32),
+            jax.ShapeDtypeStruct((1, PAD), f32),
             jax.ShapeDtypeStruct((D, 3 * heads * HD), bf16),
         ],
         in_specs=[pl.BlockSpec(memory_space=pltpu.SMEM)]
@@ -658,6 +665,7 @@
             pltpu.VMEM((heads, HD, tokens), f32),
             pltpu.VMEM((2,) + units.shape[1:], bf16),
             pltpu.VMEM((3 * heads * HD, D), f32),
+            pltpu.VMEM((heads, HD, PAD), f32),
             pltpu.SemaphoreType.DMA((2,)),
         ],
         compiler_params=params(),
@@ -878,31 +886,35 @@
     wt_ref,
     u_ref,
     wc_ref,
-    mlp_ref,
     small_ref,
-    down_ref,
-    up_ref,
-    own_ref,
-    ugather_ref,
-    mgather_ref,
-    sgather_ref,
-    pair_ref,
-    sum_ref,
-    urecv_ref,
-    mrecv_ref,
-    part_ref,
-    column_ref,
-    smine_ref,
-    srecv_ref,
-    pair_sem,
-    sum_sem,
-    u_sem,
-    m_sem,
-    line_sem,
-    side_sem,
-    small_sem,
-    cross_sem,
+    *refs,
 ):
+    chunk_refs = refs[:groups]
+    (
+        down_ref,
+        up_ref,
+        own_ref,
+        ugather_ref,
+        mgather_ref,
+        sgather_ref,
+        pair_ref,
+        sum_ref,
+        urecv_ref,
+        mlp_ref,
+        mrecv_ref,
+        part_ref,
+        column_ref,
+        smine_ref,
+        srecv_ref,
+        pair_sem,
+        sum_sem,
+        u_sem,
+        m_sem,
+        line_sem,
+        side_sem,
+        small_sem,
+        cross_sem,
+    ) = refs[groups:]
     chips = parts // 2
     here = lax.axis_index("ctx")
     group = lax.axis_index("fsdp")
@@ -957,6 +969,11 @@
         pair_copy(index).start()
     for peer in group_peers:
         u_copy(peer, group).start()
+    share = mlp_ref.shape[2]
+    for matrix in range(3):
+        total = functools.reduce(jnp.add, [ref[matrix].astype(f32) for ref in chunk_refs])
+        for index in range(chips):
+            mlp_ref[index, matrix] = total[index * share : (index + 1) * share].astype(bf16)
     for peer in chip_peers:
         m_copy(peer, chip).start()
     for index in range(chips):
@@ -964,23 +981,17 @@
 
     rows_half = own_ref.shape[0] // 2
 
-    def partial(target):
-        def half(index, carry):
-            rows = pl.ds(pl.multiple_of(index * rows_half, rows_half), rows_half)
-            part_ref[rows, :] = dot(dq_ref[target, core, :, rows], wt_ref[core], (0, 0)) + dot(
-                pair_ref[target, :, rows], wt_ref[1 - core], (0, 0)
-            )
-            return carry
-
-        lax.fori_loop(0, 2, half, 0)
-
-    def sum_copy(way, target):
-        return send(
-            sum_ref.at[way, target],
-            sum_ref.at[way, target],
-            (sum_sem.at[0, way, target], sum_sem.at[1, way, target]),
-            {"ctx": here + (2 if way else -2)},
+    def partial(target, index):
+        rows = pl.ds(pl.multiple_of(index * rows_half, rows_half), rows_half)
+        part_ref[rows, :] = dot(dq_ref[target, core, :, rows], wt_ref[core], (0, 0)) + dot(
+            pair_ref[target, :, rows], wt_ref[1 - core], (0, 0)
         )
+        return rows
+
+    def sum_copy(way, target, index):
+        ref = sum_ref.at[way, target, pl.ds(index * rows_half, rows_half)]
+        sems = (sum_sem.at[0, way, target, index], sum_sem.at[1, way, target, index])
+        return send(ref, ref, sems, {"ctx": here + (2 if way else -2)})
 
     def reduce_step(step):
         last = step == chips - 2
@@ -991,23 +1002,27 @@
 
             @pl.when(active)
             def _():
-                partial(target)
-
-                @pl.when(first)
-                def _():
-                    sum_ref[way, target] = part_ref[...].astype(bf16)
-
-                @pl.when(jnp.logical_not(first))
-                def _():
-                    sum_copy(way, target).wait_recv()
-                    sum_ref[way, target] = (
-                        part_ref[...] + sum_ref[way, target].astype(f32)
-                    ).astype(bf16)
-
-                if last:
-                    out_ref[...] = sum_ref[way, target]
-                else:
-                    sum_copy(way, target).start()
+                def half(index, carry):
+                    rows = partial(target, index)
+
+                    @pl.when(first)
+                    def _():
+                        sum_ref[way, target, rows] = part_ref[rows, :].astype(bf16)
+
+                    @pl.when(jnp.logical_not(first))
+                    def _():
+                        sum_copy(way, target, index).wait_recv()
+                        sum_ref[way, target, rows] = (
+                            part_ref[rows, :] + sum_ref[way, target, rows].astype(f32)
+                        ).astype(bf16)
+
+                    if last:
+                        out_ref[rows, :] = sum_ref[way, target, rows]
+                    else:
+                        sum_copy(way, target, index).start()
+                    return carry
+
+                lax.fori_loop(0, 2, half, 0)
 
             if last:
 
@@ -1092,12 +1107,14 @@
     line_sends(1, 0, lambda copy: copy.start())
 
     for step in range(1, chips):
-        if step <= chips - 2:
+        if step == 1:
             reduce_step(step)
         for which in range(2):
             line_receive(which, step - 1)
             if step <= chips - 2:
                 line_sends(which, step, lambda copy: copy.start())
+        if 1 < step <= chips - 2:
+            reduce_step(step)
         if step == 1:
             small = smine_ref[...]
             for peer in ctx_peers:
@@ -1107,8 +1124,9 @@
             for peer in group_peers:
                 cross_copy(peer, group).start()
 
-    partial(chip)
-    own_ref[...] = part_ref[...]
+    for index in range(2):
+        rows = partial(chip, index)
+        own_ref[rows, :] = part_ref[rows, :]
 
     for which in range(2):
         for piece in range(chips):
@@ -1130,15 +1148,18 @@
 
         @pl.when(step >= chips - 1 - chip)
         def _():
-            sum_copy(0, step - (chips - 1) + chip).wait_send()
+            for index in range(2):
+                sum_copy(0, step - (chips - 1) + chip, index).wait_send()
 
         @pl.when(step >= chip)
         def _():
-            sum_copy(1, chips - 1 - step + chip).wait_send()
-
-
-def reduce_gradients(parts, groups, dqkv, w_pair, u_parts, w_columns, mlp, small):
+            for index in range(2):
+                sum_copy(1, chips - 1 - step + chip, index).wait_send()
+
+
+def reduce_gradients(parts, groups, dqkv, w_pair, u_parts, w_columns, small, chunks):
     chips = parts // 2
+    mlp_shape = (chips, 3, chunks[0].shape[1] // chips, D)
     rows_dev = dqkv.shape[3]
     rows, width = w_columns.shape
     lanes = -(-rows // PAD) * PAD
@@ -1151,22 +1172,23 @@
             jax.ShapeDtypeStruct((rows_dev, D), bf16),
             jax.ShapeDtypeStruct((rows_dev, D), f32),
             jax.ShapeDtypeStruct((parts, rows, width), bf16),
-            jax.ShapeDtypeStruct((parts,) + mlp.shape[1:], bf16),
+            jax.ShapeDtypeStruct((parts,) + mlp_shape[1:], bf16),
             jax.ShapeDtypeStruct((groups,) + small.shape, f32),
         ],
-        in_specs=in_vmem(6),
+        in_specs=in_vmem(5 + groups),
         out_specs=in_vmem(6),
         scratch_shapes=[
             pltpu.VMEM((chips,) + dqkv.shape[2:], bf16),
             pltpu.VMEM((2, chips, rows_dev, D), bf16),
             pltpu.VMEM(u_parts.shape, bf16),
-            pltpu.VMEM(mlp.shape, bf16),
+            pltpu.VMEM(mlp_shape, bf16),
+            pltpu.VMEM(mlp_shape, bf16),
             pltpu.VMEM((rows_dev, D), f32),
             pltpu.VMEM((lanes, PAD), f32),
             pltpu.VMEM(small.shape, f32),
             pltpu.VMEM((parts,) + small.shape, f32),
             dma((2, chips)),
-            dma((2, 2, chips)),
+            dma((2, 2, chips, 2)),
             dma((2, groups)),
             dma((2, chips)),
             dma((2, 2, 2, chips)),
@@ -1177,7 +1199,7 @@
         compiler_params=pltpu.CompilerParams(
             vmem_limit_bytes=60 * 1024 * 1024, collective_id=1, has_side_effects=True
         ),
-    )(dqkv, w_pair, u_parts, w_columns, mlp, small)
+    )(dqkv, w_pair, u_parts, w_columns, small, *chunks)
 
 
 def update_kernel(rates, qkv_ref, gain_ref, mlp_ref, *refs):
@@ -1243,6 +1265,31 @@
         compiler_params=params(),
         cost_estimate=pl.CostEstimate(flops=moved, bytes_accessed=moved, transcendentals=0),
     )(qkv, gain, mlp, *arrays)
+
+
+def finish_kernel(x_ref, dmid_ref, own_ref, down_ref, up_ref, out_ref):
+    rows = x_ref[...].astype(f32)
+    scale = rms_scale(rows)
+    unit = rows * scale
+    dunit = own_ref[...] + down_ref[...].astype(f32) + up_ref[...].astype(f32)
+    grad = dmid_ref[...] + scale * (
+        dunit - unit * jnp.mean(dunit * unit, axis=-1, keepdims=True)
+    )
+    out_ref[...] = grad.astype(bf16)
+
+
+def finish(*arrays):
+    rows = arrays[0].shape[0]
+    spec = pl.BlockSpec((PAD, D), lambda i: (i, 0))
+    return pl.pallas_call(
+        finish_kernel,
+        name="finish",
+        grid=(rows // PAD,),
+        in_specs=[spec] * len(arrays),
+        out_specs=spec,
+        out_shape=jax.ShapeDtypeStruct((rows, D), bf16),
+        compiler_params=params(),
+    )(*arrays)
 
 
 def body(
@@ -1280,23 +1327,10 @@
     group = lax.axis_index("fsdp")
     rows = w_qkv.shape[0]
 
-    def head_columns(owner):
-        return jnp.concatenate(
-            [
-                lax.dynamic_slice_in_dim(w_qkv, part * D + owner * width, width, 1)
-                for part in range(3)
-            ],
-            axis=1,
-        )
-
     gain_rows = lax.dynamic_slice_in_dim(gain_one, group * rows, rows, 0)[:, None]
-    w_columns = head_columns(here).astype(bf16)
-    layer_in = inputs[0].astype(f32)
-    scale_one = rms_scale(layer_in)
-    unit_one = layer_in * scale_one
     factor = scale_base / math.sqrt(HD) * jax.nn.softplus(query_scale)
     factor_two = (factor * LOG2E)[:, None]
-    unit_all, mlp_full, w_pair, qt, kt, vt, kn, vn = gather_rows(
+    unit_all, mlp_full, w_pair, qt, kt, vt, kn, vn, w_columns = gather_rows(
         parts, groups, heads, inputs[0], w_qkv, gain_rows, w_out, w_up, w_down, factor_two
     )
     lse, mixed = attention_forward(slots, qt, kt, kn, vt, parts)
@@ -1310,17 +1344,13 @@
         mlp_full.reshape(3, D, D),
         gain_two[None],
     )
-    mlp_sum = chunks[0].astype(f32)
     for step in range(1, groups):
         swap = [(i, i ^ step) for i in range(groups)]
-        mlp_sum = mlp_sum + lax.ppermute(chunks[step], "fsdp", swap).astype(f32)
-    mlp_part = (
-        mlp_sum.astype(bf16).reshape(3, parts // 2, rows // parts, D).transpose(1, 0, 2, 3)
-    )
+        chunks[step] = lax.ppermute(chunks[step], "fsdp", swap)
     dqkv, dscale, u_parts = attention_backward(slots, kept, mixed, dmixed, factor_two, unit_all)
     u_parts = u_parts.reshape(groups, rows, 3 * width)
     scale_grad = (
-        jnp.sum(dscale, axis=(0, 2))
+        dscale[0, :HD]
         / factor_two[:, 0]
         * (scale_base / math.sqrt(HD))
         * jax.nn.sigmoid(query_scale)
@@ -1336,8 +1366,8 @@
         w_pair,
         u_parts,
         w_columns,
-        mlp_part,
         small,
+        chunks,
     )
     got_down = lax.ppermute(send_down, "ctx", [(i, i - 2) for i in range(2, parts)])
     got_up = lax.ppermute(send_up, "ctx", [(i, i + 2) for i in range(parts - 2)])
@@ -1368,13 +1398,10 @@
     rest = jnp.sum(flat[:, lanes : lanes + D + HD], axis=0)
     small_total = jnp.concatenate([flat[:, :rows].reshape(D), rest])
     small_set = adamw(small_params, small_m, small_v, small_total, small_rate, 0.0)
-    dunit_one = own_part + got_down.astype(f32) + got_up.astype(f32)
-    input_grad = dmid + scale_one * (
-        dunit_one - unit_one * jnp.mean(dunit_one * unit_one, axis=-1, keepdims=True)
-    )
+    input_grad = finish(inputs[0], dmid, own_part, got_down, got_up)
     return (
         output[None],
-        input_grad.astype(bf16)[None],
+        input_grad[None],
         *updated,
         *small_set,
     )

time: 438 us -> 420 us (0.959)
  other arithmetic: 14.5 us -> 3.95 us
  Pallas kernels: 403 us -> 395 us
    pallas_call x1, Pallas kernels: 125 us -> 111 us  [reduce_gradients(): pl.pallas_call(functools.partial(reduce_kernel, parts, groups), name='red...]
    pallas_call x0 -> x1, Pallas kernels: none -> 5.58 us  [finish(): pl.pallas_call(finish_kernel, name='finish', grid=(rows // PAD,), in_spec...]
    reduce_sum x3 -> x0, other arithmetic: 4.49 us -> none  [the longest x1 3.07 us: body(): jnp.mean(dunit_one * unit_one, axis=-1, keepdims=True)]
  transfers between devices with their start and end apart: 5 -> 5, of which waited for: 1 -> 1; matrix products, arithmetic and copies ran while one was open for 1% -> 1% of each run, Pallas kernels for 19% -> 20%
where the time goes in v7:
time: 420 us; the launch traced here: 419 us
  Pallas kernels  395 us (94%)
  starting transfers between devices  9.57 us (2%)
  local copies, waits for them, and re-layouts  8.74 us (2%)
    pallas_call x1, Pallas kernels, reduce_gradients(): pl.pallas_call(functools.partial(reduce_kernel, parts, groups), name='red...  111 us
    pallas_call x1, Pallas kernels, gather_rows(): pl.pallas_call(functools.partial(gather_kernel, parts, groups, heads), na...  110 us
    pallas_call x1, Pallas kernels, middle(): pl.pallas_call(functools.partial(middle_kernel, parts, groups), name='mid...  62.6 us
    pallas_call x1, Pallas kernels, attention_backward(): pl.pallas_call(functools.partial(backward_kernel, heads), name='attention...  56.4 us
    pallas_call x1, Pallas kernels, update(): pl.pallas_call(functools.partial(update_kernel, rates), name='update_weig...  25.5 us
    pallas_call x1, Pallas kernels, attention_forward(): pl.pallas_call(functools.partial(forward_kernel, heads), name='attention_...  24.4 us
  transfers between devices with their start and end apart: 5, of which 1 were waited for; matrix products, arithmetic and copies ran while one was open for 1% of the time, Pallas kernels for 20%

profile of v7, /device:TPU:0, one launch (start us, length us, event | category | flops | bytes accessed | tf_op | source)
XLA Modules:
  0.0 419.1 jit_solution(6695780200174241684)
XLA Ops:
  0.7 0.8 fusion.4
  1.4 0.7 fusion.5
  2.1 1.3 select_reduce_fusion.slot_ref
  3.4 0.1 dynamic_slice.3
  3.5 0.8 broadcast_in_dim.40.gain_ref
  4.3 0.7 copy.46.factor_ref
  5.0 0.6 broadcast_in_dim.36.gain_ref
  5.6 109.8 %gather_rows.1 = (bf16[8,512,1280]{2,1,0:T(8,128)(2,1)}, bf16[3,4,2,160,1280]{4,3,2,1,0:T(8,128)(2,1)}, bf16[2,480,1280]{2,1,0:T(8,128)(2,1)}, bf16[2,128,4096]{...) custom-call(bf16[512,1280]{1,0:T(8,128)(2,1)} %bitcast.20, ...), custom_call_target="tpu_custom_call" | custom-call | tf_op jit(solution)/shard_map/gather_rows/pallas_call | solution.py:326
  115.4 24.4 %attention_forward.1 = (f32[2,1,4096]{2,1,0:T(1,128)}, bf16[8,160,512]{2,1,0:T(8,128)(2,1)}) custom-call(s32[16]{0:T(128)} %select_reduce_fusion.slot_ref, bf16[2,128,4096]{2,1,0:T(8,128)(2,1)} %get-tuple-element.65.qt_ref, bf16[2,80,4096]{2,1,0:T(8,128)(2,1)} %get-tuple-element.66.kt_ref, bf16[2,4096,128]{2,1,0:T(8,128)(2,1)} %get-tuple-element.67.kn_ref, ...), custom_call_target="tpu_custom_call" | custom-call | flops 17179869184 | bytes 5242880 | tf_op jit(solution)/shard_map/attention_forward/pallas_call | solution.py:620
  139.8 62.6 %middle.1 = (bf16[512,1280]{1,0:T(8,128)(2,1)}, f32[512,1280]{1,0:T(8,128)}, bf16[8,160,512]{2,1,0:T(8,128)(2,1)}, f32[1,1280]{1,0:T(1,128)}, bf16[3,160,1280]{2...) custom-call(bf16[8,160,512]{2,1,0:T(8,128)(2,1)} %get-tuple-element., ...), custom_call_target="tpu_custom_call" | custom-call | tf_op jit(solution)/shard_map/middle/pallas_call | solution.py:849
  202.5 0.9 collective-permute-start
  203.4 2.2 collective-permute-start.1
  205.6 0.5 collective-permute-start.2
  206.1 56.4 %attention_backward.1 = (bf16[8,480,512]{2,1,0:T(8,128)(2,1)}, f32[1,128]{1,0:T(1,128)}, bf16[1280,480]{1,0:T(8,128)(2,1)}) custom-call(s32[16]{0:T(128)} %select_reduce_fusion.slot_ref, bf16[2,128,4096]{2,1,0:T(8,128)(2,1)} %get-tuple-element.65.qt_ref, bf16[2,80,4096]{2,1,0:T(8,128)(2,1)} %get-tuple-element.66.kt_ref, ...), custom_call_target="tpu_custom_call" | custom-call | flops 42949672960 | bytes 5242880 | tf_op jit(solution)/shard_map/attention_backward/pallas_call | solution.py:648
  262.6 0.7 divide_multiply_fusion
  263.3 0.6 fusion.1.small_ref
  263.9 0.0 copy-start.3
  263.9 0.0 collective-permute-done.2.refs_3_
  263.9 1.0 copy-done.2
  264.9 0.4 copy-done.3
  265.3 110.6 %reduce_gradients.1 = (bf16[512,1280]{1,0:T(8,128)(2,1)}, bf16[512,1280]{1,0:T(8,128)(2,1)}, f32[512,1280]{1,0:T(8,128)}, bf16[8,320,480]{2,1,0:T(8,128)(2,1)}, ...) custom-call(bf16[4,2,480,512]{3,2,1,0:T(8,128)(2,1)} %bitcast.24, ...), custom_call_target="tpu_custom_call" | custom-call | tf_op jit(solution)/shard_map/reduce_gradients/pallas_call | solution.py:1167
  375.9 1.3 collective-permute-start.3
  377.2 4.6 %collective-permute-start.4 = (bf16[512,1280]{1,0:T(8,128)(2,1)}, bf16[512,1280]{1,0:T(8,128)(2,1)S(1)}, u32[]{:S(2)}, u32[]{:S(2)}) collective-permute-start(bf16[512,1280]{1,0:T(8,128)(2,1)} %get-tuple-element.89), channel_id=1, source_target_pairs={{0,8},{4,12},{8,16},{12,20},{16,24},{20,28},{1,9},{5,13},{9,17},{1... | collective-permute-start | bytes 3932168 | tf_op jit(solution)/shard_map/ppermute | solution.py:1373
  381.9 0.8 copy.51
  382.7 0.1 reshape.65
  382.7 25.5 %update_weights.1 = (f32[320,3840]{1,0:T(8,128)}, f32[320,3840]{1,0:T(8,128)}, f32[320,3840]{1,0:T(8,128)}, bf16[320,3840]{1,0:T(8,128)(2,1)}, f32[320,1280]{1,0...) custom-call(bf16[8,320,480]{2,1,0:T(8,128)(2,1)} %get-tuple-element., ...), custom_call_target="tpu_custom_call" | custom-call | flops 68812800 | bytes 68812800 | tf_op jit(solution)/shard_map/update_weights/pallas_call | solution.py:1258
  408.3 0.6 multiply_subtract_fusion
  409.0 1.0 collective-permute-done.4.up_ref
  410.0 0.0 copy-done
  410.0 1.1 copy-done.1
  411.1 5.6 %finish.1 = bf16[512,1280]{1,0:T(8,128)(2,1)} custom-call(bf16[512,1280]{1,0:T(8,128)(2,1)} %bitcast.22, f32[512,1280]{1,0:T(8,128)} %get-tuple-element.72.dmid_ref, f32[512,1280]{1,0:T(8,128)} %get-tuple-element.87.own_ref, bf16[512,1280]{1,0:T(8,128)(2,1)} %copy-done, bf16[512,1280]{1,0:T(8,128)(2,1)} %copy-done.1), custom_call_target="tpu_custom_call" | custom-call | tf_op jit(solution)/shard_map/finish/pallas_call | solution.py:1284
  416.7 2.5 copy.53
  (18 shorter events, 0.1 us)
Async XLA Ops:
  202.5 61.5 %collective-permute-start = (bf16[3,160,1280]{2,1,0:T(8,128)(2,1)}, bf16[3,160,1280]{2,1,0:T(8,128)(2,1)S(1)}, u32[]{:S(2)}, u32[]{:S(2)}) collective-permute-start(bf16[3,160,1280]{2,1,0:T(8,128)(2,1)} %get-tuple-element.84), channel_id=1, source_target_pairs={{0,1},{1,0},{2,3},{3,2},{4,5},{5,4},{6,7},{7,6},{8,9},{9,8},{10,11... | collective-permute-start | bytes 3686408 | tf_op jit(solution)/shard_map/ppermute | solution.py:1349
  203.4 60.5 %collective-permute-start.1 = (bf16[3,160,1280]{2,1,0:T(8,128)(2,1)}, bf16[3,160,1280]{2,1,0:T(8,128)(2,1)S(1)}, u32[]{:S(2)}, u32[]{:S(2)}) collective-permute-start(bf16[3,160,1280]{2,1,0:T(8,128)(2,1)} %get-tuple-element.85), channel_id=1, source_target_pairs={{0,2},{1,3},{2,0},{3,1},{4,6},{5,7},{6,4},{7,5},{8,10},{9,11},{10,... | collective-permute-start | bytes 3686408 | tf_op jit(solution)/shard_map/ppermute | solution.py:1349
  205.6 58.4 %collective-permute-start.2 = (bf16[3,160,1280]{2,1,0:T(8,128)(2,1)}, bf16[3,160,1280]{2,1,0:T(8,128)(2,1)}, u32[]{:S(2)}, u32[]{:S(2)}) collective-permute-start(bf16[3,160,1280]{2,1,0:T(8,128)(2,1)} %get-tuple-element.86), channel_id=1, source_target_pairs={{0,3},{1,2},{2,1},{3,0},{4,7},{5,6},{6,5},{7,4},{8,11},{9,10},{10,... | collective-permute-start | bytes 3686408 | tf_op jit(solution)/shard_map/ppermute | solution.py:1349
  206.1 56.5 %copy-start.7 = (f32[1,1280]{1,0:T(1,128)S(1)}, f32[1,1280]{1,0:T(1,128)}, u32[]{:S(2)}) copy-start(f32[1,1280]{1,0:T(1,128)} %get-tuple-element.81) | copy-start | bytes 15364
  206.1 56.5 %copy-start.4 = (f32[2640]{0:T(1024)S(1)}, f32[2640]{0:T(1024)}, u32[]{:S(2)}) copy-start(f32[2640]{0:T(1024)} %param.33) | copy-start | bytes 31684
  263.9 1.0 copy-start.2
  263.9 1.4 copy-start.3
  375.9 33.0 %collective-permute-start.3 = (bf16[512,1280]{1,0:T(8,128)(2,1)}, bf16[512,1280]{1,0:T(8,128)(2,1)S(1)}, u32[]{:S(2)}, u32[]{:S(2)}) collective-permute-start(bf16[512,1280]{1,0:T(8,128)(2,1)} %get-tuple-element.88), channel_id=1, source_target_pairs={{8,0},{12,4},{16,8},{20,12},{24,16},{28,20},{9,1},{13,5},{17,9},{2... | collective-permute-start | bytes 3932168 | tf_op jit(solution)/shard_map/ppermute | solution.py:1372
  377.2 32.8 %collective-permute-start.4 = (bf16[512,1280]{1,0:T(8,128)(2,1)}, bf16[512,1280]{1,0:T(8,128)(2,1)S(1)}, u32[]{:S(2)}, u32[]{:S(2)}) collective-permute-start(bf16[512,1280]{1,0:T(8,128)(2,1)} %get-tuple-element.89), channel_id=1, source_target_pairs={{0,8},{4,12},{8,16},{12,20},{16,24},{20,28},{1,9},{5,13},{9,17},{1... | collective-permute-start | bytes 3932168 | tf_op jit(solution)/shard_map/ppermute | solution.py:1373
  382.7 25.6 %copy-start.5 = (f32[2640]{0:T(1024)S(1)}, f32[2640]{0:T(1024)}, u32[]{:S(2)}) copy-start(f32[2640]{0:T(1024)} %param.34) | copy-start | bytes 31684
  382.7 25.6 %copy-start.6 = (f32[2640]{0:T(1024)S(1)}, f32[2640]{0:T(1024)}, u32[]{:S(2)}) copy-start(f32[2640]{0:T(1024)} %param.35) | copy-start | bytes 31684
  409.0 1.1 copy-start
  410.0 1.1 copy-start.1

commit v8 on v7

--- a/solution.py
+++ b/solution.py
@@ -112,12 +112,17 @@
     unit_ref,
     full_ref,
     wpair_ref,
+    qt_out_ref,
+    kt_out_ref,
+    vt_out_ref,
+    kn_out_ref,
+    vn_out_ref,
+    wcol_ref,
     qt_ref,
     kt_ref,
     vt_ref,
     kn_ref,
     vn_ref,
-    wcol_ref,
     rows_ref,
     wstage_ref,
     mstage_ref,
@@ -134,6 +139,8 @@
     cross_sem,
     own_sem,
     stage_sem,
+    lanes_sem,
+    sides_sem,
 ):
     chips = parts // 2
     here = lax.axis_index("ctx")
@@ -162,14 +169,30 @@
             device_id=device,
         )
 
-    def line_copy(way, step, piece):
-        ref = rows_ref.at[2 * piece + core]
-        sems = (line_sem.at[0, way, step], line_sem.at[1, way, step])
+    halves = rows_ref.shape[1] // BLOCK
+
+    def line_copy(way, step, piece, part):
+        ref = rows_ref.at[2 * piece + core, block_at(part)]
+        sems = (line_sem.at[0, way, step, part], line_sem.at[1, way, step, part])
         return send(ref, ref, sems, {"ctx": here + (2 if way else -2)})
 
-    def side_copy(piece, lane):
-        ref = rows_ref.at[2 * piece + lane]
-        return send(ref, ref, (side_sem.at[0, piece], side_sem.at[1, piece]), {"ctx": other})
+    def side_copy(piece, lane, part):
+        ref = rows_ref.at[2 * piece + lane, block_at(part)]
+        sems = (side_sem.at[0, piece, part], side_sem.at[1, piece, part])
+        return send(ref, ref, sems, {"ctx": other})
+
+    def results(slot):
+        to = block_at(slot)
+        copies = [
+            pltpu.make_async_copy(ref.at[:, :, to], out.at[:, :, to], lanes_sem.at[index, slot])
+            for index, (ref, out) in enumerate(
+                ((qt_ref, qt_out_ref), (kt_ref, kt_out_ref), (vt_ref, vt_out_ref))
+            )
+        ]
+        return copies + [
+            pltpu.make_async_copy(ref.at[:, to], out.at[:, to], sides_sem.at[index, slot])
+            for index, (ref, out) in enumerate(((kn_ref, kn_out_ref), (vn_ref, vn_out_ref)))
+        ]
 
     def w_copy(peer, source):
         sems = (w_sem.at[0, peer], w_sem.at[1, source])
@@ -202,14 +225,15 @@
     rows = x_ref[...].astype(f32)
     rows_ref[here] = (rows * rms_scale(rows)).astype(bf16)
 
-    def forward(way, step, piece):
+    def forward(way, step, piece, part):
         @pl.when((chip < chips - 1) if way else (chip > 0))
         def _():
-            line_copy(way, step, piece).start()
-
-    for way in range(2):
-        forward(way, 0, chip)
-    side_copy(chip, core).start()
+            line_copy(way, step, piece, part).start()
+
+    for part in range(halves):
+        for way in range(2):
+            forward(way, 0, chip, part)
+        side_copy(chip, core, part).start()
     shift = lax.rem(D - here * width, D)
     stages[0].wait()
     for part in range(3):
@@ -238,38 +262,40 @@
     extra = jnp.where(extra_row < 3, 1.0, 0.0)
     spare = jnp.zeros((PAD - HD, BLOCK), bf16)
 
-    def project(piece):
-        def half(index, carry):
-            at = pl.ds(pl.multiple_of(index * BLOCK, BLOCK), BLOCK)
-            to = pl.ds(pl.multiple_of((piece * 2 + index) * BLOCK, BLOCK), BLOCK)
-            result = dot(wflip_ref[...], rows_ref[piece, at, :], (1, 1))
-            for head in range(heads):
-                query, key, value = (
-                    result[part * width + head * HD : part * width + (head + 1) * HD]
-                    for part in range(3)
-                )
-                qt_ref[head, :HD, to] = (query * factor_ref[...]).astype(bf16)
-                qt_ref[head, HD:, to] = spare
-                kt_ref[head, :, to] = key.astype(bf16)
-                vt_ref[head, :HD, to] = value.astype(bf16)
-                vt_ref[head, HD:, to] = jnp.ones((EXTRA, BLOCK), bf16)
-                kn_ref[head, to, :] = jnp.concatenate([key, extra], axis=0).T.astype(bf16)
-                vn_ref[head, to, :] = jnp.concatenate([value, extra], axis=0).T.astype(bf16)
-            return carry
-
-        lax.fori_loop(0, TILE // BLOCK, half, 0)
-
-    def visit(distance, carry):
+    def project(piece, part):
+        slot = piece * halves + part
+        to = block_at(slot)
+        result = dot(wflip_ref[...], rows_ref[piece, block_at(part), :], (1, 1))
+        for head in range(heads):
+            query, key, value = (
+                result[share * width + head * HD : share * width + (head + 1) * HD]
+                for share in range(3)
+            )
+            qt_ref[head, :HD, to] = (query * factor_ref[...]).astype(bf16)
+            qt_ref[head, HD:, to] = spare
+            kt_ref[head, :, to] = key.astype(bf16)
+            vt_ref[head, :HD, to] = value.astype(bf16)
+            vt_ref[head, HD:, to] = jnp.ones((EXTRA, BLOCK), bf16)
+            kn_ref[head, to, :] = jnp.concatenate([key, extra], axis=0).T.astype(bf16)
+            vn_ref[head, to, :] = jnp.concatenate([value, extra], axis=0).T.astype(bf16)
+        for copy in results(slot):
+            copy.start()
+
+    def visit(index, carry):
+        distance, part = index // halves, lax.rem(index, halves)
         for way in range(2):
             piece = chip - distance if way else chip + distance
             valid = (piece >= 0) if way else (piece <= chips - 1)
 
             @pl.when(valid & (distance > 0))
             def _():
-                line_copy(way, distance - 1, piece).wait_recv()
-                side_copy(piece, core).start()
-                forward(way, distance, piece)
-                keep_copy(2 * piece + core).start()
+                line_copy(way, distance - 1, piece, part).wait_recv()
+                side_copy(piece, core, part).start()
+                forward(way, distance, piece, part)
+
+                @pl.when(part == halves - 1)
+                def _():
+                    keep_copy(2 * piece + core).start()
 
         for way in range(2):
             piece = chip - distance if way else chip + distance
@@ -277,14 +303,17 @@
 
             @pl.when(valid)
             def _():
-                project(2 * piece + core)
-                side_copy(piece, 1 - core).wait_recv()
-                keep_copy(2 * piece + 1 - core).start()
-                project(2 * piece + 1 - core)
+                project(2 * piece + core, part)
+                side_copy(piece, 1 - core, part).wait_recv()
+                project(2 * piece + 1 - core, part)
+
+                @pl.when(part == halves - 1)
+                def _():
+                    keep_copy(2 * piece + 1 - core).start()
 
         return carry
 
-    lax.fori_loop(0, chips, visit, 0)
+    lax.fori_loop(0, chips * halves, visit, 0)
 
     for peer in group_peers:
         mlp_copy(group, peer).wait_recv()
@@ -301,19 +330,27 @@
     def drain(piece, carry):
         keep_copy(2 * piece).wait()
         keep_copy(2 * piece + 1).wait()
-        side_copy(piece, core).wait_send()
-
-        @pl.when((piece <= chip) & (chip < chips - 1))
-        def _():
-            line_copy(1, chip - piece, piece).wait_send()
-
-        @pl.when((piece >= chip) & (chip > 0))
-        def _():
-            line_copy(0, piece - chip, piece).wait_send()
+        for part in range(halves):
+            side_copy(piece, core, part).wait_send()
+
+            @pl.when((piece <= chip) & (chip < chips - 1))
+            def _():
+                line_copy(1, chip - piece, piece, part).wait_send()
+
+            @pl.when((piece >= chip) & (chip > 0))
+            def _():
+                line_copy(0, piece - chip, piece, part).wait_send()
 
         return carry
 
     lax.fori_loop(0, chips, drain, 0)
+
+    def settle(slot, carry):
+        for copy in results(slot):
+            copy.wait()
+        return carry
+
+    lax.fori_loop(0, 2 * chips * halves, settle, 0)
 
 
 def gather_rows(parts, groups, heads, rows, w_qkv, gain, w_out, w_up, w_down, factor):
@@ -338,8 +375,13 @@
             jax.ShapeDtypeStruct((held, 3 * heads * HD), bf16),
         ],
         in_specs=in_vmem(1) + [anywhere] + in_vmem(1) + [anywhere] * 3 + in_vmem(1),
-        out_specs=[anywhere] * 2 + in_vmem(7),
+        out_specs=[anywhere] * 2 + in_vmem(1) + [anywhere] * 5 + in_vmem(1),
         scratch_shapes=[
+            pltpu.VMEM((heads, PAD, tokens), bf16),
+            pltpu.VMEM((heads, HD, tokens), bf16),
+            pltpu.VMEM((heads, HD + EXTRA, tokens), bf16),
+            pltpu.VMEM((heads, tokens, PAD), bf16),
+            pltpu.VMEM((heads, tokens, PAD), bf16),
             pltpu.VMEM((parts, rows_dev, D), bf16),
             pltpu.VMEM((held, 3 * D), f32),
             pltpu.VMEM((3, held, D), f32),
@@ -347,8 +389,8 @@
             pltpu.VMEM((3, 2, held // 2, D), bf16),
             pltpu.VMEM((groups, 3, held, heads * HD), bf16),
             pltpu.VMEM((3 * heads * HD, D), bf16),
-            dma((2, 2, chips)),
-            dma((2, chips)),
+            dma((2, 2, chips, rows_dev // BLOCK)),
+            dma((2, chips, rows_dev // BLOCK)),
             dma((parts,)),
             dma((2, groups)),
             dma((2,)),
@@ -356,6 +398,8 @@
             dma((2, groups)),
             dma,
             dma((4,)),
+            dma((3, tokens // BLOCK)),
+            dma((2, tokens // BLOCK)),
         ],
         compiler_params=pltpu.CompilerParams(
             vmem_limit_bytes=60 * 1024 * 1024, collective_id=2, has_side_effects=True
@@ -469,28 +513,15 @@
     ot_ref,
     dt_ref,
     factor_ref,
-    units_ref,
     dqkv_ref,
     dscale_ref,
-    u_ref,
     qa_ref,
     da_ref,
     dq_ref,
     dk_ref,
     dv_ref,
-    held_ref,
-    total_ref,
     scale_ref,
-    load_sem,
 ):
-    parts = units_ref.shape[0]
-
-    def load(piece):
-        slot = lax.rem(piece, 2)
-        return pltpu.make_async_copy(units_ref.at[piece], held_ref.at[slot], load_sem.at[slot])
-
-    for piece in range(2):
-        load(piece).start()
     tokens = kn_ref.shape[1]
     num_blocks = tokens // BLOCK
     num_tiles = tokens // TILE
@@ -588,20 +619,6 @@
         return carry
 
     lax.fori_loop(0, num_blocks, finish, 0)
-    total_ref[...] = jnp.zeros(total_ref.shape, f32)
-
-    def project(piece, carry):
-        load(piece).wait()
-        total_ref[...] += dot(dqkv_ref[piece], held_ref[lax.rem(piece, 2)])
-
-        @pl.when(piece + 2 < parts)
-        def _():
-            load(piece + 2).start()
-
-        return carry
-
-    lax.fori_loop(0, parts, project, 0)
-    u_ref[...] = total_ref[...].T.astype(bf16)
     sums = functools.reduce(jnp.add, [scale_ref[head] for head in range(heads)])
     sums = jnp.concatenate([sums, jnp.zeros((PAD - HD, PAD), f32)], axis=0).T
     dscale_ref[...] = jnp.sum(sums, axis=0, keepdims=True)
@@ -642,7 +659,7 @@
     )
 
 
-def attention_backward(slots, kept, mixed, dmixed, factor, units):
+def attention_backward(slots, kept, mixed, dmixed, factor):
     qt, kt, kn, vn, lse = kept
     heads, tokens = kn.shape[:2]
     return pl.pallas_call(
@@ -651,26 +668,20 @@
         out_shape=[
             jax.ShapeDtypeStruct((mixed.shape[0], 3 * heads * HD, mixed.shape[2]), bf16),
             jax.ShapeDtypeStruct((1, PAD), f32),
-            jax.ShapeDtypeStruct((D, 3 * heads * HD), bf16),
         ],
-        in_specs=[pl.BlockSpec(memory_space=pltpu.SMEM)]
-        + in_vmem(8)
-        + [pl.BlockSpec(memory_space=pl.ANY)],
-        out_specs=in_vmem(3),
+        in_specs=[pl.BlockSpec(memory_space=pltpu.SMEM)] + in_vmem(8),
+        out_specs=in_vmem(2),
         scratch_shapes=[
             pltpu.VMEM((heads, PAD, tokens), bf16),
             pltpu.VMEM((heads, PAD, tokens), bf16),
             pltpu.VMEM((heads, HD, TILE), f32),
             pltpu.VMEM((heads, HD, tokens), f32),
             pltpu.VMEM((heads, HD, tokens), f32),
-            pltpu.VMEM((2,) + units.shape[1:], bf16),
-            pltpu.VMEM((3 * heads * HD, D), f32),
             pltpu.VMEM((heads, HD, PAD), f32),
-            pltpu.SemaphoreType.DMA((2,)),
         ],
         compiler_params=params(),
         cost_estimate=attention_cost(heads, tokens, 5),
-    )(slots, qt, kt, kn, vn, lse, mixed, dmixed, factor, units)
+    )(slots, qt, kt, kn, vn, lse, mixed, dmixed, factor)
 
 
 def middle_kernel(
@@ -882,14 +893,14 @@
 def reduce_kernel(
     parts,
     groups,
-    dq_ref,
-    wt_ref,
-    u_ref,
+    dq_in_ref,
+    wt_in_ref,
+    units_ref,
     wc_ref,
     small_ref,
     *refs,
 ):
-    chunk_refs = refs[:groups]
+    chunk_in_refs = refs[:groups]
     (
         down_ref,
         up_ref,
@@ -897,6 +908,14 @@
         ugather_ref,
         mgather_ref,
         sgather_ref,
+        dq_ref,
+        wt_ref,
+        chunk_ref,
+        held_ref,
+        total_ref,
+        u_ref,
+        usum_ref,
+        msum_ref,
         pair_ref,
         sum_ref,
         urecv_ref,
@@ -914,6 +933,9 @@
         side_sem,
         small_sem,
         cross_sem,
+        load_sem,
+        held_sem,
+        keep_sem,
     ) = refs[groups:]
     chips = parts // 2
     here = lax.axis_index("ctx")
@@ -925,6 +947,22 @@
     chip_peers = [lax.rem(chip + step, chips) for step in range(1, chips)]
     group_peers = [lax.rem(group + step, groups) for step in range(1, groups)]
 
+    loads = [
+        pltpu.make_async_copy(ref, chunk_ref.at[index], load_sem.at[index])
+        for index, ref in enumerate(chunk_in_refs)
+    ]
+    loads.append(pltpu.make_async_copy(dq_in_ref, dq_ref, load_sem.at[groups]))
+    loads.append(pltpu.make_async_copy(wt_in_ref, wt_ref, load_sem.at[groups + 1]))
+    for load in loads:
+        load.start()
+
+    def unit_load(piece):
+        slot = lax.rem(piece, 2)
+        return pltpu.make_async_copy(units_ref.at[piece], held_ref.at[slot], held_sem.at[slot])
+
+    for piece in range(2):
+        unit_load(piece).start()
+
     barrier = pltpu.get_barrier_semaphore()
     for peer in ctx_peers:
         pl.semaphore_signal(barrier, inc=1, device_id={"ctx": peer})
@@ -943,7 +981,7 @@
 
     def pair_copy(index):
         return send(
-            dq_ref.at[index, 1 - core],
+            dq_in_ref.at[index, 1 - core],
             pair_ref.at[index],
             (pair_sem.at[0, index], pair_sem.at[1, index]),
             {"ctx": other},
@@ -967,11 +1005,11 @@
 
     for index in range(chips):
         pair_copy(index).start()
-    for peer in group_peers:
-        u_copy(peer, group).start()
+    for load in loads:
+        load.wait()
     share = mlp_ref.shape[2]
     for matrix in range(3):
-        total = functools.reduce(jnp.add, [ref[matrix].astype(f32) for ref in chunk_refs])
+        total = functools.reduce(jnp.add, [chunk_ref[step, matrix].astype(f32) for step in range(groups)])
         for index in range(chips):
             mlp_ref[index, matrix] = total[index * share : (index + 1) * share].astype(bf16)
     for peer in chip_peers:
@@ -989,7 +1027,7 @@
         return rows
 
     def sum_copy(way, target, index):
-        ref = sum_ref.at[way, target, pl.ds(index * rows_half, rows_half)]
+        ref = sum_ref.at[way + target, pl.ds(index * rows_half, rows_half)]
         sems = (sum_sem.at[0, way, target, index], sum_sem.at[1, way, target, index])
         return send(ref, ref, sems, {"ctx": here + (2 if way else -2)})
 
@@ -1007,17 +1045,17 @@
 
                     @pl.when(first)
                     def _():
-                        sum_ref[way, target, rows] = part_ref[rows, :].astype(bf16)
+                        sum_ref[way + target, rows] = part_ref[rows, :].astype(bf16)
 
                     @pl.when(jnp.logical_not(first))
                     def _():
                         sum_copy(way, target, index).wait_recv()
-                        sum_ref[way, target, rows] = (
-                            part_ref[rows, :] + sum_ref[way, target, rows].astype(f32)
+                        sum_ref[way + target, rows] = (
+                            part_ref[rows, :] + sum_ref[way + target, rows].astype(f32)
                         ).astype(bf16)
 
                     if last:
-                        out_ref[rows, :] = sum_ref[way, target, rows]
+                        out_ref[rows, :] = sum_ref[way + target, rows]
                     else:
                         sum_copy(way, target, index).start()
                     return carry
@@ -1031,16 +1069,21 @@
                     out_ref[...] = jnp.zeros(out_ref.shape, bf16)
 
     gathers = (ugather_ref, mgather_ref)
+    sums = (usum_ref, msum_ref)
+
+    def keep_copy(which):
+        return pltpu.make_async_copy(sums[which], gathers[which].at[here], keep_sem.at[which])
 
     def line_copy(which, way, step, piece):
         ref = gathers[which].at[2 * piece + core]
         sems = (line_sem.at[0, which, way, step], line_sem.at[1, which, way, step])
-        return send(ref, ref, sems, {"ctx": here + (2 if way else -2)})
-
-    def side_copy(which, piece, lane):
+        source = sums[which] if step == 0 else ref
+        return send(source, ref, sems, {"ctx": here + (2 if way else -2)})
+
+    def side_copy(which, piece, lane, own=False):
         ref = gathers[which].at[2 * piece + lane]
         sems = (side_sem.at[0, which, piece], side_sem.at[1, which, piece])
-        return send(ref, ref, sems, {"ctx": other})
+        return send(sums[which] if own else ref, ref, sems, {"ctx": other})
 
     def line_sends(which, step, go):
         @pl.when((chip < chips - 1) & (chip - step >= 0))
@@ -1080,12 +1123,39 @@
 
     reduce_step(0)
 
+    total_ref[...] = jnp.zeros(total_ref.shape, f32)
+
+    def accumulate(piece, carry):
+        unit_load(piece).wait()
+        total_ref[...] += dot(dq_ref[piece // 2, lax.rem(piece, 2)], held_ref[lax.rem(piece, 2)])
+
+        @pl.when(piece + 2 < parts)
+        def _():
+            unit_load(piece + 2).start()
+
+        return carry
+
+    lax.fori_loop(0, parts, accumulate, 0)
+    u_ref[...] = total_ref[...].T.astype(bf16).reshape(u_ref.shape)
+    for peer in group_peers:
+        u_copy(peer, group).start()
+
+    total = mlp_ref[chip].astype(f32)
+    for peer in chip_peers:
+        m_copy(chip, peer).wait_recv()
+        total = total + mrecv_ref[peer].astype(f32)
+    msum_ref[...] = total.astype(bf16)
+    keep_copy(1).start()
+    side_copy(1, chip, core, True).start()
+    line_sends(1, 0, lambda copy: copy.start())
+
     total = u_ref[group].astype(f32)
     for peer in group_peers:
         u_copy(group, peer).wait_recv()
         total = total + urecv_ref[peer].astype(f32)
-    ugather_ref[here] = total.astype(bf16)
-    side_copy(0, chip, core).start()
+    usum_ref[...] = total.astype(bf16)
+    keep_copy(0).start()
+    side_copy(0, chip, core, True).start()
     line_sends(0, 0, lambda copy: copy.start())
     held = total.shape[0]
     gain = jnp.sum(total * wc_ref[...].astype(f32), axis=1, keepdims=True)
@@ -1097,14 +1167,6 @@
         smine_ref[row : row + 1, :] = flat[:, row * PAD : (row + 1) * PAD]
     for peer in ctx_peers:
         small_copy(peer, here).start()
-
-    total = mlp_ref[chip].astype(f32)
-    for peer in chip_peers:
-        m_copy(chip, peer).wait_recv()
-        total = total + mrecv_ref[peer].astype(f32)
-    mgather_ref[here] = total.astype(bf16)
-    side_copy(1, chip, core).start()
-    line_sends(1, 0, lambda copy: copy.start())
 
     for step in range(1, chips):
         if step == 1:
@@ -1126,9 +1188,10 @@
 
     for index in range(2):
         rows = partial(chip, index)
-        own_ref[rows, :] = part_ref[rows, :]
+        own_ref[rows, :] = part_ref[rows, :].astype(bf16)
 
     for which in range(2):
+        keep_copy(which).wait()
         for piece in range(chips):
             side_copy(which, piece, 1 - core).wait_recv()
             side_copy(which, piece, core).wait_send()
@@ -1157,30 +1220,40 @@
                 sum_copy(1, chips - 1 - step + chip, index).wait_send()
 
 
-def reduce_gradients(parts, groups, dqkv, w_pair, u_parts, w_columns, small, chunks):
+def reduce_gradients(parts, groups, dqkv, w_pair, units, w_columns, small, chunks):
     chips = parts // 2
     mlp_shape = (chips, 3, chunks[0].shape[1] // chips, D)
     rows_dev = dqkv.shape[3]
     rows, width = w_columns.shape
     lanes = -(-rows // PAD) * PAD
     dma = pltpu.SemaphoreType.DMA
+    anywhere = pl.BlockSpec(memory_space=pl.ANY)
+    u_shape = (groups, rows, width)
     return pl.pallas_call(
         functools.partial(reduce_kernel, parts, groups),
         name="reduce_gradients",
         out_shape=[
             jax.ShapeDtypeStruct((rows_dev, D), bf16),
             jax.ShapeDtypeStruct((rows_dev, D), bf16),
-            jax.ShapeDtypeStruct((rows_dev, D), f32),
+            jax.ShapeDtypeStruct((rows_dev, D), bf16),
             jax.ShapeDtypeStruct((parts, rows, width), bf16),
             jax.ShapeDtypeStruct((parts,) + mlp_shape[1:], bf16),
             jax.ShapeDtypeStruct((groups,) + small.shape, f32),
         ],
-        in_specs=in_vmem(5 + groups),
-        out_specs=in_vmem(6),
+        in_specs=[anywhere] * 3 + in_vmem(2) + [anywhere] * groups,
+        out_specs=in_vmem(3) + [anywhere] * 2 + in_vmem(1),
         scratch_shapes=[
+            pltpu.VMEM(dqkv.shape, bf16),
+            pltpu.VMEM(w_pair.shape, bf16),
+            pltpu.VMEM((groups,) + chunks[0].shape, bf16),
+            pltpu.VMEM((2,) + units.shape[1:], bf16),
+            pltpu.VMEM((width, D), f32),
+            pltpu.VMEM(u_shape, bf16),
+            pltpu.VMEM(u_shape[1:], bf16),
+            pltpu.VMEM(mlp_shape[1:], bf16),
             pltpu.VMEM((chips,) + dqkv.shape[2:], bf16),
-            pltpu.VMEM((2, chips, rows_dev, D), bf16),
-            pltpu.VMEM(u_parts.shape, bf16),
+            pltpu.VMEM((chips + 1, rows_dev, D), bf16),
+            pltpu.VMEM(u_shape, bf16),
             pltpu.VMEM(mlp_shape, bf16),
             pltpu.VMEM(mlp_shape, bf16),
             pltpu.VMEM((rows_dev, D), f32),
@@ -1195,11 +1268,14 @@
             dma((2, 2, chips)),
             dma((2, parts)),
             dma((2, groups)),
+            dma((groups + 2,)),
+            dma((2,)),
+            dma((2,)),
         ],
         compiler_params=pltpu.CompilerParams(
             vmem_limit_bytes=60 * 1024 * 1024, collective_id=1, has_side_effects=True
         ),
-    )(dqkv, w_pair, u_parts, w_columns, small, *chunks)
+    )(dqkv, w_pair, units, w_columns, small, *chunks)
 
 
 def update_kernel(rates, qkv_ref, gain_ref, mlp_ref, *refs):
@@ -1267,15 +1343,16 @@
     )(qkv, gain, mlp, *arrays)
 
 
-def finish_kernel(x_ref, dmid_ref, own_ref, down_ref, up_ref, out_ref):
+def finish_kernel(x_ref, dmid_ref, own_ref, down_ref, up_ref, layer_ref, out_ref, same_ref):
     rows = x_ref[...].astype(f32)
     scale = rms_scale(rows)
     unit = rows * scale
-    dunit = own_ref[...] + down_ref[...].astype(f32) + up_ref[...].astype(f32)
+    dunit = own_ref[...].astype(f32) + down_ref[...].astype(f32) + up_ref[...].astype(f32)
     grad = dmid_ref[...] + scale * (
         dunit - unit * jnp.mean(dunit * unit, axis=-1, keepdims=True)
     )
     out_ref[...] = grad.astype(bf16)
+    same_ref[...] = layer_ref[...]
 
 
 def finish(*arrays):
@@ -1286,8 +1363,8 @@
         name="finish",
         grid=(rows // PAD,),
         in_specs=[spec] * len(arrays),
-        out_specs=spec,
-        out_shape=jax.ShapeDtypeStruct((rows, D), bf16),
+        out_specs=[spec] * 2,
+        out_shape=[jax.ShapeDtypeStruct((rows, D), bf16)] * 2,
         compiler_params=params(),
     )(*arrays)
 
@@ -1347,8 +1424,7 @@
     for step in range(1, groups):
         swap = [(i, i ^ step) for i in range(groups)]
         chunks[step] = lax.ppermute(chunks[step], "fsdp", swap)
-    dqkv, dscale, u_parts = attention_backward(slots, kept, mixed, dmixed, factor_two, unit_all)
-    u_parts = u_parts.reshape(groups, rows, 3 * width)
+    dqkv, dscale = attention_backward(slots, kept, mixed, dmixed, factor_two)
     scale_grad = (
         dscale[0, :HD]
         / factor_two[:, 0]
@@ -1364,7 +1440,7 @@
         groups,
         dqkv.reshape(parts // 2, 2, 3 * width, rows_dev),
         w_pair,
-        u_parts,
+        unit_all,
         w_columns,
         small,
         chunks,
@@ -1398,7 +1474,7 @@
     rest = jnp.sum(flat[:, lanes : lanes + D + HD], axis=0)
     small_total = jnp.concatenate([flat[:, :rows].reshape(D), rest])
     small_set = adamw(small_params, small_m, small_v, small_total, small_rate, 0.0)
-    input_grad = finish(inputs[0], dmid, own_part, got_down, got_up)
+    input_grad, output = finish(inputs[0], dmid, own_part, got_down, got_up, output)
     return (
         output[None],
         input_grad[None],

time: 420 us -> 405 us (0.964)
  Pallas kernels: 395 us -> 379 us
    pallas_call x1, Pallas kernels: 56.4 us -> 49.4 us  [attention_backward(): pl.pallas_call(functools.partial(backward_kernel, heads), name='attention...]
    pallas_call x1, Pallas kernels: 111 us -> 105 us  [reduce_gradients(): pl.pallas_call(functools.partial(reduce_kernel, parts, groups), name='red...]
  transfers between devices with their start and end apart: 5 -> 5, of which waited for: 1 -> 3; matrix products, arithmetic and copies ran while one was open for 1% -> 1% of each run, Pallas kernels for 20% -> 19%
where the time goes in v8:
time: 405 us; the launch traced here: 404 us
  Pallas kernels  379 us (94%)
  starting transfers between devices  10.3 us (3%)
  local copies, waits for them, and re-layouts  4.9 us (1%)
  waiting for transfers between devices  4.66 us (1%)
    pallas_call x1, Pallas kernels, gather_rows(): pl.pallas_call(functools.partial(gather_kernel, parts, groups, heads), na...  106 us
    pallas_call x1, Pallas kernels, reduce_gradients(): pl.pallas_call(functools.partial(reduce_kernel, parts, groups), name='red...  105 us
    pallas_call x1, Pallas kernels, middle(): pl.pallas_call(functools.partial(middle_kernel, parts, groups), name='mid...  62.6 us
    pallas_call x1, Pallas kernels, attention_backward(): pl.pallas_call(functools.partial(backward_kernel, heads), name='attention...  49.4 us
    pallas_call x1, Pallas kernels, update(): pl.pallas_call(functools.partial(update_kernel, rates), name='update_weig...  25.8 us
    pallas_call x1, Pallas kernels, attention_forward(): pl.pallas_call(functools.partial(forward_kernel, heads), name='attention_...  24.6 us
  transfers between devices with their start and end apart: 5, of which 3 were waited for; matrix products, arithmetic and copies ran while one was open for 1% of the time, Pallas kernels for 19%

profile of v8, /device:TPU:0, one launch (start us, length us, event | category | flops | bytes accessed | tf_op | source)
XLA Modules:
  0.0 403.8 jit_solution(316014960890904527)
XLA Ops:
  0.7 0.8 fusion.4
  1.4 0.7 fusion.5
  2.1 1.3 select_reduce_fusion.slot_ref
  3.4 0.1 dynamic_slice.3
  3.5 0.8 broadcast_in_dim.40.gain_ref
  4.3 0.7 copy.46.factor_ref
  5.0 0.6 broadcast_in_dim.36.gain_ref
  5.6 106.5 %gather_rows.1 = (bf16[8,512,1280]{2,1,0:T(8,128)(2,1)}, bf16[3,4,2,160,1280]{4,3,2,1,0:T(8,128)(2,1)}, bf16[2,480,1280]{2,1,0:T(8,128)(2,1)}, bf16[2,128,4096]{...) custom-call(bf16[512,1280]{1,0:T(8,128)(2,1)} %bitcast.19, ...), custom_call_target="tpu_custom_call" | custom-call | tf_op jit(solution)/shard_map/gather_rows/pallas_call | solution.py:363
  112.1 24.6 %attention_forward.1 = (f32[2,1,4096]{2,1,0:T(1,128)}, bf16[8,160,512]{2,1,0:T(8,128)(2,1)}) custom-call(s32[16]{0:T(128)} %select_reduce_fusion.slot_ref, bf16[2,128,4096]{2,1,0:T(8,128)(2,1)} %get-tuple-element.66.qt_ref, bf16[2,80,4096]{2,1,0:T(8,128)(2,1)} %get-tuple-element.67.kt_ref, bf16[2,4096,128]{2,1,0:T(8,128)(2,1)} %get-tuple-element.68.kn_ref, ...), custom_call_target="tpu_custom_call" | custom-call | flops 17179869184 | bytes 5242880 | tf_op jit(solution)/shard_map/attention_forward/pallas_call | solution.py:637
  136.6 62.6 %middle.1 = (bf16[512,1280]{1,0:T(8,128)(2,1)}, f32[512,1280]{1,0:T(8,128)}, bf16[8,160,512]{2,1,0:T(8,128)(2,1)}, f32[1,1280]{1,0:T(1,128)}, bf16[3,160,1280]{2...) custom-call(bf16[8,160,512]{2,1,0:T(8,128)(2,1)} %get-tuple-element., ...), custom_call_target="tpu_custom_call" | custom-call | tf_op jit(solution)/shard_map/middle/pallas_call | solution.py:860
  199.2 1.7 collective-permute-start
  200.9 2.0 collective-permute-start.1
  202.8 0.7 collective-permute-start.2
  203.6 49.4 %attention_backward.1 = (bf16[8,480,512]{2,1,0:T(8,128)(2,1)}, f32[1,128]{1,0:T(1,128)}) custom-call(s32[16]{0:T(128)} %select_reduce_fusion.slot_ref, bf16[2,128,4096]{2,1,0:T(8,128)(2,1)} %get-tuple-element.66.qt_ref, bf16[2,80,4096]{2,1,0:T(8,128)(2,1)} %get-tuple-element.67.kt_ref, bf16[2,4096,128]{2,1,0:T(8,128)(2,1)} %get-tuple-element.68.kn_ref, ...), custom_call_target="tpu_custom_call" | custom-call | flops 42949672960 | bytes 5242880 | tf_op jit(solution)/shard_map/attention_backward/pallas_call | solution.py:665
  253.0 0.7 divide_multiply_fusion
  253.7 0.6 fusion.1.small_ref
  254.3 0.0 collective-permute-done.refs_1_
  254.3 1.8 collective-permute-done.1.refs_2_
  256.1 1.7 collective-permute-done.2.refs_3_
  257.8 104.5 %reduce_gradients.1 = (bf16[512,1280]{1,0:T(8,128)(2,1)}, bf16[512,1280]{1,0:T(8,128)(2,1)}, bf16[512,1280]{1,0:T(8,128)(2,1)}, bf16[8,320,480]{2,1,0:T(8,128)(2...) custom-call(bf16[4,2,480,512]{3,2,1,0:T(8,128)(2,1)} %bitcast.23, ...), custom_call_target="tpu_custom_call" | custom-call | tf_op jit(solution)/shard_map/reduce_gradients/pallas_call | solution.py:1232
  362.4 1.3 collective-permute-start.3
  363.7 4.6 %collective-permute-start.4 = (bf16[512,1280]{1,0:T(8,128)(2,1)}, bf16[512,1280]{1,0:T(8,128)(2,1)S(1)}, u32[]{:S(2)}, u32[]{:S(2)}) collective-permute-start(bf16[512,1280]{1,0:T(8,128)(2,1)} %get-tuple-element.88), channel_id=1, source_target_pairs={{0,8},{4,12},{8,16},{12,20},{16,24},{20,28},{1,9},{5,13},{9,17},{1... | collective-permute-start | bytes 3932168 | tf_op jit(solution)/shard_map/ppermute | solution.py:1449
  368.3 0.8 copy.51
  369.1 0.1 reshape.61
  369.2 25.8 %update_weights.1 = (f32[320,3840]{1,0:T(8,128)}, f32[320,3840]{1,0:T(8,128)}, f32[320,3840]{1,0:T(8,128)}, bf16[320,3840]{1,0:T(8,128)(2,1)}, f32[320,1280]{1,0...) custom-call(bf16[8,320,480]{2,1,0:T(8,128)(2,1)} %get-tuple-element., ...), custom_call_target="tpu_custom_call" | custom-call | flops 68812800 | bytes 68812800 | tf_op jit(solution)/shard_map/update_weights/pallas_call | solution.py:1334
  395.0 0.0 copy-done.5
  395.0 0.0 copy-done.6
  395.0 0.6 multiply_subtract_fusion
  395.7 0.0 collective-permute-done.3.down_ref
  395.7 1.1 collective-permute-done.4.up_ref
  396.8 1.1 copy-done.1
  397.9 5.9 %finish.1 = (bf16[512,1280]{1,0:T(8,128)(2,1)}, bf16[512,1280]{1,0:T(8,128)(2,1)}) custom-call(bf16[512,1280]{1,0:T(8,128)(2,1)} %bitcast.21, f32[512,1280]{1,0:T(8,128)} %get-tuple-element.72.dmid_ref, bf16[512,1280]{1,0:T(8,128)(2,1)} %get-tuple-element.86.own_ref, bf16[512,1280]{1,0:T(8,128)(2,1)} %copy-done, bf16[512,1280]{1,0:T(8,128)(2,1)} %copy-done.1, ...), custom_call_target="tpu_custom_call" | custom-call | tf_op jit(solution)/shard_map/finish/pallas_call | solution.py:1361
  (17 shorter events, 0.1 us)
Async XLA Ops:
  199.2 55.1 %collective-permute-start = (bf16[3,160,1280]{2,1,0:T(8,128)(2,1)}, bf16[3,160,1280]{2,1,0:T(8,128)(2,1)S(1)}, u32[]{:S(2)}, u32[]{:S(2)}) collective-permute-start(bf16[3,160,1280]{2,1,0:T(8,128)(2,1)} %get-tuple-element.83), channel_id=1, source_target_pairs={{0,1},{1,0},{2,3},{3,2},{4,5},{5,4},{6,7},{7,6},{8,9},{9,8},{10,11... | collective-permute-start | bytes 3686408 | tf_op jit(solution)/shard_map/ppermute | solution.py:1426
  200.9 55.2 %collective-permute-start.1 = (bf16[3,160,1280]{2,1,0:T(8,128)(2,1)}, bf16[3,160,1280]{2,1,0:T(8,128)(2,1)S(1)}, u32[]{:S(2)}, u32[]{:S(2)}) collective-permute-start(bf16[3,160,1280]{2,1,0:T(8,128)(2,1)} %get-tuple-element.84), channel_id=1, source_target_pairs={{0,2},{1,3},{2,0},{3,1},{4,6},{5,7},{6,4},{7,5},{8,10},{9,11},{10,... | collective-permute-start | bytes 3686408 | tf_op jit(solution)/shard_map/ppermute | solution.py:1426
  202.8 55.0 %collective-permute-start.2 = (bf16[3,160,1280]{2,1,0:T(8,128)(2,1)}, bf16[3,160,1280]{2,1,0:T(8,128)(2,1)}, u32[]{:S(2)}, u32[]{:S(2)}) collective-permute-start(bf16[3,160,1280]{2,1,0:T(8,128)(2,1)} %get-tuple-element.85), channel_id=1, source_target_pairs={{0,3},{1,2},{2,1},{3,0},{4,7},{5,6},{6,5},{7,4},{8,11},{9,10},{10,... | collective-permute-start | bytes 3686408 | tf_op jit(solution)/shard_map/ppermute | solution.py:1426
  203.6 49.4 %copy-start.7 = (f32[1,1280]{1,0:T(1,128)S(1)}, f32[1,1280]{1,0:T(1,128)}, u32[]{:S(2)}) copy-start(f32[1,1280]{1,0:T(1,128)} %get-tuple-element.80) | copy-start | bytes 15364
  203.6 49.4 %copy-start.4 = (f32[2640]{0:T(1024)S(1)}, f32[2640]{0:T(1024)}, u32[]{:S(2)}) copy-start(f32[2640]{0:T(1024)} %param.33) | copy-start | bytes 31684
  254.3 3.5 copy-start.2
  256.1 1.8 copy-start.3
  362.4 33.3 %collective-permute-start.3 = (bf16[512,1280]{1,0:T(8,128)(2,1)}, bf16[512,1280]{1,0:T(8,128)(2,1)S(1)}, u32[]{:S(2)}, u32[]{:S(2)}) collective-permute-start(bf16[512,1280]{1,0:T(8,128)(2,1)} %get-tuple-element.87), channel_id=1, source_target_pairs={{8,0},{12,4},{16,8},{20,12},{24,16},{28,20},{9,1},{13,5},{17,9},{2... | collective-permute-start | bytes 3932168 | tf_op jit(solution)/shard_map/ppermute | solution.py:1448
  363.7 33.1 %collective-permute-start.4 = (bf16[512,1280]{1,0:T(8,128)(2,1)}, bf16[512,1280]{1,0:T(8,128)(2,1)S(1)}, u32[]{:S(2)}, u32[]{:S(2)}) collective-permute-start(bf16[512,1280]{1,0:T(8,128)(2,1)} %get-tuple-element.88), channel_id=1, source_target_pairs={{0,8},{4,12},{8,16},{12,20},{16,24},{20,28},{1,9},{5,13},{9,17},{1... | collective-permute-start | bytes 3932168 | tf_op jit(solution)/shard_map/ppermute | solution.py:1449
  369.2 25.8 %copy-start.5 = (f32[2640]{0:T(1024)S(1)}, f32[2640]{0:T(1024)}, u32[]{:S(2)}) copy-start(f32[2640]{0:T(1024)} %param.34) | copy-start | bytes 31684
  369.2 25.8 %copy-start.6 = (f32[2640]{0:T(1024)S(1)}, f32[2640]{0:T(1024)}, u32[]{:S(2)}) copy-start(f32[2640]{0:T(1024)} %param.35) | copy-start | bytes 31684
  395.7 1.1 copy-start
  396.8 1.1 copy-start.1

commit v9 on v8

--- a/solution.py
+++ b/solution.py
@@ -55,6 +55,14 @@
     )
 
 
+def fill_slots(order_ref, slot_ref):
+    def place(slot, carry):
+        slot_ref[order_ref[slot]] = slot
+        return carry
+
+    lax.fori_loop(0, order_ref.shape[0], place, 0)
+
+
 def three_rows(row):
     high = row.astype(bf16)
     rest = row - high.astype(f32)
@@ -104,11 +112,10 @@
     heads,
     x_ref,
     wqkv_ref,
-    gain_ref,
     wout_ref,
     wup_ref,
     wdown_ref,
-    factor_ref,
+    small_ref,
     unit_ref,
     full_ref,
     wpair_ref,
@@ -118,6 +125,8 @@
     kn_out_ref,
     vn_out_ref,
     wcol_ref,
+    gain_ref,
+    factor_ref,
     qt_ref,
     kt_ref,
     vt_ref,
@@ -234,6 +243,14 @@
         for way in range(2):
             forward(way, 0, chip, part)
         side_copy(chip, core, part).start()
+    held = gain_ref.shape[0]
+    lanes = -(-held // PAD) * PAD
+    gains = jnp.broadcast_to(small_ref[:, :D], (8, D))
+    gains = pltpu.roll(gains, lax.rem(D - group * held, D), 1)[:1, :lanes]
+    gain_ref[...] = jnp.broadcast_to(gains, (PAD, lanes)).T[:held, :1]
+    soft = jnp.log(1.0 + jnp.exp(small_ref[:, 2 * D :])) * (scale_base / math.sqrt(HD) * LOG2E)
+    soft = jnp.concatenate([soft, jnp.zeros((1, PAD - HD), f32)], axis=1)
+    factor_ref[...] = jnp.broadcast_to(soft, (PAD, PAD)).T[:HD, :1]
     shift = lax.rem(D - here * width, D)
     stages[0].wait()
     for part in range(3):
@@ -353,7 +370,7 @@
     lax.fori_loop(0, 2 * chips * halves, settle, 0)
 
 
-def gather_rows(parts, groups, heads, rows, w_qkv, gain, w_out, w_up, w_down, factor):
+def gather_rows(parts, groups, heads, rows, w_qkv, w_out, w_up, w_down, small):
     rows_dev = rows.shape[0]
     held = w_qkv.shape[0]
     tokens = parts * rows_dev
@@ -373,9 +390,11 @@
             jax.ShapeDtypeStruct((heads, tokens, PAD), bf16),
             jax.ShapeDtypeStruct((heads, tokens, PAD), bf16),
             jax.ShapeDtypeStruct((held, 3 * heads * HD), bf16),
+            jax.ShapeDtypeStruct((held, 1), f32),
+            jax.ShapeDtypeStruct((HD, 1), f32),
         ],
-        in_specs=in_vmem(1) + [anywhere] + in_vmem(1) + [anywhere] * 3 + in_vmem(1),
-        out_specs=[anywhere] * 2 + in_vmem(1) + [anywhere] * 5 + in_vmem(1),
+        in_specs=in_vmem(1) + [anywhere] * 4 + in_vmem(1),
+        out_specs=[anywhere] * 2 + in_vmem(1) + [anywhere] * 5 + in_vmem(3),
         scratch_shapes=[
             pltpu.VMEM((heads, PAD, tokens), bf16),
             pltpu.VMEM((heads, HD, tokens), bf16),
@@ -404,21 +423,32 @@
         compiler_params=pltpu.CompilerParams(
             vmem_limit_bytes=60 * 1024 * 1024, collective_id=2, has_side_effects=True
         ),
-    )(rows, w_qkv, gain, w_out, w_up, w_down, factor)
+    )(rows, w_qkv, w_out, w_up, w_down, small)
 
 
 def forward_kernel(
     heads,
-    slot_ref,
+    order_ref,
     qt_ref,
     kt_ref,
+    kn_in_ref,
+    vt_in_ref,
+    lse_ref,
+    ot_ref,
+    slot_ref,
     kn_ref,
     vt_ref,
-    lse_ref,
-    ot_ref,
     acc_ref,
     top_ref,
+    load_sem,
 ):
+    loads = [
+        pltpu.make_async_copy(source, target, load_sem.at[index])
+        for index, (source, target) in enumerate(((kn_in_ref, kn_ref), (vt_in_ref, vt_ref)))
+    ]
+    for load in loads:
+        load.start()
+    fill_slots(order_ref, slot_ref)
     tokens = kn_ref.shape[1]
     num_tiles = tokens // TILE
     prompt_tiles = num_tiles // 2
@@ -432,6 +462,9 @@
         return jnp.max(lax.fori_loop(0, tokens // BLOCK, visit, jnp.zeros((1, BLOCK), f32)))
 
     bounded = longest(qt_ref) * longest(kt_ref) <= SCORE_BOUND * SCORE_BOUND
+
+    for load in loads:
+        load.wait()
 
     def run(shifted):
         def query_tile(tile, carry):
@@ -504,24 +537,38 @@
 
 def backward_kernel(
     heads,
-    slot_ref,
+    order_ref,
     qt_ref,
-    kt_ref,
-    kn_ref,
-    vn_ref,
+    kt_in_ref,
+    kn_in_ref,
+    vn_in_ref,
     lse_ref,
     ot_ref,
     dt_ref,
     factor_ref,
     dqkv_ref,
     dscale_ref,
+    slot_ref,
+    kt_ref,
+    kn_ref,
+    vn_ref,
     qa_ref,
     da_ref,
     dq_ref,
     dk_ref,
     dv_ref,
     scale_ref,
+    load_sem,
 ):
+    loads = [
+        pltpu.make_async_copy(source, target, load_sem.at[index])
+        for index, (source, target) in enumerate(
+            ((kn_in_ref, kn_ref), (vn_in_ref, vn_ref), (kt_in_ref, kt_ref))
+        )
+    ]
+    for load in loads:
+        load.start()
+    fill_slots(order_ref, slot_ref)
     tokens = kn_ref.shape[1]
     num_blocks = tokens // BLOCK
     num_tiles = tokens // TILE
@@ -548,6 +595,8 @@
     dk_ref[...] = jnp.zeros(dk_ref.shape, f32)
     dv_ref[...] = jnp.zeros(dv_ref.shape, f32)
     scale_ref[...] = jnp.zeros(scale_ref.shape, f32)
+    for load in loads:
+        load.wait()
 
     def query_tile(tile, carry):
         here = tile_at(tile)
@@ -632,7 +681,7 @@
     return pltpu.CompilerParams(vmem_limit_bytes=60 * 1024 * 1024)
 
 
-def attention_forward(slots, qt, kt, kn, vt, parts):
+def attention_forward(order, qt, kt, kn, vt, parts):
     heads, tokens = kn.shape[:2]
     return pl.pallas_call(
         functools.partial(forward_kernel, heads),
@@ -641,15 +690,21 @@
             jax.ShapeDtypeStruct((heads, 1, tokens), f32),
             jax.ShapeDtypeStruct((parts, heads * HD, tokens // parts), bf16),
         ],
-        in_specs=[pl.BlockSpec(memory_space=pltpu.SMEM)] + in_vmem(4),
+        in_specs=[pl.BlockSpec(memory_space=pltpu.SMEM)]
+        + in_vmem(2)
+        + [pl.BlockSpec(memory_space=pl.ANY)] * 2,
         out_specs=in_vmem(2),
         scratch_shapes=[
+            pltpu.SMEM(order.shape, jnp.int32),
+            pltpu.VMEM(kn.shape, bf16),
+            pltpu.VMEM(vt.shape, bf16),
             pltpu.VMEM((heads, HD + EXTRA, TILE), f32),
             pltpu.VMEM((heads, 1, TILE), f32),
+            pltpu.SemaphoreType.DMA((2,)),
         ],
         compiler_params=params(),
         cost_estimate=attention_cost(heads, tokens, 2),
-    )(slots, qt, kt, kn, vt)
+    )(order, qt, kt, kn, vt)
 
 
 def attention_cost(heads, tokens, passes):
@@ -659,7 +714,7 @@
     )
 
 
-def attention_backward(slots, kept, mixed, dmixed, factor):
+def attention_backward(order, kept, mixed, dmixed, factor):
     qt, kt, kn, vn, lse = kept
     heads, tokens = kn.shape[:2]
     return pl.pallas_call(
@@ -669,19 +724,27 @@
             jax.ShapeDtypeStruct((mixed.shape[0], 3 * heads * HD, mixed.shape[2]), bf16),
             jax.ShapeDtypeStruct((1, PAD), f32),
         ],
-        in_specs=[pl.BlockSpec(memory_space=pltpu.SMEM)] + in_vmem(8),
+        in_specs=[pl.BlockSpec(memory_space=pltpu.SMEM)]
+        + in_vmem(1)
+        + [pl.BlockSpec(memory_space=pl.ANY)] * 3
+        + in_vmem(4),
         out_specs=in_vmem(2),
         scratch_shapes=[
+            pltpu.SMEM(order.shape, jnp.int32),
+            pltpu.VMEM(kt.shape, bf16),
+            pltpu.VMEM(kn.shape, bf16),
+            pltpu.VMEM(vn.shape, bf16),
             pltpu.VMEM((heads, PAD, tokens), bf16),
             pltpu.VMEM((heads, PAD, tokens), bf16),
             pltpu.VMEM((heads, HD, TILE), f32),
             pltpu.VMEM((heads, HD, tokens), f32),
             pltpu.VMEM((heads, HD, tokens), f32),
             pltpu.VMEM((heads, HD, PAD), f32),
+            pltpu.SemaphoreType.DMA((3,)),
         ],
         compiler_params=params(),
         cost_estimate=attention_cost(heads, tokens, 5),
-    )(slots, qt, kt, kn, vn, lse, mixed, dmixed, factor)
+    )(order, qt, kt, kn, vn, lse, mixed, dmixed, factor)
 
 
 def middle_kernel(
@@ -1357,11 +1420,11 @@
 
 def finish(*arrays):
     rows = arrays[0].shape[0]
-    spec = pl.BlockSpec((PAD, D), lambda i: (i, 0))
+    spec = pl.BlockSpec((PAD // 2, D), lambda i: (i, 0))
     return pl.pallas_call(
         finish_kernel,
         name="finish",
-        grid=(rows // PAD,),
+        grid=(2 * rows // PAD,),
         in_specs=[spec] * len(arrays),
         out_specs=[spec] * 2,
         out_shape=[jax.ShapeDtypeStruct((rows, D), bf16)] * 2,
@@ -1396,21 +1459,28 @@
     rows_dev = inputs.shape[1]
     tokens = rows_dev * parts
     here = lax.axis_index("ctx")
-    index = jnp.arange(block_order.shape[1], dtype=jnp.int32)
-    slots = jnp.sum(jnp.where(block_order[0][None] == index[:, None], index[None], 0), axis=1)
-    gain_one = small_params[:D]
+    order = block_order[0]
     gain_two = small_params[D : 2 * D]
     query_scale = small_params[2 * D :]
     group = lax.axis_index("fsdp")
     rows = w_qkv.shape[0]
 
-    gain_rows = lax.dynamic_slice_in_dim(gain_one, group * rows, rows, 0)[:, None]
-    factor = scale_base / math.sqrt(HD) * jax.nn.softplus(query_scale)
-    factor_two = (factor * LOG2E)[:, None]
-    unit_all, mlp_full, w_pair, qt, kt, vt, kn, vn, w_columns = gather_rows(
-        parts, groups, heads, inputs[0], w_qkv, gain_rows, w_out, w_up, w_down, factor_two
+    (
+        unit_all,
+        mlp_full,
+        w_pair,
+        qt,
+        kt,
+        vt,
+        kn,
+        vn,
+        w_columns,
+        gain_rows,
+        factor_two,
+    ) = gather_rows(
+        parts, groups, heads, inputs[0], w_qkv, w_out, w_up, w_down, small_params[None]
     )
-    lse, mixed = attention_forward(slots, qt, kt, kn, vt, parts)
+    lse, mixed = attention_forward(order, qt, kt, kn, vt, parts)
     kept = (qt, kt, kn, vn, lse)
     output, dmid, dmixed, gain_two_grad, *chunks = middle(
         parts,
@@ -1424,7 +1494,7 @@
     for step in range(1, groups):
         swap = [(i, i ^ step) for i in range(groups)]
         chunks[step] = lax.ppermute(chunks[step], "fsdp", swap)
-    dqkv, dscale = attention_backward(slots, kept, mixed, dmixed, factor_two)
+    dqkv, dscale = attention_backward(order, kept, mixed, dmixed, factor_two)
     scale_grad = (
         dscale[0, :HD]
         / factor_two[:, 0]

time: 405 us -> 405 us (level)
  transfers between devices with their start and end apart: 5 -> 5, of which waited for: 3 -> 4; matrix products, arithmetic and copies ran while one was open for 1% -> 1% of each run, Pallas kernels for 19% -> 19%
where the time goes in v9:
time: 405 us; the launch traced here: 403 us
  Pallas kernels  381 us (94%)
  starting transfers between devices  10.3 us (3%)
  waiting for transfers between devices  4.88 us (1%)
  local copies, waits for them, and re-layouts  4.58 us (1%)
    pallas_call x1, Pallas kernels, gather_rows(): pl.pallas_call(functools.partial(gather_kernel, parts, groups, heads), na...  106 us
    pallas_call x1, Pallas kernels, reduce_gradients(): pl.pallas_call(functools.partial(reduce_kernel, parts, groups), name='red...  105 us
    pallas_call x1, Pallas kernels, middle(): pl.pallas_call(functools.partial(middle_kernel, parts, groups), name='mid...  62.6 us
    pallas_call x1, Pallas kernels, attention_backward(): pl.pallas_call(functools.partial(backward_kernel, heads), name='attention...  49.3 us
    pallas_call x1, Pallas kernels, update(): pl.pallas_call(functools.partial(update_kernel, rates), name='update_weig...  25.5 us
    pallas_call x1, Pallas kernels, attention_forward(): pl.pallas_call(functools.partial(forward_kernel, heads), name='attention_...  24.5 us
  transfers between devices with their start and end apart: 5, of which 4 were waited for; matrix products, arithmetic and copies ran while one was open for 1% of the time, Pallas kernels for 19%

profile of v9, /device:TPU:0, one launch (start us, length us, event | category | flops | bytes accessed | tf_op | source)
XLA Modules:
  0.0 403.2 jit_solution(11824098886859536645)
XLA Ops:
  0.7 1.3 broadcast_in_dim.15.small_ref
  2.0 0.7 slice.15
  2.7 0.6 broadcast_in_dim.16.gain_ref
  3.3 106.5 %gather_rows.1 = (bf16[8,512,1280]{2,1,0:T(8,128)(2,1)}, bf16[3,4,2,160,1280]{4,3,2,1,0:T(8,128)(2,1)}, bf16[2,480,1280]{2,1,0:T(8,128)(2,1)}, bf16[2,128,4096]{...) custom-call(bf16[512,1280]{1,0:T(8,128)(2,1)} %bitcast.17, ...), custom_call_target="tpu_custom_call" | custom-call | tf_op jit(solution)/shard_map/gather_rows/pallas_call | solution.py:380
  109.8 24.5 %attention_forward.1 = (f32[2,1,4096]{2,1,0:T(1,128)}, bf16[8,160,512]{2,1,0:T(8,128)(2,1)}) custom-call(s32[16]{0:T(128)} %bitcast.28, bf16[2,128,4096]{2,1,0:T(8,128)(2,1)} %get-tuple-element.68.qt_ref, bf16[2,80,4096]{2,1,0:T(8,128)(2,1)} %get-tuple-element.69.kt_ref.kt_in_ref, bf16[2,4096,128]{2,1,0:T(8,128)(2,1)} %get-tuple-element.70.kn_in_ref, ...), custom_call_target="tpu_custom_call" | custom-call | flops 17179869184 | bytes 5242880 | tf_op jit(solution)/shard_map/attention_forward/pallas_call | solution.py:686
  134.2 62.6 %middle.1 = (bf16[512,1280]{1,0:T(8,128)(2,1)}, f32[512,1280]{1,0:T(8,128)}, bf16[8,160,512]{2,1,0:T(8,128)(2,1)}, f32[1,1280]{1,0:T(1,128)}, bf16[3,160,1280]{2...) custom-call(bf16[8,160,512]{2,1,0:T(8,128)(2,1)} %get-tuple-element., ...), custom_call_target="tpu_custom_call" | custom-call | tf_op jit(solution)/shard_map/middle/pallas_call | solution.py:923
  196.9 1.7 collective-permute-start
  198.6 2.0 collective-permute-start.1
  200.6 0.7 collective-permute-start.2
  201.2 49.3 %attention_backward.1 = (bf16[8,480,512]{2,1,0:T(8,128)(2,1)}, f32[1,128]{1,0:T(1,128)}) custom-call(s32[16]{0:T(128)} %bitcast.29, bf16[2,128,4096]{2,1,0:T(8,128)(2,1)} %get-tuple-element.68.qt_ref, bf16[2,80,4096]{2,1,0:T(8,128)(2,1)} %get-tuple-element.69.kt_ref.kt_in_ref, bf16[2,4096,128]{2,1,0:T(8,128)(2,1)} %get-tuple-element.70.kn_in_ref, ...), custom_call_target="tpu_custom_call" | custom-call | flops 42949672960 | bytes 5242880 | tf_op jit(solution)/shard_map/attention_backward/pallas_call | solution.py:720
  250.5 0.0 copy-done.5
  250.5 0.1 reduce.1
  250.7 0.0 copy-done.4
  250.7 0.7 divide_multiply_fusion
  251.4 0.6 fusion.1.small_ref
  252.0 0.0 collective-permute-done.refs_1_
  252.0 1.8 collective-permute-done.1.refs_2_
  253.8 1.7 collective-permute-done.2.refs_3_
  255.5 0.0 copy-done.2
  255.5 104.5 %reduce_gradients.1 = (bf16[512,1280]{1,0:T(8,128)(2,1)}, bf16[512,1280]{1,0:T(8,128)(2,1)}, bf16[512,1280]{1,0:T(8,128)(2,1)}, bf16[8,320,480]{2,1,0:T(8,128)(2...) custom-call(bf16[4,2,480,512]{3,2,1,0:T(8,128)(2,1)} %bitcast.21, ...), custom_call_target="tpu_custom_call" | custom-call | tf_op jit(solution)/shard_map/reduce_gradients/pallas_call | solution.py:1295
  360.0 1.3 collective-permute-start.3
  361.3 4.6 %collective-permute-start.4 = (bf16[512,1280]{1,0:T(8,128)(2,1)}, bf16[512,1280]{1,0:T(8,128)(2,1)S(1)}, u32[]{:S(2)}, u32[]{:S(2)}) collective-permute-start(bf16[512,1280]{1,0:T(8,128)(2,1)} %get-tuple-element.91), channel_id=1, source_target_pairs={{0,8},{4,12},{8,16},{12,20},{16,24},{20,28},{1,9},{5,13},{9,17},{1... | collective-permute-start | bytes 3932168 | tf_op jit(solution)/shard_map/ppermute | solution.py:1519
  365.9 0.8 copy.41
  366.7 0.1 reshape.61
  366.8 25.5 %update_weights.1 = (f32[320,3840]{1,0:T(8,128)}, f32[320,3840]{1,0:T(8,128)}, f32[320,3840]{1,0:T(8,128)}, bf16[320,3840]{1,0:T(8,128)(2,1)}, f32[320,1280]{1,0...) custom-call(bf16[8,320,480]{2,1,0:T(8,128)(2,1)} %get-tuple-element., ...), custom_call_target="tpu_custom_call" | custom-call | flops 68812800 | bytes 68812800 | tf_op jit(solution)/shard_map/update_weights/pallas_call | solution.py:1397
  392.4 0.0 copy-done.6
  392.4 0.0 copy-done.7
  392.4 0.6 multiply_subtract_fusion
  393.0 0.1 collective-permute-done.3.down_ref
  393.1 1.3 collective-permute-done.4.up_ref
  394.4 1.1 copy-done.1
  395.5 7.7 %finish.1 = (bf16[512,1280]{1,0:T(8,128)(2,1)}, bf16[512,1280]{1,0:T(8,128)(2,1)}) custom-call(bf16[512,1280]{1,0:T(8,128)(2,1)} %bitcast.19, f32[512,1280]{1,0:T(8,128)} %get-tuple-element.74.dmid_ref, bf16[512,1280]{1,0:T(8,128)(2,1)} %get-tuple-element.89.own_ref, bf16[512,1280]{1,0:T(8,128)(2,1)} %copy-done, bf16[512,1280]{1,0:T(8,128)(2,1)} %copy-done.1, ...), custom_call_target="tpu_custom_call" | custom-call | tf_op jit(solution)/shard_map/finish/pallas_call | solution.py:1424
  (16 shorter events, 0.1 us)
Async XLA Ops:
  196.9 55.1 %collective-permute-start = (bf16[3,160,1280]{2,1,0:T(8,128)(2,1)}, bf16[3,160,1280]{2,1,0:T(8,128)(2,1)S(1)}, u32[]{:S(2)}, u32[]{:S(2)}) collective-permute-start(bf16[3,160,1280]{2,1,0:T(8,128)(2,1)} %get-tuple-element.86), channel_id=1, source_target_pairs={{0,1},{1,0},{2,3},{3,2},{4,5},{5,4},{6,7},{7,6},{8,9},{9,8},{10,11... | collective-permute-start | bytes 3686408 | tf_op jit(solution)/shard_map/ppermute | solution.py:1496
  198.6 55.2 %collective-permute-start.1 = (bf16[3,160,1280]{2,1,0:T(8,128)(2,1)}, bf16[3,160,1280]{2,1,0:T(8,128)(2,1)S(1)}, u32[]{:S(2)}, u32[]{:S(2)}) collective-permute-start(bf16[3,160,1280]{2,1,0:T(8,128)(2,1)} %get-tuple-element.87), channel_id=1, source_target_pairs={{0,2},{1,3},{2,0},{3,1},{4,6},{5,7},{6,4},{7,5},{8,10},{9,11},{10,... | collective-permute-start | bytes 3686408 | tf_op jit(solution)/shard_map/ppermute | solution.py:1496
  200.6 54.9 %collective-permute-start.2 = (bf16[3,160,1280]{2,1,0:T(8,128)(2,1)}, bf16[3,160,1280]{2,1,0:T(8,128)(2,1)}, u32[]{:S(2)}, u32[]{:S(2)}) collective-permute-start(bf16[3,160,1280]{2,1,0:T(8,128)(2,1)} %get-tuple-element.88), channel_id=1, source_target_pairs={{0,3},{1,2},{2,1},{3,0},{4,7},{5,6},{6,5},{7,4},{8,11},{9,10},{10,... | collective-permute-start | bytes 3686408 | tf_op jit(solution)/shard_map/ppermute | solution.py:1496
  201.2 49.3 %copy-start.5 = (f32[80,1]{1,0:T(8,128)S(1)}, f32[80,1]{1,0:T(8,128)}, u32[]{:S(2)}) copy-start(f32[80,1]{1,0:T(8,128)} %get-tuple-element.78.factor_ref) | copy-start | bytes 964
  201.2 49.4 %copy-start.8 = (f32[1,1280]{1,0:T(1,128)S(1)}, f32[1,1280]{1,0:T(1,128)}, u32[]{:S(2)}) copy-start(f32[1,1280]{1,0:T(1,128)} %get-tuple-element.83) | copy-start | bytes 15364
  201.2 49.4 %copy-start.4 = (f32[2640]{0:T(1024)S(1)}, f32[2640]{0:T(1024)}, u32[]{:S(2)}) copy-start(f32[2640]{0:T(1024)} %param.33) | copy-start | bytes 31684
  252.0 3.5 copy-start.2
  253.8 1.7 copy-start.3
  360.0 33.1 %collective-permute-start.3 = (bf16[512,1280]{1,0:T(8,128)(2,1)}, bf16[512,1280]{1,0:T(8,128)(2,1)S(1)}, u32[]{:S(2)}, u32[]{:S(2)}) collective-permute-start(bf16[512,1280]{1,0:T(8,128)(2,1)} %get-tuple-element.90), channel_id=1, source_target_pairs={{8,0},{12,4},{16,8},{20,12},{24,16},{28,20},{9,1},{13,5},{17,9},{2... | collective-permute-start | bytes 3932168 | tf_op jit(solution)/shard_map/ppermute | solution.py:1518
  361.3 33.1 %collective-permute-start.4 = (bf16[512,1280]{1,0:T(8,128)(2,1)}, bf16[512,1280]{1,0:T(8,128)(2,1)S(1)}, u32[]{:S(2)}, u32[]{:S(2)}) collective-permute-start(bf16[512,1280]{1,0:T(8,128)(2,1)} %get-tuple-element.91), channel_id=1, source_target_pairs={{0,8},{4,12},{8,16},{12,20},{16,24},{20,28},{1,9},{5,13},{9,17},{1... | collective-permute-start | bytes 3932168 | tf_op jit(solution)/shard_map/ppermute | solution.py:1519
  366.8 25.6 %copy-start.6 = (f32[2640]{0:T(1024)S(1)}, f32[2640]{0:T(1024)}, u32[]{:S(2)}) copy-start(f32[2640]{0:T(1024)} %param.34) | copy-start | bytes 31684
  366.8 25.6 %copy-start.7 = (f32[2640]{0:T(1024)S(1)}, f32[2640]{0:T(1024)}, u32[]{:S(2)}) copy-start(f32[2640]{0:T(1024)} %param.35) | copy-start | bytes 31684
  393.1 1.3 copy-start
  394.4 1.1 copy-start.1

commit v10 on v9

--- a/solution.py
+++ b/solution.py
@@ -18,7 +18,7 @@
 PAD = 128
 EXTRA = 16
 TILE = CONT
-SCORE_BOUND = 96.0
+SCORE_BOUND = 95.0
 
 bf16 = jnp.bfloat16
 f32 = jnp.float32
@@ -127,6 +127,7 @@
     wcol_ref,
     gain_ref,
     factor_ref,
+    most_ref,
     qt_ref,
     kt_ref,
     vt_ref,
@@ -167,7 +168,6 @@
     for step in (1, chips - 1):
         peer = lax.rem(chip + step, chips) * 2 + core
         pl.semaphore_signal(barrier, inc=1, device_id={"ctx": peer})
-    pl.semaphore_wait(barrier, groups + 2)
 
     def send(source, target, sems, device):
         return pltpu.make_async_remote_copy(
@@ -233,6 +233,7 @@
         stage.start()
     rows = x_ref[...].astype(f32)
     rows_ref[here] = (rows * rms_scale(rows)).astype(bf16)
+    pl.semaphore_wait(barrier, groups + 2)
 
     def forward(way, step, piece, part):
         @pl.when((chip < chips - 1) if way else (chip > 0))
@@ -279,6 +280,8 @@
     extra = jnp.where(extra_row < 3, 1.0, 0.0)
     spare = jnp.zeros((PAD - HD, BLOCK), bf16)
 
+    most_ref[...] = jnp.zeros(most_ref.shape, f32)
+
     def project(piece, part):
         slot = piece * halves + part
         to = block_at(slot)
@@ -288,7 +291,12 @@
                 result[share * width + head * HD : share * width + (head + 1) * HD]
                 for share in range(3)
             )
-            qt_ref[head, :HD, to] = (query * factor_ref[...]).astype(bf16)
+            query = query * factor_ref[...]
+            for row, rows in enumerate((query, key)):
+                most_ref[row : row + 1] = jnp.maximum(
+                    most_ref[row : row + 1], jnp.sum(rows * rows, axis=0, keepdims=True)
+                )
+            qt_ref[head, :HD, to] = query.astype(bf16)
             qt_ref[head, HD:, to] = spare
             kt_ref[head, :, to] = key.astype(bf16)
             vt_ref[head, :HD, to] = value.astype(bf16)
@@ -392,9 +400,10 @@
             jax.ShapeDtypeStruct((held, 3 * heads * HD), bf16),
             jax.ShapeDtypeStruct((held, 1), f32),
             jax.ShapeDtypeStruct((HD, 1), f32),
+            jax.ShapeDtypeStruct((8, BLOCK), f32),
         ],
         in_specs=in_vmem(1) + [anywhere] * 4 + in_vmem(1),
-        out_specs=[anywhere] * 2 + in_vmem(1) + [anywhere] * 5 + in_vmem(3),
+        out_specs=[anywhere] * 2 + in_vmem(1) + [anywhere] * 5 + in_vmem(4),
         scratch_shapes=[
             pltpu.VMEM((heads, PAD, tokens), bf16),
             pltpu.VMEM((heads, HD, tokens), bf16),
@@ -429,8 +438,8 @@
 def forward_kernel(
     heads,
     order_ref,
+    most_ref,
     qt_ref,
-    kt_ref,
     kn_in_ref,
     vt_in_ref,
     lse_ref,
@@ -453,16 +462,9 @@
     num_tiles = tokens // TILE
     prompt_tiles = num_tiles // 2
 
-    def longest(ref):
-        def visit(slot, most):
-            rows = [ref[head, :HD, block_at(slot)].astype(f32) for head in range(heads)]
-            sums = [jnp.sum(row * row, axis=0, keepdims=True) for row in rows]
-            return functools.reduce(jnp.maximum, sums, most)
-
-        return jnp.max(lax.fori_loop(0, tokens // BLOCK, visit, jnp.zeros((1, BLOCK), f32)))
-
-    bounded = longest(qt_ref) * longest(kt_ref) <= SCORE_BOUND * SCORE_BOUND
-
+    bounded = (
+        jnp.max(most_ref[0:1]) * jnp.max(most_ref[1:2]) <= SCORE_BOUND * SCORE_BOUND
+    )
     for load in loads:
         load.wait()
 
@@ -681,7 +683,7 @@
     return pltpu.CompilerParams(vmem_limit_bytes=60 * 1024 * 1024)
 
 
-def attention_forward(order, qt, kt, kn, vt, parts):
+def attention_forward(order, most, qt, kn, vt, parts):
     heads, tokens = kn.shape[:2]
     return pl.pallas_call(
         functools.partial(forward_kernel, heads),
@@ -704,7 +706,7 @@
         ],
         compiler_params=params(),
         cost_estimate=attention_cost(heads, tokens, 2),
-    )(order, qt, kt, kn, vt)
+    )(order, most, qt, kn, vt)
 
 
 def attention_cost(heads, tokens, passes):
@@ -1031,7 +1033,6 @@
         pl.semaphore_signal(barrier, inc=1, device_id={"ctx": peer})
     for peer in group_peers:
         pl.semaphore_signal(barrier, inc=1, device_id={"fsdp": peer})
-    pl.semaphore_wait(barrier, parts + groups - 2)
 
     def send(source, target, sems, device):
         return pltpu.make_async_remote_copy(
@@ -1066,19 +1067,22 @@
             {"ctx": 2 * peer + core},
         )
 
-    for index in range(chips):
-        pair_copy(index).start()
-    for load in loads:
+    for load in loads[:groups]:
         load.wait()
     share = mlp_ref.shape[2]
     for matrix in range(3):
-        total = functools.reduce(jnp.add, [chunk_ref[step, matrix].astype(f32) for step in range(groups)])
+        total = functools.reduce(
+            jnp.add, [chunk_ref[step, matrix].astype(f32) for step in range(groups)]
+        )
         for index in range(chips):
             mlp_ref[index, matrix] = total[index * share : (index + 1) * share].astype(bf16)
+    pl.semaphore_wait(barrier, parts + groups - 2)
     for peer in chip_peers:
         m_copy(peer, chip).start()
     for index in range(chips):
-        pair_copy(index).wait_recv()
+        pair_copy(index).start()
+    for load in loads[groups:]:
+        load.wait()
 
     rows_half = own_ref.shape[0] // 2
 
@@ -1184,6 +1188,8 @@
             {"fsdp": peer},
         )
 
+    for index in range(chips):
+        pair_copy(index).wait_recv()
     reduce_step(0)
 
     total_ref[...] = jnp.zeros(total_ref.shape, f32)
@@ -1406,11 +1412,14 @@
     )(qkv, gain, mlp, *arrays)
 
 
-def finish_kernel(x_ref, dmid_ref, own_ref, down_ref, up_ref, layer_ref, out_ref, same_ref):
+def finish_kernel(down_ref, up_ref, own_ref, x_ref, dmid_ref, layer_ref, out_ref, same_ref):
+    here = pl.ds(pl.multiple_of(pl.program_id(0) * PAD, PAD), PAD)
     rows = x_ref[...].astype(f32)
     scale = rms_scale(rows)
     unit = rows * scale
-    dunit = own_ref[...].astype(f32) + down_ref[...].astype(f32) + up_ref[...].astype(f32)
+    dunit = (
+        own_ref[...].astype(f32) + down_ref[here, :].astype(f32) + up_ref[here, :].astype(f32)
+    )
     grad = dmid_ref[...] + scale * (
         dunit - unit * jnp.mean(dunit * unit, axis=-1, keepdims=True)
     )
@@ -1420,15 +1429,15 @@
 
 def finish(*arrays):
     rows = arrays[0].shape[0]
-    spec = pl.BlockSpec((PAD // 2, D), lambda i: (i, 0))
+    spec = pl.BlockSpec((PAD, D), lambda i: (i, 0))
     return pl.pallas_call(
         finish_kernel,
         name="finish",
-        grid=(2 * rows // PAD,),
-        in_specs=[spec] * len(arrays),
+        grid=(rows // PAD,),
+        in_specs=in_vmem(2) + [spec] * 4,
         out_specs=[spec] * 2,
         out_shape=[jax.ShapeDtypeStruct((rows, D), bf16)] * 2,
-        compiler_params=params(),
+        compiler_params=pltpu.CompilerParams(vmem_limit_bytes=40 * 1024 * 1024),
     )(*arrays)
 
 
@@ -1477,10 +1486,11 @@
         w_columns,
         gain_rows,
         factor_two,
+        most,
     ) = gather_rows(
         parts, groups, heads, inputs[0], w_qkv, w_out, w_up, w_down, small_params[None]
     )
-    lse, mixed = attention_forward(order, qt, kt, kn, vt, parts)
+    lse, mixed = attention_forward(order, most, qt, kn, vt, parts)
     kept = (qt, kt, kn, vn, lse)
     output, dmid, dmixed, gain_two_grad, *chunks = middle(
         parts,
@@ -1544,7 +1554,7 @@
     rest = jnp.sum(flat[:, lanes : lanes + D + HD], axis=0)
     small_total = jnp.concatenate([flat[:, :rows].reshape(D), rest])
     small_set = adamw(small_params, small_m, small_v, small_total, small_rate, 0.0)
-    input_grad, output = finish(inputs[0], dmid, own_part, got_down, got_up, output)
+    input_grad, output = finish(got_down, got_up, own_part, inputs[0], dmid, output)
     return (
         output[None],
         input_grad[None],

time: 405 us -> 401 us (level)
  Pallas kernels: 381 us -> 376 us
  transfers between devices with their start and end apart: 5 -> 5, of which waited for: 4 -> 1; matrix products, arithmetic and copies ran while one was open for 1% -> 1% of each run, Pallas kernels for 19% -> 19%
where the time goes in v10:
time: 401 us; the launch traced here: 400 us
  Pallas kernels  376 us (94%)
  starting transfers between devices  10.6 us (3%)
  local copies, waits for them, and re-layouts  7.13 us (2%)
    pallas_call x1, Pallas kernels, gather_rows(): pl.pallas_call(functools.partial(gather_kernel, parts, groups, heads), na...  105 us
    pallas_call x1, Pallas kernels, reduce_gradients(): pl.pallas_call(functools.partial(reduce_kernel, parts, groups), name='red...  104 us
    pallas_call x1, Pallas kernels, middle(): pl.pallas_call(functools.partial(middle_kernel, parts, groups), name='mid...  62.7 us
    pallas_call x1, Pallas kernels, attention_backward(): pl.pallas_call(functools.partial(backward_kernel, heads), name='attention...  49.3 us
    pallas_call x1, Pallas kernels, update(): pl.pallas_call(functools.partial(update_kernel, rates), name='update_weig...  26.1 us
    pallas_call x1, Pallas kernels, attention_forward(): pl.pallas_call(functools.partial(forward_kernel, heads), name='attention_...  24.2 us
  transfers between devices with their start and end apart: 5, of which 1 were waited for; matrix products, arithmetic and copies ran while one was open for 1% of the time, Pallas kernels for 19%

profile of v10, /device:TPU:0, one launch (start us, length us, event | category | flops | bytes accessed | tf_op | source)
XLA Modules:
  0.0 400.4 jit_solution(11011842324717515717)
XLA Ops:
  0.7 1.3 broadcast_in_dim.15.small_ref
  2.0 0.7 slice.15
  2.7 0.6 broadcast_in_dim.16.gain_ref
  3.3 105.4 %gather_rows.1 = (bf16[8,512,1280]{2,1,0:T(8,128)(2,1)}, bf16[3,4,2,160,1280]{4,3,2,1,0:T(8,128)(2,1)}, bf16[2,480,1280]{2,1,0:T(8,128)(2,1)}, bf16[2,128,4096]{...) custom-call(bf16[512,1280]{1,0:T(8,128)(2,1)} %bitcast.17, ...), custom_call_target="tpu_custom_call" | custom-call | tf_op jit(solution)/shard_map/gather_rows/pallas_call | solution.py:388
  108.6 24.2 %attention_forward.1 = (f32[2,1,4096]{2,1,0:T(1,128)}, bf16[8,160,512]{2,1,0:T(8,128)(2,1)}) custom-call(s32[16]{0:T(128)} %bitcast.28, f32[8,256]{1,0:T(8,128)} %get-tuple-element.73.most_ref, bf16[2,128,4096]{2,1,0:T(8,128)(2,1)} %get-tuple-element.69.qt_ref, bf16[2,4096,128]{2,1,0:T(8,128)(2,1)} %get-tuple-element.71.kn_in_ref, ...), custom_call_target="tpu_custom_call" | custom-call | flops 17179869184 | bytes 5242880 | tf_op jit(solution)/shard_map/attention_forward/pallas_call | solution.py:688
  132.8 62.7 %middle.1 = (bf16[512,1280]{1,0:T(8,128)(2,1)}, f32[512,1280]{1,0:T(8,128)}, bf16[8,160,512]{2,1,0:T(8,128)(2,1)}, f32[1,1280]{1,0:T(1,128)}, bf16[3,160,1280]{2...) custom-call(bf16[8,160,512]{2,1,0:T(8,128)(2,1)} %get-tuple-element., ...), custom_call_target="tpu_custom_call" | custom-call | tf_op jit(solution)/shard_map/middle/pallas_call | solution.py:925
  195.5 1.8 collective-permute-start
  197.3 0.8 collective-permute-start.1
  198.1 1.0 collective-permute-start.2
  199.2 49.3 %attention_backward.1 = (bf16[8,480,512]{2,1,0:T(8,128)(2,1)}, f32[1,128]{1,0:T(1,128)}) custom-call(s32[16]{0:T(128)} %bitcast.29, bf16[2,128,4096]{2,1,0:T(8,128)(2,1)} %get-tuple-element.69.qt_ref, bf16[2,80,4096]{2,1,0:T(8,128)(2,1)} %get-tuple-element.70.kt_in_ref, bf16[2,4096,128]{2,1,0:T(8,128)(2,1)} %get-tuple-element.71.kn_in_ref, ...), custom_call_target="tpu_custom_call" | custom-call | flops 42949672960 | bytes 5242880 | tf_op jit(solution)/shard_map/attention_backward/pallas_call | solution.py:722
  248.5 0.0 copy-done.7
  248.5 0.1 reduce.1
  248.6 0.0 copy-done.10
  248.6 0.0 copy-done.6
  248.7 0.7 divide_multiply_fusion
  249.3 0.6 fusion.1.small_ref
  249.9 0.0 collective-permute-done.refs_1_
  250.0 3.5 collective-permute-done.1.refs_2_
  253.5 0.0 collective-permute-done.2.refs_3_
  253.5 1.0 copy-done.5
  254.5 104.2 %reduce_gradients.1 = (bf16[512,1280]{1,0:T(8,128)(2,1)}, bf16[512,1280]{1,0:T(8,128)(2,1)}, bf16[512,1280]{1,0:T(8,128)(2,1)}, bf16[8,320,480]{2,1,0:T(8,128)(2...) custom-call(bf16[4,2,480,512]{3,2,1,0:T(8,128)(2,1)} %bitcast.21, ...), custom_call_target="tpu_custom_call" | custom-call | tf_op jit(solution)/shard_map/reduce_gradients/pallas_call | solution.py:1301
  358.7 1.3 collective-permute-start.3
  360.0 5.6 %collective-permute-start.4 = (bf16[512,1280]{1,0:T(8,128)(2,1)}, bf16[512,1280]{1,0:T(8,128)(2,1)}, u32[]{:S(2)}, u32[]{:S(2)}) collective-permute-start(bf16[512,1280]{1,0:T(8,128)(2,1)} %get-tuple-element.91), channel_id=1, source_target_pairs={{0,8},{4,12},{8,16},{12,20},{16,24},{20,28},{1,9},{5,13},{9,17},{1... | collective-permute-start | bytes 3932168 | tf_op jit(solution)/shard_map/ppermute | solution.py:1529
  365.7 0.8 copy.41
  366.5 0.1 reshape.61
  366.6 26.1 %update_weights.1 = (f32[320,3840]{1,0:T(8,128)}, f32[320,3840]{1,0:T(8,128)}, f32[320,3840]{1,0:T(8,128)}, bf16[320,3840]{1,0:T(8,128)(2,1)}, f32[320,1280]{1,0...) custom-call(bf16[8,320,480]{2,1,0:T(8,128)(2,1)} %get-tuple-element., ...), custom_call_target="tpu_custom_call" | custom-call | flops 68812800 | bytes 68812800 | tf_op jit(solution)/shard_map/update_weights/pallas_call | solution.py:1403
  392.7 0.6 multiply_subtract_fusion
  393.3 0.0 collective-permute-done.3.down_ref
  393.3 0.0 collective-permute-done.4.up_ref
  393.4 1.3 copy-done.2
  394.7 1.3 copy-done.3
  396.0 4.5 %finish.1 = (bf16[512,1280]{1,0:T(8,128)(2,1)}, bf16[512,1280]{1,0:T(8,128)(2,1)}) custom-call(bf16[512,1280]{1,0:T(8,128)(2,1)} %collective-permute-done.3.down_ref, bf16[512,1280]{1,0:T(8,128)(2,1)} %collective-permute-done.4.up_ref, bf16[512,1280]{1,0:T(8,128)(2,1)S(1)} %copy-done.3, bf16[512,1280]{1,0:T(8,128)(2,1)S(1)} %bitcast.19, ...), custom_call_target="tpu_custom_call" | custom-call | tf_op jit(solution)/shard_map/finish/pallas_call | solution.py:1433
  (20 shorter events, 0.1 us)
Async XLA Ops:
  195.5 54.4 %collective-permute-start = (bf16[3,160,1280]{2,1,0:T(8,128)(2,1)}, bf16[3,160,1280]{2,1,0:T(8,128)(2,1)S(1)}, u32[]{:S(2)}, u32[]{:S(2)}) collective-permute-start(bf16[3,160,1280]{2,1,0:T(8,128)(2,1)} %get-tuple-element.87), channel_id=1, source_target_pairs={{0,1},{1,0},{2,3},{3,2},{4,5},{5,4},{6,7},{7,6},{8,9},{9,8},{10,11... | collective-permute-start | bytes 3686408 | tf_op jit(solution)/shard_map/ppermute | solution.py:1506
  197.3 56.2 %collective-permute-start.1 = (bf16[3,160,1280]{2,1,0:T(8,128)(2,1)}, bf16[3,160,1280]{2,1,0:T(8,128)(2,1)S(1)}, u32[]{:S(2)}, u32[]{:S(2)}) collective-permute-start(bf16[3,160,1280]{2,1,0:T(8,128)(2,1)} %get-tuple-element.88), channel_id=1, source_target_pairs={{0,2},{1,3},{2,0},{3,1},{4,6},{5,7},{6,4},{7,5},{8,10},{9,11},{10,... | collective-permute-start | bytes 3686408 | tf_op jit(solution)/shard_map/ppermute | solution.py:1506
  198.1 55.4 %collective-permute-start.2 = (bf16[3,160,1280]{2,1,0:T(8,128)(2,1)}, bf16[3,160,1280]{2,1,0:T(8,128)(2,1)}, u32[]{:S(2)}, u32[]{:S(2)}) collective-permute-start(bf16[3,160,1280]{2,1,0:T(8,128)(2,1)} %get-tuple-element.89), channel_id=1, source_target_pairs={{0,3},{1,2},{2,1},{3,0},{4,7},{5,6},{6,5},{7,4},{8,11},{9,10},{10,... | collective-permute-start | bytes 3686408 | tf_op jit(solution)/shard_map/ppermute | solution.py:1506
  199.2 49.3 %copy-start.7 = (f32[80,1]{1,0:T(8,128)S(1)}, f32[80,1]{1,0:T(8,128)}, u32[]{:S(2)}) copy-start(f32[80,1]{1,0:T(8,128)} %get-tuple-element.79.factor_ref) | copy-start | bytes 964
  199.2 49.4 %copy-start.10 = (f32[1,1280]{1,0:T(1,128)S(1)}, f32[1,1280]{1,0:T(1,128)}, u32[]{:S(2)}) copy-start(f32[1,1280]{1,0:T(1,128)} %get-tuple-element.84) | copy-start | bytes 15364
  199.2 49.5 %copy-start.6 = (f32[2640]{0:T(1024)S(1)}, f32[2640]{0:T(1024)}, u32[]{:S(2)}) copy-start(f32[2640]{0:T(1024)} %param.33) | copy-start | bytes 31684
  249.9 3.6 copy-start.4
  253.5 1.0 copy-start.5
  358.7 34.6 %collective-permute-start.3 = (bf16[512,1280]{1,0:T(8,128)(2,1)}, bf16[512,1280]{1,0:T(8,128)(2,1)}, u32[]{:S(2)}, u32[]{:S(2)}) collective-permute-start(bf16[512,1280]{1,0:T(8,128)(2,1)} %get-tuple-element.90), channel_id=1, source_target_pairs={{8,0},{12,4},{16,8},{20,12},{24,16},{28,20},{9,1},{13,5},{17,9},{2... | collective-permute-start | bytes 3932168 | tf_op jit(solution)/shard_map/ppermute | solution.py:1528
  360.0 33.3 %collective-permute-start.4 = (bf16[512,1280]{1,0:T(8,128)(2,1)}, bf16[512,1280]{1,0:T(8,128)(2,1)}, u32[]{:S(2)}, u32[]{:S(2)}) collective-permute-start(bf16[512,1280]{1,0:T(8,128)(2,1)} %get-tuple-element.91), channel_id=1, source_target_pairs={{0,8},{4,12},{8,16},{12,20},{16,24},{20,28},{1,9},{5,13},{9,17},{1... | collective-permute-start | bytes 3932168 | tf_op jit(solution)/shard_map/ppermute | solution.py:1529
  366.5 26.1 %copy-start.8 = (f32[2640]{0:T(1024)S(1)}, f32[2640]{0:T(1024)}, u32[]{:S(2)}) copy-start(f32[2640]{0:T(1024)} %param.34) | copy-start | bytes 31684
  366.5 26.1 %copy-start.9 = (f32[2640]{0:T(1024)S(1)}, f32[2640]{0:T(1024)}, u32[]{:S(2)}) copy-start(f32[2640]{0:T(1024)} %param.35) | copy-start | bytes 31684
  366.5 26.8 %copy-start = (bf16[1,512,1280]{2,1,0:T(8,128)(2,1)S(1)}, bf16[1,512,1280]{2,1,0:T(8,128)(2,1)}, u32[]{:S(2)}) copy-start(bf16[1,512,1280]{2,1,0:T(8,128)(2,1)} %param.18) | copy-start | bytes 3932164
  366.6 26.8 %copy-start.1 = (f32[512,1280]{1,0:T(8,128)S(1)}, f32[512,1280]{1,0:T(8,128)}, u32[]{:S(2)}) copy-start(f32[512,1280]{1,0:T(8,128)} %get-tuple-element.93.dmid_ref) | copy-start | bytes 7864324
  393.3 1.3 copy-start.2
  394.7 1.3 copy-start.3

commit v11 on v10

--- a/solution.py
+++ b/solution.py
@@ -679,8 +679,8 @@
     return [pl.BlockSpec(memory_space=pltpu.VMEM)] * count
 
 
-def params():
-    return pltpu.CompilerParams(vmem_limit_bytes=60 * 1024 * 1024)
+def params(mebibytes):
+    return pltpu.CompilerParams(vmem_limit_bytes=mebibytes * 1024 * 1024)
 
 
 def attention_forward(order, most, qt, kn, vt, parts):
@@ -704,7 +704,7 @@
             pltpu.VMEM((heads, 1, TILE), f32),
             pltpu.SemaphoreType.DMA((2,)),
         ],
-        compiler_params=params(),
+        compiler_params=params(60),
         cost_estimate=attention_cost(heads, tokens, 2),
     )(order, most, qt, kn, vt)
 
@@ -744,7 +744,7 @@
             pltpu.VMEM((heads, HD, PAD), f32),
             pltpu.SemaphoreType.DMA((3,)),
         ],
-        compiler_params=params(),
+        compiler_params=params(60),
         cost_estimate=attention_cost(heads, tokens, 5),
     )(order, qt, kt, kn, vn, lse, mixed, dmixed, factor)
 
@@ -1407,7 +1407,7 @@
         in_specs=in_specs,
         out_specs=specs,
         out_shape=shapes,
-        compiler_params=params(),
+        compiler_params=params(55),
         cost_estimate=pl.CostEstimate(flops=moved, bytes_accessed=moved, transcendentals=0),
     )(qkv, gain, mlp, *arrays)
 
@@ -1437,7 +1437,7 @@
         in_specs=in_vmem(2) + [spec] * 4,
         out_specs=[spec] * 2,
         out_shape=[jax.ShapeDtypeStruct((rows, D), bf16)] * 2,
-        compiler_params=pltpu.CompilerParams(vmem_limit_bytes=40 * 1024 * 1024),
+        compiler_params=params(40),
     )(*arrays)
 
 

time: 401 us -> 396 us (0.988)
  transfers between devices with their start and end apart: 5 -> 5, of which waited for: 1 -> 2; matrix products, arithmetic and copies ran while one was open for 1% -> 1% of each run, Pallas kernels for 19% -> 19%
where the time goes in v11:
time: 396 us
  Pallas kernels  375 us (95%)
  starting transfers between devices  9.53 us (2%)
  local copies, waits for them, and re-layouts  4.53 us (1%)
  waiting for transfers between devices  4.07 us (1%)
    pallas_call x1, Pallas kernels, gather_rows(): pl.pallas_call(functools.partial(gather_kernel, parts, groups, heads), na...  105 us
    pallas_call x1, Pallas kernels, reduce_gradients(): pl.pallas_call(functools.partial(reduce_kernel, parts, groups), name='red...  104 us
    pallas_call x1, Pallas kernels, middle(): pl.pallas_call(functools.partial(middle_kernel, parts, groups), name='mid...  62.7 us
    pallas_call x1, Pallas kernels, attention_backward(): pl.pallas_call(functools.partial(backward_kernel, heads), name='attention...  49 us
    pallas_call x1, Pallas kernels, update(): pl.pallas_call(functools.partial(update_kernel, rates), name='update_weig...  26.8 us
    pallas_call x1, Pallas kernels, attention_forward(): pl.pallas_call(functools.partial(forward_kernel, heads), name='attention_...  24.1 us
  transfers between devices with their start and end apart: 5, of which 2 were waited for; matrix products, arithmetic and copies ran while one was open for 1% of the time, Pallas kernels for 19%

profile of v11, /device:TPU:0, one launch (start us, length us, event | category | flops | bytes accessed | tf_op | source)
XLA Modules:
  0.0 395.9 jit_solution(1883716504551548517)
XLA Ops:
  0.7 1.3 broadcast_in_dim.15.small_ref
  2.0 0.7 slice.15
  2.7 0.6 broadcast_in_dim.16.gain_ref
  3.3 105.4 %gather_rows.1 = (bf16[8,512,1280]{2,1,0:T(8,128)(2,1)}, bf16[3,4,2,160,1280]{4,3,2,1,0:T(8,128)(2,1)}, bf16[2,480,1280]{2,1,0:T(8,128)(2,1)}, bf16[2,128,4096]{...) custom-call(bf16[512,1280]{1,0:T(8,128)(2,1)} %bitcast.17, ...), custom_call_target="tpu_custom_call" | custom-call | tf_op jit(solution)/shard_map/gather_rows/pallas_call | solution.py:388
  108.7 24.1 %attention_forward.1 = (f32[2,1,4096]{2,1,0:T(1,128)}, bf16[8,160,512]{2,1,0:T(8,128)(2,1)}) custom-call(s32[16]{0:T(128)} %bitcast.28, f32[8,256]{1,0:T(8,128)} %get-tuple-element.73.most_ref, bf16[2,128,4096]{2,1,0:T(8,128)(2,1)} %get-tuple-element.69.qt_ref, bf16[2,4096,128]{2,1,0:T(8,128)(2,1)} %get-tuple-element.71.kn_in_ref, ...), custom_call_target="tpu_custom_call" | custom-call | flops 17179869184 | bytes 5242880 | tf_op jit(solution)/shard_map/attention_forward/pallas_call | solution.py:688
  132.8 62.7 %middle.1 = (bf16[512,1280]{1,0:T(8,128)(2,1)}, f32[512,1280]{1,0:T(8,128)}, bf16[8,160,512]{2,1,0:T(8,128)(2,1)}, f32[1,1280]{1,0:T(1,128)}, bf16[3,160,1280]{2...) custom-call(bf16[8,160,512]{2,1,0:T(8,128)(2,1)} %get-tuple-element., ...), custom_call_target="tpu_custom_call" | custom-call | tf_op jit(solution)/shard_map/middle/pallas_call | solution.py:925
  195.4 1.8 collective-permute-start
  197.3 0.8 collective-permute-start.1
  198.1 1.0 collective-permute-start.2
  199.1 49.0 %attention_backward.1 = (bf16[8,480,512]{2,1,0:T(8,128)(2,1)}, f32[1,128]{1,0:T(1,128)}) custom-call(s32[16]{0:T(128)} %bitcast.29, bf16[2,128,4096]{2,1,0:T(8,128)(2,1)} %get-tuple-element.69.qt_ref, bf16[2,80,4096]{2,1,0:T(8,128)(2,1)} %get-tuple-element.70.kt_in_ref, bf16[2,4096,128]{2,1,0:T(8,128)(2,1)} %get-tuple-element.71.kn_in_ref, ...), custom_call_target="tpu_custom_call" | custom-call | flops 42949672960 | bytes 5242880 | tf_op jit(solution)/shard_map/attention_backward/pallas_call | solution.py:722
  248.1 0.0 copy-done.7
  248.1 0.1 reduce.1
  248.2 0.0 copy-done.10
  248.2 0.0 copy-done.6
  248.2 0.7 divide_multiply_fusion
  248.9 0.6 fusion.1.small_ref
  249.5 0.0 collective-permute-done.refs_1_
  249.5 3.9 collective-permute-done.1.refs_2_
  253.5 0.0 collective-permute-done.2.refs_3_
  253.5 0.0 copy-done.4
  253.5 1.0 copy-done.5
  254.5 104.2 %reduce_gradients.1 = (bf16[512,1280]{1,0:T(8,128)(2,1)}, bf16[512,1280]{1,0:T(8,128)(2,1)}, bf16[512,1280]{1,0:T(8,128)(2,1)}, bf16[8,320,480]{2,1,0:T(8,128)(2...) custom-call(bf16[4,2,480,512]{3,2,1,0:T(8,128)(2,1)} %bitcast.21, ...), custom_call_target="tpu_custom_call" | custom-call | tf_op jit(solution)/shard_map/reduce_gradients/pallas_call | solution.py:1301
  358.7 1.3 collective-permute-start.3
  360.0 4.6 %collective-permute-start.4 = (bf16[512,1280]{1,0:T(8,128)(2,1)}, bf16[512,1280]{1,0:T(8,128)(2,1)S(1)}, u32[]{:S(2)}, u32[]{:S(2)}) collective-permute-start(bf16[512,1280]{1,0:T(8,128)(2,1)} %get-tuple-element.91), channel_id=1, source_target_pairs={{0,8},{4,12},{8,16},{12,20},{16,24},{20,28},{1,9},{5,13},{9,17},{1... | collective-permute-start | bytes 3932168 | tf_op jit(solution)/shard_map/ppermute | solution.py:1529
  364.7 0.8 copy.41
  365.4 0.1 reshape.61
  365.6 26.8 %update_weights.1 = (f32[320,3840]{1,0:T(8,128)}, f32[320,3840]{1,0:T(8,128)}, f32[320,3840]{1,0:T(8,128)}, bf16[320,3840]{1,0:T(8,128)(2,1)}, f32[320,1280]{1,0...) custom-call(bf16[8,320,480]{2,1,0:T(8,128)(2,1)} %get-tuple-element., ...), custom_call_target="tpu_custom_call" | custom-call | flops 68812800 | bytes 68812800 | tf_op jit(solution)/shard_map/update_weights/pallas_call | solution.py:1403
  392.4 0.6 multiply_subtract_fusion
  393.0 0.0 collective-permute-done.3.down_ref
  393.0 0.1 collective-permute-done.4.up_ref
  393.1 0.0 copy-done.1
  393.2 2.7 finish.1
  (20 shorter events, 0.1 us)
Async XLA Ops:
  195.4 54.1 %collective-permute-start = (bf16[3,160,1280]{2,1,0:T(8,128)(2,1)}, bf16[3,160,1280]{2,1,0:T(8,128)(2,1)S(1)}, u32[]{:S(2)}, u32[]{:S(2)}) collective-permute-start(bf16[3,160,1280]{2,1,0:T(8,128)(2,1)} %get-tuple-element.87), channel_id=1, source_target_pairs={{0,1},{1,0},{2,3},{3,2},{4,5},{5,4},{6,7},{7,6},{8,9},{9,8},{10,11... | collective-permute-start | bytes 3686408 | tf_op jit(solution)/shard_map/ppermute | solution.py:1506
  197.3 56.2 %collective-permute-start.1 = (bf16[3,160,1280]{2,1,0:T(8,128)(2,1)}, bf16[3,160,1280]{2,1,0:T(8,128)(2,1)S(1)}, u32[]{:S(2)}, u32[]{:S(2)}) collective-permute-start(bf16[3,160,1280]{2,1,0:T(8,128)(2,1)} %get-tuple-element.88), channel_id=1, source_target_pairs={{0,2},{1,3},{2,0},{3,1},{4,6},{5,7},{6,4},{7,5},{8,10},{9,11},{10,... | collective-permute-start | bytes 3686408 | tf_op jit(solution)/shard_map/ppermute | solution.py:1506
  198.1 55.4 %collective-permute-start.2 = (bf16[3,160,1280]{2,1,0:T(8,128)(2,1)}, bf16[3,160,1280]{2,1,0:T(8,128)(2,1)}, u32[]{:S(2)}, u32[]{:S(2)}) collective-permute-start(bf16[3,160,1280]{2,1,0:T(8,128)(2,1)} %get-tuple-element.89), channel_id=1, source_target_pairs={{0,3},{1,2},{2,1},{3,0},{4,7},{5,6},{6,5},{7,4},{8,11},{9,10},{10,... | collective-permute-start | bytes 3686408 | tf_op jit(solution)/shard_map/ppermute | solution.py:1506
  199.0 49.0 %copy-start.7 = (f32[80,1]{1,0:T(8,128)S(1)}, f32[80,1]{1,0:T(8,128)}, u32[]{:S(2)}) copy-start(f32[80,1]{1,0:T(8,128)} %get-tuple-element.79.factor_ref) | copy-start | bytes 964
  199.1 49.1 %copy-start.10 = (f32[1,1280]{1,0:T(1,128)S(1)}, f32[1,1280]{1,0:T(1,128)}, u32[]{:S(2)}) copy-start(f32[1,1280]{1,0:T(1,128)} %get-tuple-element.84) | copy-start | bytes 15364
  199.1 49.2 %copy-start.6 = (f32[2640]{0:T(1024)S(1)}, f32[2640]{0:T(1024)}, u32[]{:S(2)}) copy-start(f32[2640]{0:T(1024)} %param.33) | copy-start | bytes 31684
  249.5 3.9 copy-start.4
  253.5 1.0 copy-start.5
  358.7 34.3 %collective-permute-start.3 = (bf16[512,1280]{1,0:T(8,128)(2,1)}, bf16[512,1280]{1,0:T(8,128)(2,1)S(1)}, u32[]{:S(2)}, u32[]{:S(2)}) collective-permute-start(bf16[512,1280]{1,0:T(8,128)(2,1)} %get-tuple-element.90), channel_id=1, source_target_pairs={{8,0},{12,4},{16,8},{20,12},{24,16},{28,20},{9,1},{13,5},{17,9},{2... | collective-permute-start | bytes 3932168 | tf_op jit(solution)/shard_map/ppermute | solution.py:1528
  360.0 33.1 %collective-permute-start.4 = (bf16[512,1280]{1,0:T(8,128)(2,1)}, bf16[512,1280]{1,0:T(8,128)(2,1)S(1)}, u32[]{:S(2)}, u32[]{:S(2)}) collective-permute-start(bf16[512,1280]{1,0:T(8,128)(2,1)} %get-tuple-element.91), channel_id=1, source_target_pairs={{0,8},{4,12},{8,16},{12,20},{16,24},{20,28},{1,9},{5,13},{9,17},{1... | collective-permute-start | bytes 3932168 | tf_op jit(solution)/shard_map/ppermute | solution.py:1529
  365.5 26.8 %copy-start.8 = (f32[2640]{0:T(1024)S(1)}, f32[2640]{0:T(1024)}, u32[]{:S(2)}) copy-start(f32[2640]{0:T(1024)} %param.34) | copy-start | bytes 31684
  365.5 26.9 %copy-start.9 = (f32[2640]{0:T(1024)S(1)}, f32[2640]{0:T(1024)}, u32[]{:S(2)}) copy-start(f32[2640]{0:T(1024)} %param.35) | copy-start | bytes 31684
  365.5 27.6 %copy-start = (bf16[1,512,1280]{2,1,0:T(8,128)(2,1)S(1)}, bf16[1,512,1280]{2,1,0:T(8,128)(2,1)}, u32[]{:S(2)}) copy-start(bf16[1,512,1280]{2,1,0:T(8,128)(2,1)} %param.18) | copy-start | bytes 3932164
  365.5 27.6 %copy-start.1 = (f32[512,1280]{1,0:T(8,128)S(1)}, f32[512,1280]{1,0:T(8,128)}, u32[]{:S(2)}) copy-start(f32[512,1280]{1,0:T(8,128)} %get-tuple-element.93.dmid_ref) | copy-start | bytes 7864324
  365.5 27.6 %copy-start.2 = (bf16[512,1280]{1,0:T(8,128)(2,1)S(1)}, bf16[512,1280]{1,0:T(8,128)(2,1)}, u32[]{:S(2)}) copy-start(bf16[512,1280]{1,0:T(8,128)(2,1)} %get-tuple-element.94.layer_ref) | copy-start | bytes 3932164
  365.5 27.6 %copy-start.3 = (bf16[512,1280]{1,0:T(8,128)(2,1)S(1)}, bf16[512,1280]{1,0:T(8,128)(2,1)}, u32[]{:S(2)}) copy-start(bf16[512,1280]{1,0:T(8,128)(2,1)} %get-tuple-element.92.own_ref) | copy-start | bytes 3932164

commit v12 on v11

--- a/solution.py
+++ b/solution.py
@@ -246,10 +246,11 @@
         side_copy(chip, core, part).start()
     held = gain_ref.shape[0]
     lanes = -(-held // PAD) * PAD
-    gains = jnp.broadcast_to(small_ref[:, :D], (8, D))
+    gains = jnp.broadcast_to(small_ref[:D].reshape(1, D), (8, D))
     gains = pltpu.roll(gains, lax.rem(D - group * held, D), 1)[:1, :lanes]
     gain_ref[...] = jnp.broadcast_to(gains, (PAD, lanes)).T[:held, :1]
-    soft = jnp.log(1.0 + jnp.exp(small_ref[:, 2 * D :])) * (scale_base / math.sqrt(HD) * LOG2E)
+    scales = small_ref[2 * D :].reshape(1, HD)
+    soft = jnp.log(1.0 + jnp.exp(scales)) * (scale_base / math.sqrt(HD) * LOG2E)
     soft = jnp.concatenate([soft, jnp.zeros((1, PAD - HD), f32)], axis=1)
     factor_ref[...] = jnp.broadcast_to(soft, (PAD, PAD)).T[:HD, :1]
     shift = lax.rem(D - here * width, D)
@@ -1488,7 +1489,7 @@
         factor_two,
         most,
     ) = gather_rows(
-        parts, groups, heads, inputs[0], w_qkv, w_out, w_up, w_down, small_params[None]
+        parts, groups, heads, inputs[0], w_qkv, w_out, w_up, w_down, small_params
     )
     lse, mixed = attention_forward(order, most, qt, kn, vt, parts)
     kept = (qt, kt, kn, vn, lse)

time: 396 us -> 395 us (level)
  no operation moved by 1% of the time
where the time goes in v12:
time: 395 us
  Pallas kernels  375 us (95%)
  starting transfers between devices  9.5 us (2%)
  waiting for transfers between devices  4.03 us (1%)
    pallas_call x1, Pallas kernels, gather_rows(): pl.pallas_call(functools.partial(gather_kernel, parts, groups, heads), na...  105 us
    pallas_call x1, Pallas kernels, reduce_gradients(): pl.pallas_call(functools.partial(reduce_kernel, parts, groups), name='red...  104 us
    pallas_call x1, Pallas kernels, middle(): pl.pallas_call(functools.partial(middle_kernel, parts, groups), name='mid...  62.7 us
    pallas_call x1, Pallas kernels, attention_backward(): pl.pallas_call(functools.partial(backward_kernel, heads), name='attention...  49 us
    pallas_call x1, Pallas kernels, update(): pl.pallas_call(functools.partial(update_kernel, rates), name='update_weig...  26.8 us
    pallas_call x1, Pallas kernels, attention_forward(): pl.pallas_call(functools.partial(forward_kernel, heads), name='attention_...  24.1 us
  transfers between devices with their start and end apart: 5, of which 2 were waited for; matrix products, arithmetic and copies ran while one was open for 1% of the time, Pallas kernels for 19%

profile of v12, /device:TPU:0, one launch (start us, length us, event | category | flops | bytes accessed | tf_op | source)
XLA Modules:
  0.0 394.5 jit_solution(13674050880606549613)
XLA Ops:
  0.7 0.7 slice.15
  1.4 0.6 broadcast_in_dim.12.gain_ref
  2.0 105.4 %gather_rows.1 = (bf16[8,512,1280]{2,1,0:T(8,128)(2,1)}, bf16[3,4,2,160,1280]{4,3,2,1,0:T(8,128)(2,1)}, bf16[2,480,1280]{2,1,0:T(8,128)(2,1)}, bf16[2,128,4096]{...) custom-call(bf16[512,1280]{1,0:T(8,128)(2,1)} %bitcast.17, ...), custom_call_target="tpu_custom_call" | custom-call | tf_op jit(solution)/shard_map/gather_rows/pallas_call | solution.py:389
  107.4 24.1 %attention_forward.1 = (f32[2,1,4096]{2,1,0:T(1,128)}, bf16[8,160,512]{2,1,0:T(8,128)(2,1)}) custom-call(s32[16]{0:T(128)} %bitcast.28, f32[8,256]{1,0:T(8,128)} %get-tuple-element.73.most_ref, bf16[2,128,4096]{2,1,0:T(8,128)(2,1)} %get-tuple-element.69.qt_ref, bf16[2,4096,128]{2,1,0:T(8,128)(2,1)} %get-tuple-element.71.kn_in_ref, ...), custom_call_target="tpu_custom_call" | custom-call | flops 17179869184 | bytes 5242880 | tf_op jit(solution)/shard_map/attention_forward/pallas_call | solution.py:689
  131.5 62.7 %middle.1 = (bf16[512,1280]{1,0:T(8,128)(2,1)}, f32[512,1280]{1,0:T(8,128)}, bf16[8,160,512]{2,1,0:T(8,128)(2,1)}, f32[1,1280]{1,0:T(1,128)}, bf16[3,160,1280]{2...) custom-call(bf16[8,160,512]{2,1,0:T(8,128)(2,1)} %get-tuple-element., ...), custom_call_target="tpu_custom_call" | custom-call | tf_op jit(solution)/shard_map/middle/pallas_call | solution.py:926
  194.1 1.8 collective-permute-start
  195.9 0.7 collective-permute-start.1
  196.7 1.0 collective-permute-start.2
  197.7 49.0 %attention_backward.1 = (bf16[8,480,512]{2,1,0:T(8,128)(2,1)}, f32[1,128]{1,0:T(1,128)}) custom-call(s32[16]{0:T(128)} %bitcast.29, bf16[2,128,4096]{2,1,0:T(8,128)(2,1)} %get-tuple-element.69.qt_ref, bf16[2,80,4096]{2,1,0:T(8,128)(2,1)} %get-tuple-element.70.kt_in_ref, bf16[2,4096,128]{2,1,0:T(8,128)(2,1)} %get-tuple-element.71.kn_in_ref, ...), custom_call_target="tpu_custom_call" | custom-call | flops 42949672960 | bytes 5242880 | tf_op jit(solution)/shard_map/attention_backward/pallas_call | solution.py:723
  246.8 0.0 copy-done.7
  246.8 0.1 reduce.1
  246.9 0.0 copy-done.10
  246.9 0.0 copy-done.6
  246.9 0.7 divide_multiply_fusion
  247.6 0.6 fusion.1.small_ref
  248.2 0.0 collective-permute-done.refs_1_
  248.2 3.9 collective-permute-done.1.refs_2_
  252.1 0.0 collective-permute-done.2.refs_3_
  252.1 0.0 copy-done.4
  252.1 1.0 copy-done.5
  253.1 104.2 %reduce_gradients.1 = (bf16[512,1280]{1,0:T(8,128)(2,1)}, bf16[512,1280]{1,0:T(8,128)(2,1)}, bf16[512,1280]{1,0:T(8,128)(2,1)}, bf16[8,320,480]{2,1,0:T(8,128)(2...) custom-call(bf16[4,2,480,512]{3,2,1,0:T(8,128)(2,1)} %bitcast.21, ...), custom_call_target="tpu_custom_call" | custom-call | tf_op jit(solution)/shard_map/reduce_gradients/pallas_call | solution.py:1302
  357.4 1.3 collective-permute-start.3
  358.7 4.6 %collective-permute-start.4 = (bf16[512,1280]{1,0:T(8,128)(2,1)}, bf16[512,1280]{1,0:T(8,128)(2,1)S(1)}, u32[]{:S(2)}, u32[]{:S(2)}) collective-permute-start(bf16[512,1280]{1,0:T(8,128)(2,1)} %get-tuple-element.91), channel_id=1, source_target_pairs={{0,8},{4,12},{8,16},{12,20},{16,24},{20,28},{1,9},{5,13},{9,17},{1... | collective-permute-start | bytes 3932168 | tf_op jit(solution)/shard_map/ppermute | solution.py:1530
  363.3 0.8 copy.41
  364.1 0.1 reshape.61
  364.2 0.0 copy-start.2
  364.2 26.8 %update_weights.1 = (f32[320,3840]{1,0:T(8,128)}, f32[320,3840]{1,0:T(8,128)}, f32[320,3840]{1,0:T(8,128)}, bf16[320,3840]{1,0:T(8,128)(2,1)}, f32[320,1280]{1,0...) custom-call(bf16[8,320,480]{2,1,0:T(8,128)(2,1)} %get-tuple-element., ...), custom_call_target="tpu_custom_call" | custom-call | flops 68812800 | bytes 68812800 | tf_op jit(solution)/shard_map/update_weights/pallas_call | solution.py:1404
  391.0 0.6 multiply_subtract_fusion
  391.7 0.0 collective-permute-done.3.down_ref
  391.7 0.1 collective-permute-done.4.up_ref
  391.8 0.0 copy-done.1
  391.8 2.7 finish.1
  (19 shorter events, 0.1 us)
Async XLA Ops:
  194.1 54.1 %collective-permute-start = (bf16[3,160,1280]{2,1,0:T(8,128)(2,1)}, bf16[3,160,1280]{2,1,0:T(8,128)(2,1)S(1)}, u32[]{:S(2)}, u32[]{:S(2)}) collective-permute-start(bf16[3,160,1280]{2,1,0:T(8,128)(2,1)} %get-tuple-element.87), channel_id=1, source_target_pairs={{0,1},{1,0},{2,3},{3,2},{4,5},{5,4},{6,7},{7,6},{8,9},{9,8},{10,11... | collective-permute-start | bytes 3686408 | tf_op jit(solution)/shard_map/ppermute | solution.py:1507
  195.9 56.2 %collective-permute-start.1 = (bf16[3,160,1280]{2,1,0:T(8,128)(2,1)}, bf16[3,160,1280]{2,1,0:T(8,128)(2,1)S(1)}, u32[]{:S(2)}, u32[]{:S(2)}) collective-permute-start(bf16[3,160,1280]{2,1,0:T(8,128)(2,1)} %get-tuple-element.88), channel_id=1, source_target_pairs={{0,2},{1,3},{2,0},{3,1},{4,6},{5,7},{6,4},{7,5},{8,10},{9,11},{10,... | collective-permute-start | bytes 3686408 | tf_op jit(solution)/shard_map/ppermute | solution.py:1507
  196.7 55.4 %collective-permute-start.2 = (bf16[3,160,1280]{2,1,0:T(8,128)(2,1)}, bf16[3,160,1280]{2,1,0:T(8,128)(2,1)}, u32[]{:S(2)}, u32[]{:S(2)}) collective-permute-start(bf16[3,160,1280]{2,1,0:T(8,128)(2,1)} %get-tuple-element.89), channel_id=1, source_target_pairs={{0,3},{1,2},{2,1},{3,0},{4,7},{5,6},{6,5},{7,4},{8,11},{9,10},{10,... | collective-permute-start | bytes 3686408 | tf_op jit(solution)/shard_map/ppermute | solution.py:1507
  197.7 49.1 %copy-start.7 = (f32[80,1]{1,0:T(8,128)S(1)}, f32[80,1]{1,0:T(8,128)}, u32[]{:S(2)}) copy-start(f32[80,1]{1,0:T(8,128)} %get-tuple-element.79.factor_ref) | copy-start | bytes 964
  197.7 49.2 %copy-start.10 = (f32[1,1280]{1,0:T(1,128)S(1)}, f32[1,1280]{1,0:T(1,128)}, u32[]{:S(2)}) copy-start(f32[1,1280]{1,0:T(1,128)} %get-tuple-element.84) | copy-start | bytes 15364
  197.7 49.2 %copy-start.6 = (f32[2640]{0:T(1024)S(1)}, f32[2640]{0:T(1024)}, u32[]{:S(2)}) copy-start(f32[2640]{0:T(1024)} %small_ref.1) | copy-start | bytes 31684
  248.2 3.9 copy-start.4
  252.1 1.0 copy-start.5
  357.4 34.3 %collective-permute-start.3 = (bf16[512,1280]{1,0:T(8,128)(2,1)}, bf16[512,1280]{1,0:T(8,128)(2,1)S(1)}, u32[]{:S(2)}, u32[]{:S(2)}) collective-permute-start(bf16[512,1280]{1,0:T(8,128)(2,1)} %get-tuple-element.90), channel_id=1, source_target_pairs={{8,0},{12,4},{16,8},{20,12},{24,16},{28,20},{9,1},{13,5},{17,9},{2... | collective-permute-start | bytes 3932168 | tf_op jit(solution)/shard_map/ppermute | solution.py:1529
  358.7 33.1 %collective-permute-start.4 = (bf16[512,1280]{1,0:T(8,128)(2,1)}, bf16[512,1280]{1,0:T(8,128)(2,1)S(1)}, u32[]{:S(2)}, u32[]{:S(2)}) collective-permute-start(bf16[512,1280]{1,0:T(8,128)(2,1)} %get-tuple-element.91), channel_id=1, source_target_pairs={{0,8},{4,12},{8,16},{12,20},{16,24},{20,28},{1,9},{5,13},{9,17},{1... | collective-permute-start | bytes 3932168 | tf_op jit(solution)/shard_map/ppermute | solution.py:1530
  364.2 26.8 %copy-start.8 = (f32[2640]{0:T(1024)S(1)}, f32[2640]{0:T(1024)}, u32[]{:S(2)}) copy-start(f32[2640]{0:T(1024)} %param.34) | copy-start | bytes 31684
  364.2 26.9 %copy-start.9 = (f32[2640]{0:T(1024)S(1)}, f32[2640]{0:T(1024)}, u32[]{:S(2)}) copy-start(f32[2640]{0:T(1024)} %param.35) | copy-start | bytes 31684
  364.2 27.6 %copy-start = (bf16[1,512,1280]{2,1,0:T(8,128)(2,1)S(1)}, bf16[1,512,1280]{2,1,0:T(8,128)(2,1)}, u32[]{:S(2)}) copy-start(bf16[1,512,1280]{2,1,0:T(8,128)(2,1)} %param.18) | copy-start | bytes 3932164
  364.2 27.6 %copy-start.1 = (f32[512,1280]{1,0:T(8,128)S(1)}, f32[512,1280]{1,0:T(8,128)}, u32[]{:S(2)}) copy-start(f32[512,1280]{1,0:T(8,128)} %get-tuple-element.93.dmid_ref) | copy-start | bytes 7864324
  364.2 27.6 %copy-start.2 = (bf16[512,1280]{1,0:T(8,128)(2,1)S(1)}, bf16[512,1280]{1,0:T(8,128)(2,1)}, u32[]{:S(2)}) copy-start(bf16[512,1280]{1,0:T(8,128)(2,1)} %get-tuple-element.94.layer_ref) | copy-start | bytes 3932164
  364.2 27.6 %copy-start.3 = (bf16[512,1280]{1,0:T(8,128)(2,1)S(1)}, bf16[512,1280]{1,0:T(8,128)(2,1)}, u32[]{:S(2)}) copy-start(bf16[512,1280]{1,0:T(8,128)(2,1)} %get-tuple-element.92.own_ref) | copy-start | bytes 3932164

commit v13 on v12

--- a/solution.py
+++ b/solution.py
@@ -506,7 +506,12 @@
                 )
                 return inner
 
-            lax.fori_loop(0, jnp.minimum(tile, prompt_tiles), full, 0)
+            def double(pair, inner):
+                return full(2 * pair + 1, full(2 * pair, inner))
+
+            count = jnp.minimum(tile, prompt_tiles)
+            lax.fori_loop(0, count // 2, double, 0)
+            lax.fori_loop(count // 2 * 2, count, full, 0)
             for part in range(TILE // BLOCK):
                 block = block_at(slot_ref[tile * (TILE // BLOCK) + part])
                 step(
@@ -632,7 +637,12 @@
             )
             return inner
 
-        lax.fori_loop(0, jnp.minimum(tile, prompt_tiles), full, 0)
+        def double(pair, inner):
+            return full(2 * pair + 1, full(2 * pair, inner))
+
+        count = jnp.minimum(tile, prompt_tiles)
+        lax.fori_loop(0, count // 2, double, 0)
+        lax.fori_loop(count // 2 * 2, count, full, 0)
         for part in range(TILE // BLOCK):
             position = tile * (TILE // BLOCK) + part
             block = block_at(slot_ref[position])

time: 395 us -> 401 us (1.015); the launches traced: 395 us -> 394 us
  no operation moved by 1% of the time
where the time goes in v13:
time: 401 us; the launch traced here: 394 us
  Pallas kernels  372 us (93%)
  starting transfers between devices  9.56 us (2%)
  waiting for transfers between devices  5.31 us (1%)
    pallas_call x1, Pallas kernels, gather_rows(): pl.pallas_call(functools.partial(gather_kernel, parts, groups, heads), na...  105 us
    pallas_call x1, Pallas kernels, reduce_gradients(): pl.pallas_call(functools.partial(reduce_kernel, parts, groups), name='red...  104 us
    pallas_call x1, Pallas kernels, middle(): pl.pallas_call(functools.partial(middle_kernel, parts, groups), name='mid...  62.6 us
    pallas_call x1, Pallas kernels, attention_backward(): pl.pallas_call(functools.partial(backward_kernel, heads), name='attention...  47.8 us
    pallas_call x1, Pallas kernels, update(): pl.pallas_call(functools.partial(update_kernel, rates), name='update_weig...  26.7 us
    pallas_call x1, Pallas kernels, attention_forward(): pl.pallas_call(functools.partial(forward_kernel, heads), name='attention_...  22.7 us
  transfers between devices with their start and end apart: 5, of which 2 were waited for; matrix products, arithmetic and copies ran while one was open for 1% of the time, Pallas kernels for 19%

profile of v13, /device:TPU:0, one launch (start us, length us, event | category | flops | bytes accessed | tf_op | source)
XLA Modules:
  0.0 393.6 jit_solution(8775676908494103732)
XLA Ops:
  0.7 0.7 slice.15
  1.4 0.6 broadcast_in_dim.12.gain_ref
  2.0 105.4 %gather_rows.1 = (bf16[8,512,1280]{2,1,0:T(8,128)(2,1)}, bf16[3,4,2,160,1280]{4,3,2,1,0:T(8,128)(2,1)}, bf16[2,480,1280]{2,1,0:T(8,128)(2,1)}, bf16[2,128,4096]{...) custom-call(bf16[512,1280]{1,0:T(8,128)(2,1)} %bitcast.17, ...), custom_call_target="tpu_custom_call" | custom-call | tf_op jit(solution)/shard_map/gather_rows/pallas_call | solution.py:389
  107.4 22.7 %attention_forward.1 = (f32[2,1,4096]{2,1,0:T(1,128)}, bf16[8,160,512]{2,1,0:T(8,128)(2,1)}) custom-call(s32[16]{0:T(128)} %bitcast.28, f32[8,256]{1,0:T(8,128)} %get-tuple-element.73.most_ref, bf16[2,128,4096]{2,1,0:T(8,128)(2,1)} %get-tuple-element.69.qt_ref, bf16[2,4096,128]{2,1,0:T(8,128)(2,1)} %get-tuple-element.71.kn_in_ref, ...), custom_call_target="tpu_custom_call" | custom-call | flops 17179869184 | bytes 5242880 | tf_op jit(solution)/shard_map/attention_forward/pallas_call | solution.py:699
  130.1 62.6 %middle.1 = (bf16[512,1280]{1,0:T(8,128)(2,1)}, f32[512,1280]{1,0:T(8,128)}, bf16[8,160,512]{2,1,0:T(8,128)(2,1)}, f32[1,1280]{1,0:T(1,128)}, bf16[3,160,1280]{2...) custom-call(bf16[8,160,512]{2,1,0:T(8,128)(2,1)} %get-tuple-element., ...), custom_call_target="tpu_custom_call" | custom-call | tf_op jit(solution)/shard_map/middle/pallas_call | solution.py:936
  192.7 1.8 collective-permute-start
  194.5 0.8 collective-permute-start.1
  195.3 1.0 collective-permute-start.2
  196.4 47.8 %attention_backward.1 = (bf16[8,480,512]{2,1,0:T(8,128)(2,1)}, f32[1,128]{1,0:T(1,128)}) custom-call(s32[16]{0:T(128)} %bitcast.29, bf16[2,128,4096]{2,1,0:T(8,128)(2,1)} %get-tuple-element.69.qt_ref, bf16[2,80,4096]{2,1,0:T(8,128)(2,1)} %get-tuple-element.70.kt_in_ref, bf16[2,4096,128]{2,1,0:T(8,128)(2,1)} %get-tuple-element.71.kn_in_ref, ...), custom_call_target="tpu_custom_call" | custom-call | flops 42949672960 | bytes 5242880 | tf_op jit(solution)/shard_map/attention_backward/pallas_call | solution.py:733
  244.2 0.0 copy-done.7
  244.2 0.1 reduce.1
  244.3 0.0 copy-done.10
  244.4 0.0 copy-done.6
  244.4 0.7 divide_multiply_fusion
  245.0 0.6 fusion.1.small_ref
  245.7 0.0 collective-permute-done.refs_1_
  245.7 5.1 %collective-permute-done.1.refs_2_ = bf16[3,160,1280]{2,1,0:T(8,128)(2,1)S(1)} collective-permute-done((bf16[3,160,1280]{2,1,0:T(8,128)(2,1)}, bf16[3,160,1280]{2,1,0:T(8,128)(2,1)S(1)}, u32[]{:S(2)}, u32[]{:S(2)}) %collective-permute-start.1) | collective-permute-done | bytes 1228832 | tf_op jit(solution)/shard_map/ppermute | solution.py:1517
  250.7 0.0 collective-permute-done.2.refs_3_
  250.7 0.0 copy-done.4
  250.7 1.0 copy-done.5
  251.8 104.2 %reduce_gradients.1 = (bf16[512,1280]{1,0:T(8,128)(2,1)}, bf16[512,1280]{1,0:T(8,128)(2,1)}, bf16[512,1280]{1,0:T(8,128)(2,1)}, bf16[8,320,480]{2,1,0:T(8,128)(2...) custom-call(bf16[4,2,480,512]{3,2,1,0:T(8,128)(2,1)} %bitcast.21, ...), custom_call_target="tpu_custom_call" | custom-call | tf_op jit(solution)/shard_map/reduce_gradients/pallas_call | solution.py:1312
  356.0 1.3 collective-permute-start.3
  357.3 4.6 %collective-permute-start.4 = (bf16[512,1280]{1,0:T(8,128)(2,1)}, bf16[512,1280]{1,0:T(8,128)(2,1)S(1)}, u32[]{:S(2)}, u32[]{:S(2)}) collective-permute-start(bf16[512,1280]{1,0:T(8,128)(2,1)} %get-tuple-element.91), channel_id=1, source_target_pairs={{0,8},{4,12},{8,16},{12,20},{16,24},{20,28},{1,9},{5,13},{9,17},{1... | collective-permute-start | bytes 3932168 | tf_op jit(solution)/shard_map/ppermute | solution.py:1540
  361.9 0.8 copy.41
  362.7 0.1 reshape.61
  362.8 26.7 %update_weights.1 = (f32[320,3840]{1,0:T(8,128)}, f32[320,3840]{1,0:T(8,128)}, f32[320,3840]{1,0:T(8,128)}, bf16[320,3840]{1,0:T(8,128)(2,1)}, f32[320,1280]{1,0...) custom-call(bf16[8,320,480]{2,1,0:T(8,128)(2,1)} %get-tuple-element., ...), custom_call_target="tpu_custom_call" | custom-call | flops 68812800 | bytes 68812800 | tf_op jit(solution)/shard_map/update_weights/pallas_call | solution.py:1414
  389.5 0.6 multiply_subtract_fusion
  390.1 0.0 collective-permute-done.3.down_ref
  390.1 0.2 collective-permute-done.4.up_ref
  390.4 0.0 copy-done.1
  390.4 0.0 copy-done.3
  390.4 2.7 finish.1
  (19 shorter events, 0.1 us)
Async XLA Ops:
  192.7 52.9 %collective-permute-start = (bf16[3,160,1280]{2,1,0:T(8,128)(2,1)}, bf16[3,160,1280]{2,1,0:T(8,128)(2,1)S(1)}, u32[]{:S(2)}, u32[]{:S(2)}) collective-permute-start(bf16[3,160,1280]{2,1,0:T(8,128)(2,1)} %get-tuple-element.87), channel_id=1, source_target_pairs={{0,1},{1,0},{2,3},{3,2},{4,5},{5,4},{6,7},{7,6},{8,9},{9,8},{10,11... | collective-permute-start | bytes 3686408 | tf_op jit(solution)/shard_map/ppermute | solution.py:1517
  194.5 56.2 %collective-permute-start.1 = (bf16[3,160,1280]{2,1,0:T(8,128)(2,1)}, bf16[3,160,1280]{2,1,0:T(8,128)(2,1)S(1)}, u32[]{:S(2)}, u32[]{:S(2)}) collective-permute-start(bf16[3,160,1280]{2,1,0:T(8,128)(2,1)} %get-tuple-element.88), channel_id=1, source_target_pairs={{0,2},{1,3},{2,0},{3,1},{4,6},{5,7},{6,4},{7,5},{8,10},{9,11},{10,... | collective-permute-start | bytes 3686408 | tf_op jit(solution)/shard_map/ppermute | solution.py:1517
  195.3 55.4 %collective-permute-start.2 = (bf16[3,160,1280]{2,1,0:T(8,128)(2,1)}, bf16[3,160,1280]{2,1,0:T(8,128)(2,1)}, u32[]{:S(2)}, u32[]{:S(2)}) collective-permute-start(bf16[3,160,1280]{2,1,0:T(8,128)(2,1)} %get-tuple-element.89), channel_id=1, source_target_pairs={{0,3},{1,2},{2,1},{3,0},{4,7},{5,6},{6,5},{7,4},{8,11},{9,10},{10,... | collective-permute-start | bytes 3686408 | tf_op jit(solution)/shard_map/ppermute | solution.py:1517
  196.4 47.8 %copy-start.7 = (f32[80,1]{1,0:T(8,128)S(1)}, f32[80,1]{1,0:T(8,128)}, u32[]{:S(2)}) copy-start(f32[80,1]{1,0:T(8,128)} %get-tuple-element.79.factor_ref) | copy-start | bytes 964
  196.4 48.0 %copy-start.10 = (f32[1,1280]{1,0:T(1,128)S(1)}, f32[1,1280]{1,0:T(1,128)}, u32[]{:S(2)}) copy-start(f32[1,1280]{1,0:T(1,128)} %get-tuple-element.84) | copy-start | bytes 15364
  196.4 48.0 %copy-start.6 = (f32[2640]{0:T(1024)S(1)}, f32[2640]{0:T(1024)}, u32[]{:S(2)}) copy-start(f32[2640]{0:T(1024)} %small_ref.1) | copy-start | bytes 31684
  245.7 5.1 %copy-start.4 = (bf16[3,160,1280]{2,1,0:T(8,128)(2,1)}, bf16[3,160,1280]{2,1,0:T(8,128)(2,1)S(1)}, u32[]{:S(2)}) copy-start(bf16[3,160,1280]{2,1,0:T(8,128)(2,1)S(1)} %collective-permute-done.refs_1_) | copy-start | bytes 3686404
  250.7 1.0 copy-start.5
  356.0 34.2 %collective-permute-start.3 = (bf16[512,1280]{1,0:T(8,128)(2,1)}, bf16[512,1280]{1,0:T(8,128)(2,1)S(1)}, u32[]{:S(2)}, u32[]{:S(2)}) collective-permute-start(bf16[512,1280]{1,0:T(8,128)(2,1)} %get-tuple-element.90), channel_id=1, source_target_pairs={{8,0},{12,4},{16,8},{20,12},{24,16},{28,20},{9,1},{13,5},{17,9},{2... | collective-permute-start | bytes 3932168 | tf_op jit(solution)/shard_map/ppermute | solution.py:1539
  357.3 33.1 %collective-permute-start.4 = (bf16[512,1280]{1,0:T(8,128)(2,1)}, bf16[512,1280]{1,0:T(8,128)(2,1)S(1)}, u32[]{:S(2)}, u32[]{:S(2)}) collective-permute-start(bf16[512,1280]{1,0:T(8,128)(2,1)} %get-tuple-element.91), channel_id=1, source_target_pairs={{0,8},{4,12},{8,16},{12,20},{16,24},{20,28},{1,9},{5,13},{9,17},{1... | collective-permute-start | bytes 3932168 | tf_op jit(solution)/shard_map/ppermute | solution.py:1540
  362.8 26.7 %copy-start.8 = (f32[2640]{0:T(1024)S(1)}, f32[2640]{0:T(1024)}, u32[]{:S(2)}) copy-start(f32[2640]{0:T(1024)} %param.34) | copy-start | bytes 31684
  362.8 26.7 %copy-start.9 = (f32[2640]{0:T(1024)S(1)}, f32[2640]{0:T(1024)}, u32[]{:S(2)}) copy-start(f32[2640]{0:T(1024)} %param.35) | copy-start | bytes 31684
  362.8 27.6 %copy-start = (bf16[1,512,1280]{2,1,0:T(8,128)(2,1)S(1)}, bf16[1,512,1280]{2,1,0:T(8,128)(2,1)}, u32[]{:S(2)}) copy-start(bf16[1,512,1280]{2,1,0:T(8,128)(2,1)} %param.18) | copy-start | bytes 3932164
  362.8 27.6 %copy-start.1 = (f32[512,1280]{1,0:T(8,128)S(1)}, f32[512,1280]{1,0:T(8,128)}, u32[]{:S(2)}) copy-start(f32[512,1280]{1,0:T(8,128)} %get-tuple-element.93.dmid_ref) | copy-start | bytes 7864324
  362.8 27.6 %copy-start.2 = (bf16[512,1280]{1,0:T(8,128)(2,1)S(1)}, bf16[512,1280]{1,0:T(8,128)(2,1)}, u32[]{:S(2)}) copy-start(bf16[512,1280]{1,0:T(8,128)(2,1)} %get-tuple-element.94.layer_ref) | copy-start | bytes 3932164
  362.8 27.6 %copy-start.3 = (bf16[512,1280]{1,0:T(8,128)(2,1)S(1)}, bf16[512,1280]{1,0:T(8,128)(2,1)}, u32[]{:S(2)}) copy-start(bf16[512,1280]{1,0:T(8,128)(2,1)} %get-tuple-element.92.own_ref) | copy-start | bytes 3932164
